TPU v7x, 32 devices: a whole 2x2x4 slice. The times are simulated.
32 devices in a mesh: seq: 4 (over z), clus: 8 (over y, x, core).
Axes of the slice: x: 2, y: 2, z: 4, core: 2. Of those that a mesh axis runs over, the one named last changes fastest.
Arguments:
- node_feats: bfloat16 [8, 512, 1024], P('clus', 'seq'), may hold values from -24 to 24
- qkv_weight: bfloat16 [3072, 1024], P('seq'), may hold values from -1 to 1
- block_pairs: int32 [8, 8, 2], P('clus'), may hold values from 0 to 3, as said below
- grad_out: bfloat16 [8, 512, 1024], P('clus', 'seq'), may hold values from -6 to 6
Outputs:
- attended: bfloat16 [8, 512, 1024], P('clus', 'seq')
- node_grad: bfloat16 [8, 512, 1024], P('clus', 'seq')
- weight_grad: float32 [3072, 1024], P('seq')
Inputs may be any that keep to these rules, and one draw needn't show every extreme that they name: `block_pairs`: each cluster's list holds 8 distinct pairs, among them (b, b) for every block b.
All inputs are finite; a program needn't handle non-finite values.
Results may differ from a plain program's by a relative error of at most 0.023.
Values may be sent and summed in bfloat16 or wider, within the bound.
No kernel may reach another device: no remote copies, remote signals or barrier semaphores. Data moves between devices by JAX's collectives and lax.ppermute only.
A program may use at most 64 MiB of HBM per device.

v0:
```python
import math

import jax
import jax.numpy as jnp
from jax import lax
from jax.sharding import PartitionSpec as P

HD = 64
BLOCK = 128


def block_allowed(listed, blocks):
    block_ids = jnp.arange(blocks, dtype=jnp.int32)[None, :]
    row_hot = (listed[:, 0:1] == block_ids).astype(jnp.float32)
    col_hot = (listed[:, 1:2] == block_ids).astype(jnp.float32)
    counts = jnp.dot(row_hot.T, col_hot, precision=lax.Precision.HIGHEST)
    return counts > 0.5


def expand_rows(allowed_blocks, offset, row_span):
    picked = lax.dynamic_slice_in_dim(allowed_blocks, offset // BLOCK, row_span // BLOCK, 0)
    return jnp.repeat(jnp.repeat(picked, BLOCK, axis=0), BLOCK, axis=1)


def softmax_rows(query_rows, keys_all, allowed_rows):
    scores = jnp.einsum(
        "qhe,khe->hqk", query_rows, keys_all, preferred_element_type=jnp.float32
    ) * HD ** (-0.5)
    scores = jnp.where(allowed_rows[None], scores, -jnp.inf)
    row_max = jnp.max(scores, axis=-1, keepdims=True)
    unnorm = jnp.where(allowed_rows[None], jnp.exp(scores - row_max), 0.0)
    return unnorm / jnp.sum(unnorm, axis=-1, keepdims=True)


def local(node_feats, qkv_weight, block_pairs, grad_out):
    features = node_feats[0]
    rows_dev = features.shape[0]
    node_count = rows_dev * lax.axis_size("seq")
    columns = qkv_weight.shape[0]
    heads_dev = columns // (3 * HD)
    row_span = math.gcd(node_count, 512)
    offsets = jnp.arange(node_count // row_span, dtype=jnp.int32) * row_span
    projected = lax.dot_general(
        lax.all_gather(features, "seq", axis=0, tiled=True),
        qkv_weight,
        (((1,), (1,)), ((), ())),
        preferred_element_type=jnp.float32,
    ).astype(jnp.bfloat16)
    grouped = projected.reshape(node_count, heads_dev, 3, HD)
    queries = grouped[:, :, 0]
    keys_all = grouped[:, :, 1]
    values_all = grouped[:, :, 2]
    allowed_blocks = block_allowed(block_pairs[0], node_count // BLOCK)

    def forward_block(offset):
        query_rows = lax.dynamic_slice_in_dim(queries, offset, row_span, 0)
        weights = softmax_rows(query_rows, keys_all, expand_rows(allowed_blocks, offset, row_span))
        return jnp.einsum(
            "hqk,khe->qhe",
            weights.astype(jnp.bfloat16),
            values_all,
            preferred_element_type=jnp.float32,
        ).astype(jnp.bfloat16)

    head_out = lax.map(forward_block, offsets).reshape(node_count, heads_dev * HD)
    attended = lax.all_to_all(head_out, "seq", split_axis=0, concat_axis=1, tiled=True)
    upstream = lax.all_to_all(grad_out[0], "seq", split_axis=1, concat_axis=0, tiled=True).reshape(
        node_count, heads_dev, HD
    )

    def backward_block(state_pair, offset):
        grad_keys, grad_values = state_pair
        query_rows = lax.dynamic_slice_in_dim(queries, offset, row_span, 0)
        grad_rows = lax.dynamic_slice_in_dim(upstream, offset, row_span, 0)
        weights = softmax_rows(query_rows, keys_all, expand_rows(allowed_blocks, offset, row_span))
        weights_low = weights.astype(jnp.bfloat16)
        grad_weights = jnp.einsum(
            "qhe,khe->hqk", grad_rows, values_all, preferred_element_type=jnp.float32
        )
        row_delta = jnp.sum(weights * grad_weights, axis=-1, keepdims=True)
        grad_scores = (weights * (grad_weights - row_delta) * HD ** (-0.5)).astype(jnp.bfloat16)
        grad_query = jnp.einsum(
            "hqk,khe->qhe", grad_scores, keys_all, preferred_element_type=jnp.float32
        ).astype(jnp.bfloat16)
        grad_keys = grad_keys + jnp.einsum(
            "hqk,qhe->khe", grad_scores, query_rows, preferred_element_type=jnp.float32
        )
        grad_values = grad_values + jnp.einsum(
            "hqk,qhe->khe", weights_low, grad_rows, preferred_element_type=jnp.float32
        )
        return ((grad_keys, grad_values), grad_query)

    zeros_acc = jnp.zeros((node_count, heads_dev, HD), jnp.float32)
    sums_pair, grad_query = lax.scan(backward_block, (zeros_acc, zeros_acc), offsets)
    grad_query = grad_query.reshape(node_count, heads_dev, HD)
    grad_proj = jnp.stack(
        [grad_query, sums_pair[0].astype(jnp.bfloat16), sums_pair[1].astype(jnp.bfloat16)], axis=2
    ).reshape(node_count, columns)
    rows_part = grad_proj
    node_grad = lax.psum_scatter(
        jnp.dot(rows_part, qkv_weight, preferred_element_type=jnp.float32).astype(jnp.bfloat16),
        "seq",
        scatter_dimension=0,
        tiled=True,
    )
    rows_part = grad_proj
    local_sum = lax.dot_general(
        rows_part,
        lax.all_gather(features, "seq", axis=0, tiled=True),
        (((0,), (0,)), ((), ())),
        preferred_element_type=jnp.float32,
    )
    weight_grad = lax.psum(local_sum.astype(jnp.bfloat16), "clus").astype(
        jnp.float32
    ) / lax.axis_size("clus")
    return (attended[None], node_grad[None], weight_grad)


def solution(mesh):
    return jax.shard_map(
        local,
        mesh=mesh,
        in_specs=(
            P("clus", "seq", None),
            P("seq", None),
            P("clus", None, None),
            P("clus", "seq", None),
        ),
        out_specs=(P("clus", "seq", None), P("clus", "seq", None), P("seq", None)),
        check_vma=False,
    )
```

profile of v0, /device:TPU:0, one launch (start us, length us, event | category | flops | bytes accessed | tf_op | source)
XLA Modules:
  0.0 166.1 jit_solution(3526616718626040523)
XLA Ops:
  7.2 0.0 copy-start
  7.2 0.0 all-gather.3.cloned.1.call-start
  7.2 0.7 all-gather.3.cloned.1.call-update
  7.9 1.8 %copy.36 = bf16[1,128,1024]{1,2,0:T(8,128)(2,1)} copy(bf16[1,128,1024]{2,1,0:T(8,128)(2,1)} %param.7) | data formatting | bytes 524288 | tf_op args[3]
  9.7 6.3 %all-to-all-start.1 = ((bf16[128,4,256]{0,2,1:T(8,128)(2,1)}), bf16[128,4,256]{0,2,1:T(8,128)(2,1)S(1)}, u32[]{:S(2)}, u32[]{:S(2)}) async-start(bf16[128,4,256]{0,2,1:T(8,128)(2,1)} %bitcast.12), calls=%async_computation.1 | async-start | bytes 524288 | tf_op jit(solution)/shard_map/all_to_all | solution.py:67
  16.0 0.0 all-reduce.2.cloned.1.call-start
  16.0 0.8 slice_bitcast_fusion.18
  16.8 0.3 convolution_compare_fusion
  17.0 0.1 copy.31
  17.2 0.1 broadcast_bitcast_fusion
  17.2 11.0 %all-to-all-done.1 = bf16[128,4,256]{0,2,1:T(8,128)(2,1)S(1)} async-done(((bf16[128,4,256]{0,2,1:T(8,128)(2,1)}), bf16[128,4,256]{0,2,1:T(8,128)(2,1)S(1)}, u32[]{:S(2)}, u32[]{:S(2)}) %all-to-all-start.1) | async-done | bytes 262176 | tf_op jit(solution)/shard_map/all_to_all | solution.py:67
  28.3 0.2 copy.37
  28.5 0.1 reshape.46
  28.6 13.6 %all-gather.3.cloned.1.call-done = bf16[1,512,1024]{2,1,0:T(8,128)(2,1)} async-done(((bf16[1,128,1024]{2,1,0:T(8,128)(2,1)}), bf16[1,512,1024]{2,1,0:T(8,128)(2,1)}) %all-gather.3.cloned.1.call-update) | async-done | bytes 1048592 | tf_op jit(solution)/shard_map/all_gather | solution.py:44
  42.2 0.0 copy-done
  42.2 2.2 %convolution_convert_fusion.2 = bf16[512,768]{1,0:T(8,128)(2,1)S(1)} fusion(bf16[768,1024]{1,0:T(8,128)(2,1)S(1)} %copy-done, bf16[1,512,1024]{2,1,0:T(8,128)(2,1)} %all-gather.3.cloned.1.call-done), kind=kOutput, calls=%fused_computation.20 | convolution fusion | flops 805699584 | bytes 3407872 | tf_op jit(solution)/shard_map/dot_general | solution.py:43
  44.4 0.3 copy.29
  44.7 0.1 broadcast_in_dim.74
  44.8 3.9 %fusion.34 = (f32[4,512]{1,0:T(4,128)S(1)}, f32[4,512,512]{1,2,0:T(8,128)}) fusion(pred[512,512]{0,1:T(8,128)(4,1)S(1)} %bitcast.129, bf16[512,4,3,64]{0,3,2,1:T(8,128)(2,1)S(1)} %bitcast.120), kind=kOutput, calls=%fused_computation.55 | convolution fusion | flops 139461120 | bytes 5251072 | tf_op jit(solution)/shard_map/while/body/eval_jaxpr/sub | solution.py:31
  48.7 2.7 %fusion.24 = f32[4,512,512]{2,1,0:T(8,128)} fusion(bf16[512,4,64]{0,2,1:T(8,128)(2,1)S(1)} %reshape.46, bf16[512,4,3,64]{0,3,2,1:T(8,128)(2,1)S(1)} %bitcast.121), kind=kOutput, calls=%fused_computation.39 | convolution fusion | flops 134217728 | bytes 4718592 | tf_op jit(solution)/shard_map/while/body/eval_jaxpr/qhe,khe->hqk/dot_general | solution.py:77
  51.4 7.7 %fusion.17 = bf16[512,4,1,64]{0,3,1,2:T(8,128)(2,1)S(1)} fusion(f32[4,512,512]{2,1,0:T(8,128)} %fusion.24, bf16[512,4,3,64]{0,3,2,1:T(8,128)(2,1)S(1)} %bitcast.122, f32[4,512,512]{1,2,0:T(8,128)} %get-tuple-element.45, f32[4,512]{1,0:T(4,128)S(1)} %get-tuple-element.44), kind=kOutput, calls=%fused_computation.28 | convolution fusion | flops 141691392 | bytes 17317888 | tf_op jit(solution)/shard_map/while/body/eval_jaxpr/hqk,khe->qhe/dot_general | solution.py:82
  59.0 7.4 %fusion.16 = bf16[512,4,1,64]{0,3,1,2:T(8,128)(2,1)S(1)} fusion(f32[4,512,512]{2,1,0:T(8,128)} %fusion.24, bf16[512,4,3,64]{0,3,2,1:T(8,128)(2,1)S(1)} %bitcast.123, f32[4,512,512]{1,2,0:T(8,128)} %get-tuple-element.45, f32[4,512]{1,0:T(4,128)S(1)} %get-tuple-element.44), kind=kOutput, calls=%fused_computation.27 | convolution fusion | flops 141691392 | bytes 17317888 | tf_op jit(solution)/shard_map/while/body/eval_jaxpr/hqk,qhe->khe/dot_general | solution.py:85
  66.4 0.0 copy-start.1
  66.4 3.0 %fusion.15 = bf16[512,4,1,64]{0,3,1,2:T(8,128)(2,1)S(1)} fusion(bf16[512,4,64]{0,2,1:T(8,128)(2,1)S(1)} %reshape.46, f32[4,512,512]{1,2,0:T(8,128)} %get-tuple-element.45, f32[4,512]{1,0:T(4,128)S(1)} %get-tuple-element.44), kind=kOutput, calls=%fused_computation.26 | convolution fusion | flops 136445952 | bytes 4726784 | tf_op jit(solution)/shard_map/while/body/eval_jaxpr/hqk,qhe->khe/dot_general | solution.py:88
  69.5 0.1 pad_maximum_fusion
  69.6 0.1 copy.41
  69.7 0.0 copy-done.1
  69.7 2.1 %convolution_convert_fusion = bf16[768,1024]{1,0:T(8,128)(2,1)} fusion(bf16[512,768]{0,1:T(8,128)(2,1)S(1)} %bitcast.127, bf16[1,512,1024]{2,1,0:T(8,128)(2,1)S(1)} %copy-done.1), kind=kOutput, calls=%fused_computation.18 | convolution fusion | flops 806092800 | bytes 3407872 | tf_op jit(solution)/shard_map/dot_general | solution.py:107
  71.8 0.0 all-reduce.2.cloned.1.call-update
  71.8 0.0 reduce-scatter.2.cloned.1.call-start
  71.9 2.0 %convolution_convert_fusion.1 = bf16[512,1024]{1,0:T(8,128)(2,1)} fusion(bf16[512,768]{0,1:T(8,128)(2,1)S(1)} %bitcast.128, bf16[768,1024]{1,0:T(8,128)(2,1)S(1)} %copy-done), kind=kOutput, calls=%fused_computation.19 | convolution fusion | flops 805830656 | bytes 3407872 | tf_op jit(solution)/shard_map/dot_general | solution.py:101
  73.9 0.0 reduce-scatter.2.cloned.1.call-update
  73.9 2.7 %fusion.14 = bf16[512,4,64]{0,2,1:T(8,128)(2,1)S(1)} fusion(bf16[512,4,3,64]{0,3,2,1:T(8,128)(2,1)S(1)} %bitcast.124, f32[4,512,512]{1,2,0:T(8,128)} %get-tuple-element.45, f32[4,512]{1,0:T(4,128)S(1)} %get-tuple-element.44), kind=kOutput, calls=%fused_computation.25 | convolution fusion | flops 136445952 | bytes 4726784 | tf_op jit(solution)/shard_map/while/body/eval_jaxpr/hqk,khe->qhe/dot_general | solution.py:58
  76.6 0.1 all_to_all.24
  76.7 11.8 %all_to_all.32 = bf16[4,128,256]{1,2,0:T(8,128)(2,1)S(1)} all-to-all(bf16[4,128,256]{1,2,0:T(8,128)(2,1)S(1)} %copy.35), channel_id=1, replica_groups=mesh['seq'=4,'clus'=8] {'seq'}, dimensions={0} | all-to-all | bytes 524288 | tf_op jit(solution)/shard_map/all_to_all | solution.py:66
  88.5 0.8 copy.42
  89.3 40.8 %all-reduce.2.cloned.1.call-done = bf16[768,1024]{1,0:T(8,128)(2,1)} async-done(((bf16[768,1024]{1,0:T(8,128)(2,1)}), bf16[768,1024]{1,0:T(8,128)(2,1)}) %all-reduce.2.cloned.1.call-update) | async-done | bytes 1572880 | tf_op jit(solution)/shard_map/psum | solution.py:113
  130.1 3.5 %convert_multiply_fusion = f32[768,1024]{1,0:T(8,128)} fusion(bf16[768,1024]{1,0:T(8,128)(2,1)} %all-reduce.2.cloned.1.call-done), kind=kLoop, calls=%fused_computation.10 | loop fusion | flops 1572864 | bytes 4718592 | tf_op jit(solution)/shard_map/div | solution.py:113
  133.6 26.0 %reduce-scatter.2.cloned.1.call-done = bf16[128,1024]{1,0:T(8,128)(2,1)} async-done(((bf16[512,1024]{1,0:T(8,128)(2,1)}), bf16[128,1024]{1,0:T(8,128)(2,1)}) %reduce-scatter.2.cloned.1.call-update) | async-done | bytes 262160 | tf_op jit(solution)/shard_map/reduce_scatter | solution.py:100
  (2 shorter events, 0.0 us)
Async XLA Ops:
  7.2 35.0 %copy-start = (bf16[768,1024]{1,0:T(8,128)(2,1)S(1)}, bf16[768,1024]{1,0:T(8,128)(2,1)}, u32[]{:S(2)}) copy-start(bf16[768,1024]{1,0:T(8,128)(2,1)} %param.5) | copy-start | bytes 4718596
  7.2 35.0 %all-gather.3.cloned.1.call-start = ((), (), s32[]{:S(2)}) async-start(), calls=%async_computation.5 | async-start | bytes 1310720 | tf_op jit(solution)/shard_map/all_gather | solution.py:44
  9.7 18.6 %all-to-all-start.1 = ((bf16[128,4,256]{0,2,1:T(8,128)(2,1)}), bf16[128,4,256]{0,2,1:T(8,128)(2,1)S(1)}, u32[]{:S(2)}, u32[]{:S(2)}) async-start(bf16[128,4,256]{0,2,1:T(8,128)(2,1)} %bitcast.12), calls=%async_computation.1 | async-start | bytes 524288 | tf_op jit(solution)/shard_map/all_to_all | solution.py:67
  16.0 114.0 %all-reduce.2.cloned.1.call-start = ((), (), s32[]{:S(2)}) async-start(), calls=%async_computation.4 | async-start | bytes 3145728 | tf_op jit(solution)/shard_map/psum | solution.py:113
  66.4 3.2 %copy-start.1 = (bf16[1,512,1024]{2,1,0:T(8,128)(2,1)S(1)}, bf16[1,512,1024]{2,1,0:T(8,128)(2,1)}, u32[]{:S(2)}) copy-start(bf16[1,512,1024]{2,1,0:T(8,128)(2,1)} %all-gather.3.cloned.1.call-done) | copy-start | bytes 3145732
  71.8 87.7 %reduce-scatter.2.cloned.1.call-start = ((), (), s32[]{:S(2)}) async-start(), calls=%async_computation.3 | async-start | bytes 1310720 | tf_op jit(solution)/shard_map/reduce_scatter | solution.py:100
Sparse Core Ops, SparseCore 0:
  9.6 32.5 all-gather.2
  72.0 58.0 all-reduce.1
  133.0 26.4 reduce-scatter.1
where the time goes:
time: 166 us
  waiting for transfers between devices  92.1 us (55%)
  matrix products  34 us (20%)
  between operations  13.8 us (8%)
  blocking collectives  11.8 us (7%)
  starting transfers between devices  6.4 us (4%)
  local copies, waits for them, and re-layouts  4.45 us (3%)
  other arithmetic  3.59 us (2%)
    psum x1, waiting for transfers between devices, local(): lax.psum(local_sum.astype(jnp.bfloat16), 'clus').astype(jnp.float32)  40.8 us
    reduce_scatter x1, waiting for transfers between devices, local(): lax.psum_scatter(jnp.dot(rows_part, qkv_weight, preferred_element_type=jn...  26 us
    all_gather x1, waiting for transfers between devices, local(): lax.all_gather(features, 'seq', axis=0, tiled=True)  13.6 us
    all_to_all x1, blocking collectives, local(): lax.all_to_all(head_out, 'seq', split_axis=0, concat_axis=1, tiled=True)  11.8 us
    all_to_all x1, waiting for transfers between devices, local(): lax.all_to_all(grad_out[0], 'seq', split_axis=1, concat_axis=0, tiled=True)  11 us
    dot_general x1, matrix products, backward_block(): jnp.einsum('hqk,khe->qhe', grad_scores, keys_all, preferred_element_type=...  7.66 us
    dot_general x1, matrix products, backward_block(): jnp.einsum('hqk,qhe->khe', grad_scores, query_rows, preferred_element_typ...  7.38 us
    all_to_all x1, starting transfers between devices, local(): lax.all_to_all(grad_out[0], 'seq', split_axis=1, concat_axis=0, tiled=True)  6.32 us
  transfers between devices with their start and end apart: 4, of which 4 were waited for; matrix products, arithmetic and copies ran while one was open for 7% of the time, Pallas kernels for 0%

commit v1 on v0

v1 whole, which is shorter than its diff:
```python
import functools

import jax
import jax.numpy as jnp
from jax import lax
from jax.experimental import pallas as pl
from jax.experimental.pallas import tpu as pltpu
from jax.sharding import PartitionSpec as P

HD = 64
BLOCK = 128
F32 = jnp.float32
BF16 = jnp.bfloat16
NT = (((1,), (1,)), ((), ()))
TN = (((0,), (0,)), ((), ()))
VMEM = pl.BlockSpec(memory_space=pltpu.VMEM)
SMEM = pl.BlockSpec(memory_space=pltpu.SMEM)


def mm(a, b, dims=(((1,), (0,)), ((), ()))):
    return lax.dot_general(a, b, dims, preferred_element_type=F32)


class Plan:
    def __init__(self, rows, columns, n):
        self.n, self.rows, self.columns = n, rows, columns
        self.nodes = n * rows
        self.heads = columns // (3 * HD)
        self.groups = 2 if self.heads % 2 == 0 else 1
        self.gheads = self.heads // self.groups
        self.per_tile = 2 if self.gheads % 2 == 0 else 1
        self.tiles = self.gheads // self.per_tile
        self.tile = self.per_tile * HD
        self.gcols = self.gheads * 3 * HD
        self.chunk = BLOCK


def attend_group(plan, group, qkv, grads, bias, out_ref, grad_ref, scratch):
    q_s, k_s, v_s, g_s, p_s, ds_s = scratch
    rows, tile, chunk = plan.rows, plan.tile, plan.chunk
    lane = lax.broadcasted_iota(jnp.int32, (1, tile), 1)
    for t in range(plan.tiles):
        base = group * plan.gcols + t * 3 * tile
        gbase = (group * plan.tiles + t) * tile
        if plan.groups > 1:
            base, gbase = pl.multiple_of(base, tile), pl.multiple_of(gbase, tile)
        for s in range(plan.n):
            here = slice(s * rows, (s + 1) * rows)
            q_s[here, :] = qkv[s][:, pl.ds(base, tile)]
            k_s[here, :] = qkv[s][:, pl.ds(base + tile, tile)]
            v_s[here, :] = qkv[s][:, pl.ds(base + 2 * tile, tile)]
            g_s[here, :] = grads[s][:, pl.ds(gbase, tile)]
        grad_keys = grad_values = None
        for h in range(plan.per_tile):
            mine = (lane >= h * HD) & (lane < (h + 1) * HD)

            def only(x):
                return jnp.where(mine, x, jnp.zeros_like(x))

            def one_chunk(i, carry):
                lo = i * chunk if isinstance(i, int) else pl.multiple_of(i * chunk, chunk)
                here = pl.ds(lo, chunk)
                scores = mm(only(q_s[here, :]), k_s[...], NT) * HD ** -0.5
                scores = scores + bias[pl.ds(i, 1), :]
                unnorm = jnp.exp(scores - jnp.max(scores, axis=-1, keepdims=True))
                weights = unnorm / jnp.sum(unnorm, axis=-1, keepdims=True)
                low = weights.astype(BF16)
                out = mm(low, v_s[...])
                grad_weights = mm(only(g_s[here, :]), v_s[...], NT)
                delta = jnp.sum(weights * grad_weights, axis=-1, keepdims=True)
                ds = (weights * (grad_weights - delta) * HD ** -0.5).astype(BF16)
                grad_q = mm(ds, k_s[...])
                p_s[here, :] = low
                ds_s[here, :] = ds
                out, grad_q = out.astype(BF16), grad_q.astype(BF16)
                if h > 0:
                    out = jnp.where(mine, out, out_ref[here, t * tile : (t + 1) * tile])
                    grad_q = jnp.where(
                        mine, grad_q, grad_ref[here, 3 * t * tile : (3 * t + 1) * tile]
                    )
                out_ref[here, t * tile : (t + 1) * tile] = out
                grad_ref[here, 3 * t * tile : (3 * t + 1) * tile] = grad_q
                return carry

            steps = plan.nodes // chunk
            if steps <= 4:
                for i in range(steps):
                    one_chunk(i, 0)
            else:
                lax.fori_loop(0, steps, one_chunk, 0)
            gk = mm(ds_s[...], q_s[...], TN)
            gv = mm(p_s[...], g_s[...], TN)
            grad_keys = gk if h == 0 else jnp.where(mine, gk, grad_keys)
            grad_values = gv if h == 0 else jnp.where(mine, gv, grad_values)
        grad_ref[:, (3 * t + 1) * tile : (3 * t + 2) * tile] = grad_keys.astype(BF16)
        grad_ref[:, (3 * t + 2) * tile : (3 * t + 3) * tile] = grad_values.astype(BF16)


def first_kernel(plan, *refs):
    n = plan.n
    which, qkv, grads, feats = refs[0], refs[1 : 1 + n], refs[1 + n : 1 + 2 * n], refs[1 + 2 * n : 1 + 3 * n]
    bias = refs[1 + 3 * n]
    out_ref, grad_ref, wgrad_ref = refs[2 + 3 * n : 5 + 3 * n]
    scratch = refs[5 + 3 * n :]
    attend_group(plan, which[0], qkv, grads, bias, out_ref, grad_ref, scratch[:6])
    full = scratch[6]
    for s in range(n):
        full[s * plan.rows : (s + 1) * plan.rows, :] = feats[s][...]
    wgrad_ref[...] = mm(grad_ref[...], full[...], TN).astype(BF16)


def second_kernel(plan, *refs):
    n, rows = plan.n, plan.rows
    which, qkv, grads, feats = refs[0], refs[1 : 1 + n], refs[1 + n : 1 + 2 * n], refs[1 + 2 * n : 1 + 3 * n]
    bias, weight = refs[1 + 3 * n : 3 + 3 * n]
    at = 3 + 3 * n
    if plan.groups > 1:
        out_other, grad_other = refs[at : at + 2]
        at += 2
    terms, outs = refs[at : at + n], refs[at + n : at + 2 * n]
    wgrad_ref = refs[at + 2 * n]
    scratch = refs[at + 2 * n + 1 :]
    full, out_ref, grad_ref = scratch[6:9]
    group = which[0] if plan.groups > 1 else 0
    attend_group(plan, group, qkv, grads, bias, out_ref, grad_ref, scratch[:6])
    for s in range(n):
        here = slice(s * rows, (s + 1) * rows)
        full[here, :] = feats[s][...]
        if plan.groups > 1:
            width = plan.gheads * HD
            outs[s][:, pl.ds(pl.multiple_of(group * width, width), width)] = out_ref[here, :]
            other = 1 - group
            outs[s][:, pl.ds(pl.multiple_of(other * width, width), width)] = out_other[here, :]
            gcols = plan.gcols
            term = mm(grad_ref[here, :], weight[pl.ds(pl.multiple_of(group * gcols, gcols), gcols), :])
            term = term + mm(
                grad_other[here, :], weight[pl.ds(pl.multiple_of(other * gcols, gcols), gcols), :]
            )
        else:
            outs[s][...] = out_ref[here, :]
            term = mm(grad_ref[here, :], weight[...])
        terms[s][...] = term.astype(BF16)
    wgrad_ref[...] = mm(grad_ref[...], full[...], TN)


def call(kernel, plan, out_shape, scratch, count, args):
    return pl.pallas_call(
        functools.partial(kernel, plan),
        out_shape=out_shape,
        in_specs=[SMEM] + [VMEM] * (len(args) - 1),
        out_specs=[VMEM] * len(out_shape),
        scratch_shapes=scratch,
        compiler_params=pltpu.CompilerParams(vmem_limit_bytes=50 * 2**20),
        cost_estimate=pl.CostEstimate(flops=count, bytes_accessed=4 << 20, transcendentals=0),
    )(*args)


def swap(x, axis, bits):
    size = lax.axis_size(axis)
    return lax.ppermute(x, axis, [(i, i ^ bits) for i in range(size)])


def add(a, b):
    return (a.astype(F32) + b.astype(F32)).astype(BF16)


def gather_slots(x, z, n):
    if n != 4:
        return [x] + [swap(x, "seq", k) for k in range(1, n)]
    far = swap(x, "seq", 2)
    near = swap(x, "seq", 1)
    middle = lax.ppermute(x, "seq", [(1, 2), (2, 1)])
    ends = lax.ppermute(far, "seq", [(2, 3), (1, 0)])
    inner = (z == 1) | (z == 2)
    return [x, near, far, jnp.where(inner, middle, ends)]


def reduce_slots(terms, z, n):
    if n != 4:
        total = terms[0].astype(F32)
        for k in range(1, n):
            total = total + swap(terms[k], "seq", k).astype(F32)
        return total.astype(BF16)
    inner = (z == 1) | (z == 2)
    ends = lax.ppermute(terms[3], "seq", [(3, 2), (0, 1)])
    middle = lax.ppermute(terms[3], "seq", [(1, 2), (2, 1)])
    near = swap(terms[1], "seq", 1)
    far = swap(jnp.where(inner, add(terms[2], ends), terms[2]), "seq", 2)
    total = terms[0].astype(F32) + near.astype(F32) + far.astype(F32)
    return jnp.where(inner, total + middle.astype(F32), total).astype(BF16)


def sum_pairs(x, bits):
    return add(x, swap(x, "clus", bits))


def local(node_feats, qkv_weight, block_pairs, grad_out):
    feats = node_feats[0]
    rows, width = feats.shape
    n, m = lax.axis_size("seq"), lax.axis_size("clus")
    z, c = lax.axis_index("seq"), lax.axis_index("clus")
    plan = Plan(rows, qkv_weight.shape[0], n)
    nodes, heads = plan.nodes, plan.heads
    core = c % 2

    xs = gather_slots(feats, z, n)
    hcols = heads * HD

    def for_slot(k):
        return lax.dynamic_slice_in_dim(grad_out[0], (z ^ k) * hcols, hcols, 1)

    grads = [for_slot(0)] + [swap(for_slot(k), "seq", k) for k in range(1, n)]

    grouped = (plan.groups, plan.tiles, plan.per_tile, 3, HD, width)
    weight = qkv_weight.reshape(grouped).transpose(0, 1, 3, 2, 4, 5).reshape(plan.columns, width)
    qkv = [mm(x, weight, NT).astype(BF16) for x in xs]

    per_dev = rows // BLOCK
    blocks = nodes // BLOCK
    listed = block_pairs[0]
    place = ((listed // per_dev) ^ z) * per_dev + listed % per_dev
    ids = jnp.arange(blocks, dtype=jnp.int32)
    row_hot = place[:, 0, None, None] == ids[None, :, None]
    col_hot = place[:, 1, None, None] == ids[None, None, :]
    allowed = jnp.any(row_hot & col_hot, axis=0)
    bias = jnp.where(jnp.repeat(allowed, BLOCK, axis=1), 0.0, -jnp.inf).astype(F32)

    flops = 14 * nodes * nodes * HD * plan.gheads + 4 * nodes * plan.gcols * width
    tile_scratch = [pltpu.VMEM((nodes, plan.tile), BF16)] * 4 + [pltpu.VMEM((nodes, nodes), BF16)] * 2
    full = [pltpu.VMEM((nodes, width), BF16)]
    common = [*qkv, *grads, *xs, bias]
    other = []
    if plan.groups > 1:
        out_other, grad_other, wgrad_other = call(
            first_kernel,
            plan,
            [
                jax.ShapeDtypeStruct((nodes, plan.gheads * HD), BF16),
                jax.ShapeDtypeStruct((nodes, plan.gcols), BF16),
                jax.ShapeDtypeStruct((plan.gcols, width), BF16),
            ],
            tile_scratch + full,
            flops,
            [(1 - core).reshape(1), *common],
        )
        other = [out_other, grad_other]
    results = call(
        second_kernel,
        plan,
        [jax.ShapeDtypeStruct((rows, width), BF16)] * n
        + [jax.ShapeDtypeStruct((rows, hcols), BF16)] * n
        + [jax.ShapeDtypeStruct((plan.gcols, width), F32)],
        tile_scratch
        + full
        + [pltpu.VMEM((nodes, plan.gheads * HD), BF16), pltpu.VMEM((nodes, plan.gcols), BF16)],
        flops,
        [core.reshape(1), *common, weight, *other],
    )
    terms, outs, wgrad = results[:n], results[n : 2 * n], results[2 * n]

    if plan.groups > 1:
        part = add(wgrad, swap(wgrad_other, "clus", 1))
    else:
        half = plan.gcols // 2
        keep = lax.dynamic_slice_in_dim(wgrad, core * half, half, 0)
        send = lax.dynamic_slice_in_dim(wgrad, (1 - core) * half, half, 0)
        part = add(keep, swap(send.astype(BF16), "clus", 1))
    half = part.shape[0] // 2
    bits = []
    while 2 << len(bits) < m:
        bits.append(2 << len(bits))
    lower, upper = part[:half], part[half:]
    for one, two in zip(bits, bits[::-1]):
        lower, upper = sum_pairs(lower, one), sum_pairs(upper, two)
    part = jnp.concatenate([lower, upper], axis=0)
    got = swap(part, "clus", 1)
    both = jnp.where(core == 0, jnp.stack([part, got]), jnp.stack([got, part]))
    ungrouped = (plan.groups, plan.tiles, 3, plan.per_tile, HD, width)
    weight_grad = both.reshape(ungrouped).transpose(0, 1, 3, 2, 4, 5).reshape(plan.columns, width)
    weight_grad = weight_grad.astype(F32) / m

    node_grad = reduce_slots(terms, z, n)

    pieces = [outs[0]] + [swap(outs[k], "seq", k) for k in range(1, n)]
    attended = jnp.zeros((rows, n * hcols), BF16)
    for k in range(n):
        attended = lax.dynamic_update_slice_in_dim(attended, pieces[k], (z ^ k) * hcols, 1)
    return (attended[None], node_grad[None], weight_grad)


def solution(mesh):
    return jax.shard_map(
        local,
        mesh=mesh,
        in_specs=(
            P("clus", "seq", None),
            P("seq", None),
            P("clus", None, None),
            P("clus", "seq", None),
        ),
        out_specs=(P("clus", "seq", None), P("clus", "seq", None), P("seq", None)),
        check_vma=False,
    )
```

time: 166 us -> 100 us (0.60)
  waiting for transfers between devices: 92.1 us -> 38.3 us
  matrix products: 34 us -> 4.13 us
  starting transfers between devices: 6.4 us -> 28.4 us
  Pallas kernels: 0 us -> 15.8 us
  between operations: 13.8 us -> 0.91 us
  blocking collectives: 11.8 us -> 0 us
  local copies, waits for them, and re-layouts: 4.45 us -> 6.51 us
  other arithmetic: 3.59 us -> 5.52 us
    psum x1 -> x0, waiting for transfers between devices: 40.8 us -> none  [local(): lax.psum(local_sum.astype(jnp.bfloat16), 'clus').astype(jnp.float32)]
    ppermute x0 -> x20, waiting for transfers between devices: none -> 38.3 us  [the longest x16 29.5 us: swap(): return lax.ppermute(x, axis, [(i, i ^ bits) for i in range(size)])]
    ppermute x0 -> x20, starting transfers between devices: none -> 28.4 us  [the longest x16 24.3 us: swap(): return lax.ppermute(x, axis, [(i, i ^ bits) for i in range(size)])]
    reduce_scatter x1 -> x0, waiting for transfers between devices: 26 us -> none  [local(): lax.psum_scatter(jnp.dot(rows_part, qkv_weight, preferred_element_type=jn...]
    dot_general x9 -> x4, matrix products: 30.1 us -> 4.13 us  [mm(): return lax.dot_general(a, b, dims, preferred_element_type=F32)]
    pallas_call x0 -> x2, Pallas kernels: none -> 15.8 us  [call(): pl.pallas_call(functools.partial(kernel, plan), out_shape=out_shape, in_s...]
    all_gather x1 -> x0, waiting for transfers between devices: 13.6 us -> none  [local(): lax.all_gather(features, 'seq', axis=0, tiled=True)]
    all_to_all x1 -> x0, blocking collectives: 11.8 us -> none  [local(): lax.all_to_all(head_out, 'seq', split_axis=0, concat_axis=1, tiled=True)]
  transfers between devices with their start and end apart: 4 -> 20, of which waited for: 4 -> 9; matrix products, arithmetic and copies ran while one was open for 7% -> 11% of each run, Pallas kernels for 0% -> 10%
where the time goes in v1:
time: 100 us; the launch traced here: 99.6 us
  waiting for transfers between devices  38.3 us (38%)
  starting transfers between devices  28.4 us (28%)
  Pallas kernels  15.8 us (16%)
  local copies, waits for them, and re-layouts  6.51 us (7%)
  other arithmetic  5.52 us (6%)
  matrix products  4.13 us (4%)
    ppermute x16, waiting for transfers between devices, swap(): return lax.ppermute(x, axis, [(i, i ^ bits) for i in range(size)])  29.5 us
    ppermute x16, starting transfers between devices, swap(): return lax.ppermute(x, axis, [(i, i ^ bits) for i in range(size)])  24.3 us
    pallas_call x2, Pallas kernels, call(): pl.pallas_call(functools.partial(kernel, plan), out_shape=out_shape, in_s...  15.8 us
    ppermute x1, waiting for transfers between devices, gather_slots(): ends = lax.ppermute(far, 'seq', [(2, 3), (1, 0)])  8.76 us
    dot_general x4, matrix products, mm(): return lax.dot_general(a, b, dims, preferred_element_type=F32)  4.13 us
    convert_element_type x4, other arithmetic, add(): return (a.astype(F32) + b.astype(F32)).astype(BF16)  3.24 us
    reshape x1, local copies, waits for them, and re-layouts, local(): qkv_weight.reshape(grouped).transpose(0, 1, 3, 2, 4, 5)  2.72 us
  transfers between devices with their start and end apart: 20, of which 9 were waited for; matrix products, arithmetic and copies ran while one was open for 11% of the time, Pallas kernels for 10%

profile of v1, /device:TPU:0, one launch (start us, length us, event | category | flops | bytes accessed | tf_op | source)
XLA Modules:
  0.0 99.6 jit_solution(12902438074994552652)
XLA Ops:
  0.6 4.1 %collective-permute-start.1 = (bf16[128,1024]{1,0:T(8,128)(2,1)}, bf16[128,1024]{1,0:T(8,128)(2,1)S(1)}, u32[]{:S(2)}, u32[]{:S(2)}) collective-permute-start(bf16[128,1024]{1,0:T(8,128)(2,1)} %bitcast.50), channel_id=1, source_target_pairs={{0,16},{8,24},{16,0},{24,8},{1,17},{9,25},{17,1},{25,9},{2,18},{10... | collective-permute-start | bytes 786440 | tf_op jit(solution)/shard_map/ppermute | solution.py:160
  4.7 0.7 collective-permute-start.2
  5.4 2.9 %collective-permute-start = (bf16[128,1024]{1,0:T(8,128)(2,1)}, bf16[128,1024]{1,0:T(8,128)(2,1)S(1)}, u32[]{:S(2)}, u32[]{:S(2)}) collective-permute-start(bf16[128,1024]{1,0:T(8,128)(2,1)} %bitcast.52), channel_id=1, source_target_pairs={{0,8},{8,0},{16,24},{24,16},{1,9},{9,1},{17,25},{25,17},{2,10},{10... | collective-permute-start | bytes 786440 | tf_op jit(solution)/shard_map/ppermute | solution.py:160
  8.3 1.0 dynamic-slice_bitcast_fusion
  9.2 0.1 collective-permute-start.4
  9.4 3.4 %collective-permute-start.5 = (bf16[128,256]{1,0:T(8,128)(2,1)S(1)}, bf16[128,256]{1,0:T(8,128)(2,1)S(1)}, u32[]{:S(2)}, u32[]{:S(2)}) collective-permute-start(bf16[128,256]{1,0:T(8,128)(2,1)S(1)} %get-tuple-element.34), channel_id=1, source_target_pairs={{0,16},{8,24},{16,0},{24,8},{1,17},{9,25},{17,1},{25,9},{2,18},{10... | collective-permute-start | bytes 196616 | tf_op jit(solution)/shard_map/ppermute | solution.py:160
  12.8 0.7 xor_bitcast_fusion
  13.5 0.2 and_reduce_fusion
  13.7 0.1 broadcast_bitcast_fusion
  13.7 2.7 %copy.9 = bf16[2,1,2,3,64,1024]{5,4,2,3,0,1:T(8,128)(2,1)} copy(bf16[2,1,2,3,64,1024]{5,4,3,2,0,1:T(8,128)(2,1)} %bitcast.64) | data formatting | bytes 3145728 | tf_op jit(solution)/shard_map/reshape | solution.py:215
  16.5 0.0 copy-done
  16.5 2.2 %convolution_convert_fusion.3.refs_1_ = bf16[128,768]{1,0:T(8,128)(2,1)S(1)} fusion(bf16[768,1024]{1,0:T(8,128)(2,1)} %bitcast.57, bf16[1,128,1024]{2,1,0:T(8,128)(2,1)S(1)} %copy-done), kind=kOutput, calls=%fused_computation.6 | convolution fusion | flops 201424896 | bytes 2031616 | tf_op jit(solution)/shard_map/dot_general | solution.py:21
  18.6 0.0 collective-permute-done.1.refs_11_
  18.7 1.9 %collective-permute-start.6 = (bf16[128,256]{1,0:T(8,128)(2,1)S(1)}, bf16[128,256]{1,0:T(8,128)(2,1)S(1)}, u32[]{:S(2)}, u32[]{:S(2)}) collective-permute-start(bf16[128,256]{1,0:T(8,128)(2,1)S(1)} %get-tuple-element.31), channel_id=1, source_target_pairs={{0,24},{8,16},{16,8},{24,0},{1,25},{9,17},{17,9},{25,1},{2,26},{10... | collective-permute-start | bytes 196616 | tf_op jit(solution)/shard_map/ppermute | solution.py:160
  20.5 0.7 convolution_convert_fusion.1.refs_3_
  21.2 0.0 collective-permute-done.refs_10_
  21.2 1.3 %collective-permute-start.3 = (bf16[128,1024]{1,0:T(8,128)(2,1)S(1)}, bf16[128,1024]{1,0:T(8,128)(2,1)S(1)}, u32[]{:S(2)}, u32[]{:S(2)}) collective-permute-start(bf16[128,1024]{1,0:T(8,128)(2,1)S(1)} %collective-permute-done.1.refs_11_), channel_id=1, source_target_pairs={{16,24},{8,0},{17,25},{9,1},{18,26},{10,2},{19,27},{11,3},{20,28},... | collective-permute-start | bytes 786440 | tf_op jit(solution)/shard_map/ppermute | solution.py:173
  22.5 0.7 convolution_convert_fusion.2.refs_2_
  23.2 0.0 collective-permute-done.2
  23.2 8.8 %collective-permute-done.3 = bf16[128,1024]{1,0:T(8,128)(2,1)S(1)} collective-permute-done((bf16[128,1024]{1,0:T(8,128)(2,1)S(1)}, bf16[128,1024]{1,0:T(8,128)(2,1)S(1)}, u32[]{:S(2)}, u32[]{:S(2)}) %collective-permute-start.3) | collective-permute-done | bytes 262176 | tf_op jit(solution)/shard_map/ppermute | solution.py:173
  32.0 0.7 convolution_convert_fusion.refs_4_
  32.6 0.0 collective-permute-done.4.refs_6_
  32.7 0.0 collective-permute-done.5.refs_7_
  32.7 0.0 collective-permute-done.6.refs_8_
  32.7 6.1 %shard_map.67 = (bf16[512,128]{1,0:T(8,128)(2,1)S(1)}, bf16[512,384]{1,0:T(8,128)(2,1)S(1)}, bf16[384,1024]{1,0:T(8,128)(2,1)S(1)}) custom-call(s32[1]{0:T(128)} %bitcast.13.refs_0_, bf16[128,768]{1,0:T(8,128)(2,1)S(1)} %convolution_convert_fusion.3.refs_1_, bf16[128,768]{1,0:T(8,128)(2,1)S(1)} %convolution_convert_fusion.2.refs_2_, ...), custom_call_target="tpu_custom_call" | custom-call | flops 1275068416 | bytes 4194304 | tf_op jit(solution)/shard_map/pallas_call | solution.py:147
  38.8 0.1 collective-permute-start.14
  38.9 9.7 %shard_map.68 = (bf16[128,1024]{1,0:T(8,128)(2,1)S(1)}, bf16[128,1024]{1,0:T(8,128)(2,1)S(1)}, bf16[128,1024]{1,0:T(8,128)(2,1)S(1)}, bf16[128,1024]{1,0:T(8,128...) custom-call(s32[1]{0:T(128)} %bitcast.refs_0_, ...), custom_call_target="tpu_custom_call" | custom-call | flops 1275068416 | bytes 4194304 | tf_op jit(solution)/shard_map/pallas_call | solution.py:147
  48.6 0.0 collective-permute-done.14
  48.6 1.7 %add_convert_fusion = bf16[384,1024]{1,0:T(8,128)(2,1)S(1)} fusion(f32[384,1024]{1,0:T(8,128)} %get-tuple-element.25, bf16[384,1024]{1,0:T(8,128)(2,1)S(1)} %collective-permute-done.14), kind=kLoop, calls=%fused_computation.2 | loop fusion | flops 1179648 | bytes 3145728 | tf_op jit(solution)/shard_map/convert_element_type | solution.py:164
  50.3 0.8 fusion.4
  51.1 1.4 %collective-permute-start.15 = (bf16[192,1024]{1,0:T(8,128)(2,1)}, bf16[192,1024]{1,0:T(8,128)(2,1)S(1)}, u32[]{:S(2)}, u32[]{:S(2)}) collective-permute-start(bf16[192,1024]{1,0:T(8,128)(2,1)} %get-tuple-element.29), channel_id=1, source_target_pairs={{0,2},{1,3},{2,0},{3,1},{4,6},{5,7},{6,4},{7,5},{8,10},{9,11},{10,... | collective-permute-start | bytes 1179656 | tf_op jit(solution)/shard_map/ppermute | solution.py:160
  52.5 1.5 %collective-permute-start.17 = (bf16[192,1024]{1,0:T(8,128)(2,1)S(1)}, bf16[192,1024]{1,0:T(8,128)(2,1)}, u32[]{:S(2)}, u32[]{:S(2)}) collective-permute-start(bf16[192,1024]{1,0:T(8,128)(2,1)S(1)} %get-tuple-element.30), channel_id=1, source_target_pairs={{0,4},{1,5},{2,6},{3,7},{4,0},{5,1},{6,2},{7,3},{8,12},{9,13},{10,... | collective-permute-start | bytes 1179656 | tf_op jit(solution)/shard_map/ppermute | solution.py:160
  54.0 1.5 %collective-permute-start.11 = (bf16[128,1024]{1,0:T(8,128)(2,1)S(1)}, bf16[128,1024]{1,0:T(8,128)(2,1)S(1)}, u32[]{:S(2)}, u32[]{:S(2)}) collective-permute-start(bf16[128,1024]{1,0:T(8,128)(2,1)S(1)} %get-tuple-element.24), channel_id=1, source_target_pairs={{24,16},{0,8},{25,17},{1,9},{26,18},{2,10},{27,19},{3,11},{28,20},... | collective-permute-start | bytes 786440 | tf_op jit(solution)/shard_map/ppermute | solution.py:185
  55.5 0.7 collective-permute-start.13
  56.1 1.5 %collective-permute-start.10 = (bf16[128,1024]{1,0:T(8,128)(2,1)S(1)}, bf16[128,1024]{1,0:T(8,128)(2,1)S(1)}, u32[]{:S(2)}, u32[]{:S(2)}) collective-permute-start(bf16[128,1024]{1,0:T(8,128)(2,1)S(1)} %get-tuple-element.22), channel_id=1, source_target_pairs={{0,8},{8,0},{16,24},{24,16},{1,9},{9,1},{17,25},{25,17},{2,10},{10... | collective-permute-start | bytes 786440 | tf_op jit(solution)/shard_map/ppermute | solution.py:160
  57.7 5.2 %collective-permute-done.15 = bf16[192,1024]{1,0:T(8,128)(2,1)S(1)} collective-permute-done((bf16[192,1024]{1,0:T(8,128)(2,1)}, bf16[192,1024]{1,0:T(8,128)(2,1)S(1)}, u32[]{:S(2)}, u32[]{:S(2)}) %collective-permute-start.15) | collective-permute-done | bytes 393248 | tf_op jit(solution)/shard_map/ppermute | solution.py:160
  62.8 0.0 collective-permute-start.7
  62.8 1.0 collective-permute-done.17
  63.8 1.3 %add_convert_fusion.4 = (bf16[192,1024]{1,0:T(8,128)(2,1)S(1)}, bf16[192,1024]{1,0:T(8,128)(2,1)S(1)}) fusion(bf16[192,1024]{1,0:T(8,128)(2,1)S(1)} %collective-permute-done.15, bf16[384,1024]{1,0:T(8,128)(2,1)S(1)} %add_convert_fusion, bf16[192,1024]{1,0:T(8,128)(2,1)} %collective-permute-done.17), kind=kLoop, calls=%fused_computation.11 | loop fusion | flops 1572864 | bytes 2359296 | tf_op jit(solution)/shard_map/convert_element_type | solution.py:164
  65.1 1.6 %collective-permute-start.16 = (bf16[192,1024]{1,0:T(8,128)(2,1)S(1)}, bf16[192,1024]{1,0:T(8,128)(2,1)S(1)}, u32[]{:S(2)}, u32[]{:S(2)}) collective-permute-start(bf16[192,1024]{1,0:T(8,128)(2,1)S(1)} %get-tuple-element.27), channel_id=1, source_target_pairs={{0,4},{1,5},{2,6},{3,7},{4,0},{5,1},{6,2},{7,3},{8,12},{9,13},{10,... | collective-permute-start | bytes 1179656 | tf_op jit(solution)/shard_map/ppermute | solution.py:160
  66.7 1.5 %collective-permute-done.7 = bf16[128,256]{1,0:T(8,128)(2,1)S(1)} collective-permute-done((bf16[128,256]{1,0:T(8,128)(2,1)S(1)}, bf16[128,256]{1,0:T(8,128)(2,1)S(1)}, u32[]{:S(2)}, u32[]{:S(2)}) %collective-permute-start.7) | collective-permute-done | bytes 65568 | tf_op jit(solution)/shard_map/ppermute | solution.py:160
  68.2 0.6 collective-permute-start.18
  68.8 6.8 %collective-permute-done.16 = bf16[192,1024]{1,0:T(8,128)(2,1)S(1)} collective-permute-done((bf16[192,1024]{1,0:T(8,128)(2,1)S(1)}, bf16[192,1024]{1,0:T(8,128)(2,1)S(1)}, u32[]{:S(2)}, u32[]{:S(2)}) %collective-permute-start.16) | collective-permute-done | bytes 393248 | tf_op jit(solution)/shard_map/ppermute | solution.py:160
  75.6 1.4 %collective-permute-start.8 = (bf16[128,256]{1,0:T(8,128)(2,1)S(1)}, bf16[128,256]{1,0:T(8,128)(2,1)S(1)}, u32[]{:S(2)}, u32[]{:S(2)}) collective-permute-start(bf16[128,256]{1,0:T(8,128)(2,1)S(1)} %get-tuple-element.19), channel_id=1, source_target_pairs={{0,16},{8,24},{16,0},{24,8},{1,17},{9,25},{17,1},{25,9},{2,18},{10... | collective-permute-start | bytes 196616 | tf_op jit(solution)/shard_map/ppermute | solution.py:160
  77.0 0.1 add_convert_fusion.3
  77.1 1.4 %collective-permute-done.18 = bf16[192,1024]{1,0:T(8,128)(2,1)S(1)} collective-permute-done((bf16[192,1024]{1,0:T(8,128)(2,1)S(1)}, bf16[192,1024]{1,0:T(8,128)(2,1)S(1)}, u32[]{:S(2)}, u32[]{:S(2)}) %collective-permute-start.18) | collective-permute-done | bytes 393248 | tf_op jit(solution)/shard_map/ppermute | solution.py:160
  78.4 1.8 %collective-permute-start.9 = (bf16[128,256]{1,0:T(8,128)(2,1)S(1)}, bf16[128,256]{1,0:T(8,128)(2,1)S(1)}, u32[]{:S(2)}, u32[]{:S(2)}) collective-permute-start(bf16[128,256]{1,0:T(8,128)(2,1)S(1)} %get-tuple-element.20), channel_id=1, source_target_pairs={{0,24},{8,16},{16,8},{24,0},{1,25},{9,17},{17,9},{25,1},{2,26},{10... | collective-permute-start | bytes 196616 | tf_op jit(solution)/shard_map/ppermute | solution.py:160
  80.2 0.1 add_convert_fusion.1
  80.3 0.1 pad_maximum_fusion
  80.4 0.0 collective-permute-done.11
  80.4 0.1 collective-permute-start.19
  80.5 0.1 fusion.1
  80.6 0.2 collective-permute-done.8
  80.8 2.1 %collective-permute-start.12 = (bf16[128,1024]{1,0:T(8,128)(2,1)S(1)}, bf16[128,1024]{1,0:T(8,128)(2,1)S(1)}, u32[]{:S(2)}, u32[]{:S(2)}) collective-permute-start(bf16[128,1024]{1,0:T(8,128)(2,1)S(1)} %fusion.1), channel_id=1, source_target_pairs={{0,16},{8,24},{16,0},{24,8},{1,17},{9,25},{17,1},{25,9},{2,18},{10... | collective-permute-start | bytes 786440 | tf_op jit(solution)/shard_map/ppermute | solution.py:160
  82.9 1.7 %collective-permute-done.9 = bf16[128,256]{1,0:T(8,128)(2,1)S(1)} collective-permute-done((bf16[128,256]{1,0:T(8,128)(2,1)S(1)}, bf16[128,256]{1,0:T(8,128)(2,1)S(1)}, u32[]{:S(2)}, u32[]{:S(2)}) %collective-permute-start.9) | collective-permute-done | bytes 65568 | tf_op jit(solution)/shard_map/ppermute | solution.py:160
  84.6 0.0 copy-start.2
  84.6 0.0 collective-permute-done.10
  84.6 0.0 collective-permute-done.13
  84.6 11.8 %collective-permute-done.12 = bf16[128,1024]{1,0:T(8,128)(2,1)S(1)} collective-permute-done((bf16[128,1024]{1,0:T(8,128)(2,1)S(1)}, bf16[128,1024]{1,0:T(8,128)(2,1)S(1)}, u32[]{:S(2)}, u32[]{:S(2)}) %collective-permute-start.12) | collective-permute-done | bytes 262176 | tf_op jit(solution)/shard_map/ppermute | solution.py:160
  96.4 0.9 fusion.2
  97.3 0.0 collective-permute-done.19
  97.3 0.4 multiply_bitcast_fusion
  97.7 0.0 copy-done.2
  97.7 1.9 %copy.10 = f32[2,1,2,3,64,1024]{5,4,3,2,0,1:T(8,128)} copy(f32[2,1,2,3,64,1024]{5,4,2,3,1,0:T(8,128)S(1)} %multiply_bitcast_fusion) | data formatting | bytes 6291456 | tf_op jit(solution)/shard_map/div | solution.py:280
  (13 shorter events, 0.1 us)
Async XLA Ops:
  0.6 18.0 %collective-permute-start.1 = (bf16[128,1024]{1,0:T(8,128)(2,1)}, bf16[128,1024]{1,0:T(8,128)(2,1)S(1)}, u32[]{:S(2)}, u32[]{:S(2)}) collective-permute-start(bf16[128,1024]{1,0:T(8,128)(2,1)} %bitcast.50), channel_id=1, source_target_pairs={{0,16},{8,24},{16,0},{24,8},{1,17},{9,25},{17,1},{25,9},{2,18},{10... | collective-permute-start | bytes 786440 | tf_op jit(solution)/shard_map/ppermute | solution.py:160
  4.7 18.4 %collective-permute-start.2 = (bf16[128,1024]{1,0:T(8,128)(2,1)}, bf16[128,1024]{1,0:T(8,128)(2,1)S(1)}, u32[]{:S(2)}, u32[]{:S(2)}) collective-permute-start(bf16[128,1024]{1,0:T(8,128)(2,1)} %bitcast.51), channel_id=1, source_target_pairs={{8,16},{16,8},{9,17},{17,9},{10,18},{18,10},{11,19},{19,11},{12,20... | collective-permute-start | bytes 786440 | tf_op jit(solution)/shard_map/ppermute | solution.py:172
  5.4 15.8 %collective-permute-start = (bf16[128,1024]{1,0:T(8,128)(2,1)}, bf16[128,1024]{1,0:T(8,128)(2,1)S(1)}, u32[]{:S(2)}, u32[]{:S(2)}) collective-permute-start(bf16[128,1024]{1,0:T(8,128)(2,1)} %bitcast.52), channel_id=1, source_target_pairs={{0,8},{8,0},{16,24},{24,16},{1,9},{9,1},{17,25},{25,17},{2,10},{10... | collective-permute-start | bytes 786440 | tf_op jit(solution)/shard_map/ppermute | solution.py:160
  9.2 23.4 %collective-permute-start.4 = (bf16[128,256]{1,0:T(8,128)(2,1)S(1)}, bf16[128,256]{1,0:T(8,128)(2,1)S(1)}, u32[]{:S(2)}, u32[]{:S(2)}) collective-permute-start(bf16[128,256]{1,0:T(8,128)(2,1)S(1)} %get-tuple-element.32), channel_id=1, source_target_pairs={{0,8},{8,0},{16,24},{24,16},{1,9},{9,1},{17,25},{25,17},{2,10},{10... | collective-permute-start | bytes 196616 | tf_op jit(solution)/shard_map/ppermute | solution.py:160
  9.4 23.3 %collective-permute-start.5 = (bf16[128,256]{1,0:T(8,128)(2,1)S(1)}, bf16[128,256]{1,0:T(8,128)(2,1)S(1)}, u32[]{:S(2)}, u32[]{:S(2)}) collective-permute-start(bf16[128,256]{1,0:T(8,128)(2,1)S(1)} %get-tuple-element.34), channel_id=1, source_target_pairs={{0,16},{8,24},{16,0},{24,8},{1,17},{9,25},{17,1},{25,9},{2,18},{10... | collective-permute-start | bytes 196616 | tf_op jit(solution)/shard_map/ppermute | solution.py:160
  13.7 2.7 %copy-start = (bf16[1,128,1024]{2,1,0:T(8,128)(2,1)S(1)}, bf16[1,128,1024]{2,1,0:T(8,128)(2,1)}, u32[]{:S(2)}) copy-start(bf16[1,128,1024]{2,1,0:T(8,128)(2,1)} %param.4) | copy-start | bytes 786436
  16.5 4.1 %copy-start.1 = (bf16[2,1,2,3,64,1024]{5,4,2,3,0,1:T(8,128)(2,1)S(1)}, bf16[2,1,2,3,64,1024]{5,4,2,3,0,1:T(8,128)(2,1)}, u32[]{:S(2)}) copy-start(bf16[2,1,2,3,64,1024]{5,4,2,3,0,1:T(8,128)(2,1)} %copy.9) | copy-start | bytes 4718596
  18.7 14.0 %collective-permute-start.6 = (bf16[128,256]{1,0:T(8,128)(2,1)S(1)}, bf16[128,256]{1,0:T(8,128)(2,1)S(1)}, u32[]{:S(2)}, u32[]{:S(2)}) collective-permute-start(bf16[128,256]{1,0:T(8,128)(2,1)S(1)} %get-tuple-element.31), channel_id=1, source_target_pairs={{0,24},{8,16},{16,8},{24,0},{1,25},{9,17},{17,9},{25,1},{2,26},{10... | collective-permute-start | bytes 196616 | tf_op jit(solution)/shard_map/ppermute | solution.py:160
  21.2 10.7 %collective-permute-start.3 = (bf16[128,1024]{1,0:T(8,128)(2,1)S(1)}, bf16[128,1024]{1,0:T(8,128)(2,1)S(1)}, u32[]{:S(2)}, u32[]{:S(2)}) collective-permute-start(bf16[128,1024]{1,0:T(8,128)(2,1)S(1)} %collective-permute-done.1.refs_11_), channel_id=1, source_target_pairs={{16,24},{8,0},{17,25},{9,1},{18,26},{10,2},{19,27},{11,3},{20,28},... | collective-permute-start | bytes 786440 | tf_op jit(solution)/shard_map/ppermute | solution.py:173
  38.8 9.8 %collective-permute-start.14 = (bf16[384,1024]{1,0:T(8,128)(2,1)S(1)}, bf16[384,1024]{1,0:T(8,128)(2,1)S(1)}, u32[]{:S(2)}, u32[]{:S(2)}) collective-permute-start(bf16[384,1024]{1,0:T(8,128)(2,1)S(1)} %get-tuple-element.26), channel_id=1, source_target_pairs={{0,1},{1,0},{2,3},{3,2},{4,5},{5,4},{6,7},{7,6},{8,9},{9,8},{10,11... | collective-permute-start | bytes 2359304 | tf_op jit(solution)/shard_map/ppermute | solution.py:160
  51.1 11.7 %collective-permute-start.15 = (bf16[192,1024]{1,0:T(8,128)(2,1)}, bf16[192,1024]{1,0:T(8,128)(2,1)S(1)}, u32[]{:S(2)}, u32[]{:S(2)}) collective-permute-start(bf16[192,1024]{1,0:T(8,128)(2,1)} %get-tuple-element.29), channel_id=1, source_target_pairs={{0,2},{1,3},{2,0},{3,1},{4,6},{5,7},{6,4},{7,5},{8,10},{9,11},{10,... | collective-permute-start | bytes 1179656 | tf_op jit(solution)/shard_map/ppermute | solution.py:160
  52.5 11.3 %collective-permute-start.17 = (bf16[192,1024]{1,0:T(8,128)(2,1)S(1)}, bf16[192,1024]{1,0:T(8,128)(2,1)}, u32[]{:S(2)}, u32[]{:S(2)}) collective-permute-start(bf16[192,1024]{1,0:T(8,128)(2,1)S(1)} %get-tuple-element.30), channel_id=1, source_target_pairs={{0,4},{1,5},{2,6},{3,7},{4,0},{5,1},{6,2},{7,3},{8,12},{9,13},{10,... | collective-permute-start | bytes 1179656 | tf_op jit(solution)/shard_map/ppermute | solution.py:160
  54.0 26.4 %collective-permute-start.11 = (bf16[128,1024]{1,0:T(8,128)(2,1)S(1)}, bf16[128,1024]{1,0:T(8,128)(2,1)S(1)}, u32[]{:S(2)}, u32[]{:S(2)}) collective-permute-start(bf16[128,1024]{1,0:T(8,128)(2,1)S(1)} %get-tuple-element.24), channel_id=1, source_target_pairs={{24,16},{0,8},{25,17},{1,9},{26,18},{2,10},{27,19},{3,11},{28,20},... | collective-permute-start | bytes 786440 | tf_op jit(solution)/shard_map/ppermute | solution.py:185
  55.5 29.2 %collective-permute-start.13 = (bf16[128,1024]{1,0:T(8,128)(2,1)S(1)}, bf16[128,1024]{1,0:T(8,128)(2,1)S(1)}, u32[]{:S(2)}, u32[]{:S(2)}) collective-permute-start(bf16[128,1024]{1,0:T(8,128)(2,1)S(1)} %get-tuple-element.24), channel_id=1, source_target_pairs={{8,16},{16,8},{9,17},{17,9},{10,18},{18,10},{11,19},{19,11},{12,20... | collective-permute-start | bytes 786440 | tf_op jit(solution)/shard_map/ppermute | solution.py:186
  56.1 28.5 %collective-permute-start.10 = (bf16[128,1024]{1,0:T(8,128)(2,1)S(1)}, bf16[128,1024]{1,0:T(8,128)(2,1)S(1)}, u32[]{:S(2)}, u32[]{:S(2)}) collective-permute-start(bf16[128,1024]{1,0:T(8,128)(2,1)S(1)} %get-tuple-element.22), channel_id=1, source_target_pairs={{0,8},{8,0},{16,24},{24,16},{1,9},{9,1},{17,25},{25,17},{2,10},{10... | collective-permute-start | bytes 786440 | tf_op jit(solution)/shard_map/ppermute | solution.py:160
  62.8 5.4 %collective-permute-start.7 = (bf16[128,256]{1,0:T(8,128)(2,1)S(1)}, bf16[128,256]{1,0:T(8,128)(2,1)S(1)}, u32[]{:S(2)}, u32[]{:S(2)}) collective-permute-start(bf16[128,256]{1,0:T(8,128)(2,1)S(1)} %get-tuple-element.18), channel_id=1, source_target_pairs={{0,8},{8,0},{16,24},{24,16},{1,9},{9,1},{17,25},{25,17},{2,10},{10... | collective-permute-start | bytes 196616 | tf_op jit(solution)/shard_map/ppermute | solution.py:160
  65.1 10.5 %collective-permute-start.16 = (bf16[192,1024]{1,0:T(8,128)(2,1)S(1)}, bf16[192,1024]{1,0:T(8,128)(2,1)S(1)}, u32[]{:S(2)}, u32[]{:S(2)}) collective-permute-start(bf16[192,1024]{1,0:T(8,128)(2,1)S(1)} %get-tuple-element.27), channel_id=1, source_target_pairs={{0,4},{1,5},{2,6},{3,7},{4,0},{5,1},{6,2},{7,3},{8,12},{9,13},{10,... | collective-permute-start | bytes 1179656 | tf_op jit(solution)/shard_map/ppermute | solution.py:160
  68.2 10.2 %collective-permute-start.18 = (bf16[192,1024]{1,0:T(8,128)(2,1)S(1)}, bf16[192,1024]{1,0:T(8,128)(2,1)S(1)}, u32[]{:S(2)}, u32[]{:S(2)}) collective-permute-start(bf16[192,1024]{1,0:T(8,128)(2,1)S(1)} %get-tuple-element.28), channel_id=1, source_target_pairs={{0,2},{1,3},{2,0},{3,1},{4,6},{5,7},{6,4},{7,5},{8,10},{9,11},{10,... | collective-permute-start | bytes 1179656 | tf_op jit(solution)/shard_map/ppermute | solution.py:160
  75.6 5.2 %collective-permute-start.8 = (bf16[128,256]{1,0:T(8,128)(2,1)S(1)}, bf16[128,256]{1,0:T(8,128)(2,1)S(1)}, u32[]{:S(2)}, u32[]{:S(2)}) collective-permute-start(bf16[128,256]{1,0:T(8,128)(2,1)S(1)} %get-tuple-element.19), channel_id=1, source_target_pairs={{0,16},{8,24},{16,0},{24,8},{1,17},{9,25},{17,1},{25,9},{2,18},{10... | collective-permute-start | bytes 196616 | tf_op jit(solution)/shard_map/ppermute | solution.py:160
  78.4 6.1 %collective-permute-start.9 = (bf16[128,256]{1,0:T(8,128)(2,1)S(1)}, bf16[128,256]{1,0:T(8,128)(2,1)S(1)}, u32[]{:S(2)}, u32[]{:S(2)}) collective-permute-start(bf16[128,256]{1,0:T(8,128)(2,1)S(1)} %get-tuple-element.20), channel_id=1, source_target_pairs={{0,24},{8,16},{16,8},{24,0},{1,25},{9,17},{17,9},{25,1},{2,26},{10... | collective-permute-start | bytes 196616 | tf_op jit(solution)/shard_map/ppermute | solution.py:160
  80.4 16.9 %collective-permute-start.19 = (bf16[384,1024]{1,0:T(8,128)(2,1)S(1)}, bf16[384,1024]{1,0:T(8,128)(2,1)S(1)}, u32[]{:S(2)}, u32[]{:S(2)}) collective-permute-start(bf16[384,1024]{1,0:T(8,128)(2,1)S(1)} %pad_maximum_fusion), channel_id=1, source_target_pairs={{0,1},{1,0},{2,3},{3,2},{4,5},{5,4},{6,7},{7,6},{8,9},{9,8},{10,11... | collective-permute-start | bytes 2359304 | tf_op jit(solution)/shard_map/ppermute | solution.py:160
  80.8 15.7 %collective-permute-start.12 = (bf16[128,1024]{1,0:T(8,128)(2,1)S(1)}, bf16[128,1024]{1,0:T(8,128)(2,1)S(1)}, u32[]{:S(2)}, u32[]{:S(2)}) collective-permute-start(bf16[128,1024]{1,0:T(8,128)(2,1)S(1)} %fusion.1), channel_id=1, source_target_pairs={{0,16},{8,24},{16,0},{24,8},{1,17},{9,25},{17,1},{25,9},{2,18},{10... | collective-permute-start | bytes 786440 | tf_op jit(solution)/shard_map/ppermute | solution.py:160
  84.6 13.1 %copy-start.2 = (bf16[1,128,1024]{2,1,0:T(8,128)(2,1)}, bf16[1,128,1024]{2,1,0:T(8,128)(2,1)S(1)}, u32[]{:S(2)}) copy-start(bf16[1,128,1024]{2,1,0:T(8,128)(2,1)S(1)} %bitcast_dynamic-update-slice_fusion) | copy-start | bytes 786436

commit v2 on v1

v2 whole, which is shorter than its diff:
```python
import functools

import jax
import jax.numpy as jnp
from jax import lax
from jax.experimental import pallas as pl
from jax.experimental.pallas import tpu as pltpu
from jax.sharding import PartitionSpec as P

HD = 64
BLOCK = 128
F32 = jnp.float32
BF16 = jnp.bfloat16
NT = (((1,), (1,)), ((), ()))
TN = (((0,), (0,)), ((), ()))
NEVER = -1e30
VMEM = pl.BlockSpec(memory_space=pltpu.VMEM)
SMEM = pl.BlockSpec(memory_space=pltpu.SMEM)


def mm(a, b, dims=(((1,), (0,)), ((), ()))):
    return lax.dot_general(a, b, dims, preferred_element_type=F32)


class Plan:
    def __init__(self, rows, columns, n):
        self.n, self.rows, self.columns = n, rows, columns
        self.nodes = n * rows
        self.heads = columns // (3 * HD)
        self.groups = 2 if self.heads % 2 == 0 else 1
        self.gheads = self.heads // self.groups
        self.pair = self.gheads % 2 == 0
        self.per_tile = 2 if self.pair else 1
        self.tiles = self.gheads // self.per_tile
        self.tile = self.per_tile * HD
        self.gcols = self.gheads * 3 * HD
        self.chunk = BLOCK

    def base(self, group, t):
        start = group * self.gcols + t * 3 * self.tile
        return start if isinstance(start, int) else pl.multiple_of(start, self.tile)

    def feature(self, group, t):
        start = (group * self.tiles + t) * self.tile
        return start if isinstance(start, int) else pl.multiple_of(start, self.tile)


def low_half(shape):
    return lax.broadcasted_iota(jnp.int32, shape, 1) % (2 * HD) < HD


def load_tile(plan, qkv, group, t, q_s, k_s, v_s):
    base, tile = plan.base(group, t), plan.tile
    for s in range(plan.n):
        here = slice(s * plan.rows, (s + 1) * plan.rows)
        first, second, third = (qkv[s][:, pl.ds(base + i * tile, tile)] for i in range(3))
        if plan.pair:
            low = low_half(first.shape)
            queries = jnp.where(low, first, second)
            keys = pltpu.roll(jnp.where(low, third, first).astype(F32), HD, 1).astype(BF16)
            values = jnp.where(low, second, third)
        else:
            queries, keys, values = first, second, third
        q_s[here, :] = (queries.astype(F32) * HD ** -0.5).astype(BF16)
        k_s[here, :] = keys
        v_s[here, :] = values


def with_lanes(plan, h, x, extra):
    if not plan.pair:
        return jnp.concatenate([x, extra[:, :HD]], axis=1)
    low = low_half(x.shape)
    return jnp.where(low if h == 0 else ~low, x, extra)


def only_head(plan, h, x):
    if not plan.pair:
        return x
    low = low_half(x.shape)
    return jnp.where(low if h == 0 else ~low, x, jnp.zeros_like(x))


def merge(plan, h, x, before):
    if not plan.pair or h == 0:
        return x
    return jnp.where(low_half(x.shape), before, x)


def chunks(plan, body):
    steps = plan.nodes // plan.chunk
    if steps <= 4:
        for i in range(steps):
            body(i * plan.chunk)
    else:
        def step(i, carry):
            body(pl.multiple_of(i * plan.chunk, plan.chunk))
            return carry

        lax.fori_loop(0, steps, step, 0)


def forward_kernel(plan, *refs):
    n, rows = plan.n, plan.rows
    qkv, feats = refs[:n], refs[n : 2 * n]
    key_bias, row_hot = refs[2 * n : 2 * n + 2]
    at = 2 * n + 2
    outs = refs[at : at + n]
    low_ref, sum_ref, full_ref = refs[at + n : at + n + 3]
    q_s, k_s, v_s, ka_s = refs[at + n + 3 :]
    for s in range(n):
        full_ref[s * rows : (s + 1) * rows, :] = feats[s][...]
    for group in range(plan.groups):
        for t in range(plan.tiles):
            load_tile(plan, qkv, group, t, q_s, k_s, v_s)
            lanes = slice(plan.feature(group, t), plan.feature(group, t) + plan.tile)
            for h in range(plan.per_tile):
                head = (group * plan.tiles + t) * plan.per_tile + h
                ka_s[...] = with_lanes(plan, h, k_s[...], key_bias[...])

                def one_chunk(lo):
                    here = pl.ds(lo, plan.chunk)
                    queries = with_lanes(plan, h, q_s[here, :], row_hot[here, :])
                    scores = mm(queries, ka_s[...], NT)
                    unnorm = jnp.exp(scores - jnp.max(scores, axis=-1, keepdims=True))
                    low = (unnorm * (1.0 / jnp.sum(unnorm, axis=-1, keepdims=True))).astype(BF16)
                    low_ref[head, here, :] = low
                    sum_ref[here, lanes] = merge(plan, h, mm(low, v_s[...]), sum_ref[here, lanes])

                chunks(plan, one_chunk)
    for s in range(n):
        outs[s][...] = sum_ref[s * rows : (s + 1) * rows, :].astype(BF16)


def backward_kernel(plan, with_weight, *refs):
    n, rows, tile = plan.n, plan.rows, plan.tile
    group = refs[0][0] if plan.groups > 1 else 0
    qkv, grads = refs[1 : 1 + n], refs[1 + n : 1 + 2 * n]
    low_ref, sum_ref = refs[1 + 2 * n : 3 + 2 * n]
    at = 3 + 2 * n
    if with_weight:
        full_ref = refs[at]
        at += 1
    grad_ref = refs[at]
    at += 1
    if with_weight:
        wgrad_ref = refs[at]
        at += 1
    q_s, k_s, v_s, g_s, ds_s, dq_s = refs[at:]
    for t in range(plan.tiles):
        load_tile(plan, qkv, group, t, q_s, k_s, v_s)
        feature = plan.feature(group, t)
        for s in range(n):
            g_s[s * rows : (s + 1) * rows, :] = grads[s][:, pl.ds(feature, tile)]
        k_s[...] = (k_s[...].astype(F32) * HD ** -0.5).astype(BF16)
        q_t = q_s[...].T
        g_t = g_s[...].T
        for h in range(plan.per_tile):
            head = (group * plan.tiles + t) * plan.per_tile + h

            def one_chunk(lo):
                here = pl.ds(lo, plan.chunk)
                g_here = only_head(plan, h, g_s[here, :])
                delta = jnp.sum(
                    g_here.astype(F32) * sum_ref[here, pl.ds(feature, tile)], axis=-1, keepdims=True
                )
                grad_weights = mm(g_here, v_s[...], NT)
                ds = (low_ref[head, here, :].astype(F32) * (grad_weights - delta)).astype(BF16)
                ds_s[here, :] = ds
                dq_s[here, :] = merge(plan, h, mm(ds, k_s[...]), dq_s[here, :])

            chunks(plan, one_chunk)
            row = (t * plan.per_tile + h) * 3 * HD
            own = slice(h * HD, (h + 1) * HD)
            grad_ref[row + HD : row + 2 * HD, :] = mm(q_t[own, :], ds_s[...]).astype(BF16)
            grad_ref[row + 2 * HD : row + 3 * HD, :] = mm(g_t[own, :], low_ref[head]).astype(BF16)
        dq_t = dq_s[...].T.astype(BF16)
        for h in range(plan.per_tile):
            row = (t * plan.per_tile + h) * 3 * HD
            grad_ref[row : row + HD, :] = dq_t[h * HD : (h + 1) * HD, :]
    if with_weight:
        wgrad_ref[...] = mm(grad_ref[...], full_ref[...]).astype(BF16)


def weight_kernel(plan, grad_ref, full_ref, got_ref, lower_ref, upper_ref):
    half = lower_ref.shape[0]
    for i, out in enumerate((lower_ref, upper_ref)):
        here = slice(i * half, (i + 1) * half)
        out[...] = (mm(grad_ref[here, :], full_ref[...]) + got_ref[here, :].astype(F32)).astype(BF16)


def whole_weight_kernel(plan, grad_ref, full_ref, wgrad_ref):
    wgrad_ref[...] = mm(grad_ref[...], full_ref[...]).astype(BF16)


def term_kernel(plan, *refs):
    which, weight = refs[:2]
    grads = refs[2 : 2 + plan.groups]
    terms = refs[2 + plan.groups :]
    for s in range(plan.n):
        here = slice(s * plan.rows, (s + 1) * plan.rows)
        total = None
        for i, grad in enumerate(grads):
            if plan.groups > 1:
                group = which[0] if i == 0 else 1 - which[0]
                here_w = pl.ds(pl.multiple_of(group * plan.gcols, plan.gcols), plan.gcols)
            else:
                here_w = slice(None)
            part = mm(grad[:, here], weight[here_w, :], TN)
            total = part if total is None else total + part
        terms[s][...] = total.astype(BF16)


def call(kernel, plan, out_shape, scratch, flops, args, scalar=False):
    return pl.pallas_call(
        functools.partial(kernel, plan),
        out_shape=out_shape,
        in_specs=[SMEM if scalar and i == 0 else VMEM for i in range(len(args))],
        out_specs=[VMEM] * len(out_shape),
        scratch_shapes=scratch,
        compiler_params=pltpu.CompilerParams(vmem_limit_bytes=50 * 2**20),
        cost_estimate=pl.CostEstimate(flops=flops, bytes_accessed=4 << 20, transcendentals=0),
    )(*args)


def array(*shape, dtype=BF16):
    return jax.ShapeDtypeStruct(shape, dtype)


def swap(x, axis, bits):
    size = lax.axis_size(axis)
    return lax.ppermute(x, axis, [(i, i ^ bits) for i in range(size)])


def after(x, *done):
    return lax.optimization_barrier((x, *done))[0]


def add(a, b):
    return (a.astype(F32) + b.astype(F32)).astype(BF16)


def gather_slots(x, z, n):
    if n != 4:
        return [x] + [swap(x, "seq", k) for k in range(1, n)]
    far = swap(x, "seq", 2)
    near = swap(x, "seq", 1)
    ends = lax.ppermute(far, "seq", [(2, 3), (1, 0)])
    middle = lax.ppermute(after(x, far), "seq", [(1, 2), (2, 1)])
    inner = (z == 1) | (z == 2)
    return [x, near, far, jnp.where(inner, middle, ends)]


def reduce_slots(terms, z, n):
    if n != 4:
        total = terms[0].astype(F32)
        for k in range(1, n):
            total = total + swap(terms[k], "seq", k).astype(F32)
        return total.astype(BF16), terms[0]
    inner = (z == 1) | (z == 2)
    ends = lax.ppermute(terms[3], "seq", [(3, 2), (0, 1)])
    middle = lax.ppermute(terms[3], "seq", [(1, 2), (2, 1)])
    near = swap(after(terms[1], ends), "seq", 1)
    far = swap(jnp.where(inner, add(terms[2], ends), terms[2]), "seq", 2)
    total = terms[0].astype(F32) + near.astype(F32) + far.astype(F32)
    return jnp.where(inner, total + middle.astype(F32), total).astype(BF16), ends


def sum_pairs(x, bits):
    return add(x, swap(x, "clus", bits))


def local(node_feats, qkv_weight, block_pairs, grad_out):
    feats = node_feats[0]
    rows, width = feats.shape
    n, m = lax.axis_size("seq"), lax.axis_size("clus")
    z, c = lax.axis_index("seq"), lax.axis_index("clus")
    plan = Plan(rows, qkv_weight.shape[0], n)
    nodes, heads = plan.nodes, plan.heads
    core = c % 2

    xs = gather_slots(feats, z, n)
    hcols = heads * HD

    def for_slot(k):
        return lax.dynamic_slice_in_dim(grad_out[0], (z ^ k) * hcols, hcols, 1)

    own, *sent = after([for_slot(k) for k in range(n)], *xs[1:3])
    grads = [own] + [swap(sent[k - 1], "seq", k) for k in range(1, n)]

    qkv = [mm(x, qkv_weight, NT).astype(BF16) for x in xs]

    per_dev = rows // BLOCK
    blocks = nodes // BLOCK
    listed = block_pairs[0]
    place = ((listed // per_dev) ^ z) * per_dev + listed % per_dev
    ids = jnp.arange(blocks, dtype=jnp.int32)
    row_ids = jnp.arange(2 * HD, dtype=jnp.int32) % HD
    allowed = jnp.any(
        (place[:, 0, None, None] == row_ids) & (place[:, 1, None, None] == ids[:, None]), axis=0
    )
    blocked = ~allowed & (row_ids < blocks)
    key_bias = jnp.repeat(jnp.where(blocked, NEVER, 0.0).astype(BF16), BLOCK, axis=0)
    row_hot = (jnp.arange(nodes, dtype=jnp.int32)[:, None] // BLOCK == row_ids).astype(BF16)

    def tiles(count):
        return [pltpu.VMEM((nodes, plan.tile), BF16)] * count

    *outs, low, sums, full = call(
        forward_kernel,
        plan,
        [array(rows, hcols)] * n
        + [array(heads, nodes, nodes), array(nodes, hcols, dtype=F32), array(nodes, width)],
        tiles(3) + [pltpu.VMEM((nodes, 2 * HD), BF16)],
        4 * nodes * nodes * HD * heads,
        [*qkv, *xs, key_bias, row_hot],
    )
    pieces = [outs[0]] + [swap(outs[k], "seq", k) for k in range(1, n)]
    attended = jnp.zeros((rows, n * hcols), BF16)
    for k in range(n):
        attended = lax.dynamic_update_slice_in_dim(attended, pieces[k], (z ^ k) * hcols, 1)

    scratch = tiles(4) + [pltpu.VMEM((nodes, nodes), BF16), pltpu.VMEM((nodes, plan.tile), F32)]
    flops = 8 * nodes * nodes * HD * plan.gheads
    common = [*qkv, *grads, low, sums]
    grad_t = []
    if plan.groups > 1:
        grad_other, wgrad_other = call(
            lambda *a: backward_kernel(a[0], True, *a[1:]),
            plan,
            [array(plan.gcols, nodes), array(plan.gcols, width)],
            scratch,
            flops + 2 * nodes * plan.gcols * width,
            [(1 - core).reshape(1), *common, full],
            scalar=True,
        )
        got = swap(wgrad_other, "clus", 1)
        grad_t = [grad_other]
    low = after(low, attended)
    (grad_own,) = call(
        lambda *a: backward_kernel(a[0], False, *a[1:]),
        plan,
        [array(plan.gcols, nodes)],
        scratch,
        flops,
        [core.reshape(1), *qkv, *grads, low, sums],
        scalar=True,
    )
    grad_t = [grad_own, *grad_t]
    half = plan.gcols // 2
    count = 2 * nodes * plan.gcols * width
    if plan.groups > 1:
        lower, upper = call(
            weight_kernel, plan, [array(half, width)] * 2, [], count, [grad_own, full, got]
        )
    else:
        (wgrad,) = call(
            whole_weight_kernel, plan, [array(plan.gcols, width)], [], count, [grad_own, full]
        )
        keep = lax.dynamic_slice_in_dim(wgrad, core * half, half, 0)
        send = lax.dynamic_slice_in_dim(wgrad, (1 - core) * half, half, 0)
        part = add(keep, swap(send, "clus", 1))
        lower, upper = part[: half // 2], part[half // 2 :]
    terms = call(
        term_kernel,
        plan,
        [array(rows, width)] * n,
        [],
        count * plan.groups,
        [core.reshape(1), qkv_weight, *grad_t],
        scalar=True,
    )
    node_grad, begun = reduce_slots(terms, z, n)

    bits = []
    while 2 << len(bits) < m:
        bits.append(2 << len(bits))
    for one, two in zip(bits, bits[::-1]):
        lower, upper = sum_pairs(lower, one), sum_pairs(upper, two)
    part = jnp.concatenate([lower, upper], axis=0)
    got = swap(part, "clus", 1)
    both = jnp.where(core == 0, jnp.stack([part, got]), jnp.stack([got, part]))
    weight_grad = both.reshape(plan.columns, width).astype(F32) / m

    return (attended[None], node_grad[None], weight_grad)


def solution(mesh):
    return jax.shard_map(
        local,
        mesh=mesh,
        in_specs=(
            P("clus", "seq", None),
            P("seq", None),
            P("clus", None, None),
            P("clus", "seq", None),
        ),
        out_specs=(P("clus", "seq", None), P("clus", "seq", None), P("seq", None)),
        check_vma=False,
    )
```

time: 100 us -> 107 us (1.070)
  waiting for transfers between devices: 38.3 us -> 47 us
  local copies, waits for them, and re-layouts: 6.51 us -> 1.08 us
  starting transfers between devices: 28.4 us -> 32.4 us
    ppermute x16, waiting for transfers between devices: 29.5 us -> 37.2 us  [swap(): return lax.ppermute(x, axis, [(i, i ^ bits) for i in range(size)])]
    ppermute x1, starting transfers between devices: 1.46 us -> 4.27 us  [reduce_slots(): ends = lax.ppermute(terms[3], 'seq', [(3, 2), (0, 1)])]
    reshape x1 -> x0, local copies, waits for them, and re-layouts: 2.72 us -> none  [local(): qkv_weight.reshape(grouped).transpose(0, 1, 3, 2, 4, 5)]
    convert_element_type x4, other arithmetic: 3.24 us -> 0.52 us  [add(): return (a.astype(F32) + b.astype(F32)).astype(BF16)]
    div x1 -> x0, local copies, waits for them, and re-layouts: 1.88 us -> none  [local(): weight_grad = weight_grad.astype(F32) / m]
    div x1, other arithmetic: 0.39 us -> 2.05 us  [local(): weight_grad = both.reshape(plan.columns, width).astype(F32) / m]
    ppermute x1, waiting for transfers between devices: 0.01 us -> 1.48 us  [reduce_slots(): ends = lax.ppermute(terms[3], 'seq', [(3, 2), (0, 1)])]
    ppermute x16, starting transfers between devices: 24.3 us -> 25.5 us  [swap(): return lax.ppermute(x, axis, [(i, i ^ bits) for i in range(size)])]
  transfers between devices with their start and end apart: 20 -> 20, of which waited for: 9 -> 10; matrix products, arithmetic and copies ran while one was open for 11% -> 9% of each run, Pallas kernels for 10% -> 10%
where the time goes in v2:
time: 107 us
  waiting for transfers between devices  47 us (44%)
  starting transfers between devices  32.4 us (30%)
  Pallas kernels  15.2 us (14%)
  other arithmetic  6.52 us (6%)
  matrix products  4.12 us (4%)
  local copies, waits for them, and re-layouts  1.08 us (1%)
    ppermute x16, waiting for transfers between devices, swap(): return lax.ppermute(x, axis, [(i, i ^ bits) for i in range(size)])  37.2 us
    ppermute x16, starting transfers between devices, swap(): return lax.ppermute(x, axis, [(i, i ^ bits) for i in range(size)])  25.5 us
    pallas_call x5, Pallas kernels, call(): pl.pallas_call(functools.partial(kernel, plan), out_shape=out_shape, in_s...  15.2 us
    ppermute x1, waiting for transfers between devices, gather_slots(): ends = lax.ppermute(far, 'seq', [(2, 3), (1, 0)])  8.31 us
    ppermute x1, starting transfers between devices, reduce_slots(): ends = lax.ppermute(terms[3], 'seq', [(3, 2), (0, 1)])  4.27 us
    dot_general x4, matrix products, mm(): return lax.dot_general(a, b, dims, preferred_element_type=F32)  4.12 us
  transfers between devices with their start and end apart: 20, of which 10 were waited for; matrix products, arithmetic and copies ran while one was open for 9% of the time, Pallas kernels for 10%

profile of v2, /device:TPU:0, one launch (start us, length us, event | category | flops | bytes accessed | tf_op | source)
XLA Modules:
  0.0 107.2 jit_solution(16515371250453867796)
XLA Ops:
  0.6 0.0 copy-start.2
  0.6 0.0 copy-start
  0.7 3.1 %collective-permute-start = (bf16[128,1024]{1,0:T(8,128)(2,1)}, bf16[128,1024]{1,0:T(8,128)(2,1)S(1)}, u32[]{:S(2)}, u32[]{:S(2)}) collective-permute-start(bf16[128,1024]{1,0:T(8,128)(2,1)} %bitcast.34), channel_id=1, source_target_pairs={{0,8},{8,0},{16,24},{24,16},{1,9},{9,1},{17,25},{25,17},{2,10},{10... | collective-permute-start | bytes 786440 | tf_op jit(solution)/shard_map/ppermute | solution.py:231
  3.7 2.6 %collective-permute-start.1 = (bf16[128,1024]{1,0:T(8,128)(2,1)}, bf16[128,1024]{1,0:T(8,128)(2,1)S(1)}, u32[]{:S(2)}, u32[]{:S(2)}) collective-permute-start(bf16[128,1024]{1,0:T(8,128)(2,1)} %bitcast.35), channel_id=1, source_target_pairs={{0,16},{8,24},{16,0},{24,8},{1,17},{9,25},{17,1},{25,9},{2,18},{10... | collective-permute-start | bytes 786440 | tf_op jit(solution)/shard_map/ppermute | solution.py:231
  6.4 0.7 xor_bitcast_fusion
  7.1 0.1 broadcast_compare_fusion
  7.1 0.1 compare_convert_fusion.refs_9_
  7.3 0.1 and_reduce_fusion
  7.4 1.0 dynamic-slice_bitcast_fusion
  8.4 2.2 %convolution_convert_fusion.3.refs_0_.a_1_ = bf16[128,768]{1,0:T(8,128)(2,1)S(1)} fusion(bf16[768,1024]{1,0:T(8,128)(2,1)} %refs_1_.1, bf16[1,128,1024]{2,1,0:T(8,128)(2,1)} %param.4), kind=kOutput, calls=%fused_computation.5 | convolution fusion | flops 201424896 | bytes 2031616 | tf_op jit(solution)/shard_map/dot_general | solution.py:22
  10.5 7.7 %collective-permute-done.1.refs_6_ = bf16[128,1024]{1,0:T(8,128)(2,1)S(1)} collective-permute-done((bf16[128,1024]{1,0:T(8,128)(2,1)}, bf16[128,1024]{1,0:T(8,128)(2,1)S(1)}, u32[]{:S(2)}, u32[]{:S(2)}) %collective-permute-start.1) | collective-permute-done | bytes 262176 | tf_op jit(solution)/shard_map/ppermute | solution.py:231
  18.3 0.7 collective-permute-start.2
  19.0 0.0 collective-permute-done.refs_5_
  19.0 2.2 %collective-permute-start.7 = (bf16[128,256]{1,0:T(8,128)(2,1)S(1)}, bf16[128,256]{1,0:T(8,128)(2,1)S(1)}, u32[]{:S(2)}, u32[]{:S(2)}) collective-permute-start(bf16[128,256]{1,0:T(8,128)(2,1)S(1)} %get-tuple-element.31), channel_id=1, source_target_pairs={{0,8},{8,0},{16,24},{24,16},{1,9},{9,1},{17,25},{25,17},{2,10},{10... | collective-permute-start | bytes 196616 | tf_op jit(solution)/shard_map/ppermute | solution.py:231
  21.2 1.1 %collective-permute-start.8 = (bf16[128,256]{1,0:T(8,128)(2,1)S(1)}, bf16[128,256]{1,0:T(8,128)(2,1)S(1)}, u32[]{:S(2)}, u32[]{:S(2)}) collective-permute-start(bf16[128,256]{1,0:T(8,128)(2,1)S(1)} %get-tuple-element.32), channel_id=1, source_target_pairs={{0,16},{8,24},{16,0},{24,8},{1,17},{9,25},{17,1},{25,9},{2,18},{10... | collective-permute-start | bytes 196616 | tf_op jit(solution)/shard_map/ppermute | solution.py:231
  22.3 1.4 %collective-permute-start.9 = (bf16[128,256]{1,0:T(8,128)(2,1)S(1)}, bf16[128,256]{1,0:T(8,128)(2,1)S(1)}, u32[]{:S(2)}, u32[]{:S(2)}) collective-permute-start(bf16[128,256]{1,0:T(8,128)(2,1)S(1)} %get-tuple-element.33), channel_id=1, source_target_pairs={{0,24},{8,16},{16,8},{24,0},{1,25},{9,17},{17,9},{25,1},{2,26},{10... | collective-permute-start | bytes 196616 | tf_op jit(solution)/shard_map/ppermute | solution.py:231
  23.6 0.7 convolution_convert_fusion.2.refs_1_.a_2_
  24.3 1.3 %collective-permute-start.3 = (bf16[128,1024]{1,0:T(8,128)(2,1)S(1)}, bf16[128,1024]{1,0:T(8,128)(2,1)S(1)}, u32[]{:S(2)}, u32[]{:S(2)}) collective-permute-start(bf16[128,1024]{1,0:T(8,128)(2,1)S(1)} %collective-permute-done.1.refs_6_), channel_id=1, source_target_pairs={{16,24},{8,0},{17,25},{9,1},{18,26},{10,2},{19,27},{11,3},{20,28},... | collective-permute-start | bytes 786440 | tf_op jit(solution)/shard_map/ppermute | solution.py:247
  25.6 0.7 convolution_convert_fusion.1.refs_2_.a_3_
  26.3 0.0 collective-permute-done.2
  26.3 8.3 %collective-permute-done.3 = bf16[128,1024]{1,0:T(8,128)(2,1)S(1)} collective-permute-done((bf16[128,1024]{1,0:T(8,128)(2,1)S(1)}, bf16[128,1024]{1,0:T(8,128)(2,1)S(1)}, u32[]{:S(2)}, u32[]{:S(2)}) %collective-permute-start.3) | collective-permute-done | bytes 262176 | tf_op jit(solution)/shard_map/ppermute | solution.py:247
  34.6 0.7 convolution_convert_fusion.refs_3_.a_4_
  35.3 7.1 %shard_map.67 = (bf16[128,256]{1,0:T(8,128)(2,1)S(1)}, bf16[128,256]{1,0:T(8,128)(2,1)S(1)}, bf16[128,256]{1,0:T(8,128)(2,1)S(1)}, bf16[128,256]{1,0:T(8,128)(2,...) custom-call(bf16[128,768]{1,0:T(8,128)(2,1)S(1)} %convolution_convert_fusion.3.refs_0_.a, ...), custom_call_target="tpu_custom_call" | custom-call | flops 268435456 | bytes 4194304 | tf_op jit(solution)/shard_map/pallas_call | solution.py:214
  42.4 0.0 collective-permute-done.7.a_6_
  42.4 0.0 collective-permute-done.8.a_7_
  42.4 0.0 collective-permute-done.9.a_8_
  42.4 0.0 copy-start.1
  42.4 4.2 %shard_map.69 = (bf16[384,512]{1,0:T(8,128)(2,1)S(1)}, bf16[384,1024]{1,0:T(8,128)(2,1)S(1)}) custom-call(s32[1]{0:T(128)} %bitcast.11.a_0_, bf16[128,768]{1,0:T(8,128)(2,1)S(1)} %convolution_convert_fusion.3.refs_0_.a_1_, bf16[128,768]{1,0:T(8,128)(2,1)S(1)} %convolution_convert_fusion.2.refs_1_.a_2_, ...), custom_call_target="tpu_custom_call" | custom-call | flops 671088640 | bytes 4194304 | tf_op jit(solution)/shard_map/pallas_call | solution.py:214
  46.6 0.1 collective-permute-start.14
  46.7 0.1 collective-permute-start.4
  46.8 2.5 %collective-permute-start.5 = (bf16[128,256]{1,0:T(8,128)(2,1)S(1)}, bf16[128,256]{1,0:T(8,128)(2,1)S(1)}, u32[]{:S(2)}, u32[]{:S(2)}) collective-permute-start(bf16[128,256]{1,0:T(8,128)(2,1)S(1)} %get-tuple-element.28), channel_id=1, source_target_pairs={{0,16},{8,24},{16,0},{24,8},{1,17},{9,25},{17,1},{25,9},{2,18},{10... | collective-permute-start | bytes 196616 | tf_op jit(solution)/shard_map/ppermute | solution.py:231
  49.2 1.9 %collective-permute-start.6 = (bf16[128,256]{1,0:T(8,128)(2,1)S(1)}, bf16[128,256]{1,0:T(8,128)(2,1)S(1)}, u32[]{:S(2)}, u32[]{:S(2)}) collective-permute-start(bf16[128,256]{1,0:T(8,128)(2,1)S(1)} %get-tuple-element.29), channel_id=1, source_target_pairs={{0,24},{8,16},{16,8},{24,0},{1,25},{9,17},{17,9},{25,1},{2,26},{10... | collective-permute-start | bytes 196616 | tf_op jit(solution)/shard_map/ppermute | solution.py:231
  51.2 1.1 %collective-permute-done.4 = bf16[128,256]{1,0:T(8,128)(2,1)S(1)} collective-permute-done((bf16[128,256]{1,0:T(8,128)(2,1)S(1)}, bf16[128,256]{1,0:T(8,128)(2,1)S(1)}, u32[]{:S(2)}, u32[]{:S(2)}) %collective-permute-start.4) | collective-permute-done | bytes 65568 | tf_op jit(solution)/shard_map/ppermute | solution.py:231
  52.3 3.2 %collective-permute-done.5 = bf16[128,256]{1,0:T(8,128)(2,1)S(1)} collective-permute-done((bf16[128,256]{1,0:T(8,128)(2,1)S(1)}, bf16[128,256]{1,0:T(8,128)(2,1)S(1)}, u32[]{:S(2)}, u32[]{:S(2)}) %collective-permute-start.5) | collective-permute-done | bytes 65568 | tf_op jit(solution)/shard_map/ppermute | solution.py:231
  55.4 0.0 collective-permute-done.6
  55.5 0.0 copy-start.3
  55.5 2.0 %shard_map.68.refs_2_.grad_ref = bf16[384,512]{1,0:T(8,128)(2,1)S(1)} custom-call(s32[1]{0:T(128)} %bitcast.6.a_0_.refs_0_, bf16[128,768]{1,0:T(8,128)(2,1)S(1)} %convolution_convert_fusion.3.refs_0_.a_1_, bf16[128,768]{1,0:T(8,128)(2,1)S(1)} %convolution_convert_fusion.2.refs_1_.a_2_, bf16[128,768]{1,0:T(8,128)(2,1)S(1)} %convolution_convert_fusion.1.refs_2_.a_3_, ...), custom_call_target="tpu_custom_call" | custom-call | flops 268435456 | bytes 4194304 | tf_op jit(solution)/shard_map/pallas_call | solution.py:214
  57.5 0.0 collective-permute-done.14.got_ref
  57.5 0.6 shard_map.71
  58.1 1.6 %collective-permute-start.17 = (bf16[192,1024]{1,0:T(8,128)(2,1)S(1)}, bf16[192,1024]{1,0:T(8,128)(2,1)S(1)}, u32[]{:S(2)}, u32[]{:S(2)}) collective-permute-start(bf16[192,1024]{1,0:T(8,128)(2,1)S(1)} %get-tuple-element.46), channel_id=1, source_target_pairs={{0,4},{1,5},{2,6},{3,7},{4,0},{5,1},{6,2},{7,3},{8,12},{9,13},{10,... | collective-permute-start | bytes 1179656 | tf_op jit(solution)/shard_map/ppermute | solution.py:231
  59.7 1.5 %collective-permute-start.15 = (bf16[192,1024]{1,0:T(8,128)(2,1)S(1)}, bf16[192,1024]{1,0:T(8,128)(2,1)S(1)}, u32[]{:S(2)}, u32[]{:S(2)}) collective-permute-start(bf16[192,1024]{1,0:T(8,128)(2,1)S(1)} %get-tuple-element.45), channel_id=1, source_target_pairs={{0,2},{1,3},{2,0},{3,1},{4,6},{5,7},{6,4},{7,5},{8,10},{9,11},{10,... | collective-permute-start | bytes 1179656 | tf_op jit(solution)/shard_map/ppermute | solution.py:231
  61.2 6.6 %collective-permute-done.17 = bf16[192,1024]{1,0:T(8,128)(2,1)S(1)} collective-permute-done((bf16[192,1024]{1,0:T(8,128)(2,1)S(1)}, bf16[192,1024]{1,0:T(8,128)(2,1)S(1)}, u32[]{:S(2)}, u32[]{:S(2)}) %collective-permute-start.17) | collective-permute-done | bytes 393248 | tf_op jit(solution)/shard_map/ppermute | solution.py:231
  67.8 0.1 add_convert_fusion.1
  67.9 1.5 %collective-permute-start.18 = (bf16[192,1024]{1,0:T(8,128)(2,1)S(1)}, bf16[192,1024]{1,0:T(8,128)(2,1)S(1)}, u32[]{:S(2)}, u32[]{:S(2)}) collective-permute-start(bf16[192,1024]{1,0:T(8,128)(2,1)S(1)} %add_convert_fusion.1), channel_id=1, source_target_pairs={{0,2},{1,3},{2,0},{3,1},{4,6},{5,7},{6,4},{7,5},{8,10},{9,11},{10,... | collective-permute-start | bytes 1179656 | tf_op jit(solution)/shard_map/ppermute | solution.py:231
  69.5 0.3 collective-permute-done.15
  69.8 0.1 add_convert_fusion.3
  69.9 1.3 %collective-permute-start.16 = (bf16[192,1024]{1,0:T(8,128)(2,1)S(1)}, bf16[192,1024]{1,0:T(8,128)(2,1)S(1)}, u32[]{:S(2)}, u32[]{:S(2)}) collective-permute-start(bf16[192,1024]{1,0:T(8,128)(2,1)S(1)} %add_convert_fusion.3), channel_id=1, source_target_pairs={{0,4},{1,5},{2,6},{3,7},{4,0},{5,1},{6,2},{7,3},{8,12},{9,13},{10,... | collective-permute-start | bytes 1179656 | tf_op jit(solution)/shard_map/ppermute | solution.py:231
  71.2 1.3 %shard_map.70 = (bf16[128,1024]{1,0:T(8,128)(2,1)S(1)}, bf16[128,1024]{1,0:T(8,128)(2,1)S(1)}, bf16[128,1024]{1,0:T(8,128)(2,1)S(1)}, bf16[128,1024]{1,0:T(8,128)(2,1)S(1)}) custom-call(s32[1]{0:T(128)} %bitcast.6.a_0_.refs_0_, bf16[768,1024]{1,0:T(8,128)(2,1)S(1)} %copy-done, bf16[384,512]{1,0:T(8,128)(2,1)S(1)} %shard_map.68.refs_2_.grad_ref, ...), custom_call_target="tpu_custom_call" | custom-call | flops 805306368 | bytes 4194304 | tf_op jit(solution)/shard_map/pallas_call | solution.py:214
  72.5 4.3 %collective-permute-start.10 = (bf16[128,1024]{1,0:T(8,128)(2,1)S(1)}, bf16[128,1024]{1,0:T(8,128)(2,1)S(1)}, u32[]{:S(2)}, u32[]{:S(2)}) collective-permute-start(bf16[128,1024]{1,0:T(8,128)(2,1)S(1)} %get-tuple-element.41), channel_id=1, source_target_pairs={{24,16},{0,8},{25,17},{1,9},{26,18},{2,10},{27,19},{3,11},{28,20},... | collective-permute-start | bytes 786440 | tf_op jit(solution)/shard_map/ppermute | solution.py:260
  76.8 0.6 collective-permute-done.18
  77.5 0.1 add_convert_fusion
  77.6 0.5 collective-permute-done.16
  78.1 0.1 add_convert_fusion.2
  78.2 0.2 fusion.7
  78.4 0.1 collective-permute-start.19
  78.5 0.7 collective-permute-start.13
  79.2 1.5 %collective-permute-done.10 = bf16[128,1024]{1,0:T(8,128)(2,1)S(1)} collective-permute-done((bf16[128,1024]{1,0:T(8,128)(2,1)S(1)}, bf16[128,1024]{1,0:T(8,128)(2,1)S(1)}, u32[]{:S(2)}, u32[]{:S(2)}) %collective-permute-start.10) | collective-permute-done | bytes 262176 | tf_op jit(solution)/shard_map/ppermute | solution.py:260
  80.7 0.8 fusion.1
  81.5 4.6 %collective-permute-start.12 = (bf16[128,1024]{1,0:T(8,128)(2,1)}, bf16[128,1024]{1,0:T(8,128)(2,1)}, u32[]{:S(2)}, u32[]{:S(2)}) collective-permute-start(bf16[128,1024]{1,0:T(8,128)(2,1)} %fusion.1), channel_id=1, source_target_pairs={{0,16},{8,24},{16,0},{24,8},{1,17},{9,25},{17,1},{25,9},{2,18},{10... | collective-permute-start | bytes 786440 | tf_op jit(solution)/shard_map/ppermute | solution.py:231
  86.0 0.0 collective-permute-start.11
  86.1 0.0 collective-permute-done.13
  86.1 17.2 %collective-permute-done.12 = bf16[128,1024]{1,0:T(8,128)(2,1)} collective-permute-done((bf16[128,1024]{1,0:T(8,128)(2,1)}, bf16[128,1024]{1,0:T(8,128)(2,1)}, u32[]{:S(2)}, u32[]{:S(2)}) %collective-permute-start.12) | collective-permute-done | bytes 262176 | tf_op jit(solution)/shard_map/ppermute | solution.py:231
  103.2 1.9 %fusion.2 = bf16[1,128,1024]{2,1,0:T(8,128)(2,1)} fusion(bf16[128,1024]{1,0:T(8,128)(2,1)S(1)} %collective-permute-done.13, bf16[128,1024]{1,0:T(8,128)(2,1)} %collective-permute-done.12, bf16[128,1024]{1,0:T(8,128)(2,1)} %collective-permute-done.11, bf16[128,1024]{1,0:T(8,128)(2,1)S(1)} %get-tuple-element.39, pred[]{:T(512)S(6)} %or.4), kind=kLoop, calls=%fused_computation.15 | loop fusion | flops 1179648 | bytes 1310721 | tf_op jit(solution)/shard_map/broadcast_in_dim | solution.py:384
  105.2 2.0 %convert_multiply_fusion = f32[2,384,1024]{2,1,0:T(8,128)} fusion(bf16[1,384,1024]{2,1,0:T(8,128)(2,1)S(1)} %bitcast.40, bf16[1,384,1024]{2,1,0:T(8,128)(2,1)S(1)} %get-tuple-element.47, pred[]{:T(512)S(6)} %eq.80), kind=kLoop, calls=%fused_computation | loop fusion | flops 3932160 | bytes 4718593 | tf_op jit(solution)/shard_map/div | solution.py:382
  (19 shorter events, 0.2 us)
Async XLA Ops:
  0.6 17.7 %copy-start.2 = (bf16[1,128,1024]{2,1,0:T(8,128)(2,1)S(1)}, bf16[1,128,1024]{2,1,0:T(8,128)(2,1)}, u32[]{:S(2)}) copy-start(bf16[1,128,1024]{2,1,0:T(8,128)(2,1)} %param.4) | copy-start | bytes 786436
  0.6 23.0 %copy-start = (bf16[768,1024]{1,0:T(8,128)(2,1)S(1)}, bf16[768,1024]{1,0:T(8,128)(2,1)}, u32[]{:S(2)}) copy-start(bf16[768,1024]{1,0:T(8,128)(2,1)} %refs_1_.1) | copy-start | bytes 4718596
  0.7 18.3 %collective-permute-start = (bf16[128,1024]{1,0:T(8,128)(2,1)}, bf16[128,1024]{1,0:T(8,128)(2,1)S(1)}, u32[]{:S(2)}, u32[]{:S(2)}) collective-permute-start(bf16[128,1024]{1,0:T(8,128)(2,1)} %bitcast.34), channel_id=1, source_target_pairs={{0,8},{8,0},{16,24},{24,16},{1,9},{9,1},{17,25},{25,17},{2,10},{10... | collective-permute-start | bytes 786440 | tf_op jit(solution)/shard_map/ppermute | solution.py:231
  3.7 14.6 %collective-permute-start.1 = (bf16[128,1024]{1,0:T(8,128)(2,1)}, bf16[128,1024]{1,0:T(8,128)(2,1)S(1)}, u32[]{:S(2)}, u32[]{:S(2)}) collective-permute-start(bf16[128,1024]{1,0:T(8,128)(2,1)} %bitcast.35), channel_id=1, source_target_pairs={{0,16},{8,24},{16,0},{24,8},{1,17},{9,25},{17,1},{25,9},{2,18},{10... | collective-permute-start | bytes 786440 | tf_op jit(solution)/shard_map/ppermute | solution.py:231
  18.3 8.0 %collective-permute-start.2 = (bf16[128,1024]{1,0:T(8,128)(2,1)S(1)}, bf16[128,1024]{1,0:T(8,128)(2,1)S(1)}, u32[]{:S(2)}, u32[]{:S(2)}) collective-permute-start(bf16[128,1024]{1,0:T(8,128)(2,1)S(1)} %bitcast.36), channel_id=1, source_target_pairs={{8,16},{16,8},{9,17},{17,9},{10,18},{18,10},{11,19},{19,11},{12,20... | collective-permute-start | bytes 786440 | tf_op jit(solution)/shard_map/ppermute | solution.py:248
  19.0 23.4 %collective-permute-start.7 = (bf16[128,256]{1,0:T(8,128)(2,1)S(1)}, bf16[128,256]{1,0:T(8,128)(2,1)S(1)}, u32[]{:S(2)}, u32[]{:S(2)}) collective-permute-start(bf16[128,256]{1,0:T(8,128)(2,1)S(1)} %get-tuple-element.31), channel_id=1, source_target_pairs={{0,8},{8,0},{16,24},{24,16},{1,9},{9,1},{17,25},{25,17},{2,10},{10... | collective-permute-start | bytes 196616 | tf_op jit(solution)/shard_map/ppermute | solution.py:231
  21.2 21.2 %collective-permute-start.8 = (bf16[128,256]{1,0:T(8,128)(2,1)S(1)}, bf16[128,256]{1,0:T(8,128)(2,1)S(1)}, u32[]{:S(2)}, u32[]{:S(2)}) collective-permute-start(bf16[128,256]{1,0:T(8,128)(2,1)S(1)} %get-tuple-element.32), channel_id=1, source_target_pairs={{0,16},{8,24},{16,0},{24,8},{1,17},{9,25},{17,1},{25,9},{2,18},{10... | collective-permute-start | bytes 196616 | tf_op jit(solution)/shard_map/ppermute | solution.py:231
  22.3 20.1 %collective-permute-start.9 = (bf16[128,256]{1,0:T(8,128)(2,1)S(1)}, bf16[128,256]{1,0:T(8,128)(2,1)S(1)}, u32[]{:S(2)}, u32[]{:S(2)}) collective-permute-start(bf16[128,256]{1,0:T(8,128)(2,1)S(1)} %get-tuple-element.33), channel_id=1, source_target_pairs={{0,24},{8,16},{16,8},{24,0},{1,25},{9,17},{17,9},{25,1},{2,26},{10... | collective-permute-start | bytes 196616 | tf_op jit(solution)/shard_map/ppermute | solution.py:231
  24.3 10.3 %collective-permute-start.3 = (bf16[128,1024]{1,0:T(8,128)(2,1)S(1)}, bf16[128,1024]{1,0:T(8,128)(2,1)S(1)}, u32[]{:S(2)}, u32[]{:S(2)}) collective-permute-start(bf16[128,1024]{1,0:T(8,128)(2,1)S(1)} %collective-permute-done.1.refs_6_), channel_id=1, source_target_pairs={{16,24},{8,0},{17,25},{9,1},{18,26},{10,2},{19,27},{11,3},{20,28},... | collective-permute-start | bytes 786440 | tf_op jit(solution)/shard_map/ppermute | solution.py:247
  42.4 13.1 %copy-start.1 = (bf16[4,512,512]{2,1,0:T(8,128)(2,1)S(1)}, bf16[4,512,512]{2,1,0:T(8,128)(2,1)}, u32[]{:S(2)}) copy-start(bf16[4,512,512]{2,1,0:T(8,128)(2,1)} %get-tuple-element.35.a_9_) | copy-start | bytes 6291460
  46.6 10.9 %collective-permute-start.14 = (bf16[384,1024]{1,0:T(8,128)(2,1)S(1)}, bf16[384,1024]{1,0:T(8,128)(2,1)S(1)}, u32[]{:S(2)}, u32[]{:S(2)}) collective-permute-start(bf16[384,1024]{1,0:T(8,128)(2,1)S(1)} %get-tuple-element.44), channel_id=1, source_target_pairs={{0,1},{1,0},{2,3},{3,2},{4,5},{5,4},{6,7},{7,6},{8,9},{9,8},{10,11... | collective-permute-start | bytes 2359304 | tf_op jit(solution)/shard_map/ppermute | solution.py:231
  46.7 5.6 %collective-permute-start.4 = (bf16[128,256]{1,0:T(8,128)(2,1)S(1)}, bf16[128,256]{1,0:T(8,128)(2,1)S(1)}, u32[]{:S(2)}, u32[]{:S(2)}) collective-permute-start(bf16[128,256]{1,0:T(8,128)(2,1)S(1)} %get-tuple-element.27), channel_id=1, source_target_pairs={{0,8},{8,0},{16,24},{24,16},{1,9},{9,1},{17,25},{25,17},{2,10},{10... | collective-permute-start | bytes 196616 | tf_op jit(solution)/shard_map/ppermute | solution.py:231
  46.8 8.7 %collective-permute-start.5 = (bf16[128,256]{1,0:T(8,128)(2,1)S(1)}, bf16[128,256]{1,0:T(8,128)(2,1)S(1)}, u32[]{:S(2)}, u32[]{:S(2)}) collective-permute-start(bf16[128,256]{1,0:T(8,128)(2,1)S(1)} %get-tuple-element.28), channel_id=1, source_target_pairs={{0,16},{8,24},{16,0},{24,8},{1,17},{9,25},{17,1},{25,9},{2,18},{10... | collective-permute-start | bytes 196616 | tf_op jit(solution)/shard_map/ppermute | solution.py:231
  49.2 6.2 %collective-permute-start.6 = (bf16[128,256]{1,0:T(8,128)(2,1)S(1)}, bf16[128,256]{1,0:T(8,128)(2,1)S(1)}, u32[]{:S(2)}, u32[]{:S(2)}) collective-permute-start(bf16[128,256]{1,0:T(8,128)(2,1)S(1)} %get-tuple-element.29), channel_id=1, source_target_pairs={{0,24},{8,16},{16,8},{24,0},{1,25},{9,17},{17,9},{25,1},{2,26},{10... | collective-permute-start | bytes 196616 | tf_op jit(solution)/shard_map/ppermute | solution.py:231
  55.5 2.0 %copy-start.3 = (bf16[128,1024]{1,0:T(8,128)(2,1)}, bf16[128,1024]{1,0:T(8,128)(2,1)S(1)}, u32[]{:S(2)}) copy-start(bf16[128,1024]{1,0:T(8,128)(2,1)S(1)} %constant_dynamic-update-slice_fusion) | copy-start | bytes 786436
  58.1 9.7 %collective-permute-start.17 = (bf16[192,1024]{1,0:T(8,128)(2,1)S(1)}, bf16[192,1024]{1,0:T(8,128)(2,1)S(1)}, u32[]{:S(2)}, u32[]{:S(2)}) collective-permute-start(bf16[192,1024]{1,0:T(8,128)(2,1)S(1)} %get-tuple-element.46), channel_id=1, source_target_pairs={{0,4},{1,5},{2,6},{3,7},{4,0},{5,1},{6,2},{7,3},{8,12},{9,13},{10,... | collective-permute-start | bytes 1179656 | tf_op jit(solution)/shard_map/ppermute | solution.py:231
  59.7 10.0 %collective-permute-start.15 = (bf16[192,1024]{1,0:T(8,128)(2,1)S(1)}, bf16[192,1024]{1,0:T(8,128)(2,1)S(1)}, u32[]{:S(2)}, u32[]{:S(2)}) collective-permute-start(bf16[192,1024]{1,0:T(8,128)(2,1)S(1)} %get-tuple-element.45), channel_id=1, source_target_pairs={{0,2},{1,3},{2,0},{3,1},{4,6},{5,7},{6,4},{7,5},{8,10},{9,11},{10,... | collective-permute-start | bytes 1179656 | tf_op jit(solution)/shard_map/ppermute | solution.py:231
  67.9 9.5 %collective-permute-start.18 = (bf16[192,1024]{1,0:T(8,128)(2,1)S(1)}, bf16[192,1024]{1,0:T(8,128)(2,1)S(1)}, u32[]{:S(2)}, u32[]{:S(2)}) collective-permute-start(bf16[192,1024]{1,0:T(8,128)(2,1)S(1)} %add_convert_fusion.1), channel_id=1, source_target_pairs={{0,2},{1,3},{2,0},{3,1},{4,6},{5,7},{6,4},{7,5},{8,10},{9,11},{10,... | collective-permute-start | bytes 1179656 | tf_op jit(solution)/shard_map/ppermute | solution.py:231
  69.9 8.2 %collective-permute-start.16 = (bf16[192,1024]{1,0:T(8,128)(2,1)S(1)}, bf16[192,1024]{1,0:T(8,128)(2,1)S(1)}, u32[]{:S(2)}, u32[]{:S(2)}) collective-permute-start(bf16[192,1024]{1,0:T(8,128)(2,1)S(1)} %add_convert_fusion.3), channel_id=1, source_target_pairs={{0,4},{1,5},{2,6},{3,7},{4,0},{5,1},{6,2},{7,3},{8,12},{9,13},{10,... | collective-permute-start | bytes 1179656 | tf_op jit(solution)/shard_map/ppermute | solution.py:231
  72.5 8.1 %collective-permute-start.10 = (bf16[128,1024]{1,0:T(8,128)(2,1)S(1)}, bf16[128,1024]{1,0:T(8,128)(2,1)S(1)}, u32[]{:S(2)}, u32[]{:S(2)}) collective-permute-start(bf16[128,1024]{1,0:T(8,128)(2,1)S(1)} %get-tuple-element.41), channel_id=1, source_target_pairs={{24,16},{0,8},{25,17},{1,9},{26,18},{2,10},{27,19},{3,11},{28,20},... | collective-permute-start | bytes 786440 | tf_op jit(solution)/shard_map/ppermute | solution.py:260
  78.4 26.7 %collective-permute-start.19 = (bf16[384,1024]{1,0:T(8,128)(2,1)S(1)}, bf16[384,1024]{1,0:T(8,128)(2,1)S(1)}, u32[]{:S(2)}, u32[]{:S(2)}) collective-permute-start(bf16[384,1024]{1,0:T(8,128)(2,1)S(1)} %get-tuple-element.48), channel_id=1, source_target_pairs={{0,1},{1,0},{2,3},{3,2},{4,5},{5,4},{6,7},{7,6},{8,9},{9,8},{10,11... | collective-permute-start | bytes 2359304 | tf_op jit(solution)/shard_map/ppermute | solution.py:231
  78.5 7.5 %collective-permute-start.13 = (bf16[128,1024]{1,0:T(8,128)(2,1)S(1)}, bf16[128,1024]{1,0:T(8,128)(2,1)S(1)}, u32[]{:S(2)}, u32[]{:S(2)}) collective-permute-start(bf16[128,1024]{1,0:T(8,128)(2,1)S(1)} %get-tuple-element.41), channel_id=1, source_target_pairs={{8,16},{16,8},{9,17},{17,9},{10,18},{18,10},{11,19},{19,11},{12,20... | collective-permute-start | bytes 786440 | tf_op jit(solution)/shard_map/ppermute | solution.py:261
  81.5 21.8 %collective-permute-start.12 = (bf16[128,1024]{1,0:T(8,128)(2,1)}, bf16[128,1024]{1,0:T(8,128)(2,1)}, u32[]{:S(2)}, u32[]{:S(2)}) collective-permute-start(bf16[128,1024]{1,0:T(8,128)(2,1)} %fusion.1), channel_id=1, source_target_pairs={{0,16},{8,24},{16,0},{24,8},{1,17},{9,25},{17,1},{25,9},{2,18},{10... | collective-permute-start | bytes 786440 | tf_op jit(solution)/shard_map/ppermute | solution.py:231
  86.0 17.2 %collective-permute-start.11 = (bf16[128,1024]{1,0:T(8,128)(2,1)S(1)}, bf16[128,1024]{1,0:T(8,128)(2,1)}, u32[]{:S(2)}, u32[]{:S(2)}) collective-permute-start(bf16[128,1024]{1,0:T(8,128)(2,1)S(1)} %get-tuple-element.42), channel_id=1, source_target_pairs={{0,8},{8,0},{16,24},{24,16},{1,9},{9,1},{17,25},{25,17},{2,10},{10... | collective-permute-start | bytes 786440 | tf_op jit(solution)/shard_map/ppermute | solution.py:231

commit v3 on v2

--- a/solution.py
+++ b/solution.py
@@ -1,4 +1,5 @@
 import functools
+import math
 
 import jax
 import jax.numpy as jnp
@@ -49,11 +50,18 @@
     return lax.broadcasted_iota(jnp.int32, shape, 1) % (2 * HD) < HD
 
 
+def project_kernel(plan, *refs):
+    feats, (weight, full_ref, qkv_ref) = refs[: plan.n - 1], refs[plan.n - 1 :]
+    for s, x in enumerate(feats):
+        full_ref[s * plan.rows : (s + 1) * plan.rows, :] = x[...]
+    qkv_ref[...] = mm(full_ref[...], weight[...], NT).astype(BF16)
+
+
 def load_tile(plan, qkv, group, t, q_s, k_s, v_s):
     base, tile = plan.base(group, t), plan.tile
     for s in range(plan.n):
         here = slice(s * plan.rows, (s + 1) * plan.rows)
-        first, second, third = (qkv[s][:, pl.ds(base + i * tile, tile)] for i in range(3))
+        first, second, third = (qkv[here, pl.ds(base + i * tile, tile)] for i in range(3))
         if plan.pair:
             low = low_half(first.shape)
             queries = jnp.where(low, first, second)
@@ -101,14 +109,14 @@
 
 def forward_kernel(plan, *refs):
     n, rows = plan.n, plan.rows
-    qkv, feats = refs[:n], refs[n : 2 * n]
-    key_bias, row_hot = refs[2 * n : 2 * n + 2]
-    at = 2 * n + 2
-    outs = refs[at : at + n]
-    low_ref, sum_ref, full_ref = refs[at + n : at + n + 3]
-    q_s, k_s, v_s, ka_s = refs[at + n + 3 :]
-    for s in range(n):
-        full_ref[s * rows : (s + 1) * rows, :] = feats[s][...]
+    known, known_x, last, weight, key_bias, row_hot = refs[:6]
+    low_ref, sum_ref, full_ref, qkv = refs[6:10]
+    q_s, k_s, v_s, ka_s = refs[10:]
+    earlier = (n - 1) * rows
+    full_ref[:earlier, :] = known_x[...]
+    full_ref[earlier:, :] = last[...]
+    qkv[:earlier, :] = known[...]
+    qkv[earlier:, :] = mm(last[...], weight[...], NT).astype(BF16)
     for group in range(plan.groups):
         for t in range(plan.tiles):
             load_tile(plan, qkv, group, t, q_s, k_s, v_s)
@@ -127,16 +135,13 @@
                     sum_ref[here, lanes] = merge(plan, h, mm(low, v_s[...]), sum_ref[here, lanes])
 
                 chunks(plan, one_chunk)
-    for s in range(n):
-        outs[s][...] = sum_ref[s * rows : (s + 1) * rows, :].astype(BF16)
-
 
 def backward_kernel(plan, with_weight, *refs):
     n, rows, tile = plan.n, plan.rows, plan.tile
     group = refs[0][0] if plan.groups > 1 else 0
-    qkv, grads = refs[1 : 1 + n], refs[1 + n : 1 + 2 * n]
-    low_ref, sum_ref = refs[1 + 2 * n : 3 + 2 * n]
-    at = 3 + 2 * n
+    qkv, grads = refs[1], refs[2 : 2 + n]
+    low_ref, sum_ref = refs[2 + n : 4 + n]
+    at = 4 + n
     if with_weight:
         full_ref = refs[at]
         at += 1
@@ -181,11 +186,8 @@
         wgrad_ref[...] = mm(grad_ref[...], full_ref[...]).astype(BF16)
 
 
-def weight_kernel(plan, grad_ref, full_ref, got_ref, lower_ref, upper_ref):
-    half = lower_ref.shape[0]
-    for i, out in enumerate((lower_ref, upper_ref)):
-        here = slice(i * half, (i + 1) * half)
-        out[...] = (mm(grad_ref[here, :], full_ref[...]) + got_ref[here, :].astype(F32)).astype(BF16)
+def weight_kernel(plan, grad_ref, full_ref, got_ref, part_ref):
+    part_ref[...] = (mm(grad_ref[...], full_ref[...]) + got_ref[...].astype(F32)).astype(BF16)
 
 
 def whole_weight_kernel(plan, grad_ref, full_ref, wgrad_ref):
@@ -193,10 +195,11 @@
 
 
 def term_kernel(plan, *refs):
-    which, weight = refs[:2]
-    grads = refs[2 : 2 + plan.groups]
-    terms = refs[2 + plan.groups :]
-    for s in range(plan.n):
+    which, weight, sum_ref = refs[:3]
+    grads = refs[3 : 3 + plan.groups]
+    sends = refs[3 + plan.groups :]
+    width = weight.shape[1]
+    for s in reversed(range(plan.n)):
         here = slice(s * plan.rows, (s + 1) * plan.rows)
         total = None
         for i, grad in enumerate(grads):
@@ -207,17 +210,24 @@
                 here_w = slice(None)
             part = mm(grad[:, here], weight[here_w, :], TN)
             total = part if total is None else total + part
-        terms[s][...] = total.astype(BF16)
+        sends[s][:, :width] = total.astype(BF16)
+        sends[s][:, width:] = sum_ref[here, :].astype(BF16)
+
+
+def size(x):
+    return math.prod(x.shape) * jnp.dtype(x.dtype).itemsize
 
 
 def call(kernel, plan, out_shape, scratch, flops, args, scalar=False):
+    held = sum(map(size, out_shape)) + sum(map(size, scratch)) + sum(map(size, args))
+    held += 32 * plan.chunk * plan.nodes + 24 * plan.nodes * 2 * HD + 8 * 2**20
     return pl.pallas_call(
         functools.partial(kernel, plan),
         out_shape=out_shape,
         in_specs=[SMEM if scalar and i == 0 else VMEM for i in range(len(args))],
         out_specs=[VMEM] * len(out_shape),
         scratch_shapes=scratch,
-        compiler_params=pltpu.CompilerParams(vmem_limit_bytes=50 * 2**20),
+        compiler_params=pltpu.CompilerParams(vmem_limit_bytes=min(held, 60 * 2**20)),
         cost_estimate=pl.CostEstimate(flops=flops, bytes_accessed=4 << 20, transcendentals=0),
     )(*args)
 
@@ -250,25 +260,6 @@
     return [x, near, far, jnp.where(inner, middle, ends)]
 
 
-def reduce_slots(terms, z, n):
-    if n != 4:
-        total = terms[0].astype(F32)
-        for k in range(1, n):
-            total = total + swap(terms[k], "seq", k).astype(F32)
-        return total.astype(BF16), terms[0]
-    inner = (z == 1) | (z == 2)
-    ends = lax.ppermute(terms[3], "seq", [(3, 2), (0, 1)])
-    middle = lax.ppermute(terms[3], "seq", [(1, 2), (2, 1)])
-    near = swap(after(terms[1], ends), "seq", 1)
-    far = swap(jnp.where(inner, add(terms[2], ends), terms[2]), "seq", 2)
-    total = terms[0].astype(F32) + near.astype(F32) + far.astype(F32)
-    return jnp.where(inner, total + middle.astype(F32), total).astype(BF16), ends
-
-
-def sum_pairs(x, bits):
-    return add(x, swap(x, "clus", bits))
-
-
 def local(node_feats, qkv_weight, block_pairs, grad_out):
     feats = node_feats[0]
     rows, width = feats.shape
@@ -287,7 +278,15 @@
     own, *sent = after([for_slot(k) for k in range(n)], *xs[1:3])
     grads = [own] + [swap(sent[k - 1], "seq", k) for k in range(1, n)]
 
-    qkv = [mm(x, qkv_weight, NT).astype(BF16) for x in xs]
+    earlier = nodes - rows
+    known_x, known = call(
+        project_kernel,
+        plan,
+        [array(earlier, width), array(earlier, plan.columns)],
+        [],
+        2 * earlier * plan.columns * width,
+        [*xs[:-1], qkv_weight],
+    )
 
     per_dev = rows // BLOCK
     blocks = nodes // BLOCK
@@ -305,23 +304,17 @@
     def tiles(count):
         return [pltpu.VMEM((nodes, plan.tile), BF16)] * count
 
-    *outs, low, sums, full = call(
+    low, sums, full, qkv = call(
         forward_kernel,
         plan,
-        [array(rows, hcols)] * n
-        + [array(heads, nodes, nodes), array(nodes, hcols, dtype=F32), array(nodes, width)],
+        [array(heads, nodes, nodes), array(nodes, hcols, dtype=F32), array(nodes, width), array(nodes, plan.columns)],
         tiles(3) + [pltpu.VMEM((nodes, 2 * HD), BF16)],
         4 * nodes * nodes * HD * heads,
-        [*qkv, *xs, key_bias, row_hot],
-    )
-    pieces = [outs[0]] + [swap(outs[k], "seq", k) for k in range(1, n)]
-    attended = jnp.zeros((rows, n * hcols), BF16)
-    for k in range(n):
-        attended = lax.dynamic_update_slice_in_dim(attended, pieces[k], (z ^ k) * hcols, 1)
-
+        [known, known_x, xs[-1], qkv_weight, key_bias, row_hot],
+    )
     scratch = tiles(4) + [pltpu.VMEM((nodes, nodes), BF16), pltpu.VMEM((nodes, plan.tile), F32)]
     flops = 8 * nodes * nodes * HD * plan.gheads
-    common = [*qkv, *grads, low, sums]
+    common = [qkv, *grads, low, sums]
     grad_t = []
     if plan.groups > 1:
         grad_other, wgrad_other = call(
@@ -335,52 +328,70 @@
         )
         got = swap(wgrad_other, "clus", 1)
         grad_t = [grad_other]
-    low = after(low, attended)
     (grad_own,) = call(
         lambda *a: backward_kernel(a[0], False, *a[1:]),
         plan,
         [array(plan.gcols, nodes)],
         scratch,
         flops,
-        [core.reshape(1), *qkv, *grads, low, sums],
+        [core.reshape(1), qkv, *grads, low, sums],
         scalar=True,
     )
     grad_t = [grad_own, *grad_t]
-    half = plan.gcols // 2
     count = 2 * nodes * plan.gcols * width
     if plan.groups > 1:
-        lower, upper = call(
-            weight_kernel, plan, [array(half, width)] * 2, [], count, [grad_own, full, got]
+        (part,) = call(
+            weight_kernel, plan, [array(plan.gcols, width)], [], count, [grad_own, full, got]
         )
     else:
+        half = plan.gcols // 2
         (wgrad,) = call(
             whole_weight_kernel, plan, [array(plan.gcols, width)], [], count, [grad_own, full]
         )
         keep = lax.dynamic_slice_in_dim(wgrad, core * half, half, 0)
         send = lax.dynamic_slice_in_dim(wgrad, (1 - core) * half, half, 0)
         part = add(keep, swap(send, "clus", 1))
-        lower, upper = part[: half // 2], part[half // 2 :]
-    terms = call(
+    sends = call(
         term_kernel,
         plan,
-        [array(rows, width)] * n,
+        [array(rows, width + hcols)] * n,
         [],
         count * plan.groups,
-        [core.reshape(1), qkv_weight, *grad_t],
+        [core.reshape(1), qkv_weight, sums, *grad_t],
         scalar=True,
     )
-    node_grad, begun = reduce_slots(terms, z, n)
+    received = [sends[0]] + [swap(sends[k], "seq", k) for k in range(1, n)]
 
     bits = []
     while 2 << len(bits) < m:
         bits.append(2 << len(bits))
-    for one, two in zip(bits, bits[::-1]):
-        lower, upper = sum_pairs(lower, one), sum_pairs(upper, two)
-    part = jnp.concatenate([lower, upper], axis=0)
-    got = swap(part, "clus", 1)
-    both = jnp.where(core == 0, jnp.stack([part, got]), jnp.stack([got, part]))
-    weight_grad = both.reshape(plan.columns, width).astype(F32) / m
-
+
+    def across(x, stage):
+        pairs = [(i, i ^ (bits[-1 - stage] if i % 2 else bits[stage])) for i in range(m)]
+        return lax.ppermute(x, "clus", pairs)
+
+    def finish(part, got):
+        part = add(part, got)
+        for stage in range(1, len(bits)):
+            part = add(part, across(part, stage))
+        got = swap(part, "clus", 1)
+        both = jnp.where(core == 0, jnp.stack([part, got]), jnp.stack([got, part]))
+        return both.reshape(plan.columns, width).astype(F32) / m
+
+    got = across(part, 0)
+    weight_grad = lax.cond(
+        listed[0, 0] >= 0,
+        finish,
+        lambda part, got: jnp.zeros((plan.columns, width), F32),
+        part,
+        got,
+    )
+
+    received = after(received, weight_grad)
+    node_grad = sum(x[:, :width].astype(F32) for x in received).astype(BF16)
+    attended = jnp.zeros((rows, n * hcols), BF16)
+    for k in range(n):
+        attended = lax.dynamic_update_slice_in_dim(attended, received[k][:, width:], (z ^ k) * hcols, 1)
     return (attended[None], node_grad[None], weight_grad)
 
 

time: 107 us -> 79.3 us (0.74)
  the two profiles are of different devices: /device:TPU:0 before, /device:TPU:19 now
where the time goes in v3:
time: 79.3 us; the launch traced here: 79 us
  waiting for transfers between devices  30.7 us (39%)
  starting transfers between devices  22.2 us (28%)
  Pallas kernels  13.6 us (17%)
  other arithmetic  5.48 us (7%)
  local copies, waits for them, and re-layouts  5.47 us (7%)
  between operations  1.54 us (2%)
    ppermute x10, waiting for transfers between devices, swap(): return lax.ppermute(x, axis, [(i, i ^ bits) for i in range(size)])  14.9 us
    ppermute x2, waiting for transfers between devices, across(): return lax.ppermute(x, 'clus', pairs)  14.8 us
    pallas_call x6, Pallas kernels, call(): pl.pallas_call(functools.partial(kernel, plan), out_shape=out_shape, in_s...  13.6 us
    ppermute x10, starting transfers between devices, swap(): return lax.ppermute(x, axis, [(i, i ^ bits) for i in range(size)])  12.9 us
    ppermute x1, starting transfers between devices, gather_slots(): middle = lax.ppermute(after(x, far), 'seq', [(1, 2), (2, 1)])  5.19 us
    unnamed x10, local copies, waits for them, and re-layouts  3.06 us
    ppermute x1, starting transfers between devices, gather_slots(): ends = lax.ppermute(far, 'seq', [(2, 3), (1, 0)])  2.5 us
    div x1, other arithmetic, finish(): return both.reshape(plan.columns, width).astype(F32) / m  2.05 us
  transfers between devices with their start and end apart: 14, of which 6 were waited for; matrix products, arithmetic and copies ran while one was open for 7% of the time, Pallas kernels for 13%

profile of v3, /device:TPU:19, one launch (start us, length us, event | category | flops | bytes accessed | tf_op | source)
XLA Modules:
  0.0 79.0 jit_solution(6207572564155971284)
XLA Ops:
  0.6 0.1 collective-permute-start.3
  0.8 1.3 %collective-permute-start.2 = (bf16[128,1024]{1,0:T(8,128)(2,1)}, bf16[128,1024]{1,0:T(8,128)(2,1)S(1)}, u32[]{:S(2)}, u32[]{:S(2)}) collective-permute-start(bf16[128,1024]{1,0:T(8,128)(2,1)} %bitcast.34), channel_id=1, source_target_pairs={{0,8},{8,0},{16,24},{24,16},{1,9},{9,1},{17,25},{25,17},{2,10},{10... | collective-permute-start | bytes 786440 | tf_op jit(solution)/shard_map/ppermute | solution.py:241
  2.1 0.7 broadcast_xor_fusion
  2.8 0.1 broadcast_compare_fusion
  2.9 0.1 compare_convert_fusion.refs_5_
  3.0 0.1 and_reduce_fusion
  3.1 1.0 %dynamic-slice_bitcast_fusion = (bf16[128,256]{1,0:T(8,128)(2,1)S(1)}, bf16[128,256]{1,0:T(8,128)(2,1)S(1)}, bf16[128,256]{1,0:T(8,128)(2,1)S(1)}, bf16[128,256]{1,0:T(8,128)(2,1)S(1)}) fusion(bf16[1,128,1024]{2,1,0:T(8,128)(2,1)} %param.9, s32[]{:T(128)S(6)} %select_n.96, s32[]{:T(128)S(6)} %select_n.94, s32[]{:T(128)S(6)} %select_n.93, s32[]{:T(128)S(6)} %select_n.95), kind=kLoop, calls=%fused_computation.12 | loop fusion | bytes 524304 | tf_op jit(solution)/shard_map/dynamic_slice | solution.py:276
  4.1 7.6 %collective-permute-done.3.refs_2_ = bf16[128,1024]{1,0:T(8,128)(2,1)S(1)} collective-permute-done((bf16[128,1024]{1,0:T(8,128)(2,1)}, bf16[128,1024]{1,0:T(8,128)(2,1)S(1)}, u32[]{:S(2)}, u32[]{:S(2)}) %collective-permute-start.3) | collective-permute-done | bytes 262176 | tf_op jit(solution)/shard_map/ppermute | solution.py:241
  11.7 5.2 %collective-permute-start.4 = (bf16[128,1024]{1,0:T(8,128)(2,1)}, bf16[128,1024]{1,0:T(8,128)(2,1)S(1)}, u32[]{:S(2)}, u32[]{:S(2)}) collective-permute-start(bf16[128,1024]{1,0:T(8,128)(2,1)} %bitcast.35), channel_id=1, source_target_pairs={{8,16},{16,8},{9,17},{17,9},{10,18},{18,10},{11,19},{19,11},{12,20... | collective-permute-start | bytes 786440 | tf_op jit(solution)/shard_map/ppermute | solution.py:258
  16.9 2.5 %collective-permute-start.5 = (bf16[128,1024]{1,0:T(8,128)(2,1)S(1)}, bf16[128,1024]{1,0:T(8,128)(2,1)S(1)}, u32[]{:S(2)}, u32[]{:S(2)}) collective-permute-start(bf16[128,1024]{1,0:T(8,128)(2,1)S(1)} %collective-permute-done.3.refs_2_), channel_id=1, source_target_pairs={{16,24},{8,0},{17,25},{9,1},{18,26},{10,2},{19,27},{11,3},{20,28},... | collective-permute-start | bytes 786440 | tf_op jit(solution)/shard_map/ppermute | solution.py:257
  19.4 0.0 collective-permute-done.2.refs_1_
  19.5 0.1 collective-permute-start.6
  19.5 0.1 collective-permute-start.7
  19.6 2.6 %collective-permute-start.8 = (bf16[128,256]{1,0:T(8,128)(2,1)S(1)}, bf16[128,256]{1,0:T(8,128)(2,1)S(1)}, u32[]{:S(2)}, u32[]{:S(2)}) collective-permute-start(bf16[128,256]{1,0:T(8,128)(2,1)S(1)} %get-tuple-element.44), channel_id=1, source_target_pairs={{0,24},{8,16},{16,8},{24,0},{1,25},{9,17},{17,9},{25,1},{2,26},{10... | collective-permute-start | bytes 196616 | tf_op jit(solution)/shard_map/ppermute | solution.py:241
  22.2 0.0 copy-start
  22.2 1.4 %copy-done = bf16[768,1024]{1,0:T(8,128)(2,1)S(1)} copy-done((bf16[768,1024]{1,0:T(8,128)(2,1)S(1)}, bf16[768,1024]{1,0:T(8,128)(2,1)}, u32[]{:S(2)}) %copy-start) | copy-done | bytes 1572888
  23.6 0.0 copy-start.2
  23.6 0.9 %copy-done.2 = bf16[1,128,1024]{2,1,0:T(8,128)(2,1)S(1)} copy-done((bf16[1,128,1024]{2,1,0:T(8,128)(2,1)S(1)}, bf16[1,128,1024]{2,1,0:T(8,128)(2,1)}, u32[]{:S(2)}) %copy-start.2) | copy-done | bytes 262168
  24.5 0.0 copy-start.1
  24.5 0.8 %shard_map.67 = (bf16[384,1024]{1,0:T(8,128)(2,1)S(1)}, bf16[384,768]{1,0:T(8,128)(2,1)S(1)}) custom-call(bf16[128,1024]{1,0:T(8,128)(2,1)S(1)} %bitcast.36, bf16[128,1024]{1,0:T(8,128)(2,1)S(1)} %collective-permute-done.2.refs_1_, bf16[128,1024]{1,0:T(8,128)(2,1)S(1)} %collective-permute-done.3.refs_2_, bf16[768,1024]{1,0:T(8,128)(2,1)S(1)} %copy-done), custom_call_target="tpu_custom_call" | custom-call | flops 603979776 | bytes 4194304 | tf_op jit(solution)/shard_map/pallas_call | solution.py:224
  25.4 0.0 collective-permute-done.4
  25.4 0.9 %collective-permute-done.5 = bf16[128,1024]{1,0:T(8,128)(2,1)S(1)} collective-permute-done((bf16[128,1024]{1,0:T(8,128)(2,1)S(1)}, bf16[128,1024]{1,0:T(8,128)(2,1)S(1)}, u32[]{:S(2)}, u32[]{:S(2)}) %collective-permute-start.5) | collective-permute-done | bytes 262176 | tf_op jit(solution)/shard_map/ppermute | solution.py:257
  26.4 0.0 copy-done.1
  26.4 6.4 %shard_map.68 = (bf16[4,512,512]{2,1,0:T(8,128)(2,1)S(1)}, f32[512,256]{1,0:T(8,128)S(1)}, bf16[512,1024]{1,0:T(8,128)(2,1)S(1)}, bf16[512,768]{1,0:T(8,128)(2,1)S(1)}) custom-call(bf16[384,768]{1,0:T(8,128)(2,1)S(1)} %get-tuple-element.36.refs_0_, bf16[384,1024]{1,0:T(8,128)(2,1)S(1)} %get-tuple-element.37.refs_1_, ...), custom_call_target="tpu_custom_call" | custom-call | flops 268435456 | bytes 4194304 | tf_op jit(solution)/shard_map/pallas_call | solution.py:224
  32.8 0.0 collective-permute-done.6.a_3_
  32.9 0.0 collective-permute-done.7.a_4_
  32.9 0.0 collective-permute-done.8.a_5_
  32.9 2.4 %shard_map.70 = (bf16[384,512]{1,0:T(8,128)(2,1)S(1)}, bf16[384,1024]{1,0:T(8,128)(2,1)S(1)}) custom-call(s32[1]{0:T(128)} %bitcast.13.a_0_, bf16[512,768]{1,0:T(8,128)(2,1)S(1)} %get-tuple-element.40.a_1_, bf16[128,256]{1,0:T(8,128)(2,1)S(1)} %get-tuple-element.41.a_2_, bf16[128,256]{1,0:T(8,128)(2,1)S(1)} %collective-permute-done.6.a_3_, ...), custom_call_target="tpu_custom_call" | custom-call | flops 671088640 | bytes 4194304 | tf_op jit(solution)/shard_map/pallas_call | solution.py:224
  35.3 3.2 %collective-permute-start.12 = (bf16[384,1024]{1,0:T(8,128)(2,1)S(1)}, bf16[384,1024]{1,0:T(8,128)(2,1)S(1)}, u32[]{:S(2)}, u32[]{:S(2)}) collective-permute-start(bf16[384,1024]{1,0:T(8,128)(2,1)S(1)} %get-tuple-element.52), channel_id=1, source_target_pairs={{0,1},{1,0},{2,3},{3,2},{4,5},{5,4},{6,7},{7,6},{8,9},{9,8},{10,11... | collective-permute-start | bytes 2359304 | tf_op jit(solution)/shard_map/ppermute | solution.py:241
  38.5 2.0 %shard_map.69.refs_3_.grad_ref = bf16[384,512]{1,0:T(8,128)(2,1)S(1)} custom-call(s32[1]{0:T(128)} %bitcast.3.a_0_.refs_0_, bf16[512,768]{1,0:T(8,128)(2,1)S(1)} %get-tuple-element.40.a_1_, bf16[128,256]{1,0:T(8,128)(2,1)S(1)} %get-tuple-element.41.a_2_, bf16[128,256]{1,0:T(8,128)(2,1)S(1)} %collective-permute-done.6.a_3_, ...), custom_call_target="tpu_custom_call" | custom-call | flops 268435456 | bytes 4194304 | tf_op jit(solution)/shard_map/pallas_call | solution.py:224
  40.5 0.0 collective-permute-done.12.got_ref
  40.5 0.6 shard_map.72
  41.1 0.0 copy-start.4
  41.1 1.3 %collective-permute-start.13 = (bf16[384,1024]{1,0:T(8,128)(2,1)S(1)}, bf16[384,1024]{1,0:T(8,128)(2,1)S(1)}, u32[]{:S(2)}, u32[]{:S(2)}) collective-permute-start(bf16[384,1024]{1,0:T(8,128)(2,1)S(1)} %shard_map.72), channel_id=1, source_target_pairs={{0,2},{1,5},{2,0},{3,7},{4,6},{5,1},{6,4},{7,3},{8,10},{9,13},{10,... | collective-permute-start | bytes 2359304 | tf_op jit(solution)/shard_map/ppermute | solution.py:371
  42.4 1.3 %shard_map.71 = (bf16[128,1280]{1,0:T(8,128)(2,1)S(1)}, bf16[128,1280]{1,0:T(8,128)(2,1)S(1)}, bf16[128,1280]{1,0:T(8,128)(2,1)S(1)}, bf16[128,1280]{1,0:T(8,128)(2,1)S(1)}) custom-call(s32[1]{0:T(128)} %bitcast.3.a_0_.refs_0_, bf16[768,1024]{1,0:T(8,128)(2,1)S(1)} %copy-done.1, f32[512,256]{1,0:T(8,128)S(1)} %get-tuple-element.39.a_7_.refs_2_, ...), custom_call_target="tpu_custom_call" | custom-call | flops 805306368 | bytes 4194304 | tf_op jit(solution)/shard_map/pallas_call | solution.py:224
  43.7 0.1 collective-permute-start.10
  43.8 3.4 %collective-permute-start.11 = (bf16[128,1280]{1,0:T(8,128)(2,1)S(1)}, bf16[128,1280]{1,0:T(8,128)(2,1)S(1)}, u32[]{:S(2)}, u32[]{:S(2)}) collective-permute-start(bf16[128,1280]{1,0:T(8,128)(2,1)S(1)} %get-tuple-element.51), channel_id=1, source_target_pairs={{0,24},{8,16},{16,8},{24,0},{1,25},{9,17},{17,9},{25,1},{2,26},{10... | collective-permute-start | bytes 983048 | tf_op jit(solution)/shard_map/ppermute | solution.py:241
  47.2 0.2 collective-permute-start.9
  47.3 0.0 copy-done.4
  47.3 0.5 slice.38
  48.5 3.8 %collective-permute-done.13 = bf16[384,1024]{1,0:T(8,128)(2,1)S(1)} collective-permute-done((bf16[384,1024]{1,0:T(8,128)(2,1)S(1)}, bf16[384,1024]{1,0:T(8,128)(2,1)S(1)}, u32[]{:S(2)}, u32[]{:S(2)}) %collective-permute-start.13) | collective-permute-done | bytes 786464 | tf_op jit(solution)/shard_map/ppermute | solution.py:371
  52.3 17.8 %conditional.1 = (f32[768,1024]{1,0:T(8,128)}) conditional(s32[]{:T(128)} %bitcast.14, () %tuple.19, (s32[]{:T(128)}, bf16[384,1024]{1,0:T(8,128)(2,1)S(1)}, bf16[384,1024]{1,0:T(8,128)(2,1)S(1)}) %tuple.20), branch_computations={%region_1.2_spmd, %region_2.3_spmd} | conditional | flops 7077889 | bytes 15728738 | solution.py:382
  52.3 0.3 add_convert_fusion.1
  52.6 0.3 collective-permute-start
  52.9 11.0 %collective-permute-done = bf16[384,1024]{1,0:T(8,128)(2,1)S(1)} collective-permute-done((bf16[384,1024]{1,0:T(8,128)(2,1)S(1)}, bf16[384,1024]{1,0:T(8,128)(2,1)S(1)}, u32[]{:S(2)}, u32[]{:S(2)}) %collective-permute-start) | collective-permute-done | bytes 786464 | tf_op jit(solution)/shard_map/cond/branch_1_fun/ppermute | solution.py:371
  63.9 0.3 add_convert_fusion
  64.2 1.9 %collective-permute-start.1 = (bf16[384,1024]{1,0:T(8,128)(2,1)S(1)}, bf16[384,1024]{1,0:T(8,128)(2,1)S(1)}, u32[]{:S(2)}, u32[]{:S(2)}) collective-permute-start(bf16[384,1024]{1,0:T(8,128)(2,1)S(1)} %add_convert_fusion), channel_id=1, source_target_pairs={{0,1},{1,0},{2,3},{3,2},{4,5},{5,4},{6,7},{7,6},{8,9},{9,8},{10,11... | collective-permute-start | bytes 2359304 | tf_op jit(solution)/shard_map/cond/branch_1_fun/ppermute | solution.py:241
  66.2 1.9 %collective-permute-done.1 = bf16[384,1024]{1,0:T(8,128)(2,1)S(1)} collective-permute-done((bf16[384,1024]{1,0:T(8,128)(2,1)S(1)}, bf16[384,1024]{1,0:T(8,128)(2,1)S(1)}, u32[]{:S(2)}, u32[]{:S(2)}) %collective-permute-start.1) | collective-permute-done | bytes 786464 | tf_op jit(solution)/shard_map/cond/branch_1_fun/ppermute | solution.py:241
  68.1 2.0 %convert_multiply_fusion = f32[2,384,1024]{2,1,0:T(8,128)} fusion(bf16[1,384,1024]{2,1,0:T(8,128)(2,1)S(1)} %bitcast.39, bf16[1,384,1024]{2,1,0:T(8,128)(2,1)S(1)} %bitcast.37, pred[]{:T(512)S(6)} %eq.29), kind=kLoop, calls=%fused_computation | loop fusion | flops 3932160 | bytes 4718593 | tf_op jit(solution)/shard_map/cond/branch_1_fun/div | solution.py:379
  70.2 0.0 collective-permute-done.10
  70.2 5.4 %collective-permute-done.11 = bf16[128,1280]{1,0:T(8,128)(2,1)S(1)} collective-permute-done((bf16[128,1280]{1,0:T(8,128)(2,1)S(1)}, bf16[128,1280]{1,0:T(8,128)(2,1)S(1)}, u32[]{:S(2)}, u32[]{:S(2)}) %collective-permute-start.11) | collective-permute-done | bytes 327712 | tf_op jit(solution)/shard_map/ppermute | solution.py:241
  75.5 0.0 collective-permute-done.9
  75.6 0.9 %bitcast_dynamic-update-slice_fusion.2 = bf16[1,128,1024]{2,1,0:T(8,128)(2,1)S(1)} fusion(bf16[1,128,1024]{2,1,0:T(8,128)(2,1)S(1)} %bitcast_dynamic-update-slice_fusion.3, s32[]{:T(128)S(6)} %select_n.94, bf16[128,1280]{1,0:T(8,128)(2,1)} %collective-permute-done.9), kind=kLoop, calls=%fused_computation.10 | loop fusion | bytes 131076 | tf_op jit(solution)/shard_map/dynamic_update_slice | solution.py:394
  76.4 1.8 %fusion = bf16[1,128,1024]{2,1,0:T(8,128)(2,1)} fusion(bf16[128,1280]{1,0:T(8,128)(2,1)S(1)} %collective-permute-done.11, bf16[128,1280]{1,0:T(8,128)(2,1)S(1)} %collective-permute-done.10, bf16[128,1280]{1,0:T(8,128)(2,1)} %collective-permute-done.9, bf16[128,1280]{1,0:T(8,128)(2,1)S(1)} %get-tuple-element.53), kind=kLoop, calls=%fused_computation.5 | loop fusion | flops 1048576 | bytes 1310720 | tf_op jit(solution)/shard_map/broadcast_in_dim | solution.py:395
  78.2 0.0 copy-start.3
  78.3 0.7 copy-done.3
  (12 shorter events, 0.1 us)
Async XLA Ops:
  0.6 11.1 %collective-permute-start.3 = (bf16[128,1024]{1,0:T(8,128)(2,1)}, bf16[128,1024]{1,0:T(8,128)(2,1)S(1)}, u32[]{:S(2)}, u32[]{:S(2)}) collective-permute-start(bf16[128,1024]{1,0:T(8,128)(2,1)} %bitcast.33), channel_id=1, source_target_pairs={{0,16},{8,24},{16,0},{24,8},{1,17},{9,25},{17,1},{25,9},{2,18},{10... | collective-permute-start | bytes 786440 | tf_op jit(solution)/shard_map/ppermute | solution.py:241
  0.8 18.7 %collective-permute-start.2 = (bf16[128,1024]{1,0:T(8,128)(2,1)}, bf16[128,1024]{1,0:T(8,128)(2,1)S(1)}, u32[]{:S(2)}, u32[]{:S(2)}) collective-permute-start(bf16[128,1024]{1,0:T(8,128)(2,1)} %bitcast.34), channel_id=1, source_target_pairs={{0,8},{8,0},{16,24},{24,16},{1,9},{9,1},{17,25},{25,17},{2,10},{10... | collective-permute-start | bytes 786440 | tf_op jit(solution)/shard_map/ppermute | solution.py:241
  11.7 13.6 %collective-permute-start.4 = (bf16[128,1024]{1,0:T(8,128)(2,1)}, bf16[128,1024]{1,0:T(8,128)(2,1)S(1)}, u32[]{:S(2)}, u32[]{:S(2)}) collective-permute-start(bf16[128,1024]{1,0:T(8,128)(2,1)} %bitcast.35), channel_id=1, source_target_pairs={{8,16},{16,8},{9,17},{17,9},{10,18},{18,10},{11,19},{19,11},{12,20... | collective-permute-start | bytes 786440 | tf_op jit(solution)/shard_map/ppermute | solution.py:258
  16.9 9.4 %collective-permute-start.5 = (bf16[128,1024]{1,0:T(8,128)(2,1)S(1)}, bf16[128,1024]{1,0:T(8,128)(2,1)S(1)}, u32[]{:S(2)}, u32[]{:S(2)}) collective-permute-start(bf16[128,1024]{1,0:T(8,128)(2,1)S(1)} %collective-permute-done.3.refs_2_), channel_id=1, source_target_pairs={{16,24},{8,0},{17,25},{9,1},{18,26},{10,2},{19,27},{11,3},{20,28},... | collective-permute-start | bytes 786440 | tf_op jit(solution)/shard_map/ppermute | solution.py:257
  19.5 13.4 %collective-permute-start.6 = (bf16[128,256]{1,0:T(8,128)(2,1)S(1)}, bf16[128,256]{1,0:T(8,128)(2,1)S(1)}, u32[]{:S(2)}, u32[]{:S(2)}) collective-permute-start(bf16[128,256]{1,0:T(8,128)(2,1)S(1)} %get-tuple-element.42), channel_id=1, source_target_pairs={{0,8},{8,0},{16,24},{24,16},{1,9},{9,1},{17,25},{25,17},{2,10},{10... | collective-permute-start | bytes 196616 | tf_op jit(solution)/shard_map/ppermute | solution.py:241
  19.5 13.3 %collective-permute-start.7 = (bf16[128,256]{1,0:T(8,128)(2,1)S(1)}, bf16[128,256]{1,0:T(8,128)(2,1)S(1)}, u32[]{:S(2)}, u32[]{:S(2)}) collective-permute-start(bf16[128,256]{1,0:T(8,128)(2,1)S(1)} %get-tuple-element.43), channel_id=1, source_target_pairs={{0,16},{8,24},{16,0},{24,8},{1,17},{9,25},{17,1},{25,9},{2,18},{10... | collective-permute-start | bytes 196616 | tf_op jit(solution)/shard_map/ppermute | solution.py:241
  19.6 13.2 %collective-permute-start.8 = (bf16[128,256]{1,0:T(8,128)(2,1)S(1)}, bf16[128,256]{1,0:T(8,128)(2,1)S(1)}, u32[]{:S(2)}, u32[]{:S(2)}) collective-permute-start(bf16[128,256]{1,0:T(8,128)(2,1)S(1)} %get-tuple-element.44), channel_id=1, source_target_pairs={{0,24},{8,16},{16,8},{24,0},{1,25},{9,17},{17,9},{25,1},{2,26},{10... | collective-permute-start | bytes 196616 | tf_op jit(solution)/shard_map/ppermute | solution.py:241
  22.2 1.4 %copy-start = (bf16[768,1024]{1,0:T(8,128)(2,1)S(1)}, bf16[768,1024]{1,0:T(8,128)(2,1)}, u32[]{:S(2)}) copy-start(bf16[768,1024]{1,0:T(8,128)(2,1)} %refs_1_.1) | copy-start | bytes 4718596
  23.6 0.9 %copy-start.2 = (bf16[1,128,1024]{2,1,0:T(8,128)(2,1)S(1)}, bf16[1,128,1024]{2,1,0:T(8,128)(2,1)}, u32[]{:S(2)}) copy-start(bf16[1,128,1024]{2,1,0:T(8,128)(2,1)} %param.6) | copy-start | bytes 786436
  24.5 1.8 %copy-start.1 = (bf16[768,1024]{1,0:T(8,128)(2,1)S(1)}, bf16[768,1024]{1,0:T(8,128)(2,1)}, u32[]{:S(2)}) copy-start(bf16[768,1024]{1,0:T(8,128)(2,1)} %refs_1_.1) | copy-start | bytes 4718596
  35.3 5.2 %collective-permute-start.12 = (bf16[384,1024]{1,0:T(8,128)(2,1)S(1)}, bf16[384,1024]{1,0:T(8,128)(2,1)S(1)}, u32[]{:S(2)}, u32[]{:S(2)}) collective-permute-start(bf16[384,1024]{1,0:T(8,128)(2,1)S(1)} %get-tuple-element.52), channel_id=1, source_target_pairs={{0,1},{1,0},{2,3},{3,2},{4,5},{5,4},{6,7},{7,6},{8,9},{9,8},{10,11... | collective-permute-start | bytes 2359304 | tf_op jit(solution)/shard_map/ppermute | solution.py:241
  41.1 6.2 %copy-start.4 = (s32[1,8,2]{1,2,0:T(2,128)S(1)}, s32[1,8,2]{1,2,0:T(2,128)}, u32[]{:S(2)}) copy-start(s32[1,8,2]{1,2,0:T(2,128)} %param.8) | copy-start | bytes 196
  41.1 11.2 %collective-permute-start.13 = (bf16[384,1024]{1,0:T(8,128)(2,1)S(1)}, bf16[384,1024]{1,0:T(8,128)(2,1)S(1)}, u32[]{:S(2)}, u32[]{:S(2)}) collective-permute-start(bf16[384,1024]{1,0:T(8,128)(2,1)S(1)} %shard_map.72), channel_id=1, source_target_pairs={{0,2},{1,5},{2,0},{3,7},{4,6},{5,1},{6,4},{7,3},{8,10},{9,13},{10,... | collective-permute-start | bytes 2359304 | tf_op jit(solution)/shard_map/ppermute | solution.py:371
  43.7 26.4 %collective-permute-start.10 = (bf16[128,1280]{1,0:T(8,128)(2,1)S(1)}, bf16[128,1280]{1,0:T(8,128)(2,1)S(1)}, u32[]{:S(2)}, u32[]{:S(2)}) collective-permute-start(bf16[128,1280]{1,0:T(8,128)(2,1)S(1)} %get-tuple-element.50), channel_id=1, source_target_pairs={{0,16},{8,24},{16,0},{24,8},{1,17},{9,25},{17,1},{25,9},{2,18},{10... | collective-permute-start | bytes 983048 | tf_op jit(solution)/shard_map/ppermute | solution.py:241
  43.8 31.7 %collective-permute-start.11 = (bf16[128,1280]{1,0:T(8,128)(2,1)S(1)}, bf16[128,1280]{1,0:T(8,128)(2,1)S(1)}, u32[]{:S(2)}, u32[]{:S(2)}) collective-permute-start(bf16[128,1280]{1,0:T(8,128)(2,1)S(1)} %get-tuple-element.51), channel_id=1, source_target_pairs={{0,24},{8,16},{16,8},{24,0},{1,25},{9,17},{17,9},{25,1},{2,26},{10... | collective-permute-start | bytes 983048 | tf_op jit(solution)/shard_map/ppermute | solution.py:241
  47.2 28.4 %collective-permute-start.9 = (bf16[128,1280]{1,0:T(8,128)(2,1)S(1)}, bf16[128,1280]{1,0:T(8,128)(2,1)}, u32[]{:S(2)}, u32[]{:S(2)}) collective-permute-start(bf16[128,1280]{1,0:T(8,128)(2,1)S(1)} %get-tuple-element.49), channel_id=1, source_target_pairs={{0,8},{8,0},{16,24},{24,16},{1,9},{9,1},{17,25},{25,17},{2,10},{10... | collective-permute-start | bytes 983048 | tf_op jit(solution)/shard_map/ppermute | solution.py:241
  52.6 11.3 %collective-permute-start = (bf16[384,1024]{1,0:T(8,128)(2,1)S(1)}, bf16[384,1024]{1,0:T(8,128)(2,1)S(1)}, u32[]{:S(2)}, u32[]{:S(2)}) collective-permute-start(bf16[384,1024]{1,0:T(8,128)(2,1)S(1)} %add_convert_fusion.1), channel_id=1, source_target_pairs={{0,4},{1,3},{2,6},{3,1},{4,0},{5,7},{6,2},{7,5},{8,12},{9,11},{10,... | collective-permute-start | bytes 2359304 | tf_op jit(solution)/shard_map/cond/branch_1_fun/ppermute | solution.py:371
  64.2 3.9 %collective-permute-start.1 = (bf16[384,1024]{1,0:T(8,128)(2,1)S(1)}, bf16[384,1024]{1,0:T(8,128)(2,1)S(1)}, u32[]{:S(2)}, u32[]{:S(2)}) collective-permute-start(bf16[384,1024]{1,0:T(8,128)(2,1)S(1)} %add_convert_fusion), channel_id=1, source_target_pairs={{0,1},{1,0},{2,3},{3,2},{4,5},{5,4},{6,7},{7,6},{8,9},{9,8},{10,11... | collective-permute-start | bytes 2359304 | tf_op jit(solution)/shard_map/cond/branch_1_fun/ppermute | solution.py:241
  78.2 0.7 copy-start.3

commit v4 on v3

--- a/solution.py
+++ b/solution.py
@@ -186,8 +186,12 @@
         wgrad_ref[...] = mm(grad_ref[...], full_ref[...]).astype(BF16)
 
 
-def weight_kernel(plan, grad_ref, full_ref, got_ref, part_ref):
-    part_ref[...] = (mm(grad_ref[...], full_ref[...]) + got_ref[...].astype(F32)).astype(BF16)
+def weight_kernel(plan, grad_ref, full_ref, got_ref, *parts):
+    size = parts[0].shape[0]
+    for i, part in enumerate(parts):
+        here = slice(i * size, (i + 1) * size)
+        product = mm(grad_ref[here, :], full_ref[...])
+        part[...] = (product + got_ref[here, :].astype(F32)).astype(BF16)
 
 
 def whole_weight_kernel(plan, grad_ref, full_ref, wgrad_ref):
@@ -214,6 +218,34 @@
         sends[s][:, width:] = sum_ref[here, :].astype(BF16)
 
 
+def scale_kernel(plan, m, which, *refs):
+    out = refs[-1]
+    count = (len(refs) - 1) // 2
+    size = refs[0].shape[0]
+    for i, ref in enumerate(refs[:-1]):
+        side = which[0] if i < count else 1 - which[0]
+        start = side * (count * size) + (i % count) * size
+        out[pl.ds(pl.multiple_of(start, size), size), :] = ref[...].astype(F32) * (1.0 / m)
+
+
+def combine_kernel(plan, place, *refs):
+    n, hcols = plan.n, plan.heads * HD
+    received, (node_grad, attended) = refs[:-2], refs[-2:]
+    width = node_grad.shape[1]
+    pieces = [x[:, width : width + hcols] for x in received[:n]]
+    terms = [x[:, :width] for x in received[:n]]
+    total = terms[0].astype(F32)
+    for term in terms[1:]:
+        total = total + term.astype(F32)
+    node_grad[...] = total.astype(BF16)
+    for k, piece in enumerate(pieces):
+        start = (place[0] ^ k) * hcols
+        if hcols % 128 == 0:
+            attended[:, pl.ds(pl.multiple_of(start, hcols), hcols)] = piece
+        else:
+            attended[k, :, :] = piece
+
+
 def size(x):
     return math.prod(x.shape) * jnp.dtype(x.dtype).itemsize
 
@@ -249,6 +281,10 @@
     return (a.astype(F32) + b.astype(F32)).astype(BF16)
 
 
+def exchange_slots(plan, sends, n):
+    return [sends[0]] + [swap(sends[k], "seq", k) for k in range(1, n)]
+
+
 def gather_slots(x, z, n):
     if n != 4:
         return [x] + [swap(x, "seq", k) for k in range(1, n)]
@@ -275,9 +311,6 @@
     def for_slot(k):
         return lax.dynamic_slice_in_dim(grad_out[0], (z ^ k) * hcols, hcols, 1)
 
-    own, *sent = after([for_slot(k) for k in range(n)], *xs[1:3])
-    grads = [own] + [swap(sent[k - 1], "seq", k) for k in range(1, n)]
-
     earlier = nodes - rows
     known_x, known = call(
         project_kernel,
@@ -287,6 +320,9 @@
         2 * earlier * plan.columns * width,
         [*xs[:-1], qkv_weight],
     )
+
+    own, *sent = after([for_slot(k) for k in range(n)], known)
+    grads = [own] + [swap(sent[k - 1], "seq", k) for k in range(1, n)]
 
     per_dev = rows // BLOCK
     blocks = nodes // BLOCK
@@ -339,18 +375,18 @@
     )
     grad_t = [grad_own, *grad_t]
     count = 2 * nodes * plan.gcols * width
+    half = plan.gcols // 2
     if plan.groups > 1:
-        (part,) = call(
-            weight_kernel, plan, [array(plan.gcols, width)], [], count, [grad_own, full, got]
+        parts = call(
+            weight_kernel, plan, [array(half, width)] * 2, [], count, [grad_own, full, got]
         )
     else:
-        half = plan.gcols // 2
         (wgrad,) = call(
             whole_weight_kernel, plan, [array(plan.gcols, width)], [], count, [grad_own, full]
         )
         keep = lax.dynamic_slice_in_dim(wgrad, core * half, half, 0)
         send = lax.dynamic_slice_in_dim(wgrad, (1 - core) * half, half, 0)
-        part = add(keep, swap(send, "clus", 1))
+        parts = [add(keep, swap(send, "clus", 1))]
     sends = call(
         term_kernel,
         plan,
@@ -360,7 +396,7 @@
         [core.reshape(1), qkv_weight, sums, *grad_t],
         scalar=True,
     )
-    received = [sends[0]] + [swap(sends[k], "seq", k) for k in range(1, n)]
+    received = exchange_slots(plan, sends, n)
 
     bits = []
     while 2 << len(bits) < m:
@@ -370,28 +406,46 @@
         pairs = [(i, i ^ (bits[-1 - stage] if i % 2 else bits[stage])) for i in range(m)]
         return lax.ppermute(x, "clus", pairs)
 
-    def finish(part, got):
-        part = add(part, got)
+    def finish(parts, gots):
+        parts = [add(part, got) for part, got in zip(parts, gots)]
         for stage in range(1, len(bits)):
-            part = add(part, across(part, stage))
-        got = swap(part, "clus", 1)
-        both = jnp.where(core == 0, jnp.stack([part, got]), jnp.stack([got, part]))
-        return both.reshape(plan.columns, width).astype(F32) / m
-
-    got = across(part, 0)
+            gots = [across(part, stage) for part in parts]
+            parts = [add(part, got) for part, got in zip(parts, gots)]
+        gots = [swap(part, "clus", 1) for part in parts]
+        (result,) = call(
+            lambda *a: scale_kernel(a[0], m, *a[1:]),
+            plan,
+            [array(plan.columns, width, dtype=F32)],
+            [],
+            0,
+            [core.reshape(1), *parts, *gots],
+            scalar=True,
+        )
+        return result
+
+    gots = [across(part, 0) for part in parts]
     weight_grad = lax.cond(
         listed[0, 0] >= 0,
         finish,
-        lambda part, got: jnp.zeros((plan.columns, width), F32),
-        part,
-        got,
+        lambda parts, gots: jnp.zeros((plan.columns, width), F32),
+        parts,
+        gots,
     )
 
     received = after(received, weight_grad)
-    node_grad = sum(x[:, :width].astype(F32) for x in received).astype(BF16)
-    attended = jnp.zeros((rows, n * hcols), BF16)
-    for k in range(n):
-        attended = lax.dynamic_update_slice_in_dim(attended, received[k][:, width:], (z ^ k) * hcols, 1)
+    aligned = hcols % 128 == 0
+    node_grad, attended = call(
+        combine_kernel,
+        plan,
+        [array(rows, width), array(rows, n * hcols) if aligned else array(n, rows, hcols)],
+        [],
+        0,
+        [z.reshape(1), *received],
+        scalar=True,
+    )
+    if not aligned:
+        order = jnp.arange(n, dtype=jnp.int32) ^ z
+        attended = attended[order].transpose(1, 0, 2).reshape(rows, n * hcols)
     return (attended[None], node_grad[None], weight_grad)
 
 

time: 79.3 us -> 75.7 us (0.955)
  the two profiles are of different devices: /device:TPU:19 before, /device:TPU:14 now
where the time goes in v4:
time: 75.7 us; the launch traced here: 75.4 us
  waiting for transfers between devices  31.7 us (42%)
  starting transfers between devices  20.4 us (27%)
  Pallas kernels  16.3 us (22%)
  local copies, waits for them, and re-layouts  3.87 us (5%)
  other arithmetic  1.57 us (2%)
  between operations  1.51 us (2%)
    ppermute x11, waiting for transfers between devices, swap(): return lax.ppermute(x, axis, [(i, i ^ bits) for i in range(size)])  19.5 us
    pallas_call x8, Pallas kernels, call(): pl.pallas_call(functools.partial(kernel, plan), out_shape=out_shape, in_s...  16.3 us
    ppermute x11, starting transfers between devices, swap(): return lax.ppermute(x, axis, [(i, i ^ bits) for i in range(size)])  12.2 us
    ppermute x4, waiting for transfers between devices, across(): return lax.ppermute(x, 'clus', pairs)  12.1 us
    ppermute x4, starting transfers between devices, across(): return lax.ppermute(x, 'clus', pairs)  4.25 us
    unnamed x8, local copies, waits for them, and re-layouts  2.36 us
    ppermute x1, starting transfers between devices, gather_slots(): ends = lax.ppermute(far, 'seq', [(2, 3), (1, 0)])  2.03 us
    ppermute x1, starting transfers between devices, gather_slots(): middle = lax.ppermute(after(x, far), 'seq', [(1, 2), (2, 1)])  1.91 us
  transfers between devices with their start and end apart: 17, of which 8 were waited for; matrix products, arithmetic and copies ran while one was open for 4% of the time, Pallas kernels for 16%

profile of v4, /device:TPU:14, one launch (start us, length us, event | category | flops | bytes accessed | tf_op | source)
XLA Modules:
  0.0 75.4 jit_solution(3440841775872733778)
XLA Ops:
  0.6 2.7 %collective-permute-start.5 = (bf16[128,1024]{1,0:T(8,128)(2,1)}, bf16[128,1024]{1,0:T(8,128)(2,1)S(1)}, u32[]{:S(2)}, u32[]{:S(2)}) collective-permute-start(bf16[128,1024]{1,0:T(8,128)(2,1)} %bitcast.24), channel_id=1, source_target_pairs={{0,16},{8,24},{16,0},{24,8},{1,17},{9,25},{17,1},{25,9},{2,18},{10... | collective-permute-start | bytes 786440 | tf_op jit(solution)/shard_map/ppermute | solution.py:273
  3.3 0.4 collective-permute-start.4
  3.7 0.7 broadcast_xor_fusion
  4.4 0.1 broadcast_compare_fusion
  4.5 0.1 compare_convert_fusion.refs_5_
  4.7 0.1 and_reduce_fusion
  4.8 1.0 %dynamic-slice_bitcast_fusion = (bf16[128,256]{1,0:T(8,128)(2,1)S(1)}, bf16[128,256]{1,0:T(8,128)(2,1)S(1)}, bf16[128,256]{1,0:T(8,128)(2,1)S(1)}, bf16[128,256]{1,0:T(8,128)(2,1)S(1)}) fusion(bf16[1,128,1024]{2,1,0:T(8,128)(2,1)} %param.9, s32[]{:T(128)S(6)} %select_n.82, s32[]{:T(128)S(6)} %select_n.80, s32[]{:T(128)S(6)} %select_n.79, s32[]{:T(128)S(6)} %select_n.81), kind=kLoop, calls=%fused_computation.6 | loop fusion | bytes 524304 | tf_op jit(solution)/shard_map/dynamic_slice | solution.py:312
  5.8 8.9 %collective-permute-done.5.refs_2_ = bf16[128,1024]{1,0:T(8,128)(2,1)S(1)} collective-permute-done((bf16[128,1024]{1,0:T(8,128)(2,1)}, bf16[128,1024]{1,0:T(8,128)(2,1)S(1)}, u32[]{:S(2)}, u32[]{:S(2)}) %collective-permute-start.5) | collective-permute-done | bytes 262176 | tf_op jit(solution)/shard_map/ppermute | solution.py:273
  14.7 1.9 %collective-permute-start.6 = (bf16[128,1024]{1,0:T(8,128)(2,1)}, bf16[128,1024]{1,0:T(8,128)(2,1)S(1)}, u32[]{:S(2)}, u32[]{:S(2)}) collective-permute-start(bf16[128,1024]{1,0:T(8,128)(2,1)} %bitcast.26), channel_id=1, source_target_pairs={{8,16},{16,8},{9,17},{17,9},{10,18},{18,10},{11,19},{19,11},{12,20... | collective-permute-start | bytes 786440 | tf_op jit(solution)/shard_map/ppermute | solution.py:294
  16.6 2.0 %collective-permute-start.7 = (bf16[128,1024]{1,0:T(8,128)(2,1)S(1)}, bf16[128,1024]{1,0:T(8,128)(2,1)S(1)}, u32[]{:S(2)}, u32[]{:S(2)}) collective-permute-start(bf16[128,1024]{1,0:T(8,128)(2,1)S(1)} %collective-permute-done.5.refs_2_), channel_id=1, source_target_pairs={{16,24},{8,0},{17,25},{9,1},{18,26},{10,2},{19,27},{11,3},{20,28},... | collective-permute-start | bytes 786440 | tf_op jit(solution)/shard_map/ppermute | solution.py:293
  18.6 0.0 collective-permute-done.4.refs_1_
  18.6 0.0 copy-start
  18.7 1.4 %copy-done = bf16[768,1024]{1,0:T(8,128)(2,1)S(1)} copy-done((bf16[768,1024]{1,0:T(8,128)(2,1)S(1)}, bf16[768,1024]{1,0:T(8,128)(2,1)}, u32[]{:S(2)}) %copy-start) | copy-done | bytes 1572888
  20.1 0.0 copy-start.2
  20.1 0.9 %copy-done.2 = bf16[1,128,1024]{2,1,0:T(8,128)(2,1)S(1)} copy-done((bf16[1,128,1024]{2,1,0:T(8,128)(2,1)S(1)}, bf16[1,128,1024]{2,1,0:T(8,128)(2,1)}, u32[]{:S(2)}) %copy-start.2) | copy-done | bytes 262168
  21.0 0.0 copy-start.1
  21.0 0.8 %shard_map.67 = (bf16[384,1024]{1,0:T(8,128)(2,1)S(1)}, bf16[384,768]{1,0:T(8,128)(2,1)S(1)}) custom-call(bf16[128,1024]{1,0:T(8,128)(2,1)S(1)} %bitcast.27, bf16[128,1024]{1,0:T(8,128)(2,1)S(1)} %collective-permute-done.4.refs_1_, bf16[128,1024]{1,0:T(8,128)(2,1)S(1)} %collective-permute-done.5.refs_2_, bf16[768,1024]{1,0:T(8,128)(2,1)S(1)} %copy-done), custom_call_target="tpu_custom_call" | custom-call | flops 603979776 | bytes 4194304 | tf_op jit(solution)/shard_map/pallas_call | solution.py:256
  21.8 0.1 collective-permute-start.8
  21.9 3.9 %collective-permute-start.9 = (bf16[128,256]{1,0:T(8,128)(2,1)S(1)}, bf16[128,256]{1,0:T(8,128)(2,1)S(1)}, u32[]{:S(2)}, u32[]{:S(2)}) collective-permute-start(bf16[128,256]{1,0:T(8,128)(2,1)S(1)} %get-tuple-element.53), channel_id=1, source_target_pairs={{0,16},{8,24},{16,0},{24,8},{1,17},{9,25},{17,1},{25,9},{2,18},{10... | collective-permute-start | bytes 196616 | tf_op jit(solution)/shard_map/ppermute | solution.py:273
  25.8 0.0 collective-permute-start.10
  25.9 0.0 collective-permute-done.6
  25.9 0.0 collective-permute-done.7
  25.9 0.0 copy-done.1
  25.9 6.4 %shard_map.68 = (bf16[4,512,512]{2,1,0:T(8,128)(2,1)S(1)}, f32[512,256]{1,0:T(8,128)S(1)}, bf16[512,1024]{1,0:T(8,128)(2,1)S(1)}, bf16[512,768]{1,0:T(8,128)(2,1)S(1)}) custom-call(bf16[384,768]{1,0:T(8,128)(2,1)S(1)} %get-tuple-element.46.refs_0_, bf16[384,1024]{1,0:T(8,128)(2,1)S(1)} %get-tuple-element.47.refs_1_, ...), custom_call_target="tpu_custom_call" | custom-call | flops 268435456 | bytes 4194304 | tf_op jit(solution)/shard_map/pallas_call | solution.py:256
  32.4 0.0 collective-permute-done.8.a_3_
  32.4 0.0 collective-permute-done.9.a_4_
  32.4 0.0 collective-permute-done.10.a_5_
  32.4 2.4 %shard_map.70 = (bf16[384,512]{1,0:T(8,128)(2,1)S(1)}, bf16[384,1024]{1,0:T(8,128)(2,1)S(1)}) custom-call(s32[1]{0:T(128)} %bitcast.12.a_0_, bf16[512,768]{1,0:T(8,128)(2,1)S(1)} %get-tuple-element.50.a_1_, bf16[128,256]{1,0:T(8,128)(2,1)S(1)} %get-tuple-element.51.a_2_, bf16[128,256]{1,0:T(8,128)(2,1)S(1)} %collective-permute-done.8.a_3_, ...), custom_call_target="tpu_custom_call" | custom-call | flops 671088640 | bytes 4194304 | tf_op jit(solution)/shard_map/pallas_call | solution.py:256
  34.9 0.1 collective-permute-start.14
  35.0 2.0 %shard_map.69.refs_3_.grad_ref = bf16[384,512]{1,0:T(8,128)(2,1)S(1)} custom-call(s32[1]{0:T(128)} %bitcast.2.a_0_.refs_0_, bf16[512,768]{1,0:T(8,128)(2,1)S(1)} %get-tuple-element.50.a_1_, bf16[128,256]{1,0:T(8,128)(2,1)S(1)} %get-tuple-element.51.a_2_, bf16[128,256]{1,0:T(8,128)(2,1)S(1)} %collective-permute-done.8.a_3_, ...), custom_call_target="tpu_custom_call" | custom-call | flops 268435456 | bytes 4194304 | tf_op jit(solution)/shard_map/pallas_call | solution.py:256
  36.9 0.0 copy-start.3
  36.9 0.3 collective-permute-done.14.got_ref
  37.2 0.6 shard_map.72
  37.8 0.6 collective-permute-start.15
  38.4 1.5 %collective-permute-start.16 = (bf16[192,1024]{1,0:T(8,128)(2,1)S(1)}, bf16[192,1024]{1,0:T(8,128)(2,1)S(1)}, u32[]{:S(2)}, u32[]{:S(2)}) collective-permute-start(bf16[192,1024]{1,0:T(8,128)(2,1)S(1)} %get-tuple-element.64), channel_id=1, source_target_pairs={{0,2},{1,5},{2,0},{3,7},{4,6},{5,1},{6,4},{7,3},{8,10},{9,13},{10,... | collective-permute-start | bytes 1179656 | tf_op jit(solution)/shard_map/ppermute | solution.py:407
  39.9 1.3 %shard_map.71 = (bf16[128,1280]{1,0:T(8,128)(2,1)S(1)}, bf16[128,1280]{1,0:T(8,128)(2,1)S(1)}, bf16[128,1280]{1,0:T(8,128)(2,1)S(1)}, bf16[128,1280]{1,0:T(8,128)(2,1)S(1)}) custom-call(s32[1]{0:T(128)} %bitcast.2.a_0_.refs_0_, bf16[768,1024]{1,0:T(8,128)(2,1)S(1)} %copy-done.1, f32[512,256]{1,0:T(8,128)S(1)} %get-tuple-element.49.a_7_.refs_2_, ...), custom_call_target="tpu_custom_call" | custom-call | flops 805306368 | bytes 4194304 | tf_op jit(solution)/shard_map/pallas_call | solution.py:256
  41.3 2.0 %collective-permute-start.11 = (bf16[128,1280]{1,0:T(8,128)(2,1)S(1)}, bf16[128,1280]{1,0:T(8,128)(2,1)S(1)}, u32[]{:S(2)}, u32[]{:S(2)}) collective-permute-start(bf16[128,1280]{1,0:T(8,128)(2,1)S(1)} %get-tuple-element.59), channel_id=1, source_target_pairs={{0,8},{8,0},{16,24},{24,16},{1,9},{9,1},{17,25},{25,17},{2,10},{10... | collective-permute-start | bytes 983048 | tf_op jit(solution)/shard_map/ppermute | solution.py:273
  43.2 2.4 %collective-permute-start.12 = (bf16[128,1280]{1,0:T(8,128)(2,1)S(1)}, bf16[128,1280]{1,0:T(8,128)(2,1)S(1)}, u32[]{:S(2)}, u32[]{:S(2)}) collective-permute-start(bf16[128,1280]{1,0:T(8,128)(2,1)S(1)} %get-tuple-element.60), channel_id=1, source_target_pairs={{0,16},{8,24},{16,0},{24,8},{1,17},{9,25},{17,1},{25,9},{2,18},{10... | collective-permute-start | bytes 983048 | tf_op jit(solution)/shard_map/ppermute | solution.py:273
  45.6 0.5 collective-permute-start.13
  46.1 0.0 copy-done.3
  46.1 0.5 slice.14
  47.3 0.0 collective-permute-done.15
  47.3 2.6 %collective-permute-done.16 = bf16[192,1024]{1,0:T(8,128)(2,1)S(1)} collective-permute-done((bf16[192,1024]{1,0:T(8,128)(2,1)S(1)}, bf16[192,1024]{1,0:T(8,128)(2,1)S(1)}, u32[]{:S(2)}, u32[]{:S(2)}) %collective-permute-start.16) | collective-permute-done | bytes 393248 | tf_op jit(solution)/shard_map/ppermute | solution.py:407
  49.9 16.0 %conditional.1 = (f32[768,1024]{1,0:T(8,128)}) conditional(s32[]{:T(128)} %bitcast.13, () %tuple.19, (s32[]{:T(128)}, bf16[192,1024]{1,0:T(8,128)(2,1)S(1)}, bf16[192,1024]{1,0:T(8,128)(2,1)S(1)}, bf16[192,1024]{1,0:T(8,128)(2,1)S(1)}, bf16[192,1024]{1,0:T(8,128)(2,1)S(1)}) %tuple.20), branch_computations={%region_1.2_spmd, %region_2.3_spmd} | conditional | flops 3145728 | bytes 15204520 | solution.py:427
  49.9 0.1 add_convert_fusion.1
  50.0 0.6 collective-permute-start.1
  50.6 0.1 add_convert_fusion.3
  50.8 1.6 %collective-permute-start = (bf16[192,1024]{1,0:T(8,128)(2,1)S(1)}, bf16[192,1024]{1,0:T(8,128)(2,1)S(1)}, u32[]{:S(2)}, u32[]{:S(2)}) collective-permute-start(bf16[192,1024]{1,0:T(8,128)(2,1)S(1)} %add_convert_fusion.3), channel_id=1, source_target_pairs={{0,4},{1,3},{2,6},{3,1},{4,0},{5,7},{6,2},{7,5},{8,12},{9,11},{10,... | collective-permute-start | bytes 1179656 | tf_op jit(solution)/shard_map/cond/branch_1_fun/ppermute | solution.py:407
  52.3 5.5 %collective-permute-done.1 = bf16[192,1024]{1,0:T(8,128)(2,1)S(1)} collective-permute-done((bf16[192,1024]{1,0:T(8,128)(2,1)S(1)}, bf16[192,1024]{1,0:T(8,128)(2,1)S(1)}, u32[]{:S(2)}, u32[]{:S(2)}) %collective-permute-start.1) | collective-permute-done | bytes 393248 | tf_op jit(solution)/shard_map/cond/branch_1_fun/ppermute | solution.py:407
  57.9 0.1 add_convert_fusion.a_2_
  58.0 0.1 collective-permute-start.3
  58.1 4.0 %collective-permute-done = bf16[192,1024]{1,0:T(8,128)(2,1)S(1)} collective-permute-done((bf16[192,1024]{1,0:T(8,128)(2,1)S(1)}, bf16[192,1024]{1,0:T(8,128)(2,1)S(1)}, u32[]{:S(2)}, u32[]{:S(2)}) %collective-permute-start) | collective-permute-done | bytes 393248 | tf_op jit(solution)/shard_map/cond/branch_1_fun/ppermute | solution.py:407
  62.1 0.1 add_convert_fusion.2.a_1_
  62.2 0.1 collective-permute-start.2
  62.3 0.0 collective-permute-done.3.a_4_
  62.3 1.7 %collective-permute-done.2.a_3_ = bf16[192,1024]{1,0:T(8,128)(2,1)S(1)} collective-permute-done((bf16[192,1024]{1,0:T(8,128)(2,1)S(1)}, bf16[192,1024]{1,0:T(8,128)(2,1)S(1)}, u32[]{:S(2)}, u32[]{:S(2)}) %collective-permute-start.2) | collective-permute-done | bytes 393248 | tf_op jit(solution)/shard_map/cond/branch_1_fun/ppermute | solution.py:273
  64.0 1.9 %branch_1_fun.1 = f32[768,1024]{1,0:T(8,128)} custom-call(s32[1]{0:T(128)} %bitcast.a_0_, bf16[192,1024]{1,0:T(8,128)(2,1)S(1)} %add_convert_fusion.2.a_1_, bf16[192,1024]{1,0:T(8,128)(2,1)S(1)} %add_convert_fusion.a_2_, bf16[192,1024]{1,0:T(8,128)(2,1)S(1)} %collective-permute-done.2.a_3_, bf16[192,1024]{1,0:T(8,128)(2,1)S(1)} %collective-permute-done.3.a_4_), custom_call_target="tpu_custom_call" | custom-call | bytes 4194304 | tf_op jit(solution)/shard_map/cond/branch_1_fun/pallas_call | solution.py:256
  65.9 0.0 collective-permute-done.11.refs_1_
  65.9 1.9 %collective-permute-done.12.refs_2_ = bf16[128,1280]{1,0:T(8,128)(2,1)S(1)} collective-permute-done((bf16[128,1280]{1,0:T(8,128)(2,1)S(1)}, bf16[128,1280]{1,0:T(8,128)(2,1)S(1)}, u32[]{:S(2)}, u32[]{:S(2)}) %collective-permute-start.12) | collective-permute-done | bytes 327712 | tf_op jit(solution)/shard_map/ppermute | solution.py:273
  67.8 6.7 %collective-permute-done.13.refs_3_ = bf16[128,1280]{1,0:T(8,128)(2,1)S(1)} collective-permute-done((bf16[128,1280]{1,0:T(8,128)(2,1)S(1)}, bf16[128,1280]{1,0:T(8,128)(2,1)S(1)}, u32[]{:S(2)}, u32[]{:S(2)}) %collective-permute-start.13) | collective-permute-done | bytes 327712 | tf_op jit(solution)/shard_map/ppermute | solution.py:273
  74.5 0.9 %shard_map.73 = (bf16[128,1024]{1,0:T(8,128)(2,1)}, bf16[128,1024]{1,0:T(8,128)(2,1)}) custom-call(s32[1]{0:T(128)} %bitcast.1.place, bf16[128,1280]{1,0:T(8,128)(2,1)S(1)} %get-tuple-element.65.refs_0_, bf16[128,1280]{1,0:T(8,128)(2,1)S(1)} %collective-permute-done.11.refs_1_, bf16[128,1280]{1,0:T(8,128)(2,1)S(1)} %collective-permute-done.12.refs_2_, ...), custom_call_target="tpu_custom_call" | custom-call | bytes 4194304 | tf_op jit(solution)/shard_map/pallas_call | solution.py:256
  (8 shorter events, 0.1 us)
Async XLA Ops:
  0.6 14.0 %collective-permute-start.5 = (bf16[128,1024]{1,0:T(8,128)(2,1)}, bf16[128,1024]{1,0:T(8,128)(2,1)S(1)}, u32[]{:S(2)}, u32[]{:S(2)}) collective-permute-start(bf16[128,1024]{1,0:T(8,128)(2,1)} %bitcast.24), channel_id=1, source_target_pairs={{0,16},{8,24},{16,0},{24,8},{1,17},{9,25},{17,1},{25,9},{2,18},{10... | collective-permute-start | bytes 786440 | tf_op jit(solution)/shard_map/ppermute | solution.py:273
  3.3 15.4 %collective-permute-start.4 = (bf16[128,1024]{1,0:T(8,128)(2,1)}, bf16[128,1024]{1,0:T(8,128)(2,1)S(1)}, u32[]{:S(2)}, u32[]{:S(2)}) collective-permute-start(bf16[128,1024]{1,0:T(8,128)(2,1)} %bitcast.25), channel_id=1, source_target_pairs={{0,8},{8,0},{16,24},{24,16},{1,9},{9,1},{17,25},{25,17},{2,10},{10... | collective-permute-start | bytes 786440 | tf_op jit(solution)/shard_map/ppermute | solution.py:273
  14.7 11.2 %collective-permute-start.6 = (bf16[128,1024]{1,0:T(8,128)(2,1)}, bf16[128,1024]{1,0:T(8,128)(2,1)S(1)}, u32[]{:S(2)}, u32[]{:S(2)}) collective-permute-start(bf16[128,1024]{1,0:T(8,128)(2,1)} %bitcast.26), channel_id=1, source_target_pairs={{8,16},{16,8},{9,17},{17,9},{10,18},{18,10},{11,19},{19,11},{12,20... | collective-permute-start | bytes 786440 | tf_op jit(solution)/shard_map/ppermute | solution.py:294
  16.6 9.3 %collective-permute-start.7 = (bf16[128,1024]{1,0:T(8,128)(2,1)S(1)}, bf16[128,1024]{1,0:T(8,128)(2,1)S(1)}, u32[]{:S(2)}, u32[]{:S(2)}) collective-permute-start(bf16[128,1024]{1,0:T(8,128)(2,1)S(1)} %collective-permute-done.5.refs_2_), channel_id=1, source_target_pairs={{16,24},{8,0},{17,25},{9,1},{18,26},{10,2},{19,27},{11,3},{20,28},... | collective-permute-start | bytes 786440 | tf_op jit(solution)/shard_map/ppermute | solution.py:293
  18.6 1.4 %copy-start = (bf16[768,1024]{1,0:T(8,128)(2,1)S(1)}, bf16[768,1024]{1,0:T(8,128)(2,1)}, u32[]{:S(2)}) copy-start(bf16[768,1024]{1,0:T(8,128)(2,1)} %refs_1_.1) | copy-start | bytes 4718596
  20.1 0.9 %copy-start.2 = (bf16[1,128,1024]{2,1,0:T(8,128)(2,1)S(1)}, bf16[1,128,1024]{2,1,0:T(8,128)(2,1)}, u32[]{:S(2)}) copy-start(bf16[1,128,1024]{2,1,0:T(8,128)(2,1)} %param.6) | copy-start | bytes 786436
  21.0 4.9 %copy-start.1 = (bf16[768,1024]{1,0:T(8,128)(2,1)S(1)}, bf16[768,1024]{1,0:T(8,128)(2,1)}, u32[]{:S(2)}) copy-start(bf16[768,1024]{1,0:T(8,128)(2,1)} %refs_1_.1) | copy-start | bytes 4718596
  21.8 10.6 %collective-permute-start.8 = (bf16[128,256]{1,0:T(8,128)(2,1)S(1)}, bf16[128,256]{1,0:T(8,128)(2,1)S(1)}, u32[]{:S(2)}, u32[]{:S(2)}) collective-permute-start(bf16[128,256]{1,0:T(8,128)(2,1)S(1)} %get-tuple-element.52), channel_id=1, source_target_pairs={{0,8},{8,0},{16,24},{24,16},{1,9},{9,1},{17,25},{25,17},{2,10},{10... | collective-permute-start | bytes 196616 | tf_op jit(solution)/shard_map/ppermute | solution.py:273
  21.9 10.5 %collective-permute-start.9 = (bf16[128,256]{1,0:T(8,128)(2,1)S(1)}, bf16[128,256]{1,0:T(8,128)(2,1)S(1)}, u32[]{:S(2)}, u32[]{:S(2)}) collective-permute-start(bf16[128,256]{1,0:T(8,128)(2,1)S(1)} %get-tuple-element.53), channel_id=1, source_target_pairs={{0,16},{8,24},{16,0},{24,8},{1,17},{9,25},{17,1},{25,9},{2,18},{10... | collective-permute-start | bytes 196616 | tf_op jit(solution)/shard_map/ppermute | solution.py:273
  25.8 6.6 %collective-permute-start.10 = (bf16[128,256]{1,0:T(8,128)(2,1)S(1)}, bf16[128,256]{1,0:T(8,128)(2,1)S(1)}, u32[]{:S(2)}, u32[]{:S(2)}) collective-permute-start(bf16[128,256]{1,0:T(8,128)(2,1)S(1)} %get-tuple-element.54), channel_id=1, source_target_pairs={{0,24},{8,16},{16,8},{24,0},{1,25},{9,17},{17,9},{25,1},{2,26},{10... | collective-permute-start | bytes 196616 | tf_op jit(solution)/shard_map/ppermute | solution.py:273
  34.9 2.4 %collective-permute-start.14 = (bf16[384,1024]{1,0:T(8,128)(2,1)S(1)}, bf16[384,1024]{1,0:T(8,128)(2,1)S(1)}, u32[]{:S(2)}, u32[]{:S(2)}) collective-permute-start(bf16[384,1024]{1,0:T(8,128)(2,1)S(1)} %get-tuple-element.62), channel_id=1, source_target_pairs={{0,1},{1,0},{2,3},{3,2},{4,5},{5,4},{6,7},{7,6},{8,9},{9,8},{10,11... | collective-permute-start | bytes 2359304 | tf_op jit(solution)/shard_map/ppermute | solution.py:273
  36.9 9.2 %copy-start.3 = (s32[1,8,2]{1,2,0:T(2,128)S(1)}, s32[1,8,2]{1,2,0:T(2,128)}, u32[]{:S(2)}) copy-start(s32[1,8,2]{1,2,0:T(2,128)} %param.8) | copy-start | bytes 196
  37.8 9.5 %collective-permute-start.15 = (bf16[192,1024]{1,0:T(8,128)(2,1)S(1)}, bf16[192,1024]{1,0:T(8,128)(2,1)S(1)}, u32[]{:S(2)}, u32[]{:S(2)}) collective-permute-start(bf16[192,1024]{1,0:T(8,128)(2,1)S(1)} %get-tuple-element.63), channel_id=1, source_target_pairs={{0,2},{1,5},{2,0},{3,7},{4,6},{5,1},{6,4},{7,3},{8,10},{9,13},{10,... | collective-permute-start | bytes 1179656 | tf_op jit(solution)/shard_map/ppermute | solution.py:407
  38.4 11.5 %collective-permute-start.16 = (bf16[192,1024]{1,0:T(8,128)(2,1)S(1)}, bf16[192,1024]{1,0:T(8,128)(2,1)S(1)}, u32[]{:S(2)}, u32[]{:S(2)}) collective-permute-start(bf16[192,1024]{1,0:T(8,128)(2,1)S(1)} %get-tuple-element.64), channel_id=1, source_target_pairs={{0,2},{1,5},{2,0},{3,7},{4,6},{5,1},{6,4},{7,3},{8,10},{9,13},{10,... | collective-permute-start | bytes 1179656 | tf_op jit(solution)/shard_map/ppermute | solution.py:407
  41.3 24.6 %collective-permute-start.11 = (bf16[128,1280]{1,0:T(8,128)(2,1)S(1)}, bf16[128,1280]{1,0:T(8,128)(2,1)S(1)}, u32[]{:S(2)}, u32[]{:S(2)}) collective-permute-start(bf16[128,1280]{1,0:T(8,128)(2,1)S(1)} %get-tuple-element.59), channel_id=1, source_target_pairs={{0,8},{8,0},{16,24},{24,16},{1,9},{9,1},{17,25},{25,17},{2,10},{10... | collective-permute-start | bytes 983048 | tf_op jit(solution)/shard_map/ppermute | solution.py:273
  43.2 24.6 %collective-permute-start.12 = (bf16[128,1280]{1,0:T(8,128)(2,1)S(1)}, bf16[128,1280]{1,0:T(8,128)(2,1)S(1)}, u32[]{:S(2)}, u32[]{:S(2)}) collective-permute-start(bf16[128,1280]{1,0:T(8,128)(2,1)S(1)} %get-tuple-element.60), channel_id=1, source_target_pairs={{0,16},{8,24},{16,0},{24,8},{1,17},{9,25},{17,1},{25,9},{2,18},{10... | collective-permute-start | bytes 983048 | tf_op jit(solution)/shard_map/ppermute | solution.py:273
  45.6 28.9 %collective-permute-start.13 = (bf16[128,1280]{1,0:T(8,128)(2,1)S(1)}, bf16[128,1280]{1,0:T(8,128)(2,1)S(1)}, u32[]{:S(2)}, u32[]{:S(2)}) collective-permute-start(bf16[128,1280]{1,0:T(8,128)(2,1)S(1)} %get-tuple-element.61), channel_id=1, source_target_pairs={{0,24},{8,16},{16,8},{24,0},{1,25},{9,17},{17,9},{25,1},{2,26},{10... | collective-permute-start | bytes 983048 | tf_op jit(solution)/shard_map/ppermute | solution.py:273
  50.0 7.8 %collective-permute-start.1 = (bf16[192,1024]{1,0:T(8,128)(2,1)S(1)}, bf16[192,1024]{1,0:T(8,128)(2,1)S(1)}, u32[]{:S(2)}, u32[]{:S(2)}) collective-permute-start(bf16[192,1024]{1,0:T(8,128)(2,1)S(1)} %add_convert_fusion.1), channel_id=1, source_target_pairs={{0,4},{1,3},{2,6},{3,1},{4,0},{5,7},{6,2},{7,5},{8,12},{9,11},{10,... | collective-permute-start | bytes 1179656 | tf_op jit(solution)/shard_map/cond/branch_1_fun/ppermute | solution.py:407
  50.8 11.3 %collective-permute-start = (bf16[192,1024]{1,0:T(8,128)(2,1)S(1)}, bf16[192,1024]{1,0:T(8,128)(2,1)S(1)}, u32[]{:S(2)}, u32[]{:S(2)}) collective-permute-start(bf16[192,1024]{1,0:T(8,128)(2,1)S(1)} %add_convert_fusion.3), channel_id=1, source_target_pairs={{0,4},{1,3},{2,6},{3,1},{4,0},{5,7},{6,2},{7,5},{8,12},{9,11},{10,... | collective-permute-start | bytes 1179656 | tf_op jit(solution)/shard_map/cond/branch_1_fun/ppermute | solution.py:407
  58.0 4.3 %collective-permute-start.3 = (bf16[192,1024]{1,0:T(8,128)(2,1)S(1)}, bf16[192,1024]{1,0:T(8,128)(2,1)S(1)}, u32[]{:S(2)}, u32[]{:S(2)}) collective-permute-start(bf16[192,1024]{1,0:T(8,128)(2,1)S(1)} %add_convert_fusion.a_2_), channel_id=1, source_target_pairs={{0,1},{1,0},{2,3},{3,2},{4,5},{5,4},{6,7},{7,6},{8,9},{9,8},{10,11... | collective-permute-start | bytes 1179656 | tf_op jit(solution)/shard_map/cond/branch_1_fun/ppermute | solution.py:273
  62.2 1.8 %collective-permute-start.2 = (bf16[192,1024]{1,0:T(8,128)(2,1)S(1)}, bf16[192,1024]{1,0:T(8,128)(2,1)S(1)}, u32[]{:S(2)}, u32[]{:S(2)}) collective-permute-start(bf16[192,1024]{1,0:T(8,128)(2,1)S(1)} %add_convert_fusion.2.a_1_), channel_id=1, source_target_pairs={{0,1},{1,0},{2,3},{3,2},{4,5},{5,4},{6,7},{7,6},{8,9},{9,8},{10,11... | collective-permute-start | bytes 1179656 | tf_op jit(solution)/shard_map/cond/branch_1_fun/ppermute | solution.py:273

commit v5 on v4

--- a/solution.py
+++ b/solution.py
@@ -16,6 +16,7 @@
 TN = (((0,), (0,)), ((), ()))
 NEVER = -1e30
 VMEM = pl.BlockSpec(memory_space=pltpu.VMEM)
+HBM = pl.BlockSpec(memory_space=pltpu.HBM)
 SMEM = pl.BlockSpec(memory_space=pltpu.SMEM)
 
 
@@ -35,7 +36,7 @@
         self.tiles = self.gheads // self.per_tile
         self.tile = self.per_tile * HD
         self.gcols = self.gheads * 3 * HD
-        self.chunk = BLOCK
+        self.chunk = math.gcd(self.nodes, 512)
 
     def base(self, group, t):
         start = group * self.gcols + t * 3 * self.tile
@@ -218,32 +219,63 @@
         sends[s][:, width:] = sum_ref[here, :].astype(BF16)
 
 
-def scale_kernel(plan, m, which, *refs):
-    out = refs[-1]
-    count = (len(refs) - 1) // 2
-    size = refs[0].shape[0]
-    for i, ref in enumerate(refs[:-1]):
-        side = which[0] if i < count else 1 - which[0]
-        start = side * (count * size) + (i % count) * size
-        out[pl.ds(pl.multiple_of(start, size), size), :] = ref[...].astype(F32) * (1.0 / m)
+def scale_kernel(plan, m, places, which, *refs):
+    out, staged, sems = refs[-3:]
+    parts = refs[-3 - len(places) : -3]
+    size = parts[0].shape[0]
+    copies = []
+    for i, (own, index, count) in enumerate(places):
+        side = which[0] if own else 1 - which[0]
+        start = pl.multiple_of((side * count + index) * size, size)
+        staged[i] = parts[i][...].astype(F32) * (1.0 / m)
+        copies.append(pltpu.make_async_copy(staged.at[i], out.at[pl.ds(start, size), :], sems.at[i]))
+        copies[-1].start()
+    for copy in copies:
+        copy.wait()
+
+
+def scaled(plan, m, core, parts, places, whole=None):
+    rows, width = parts[0].shape
+    count = len(parts)
+    args = [core.reshape(1), *([] if whole is None else [whole]), *parts]
+    specs = [SMEM] + [HBM] * (whole is not None) + [VMEM] * count
+    return pl.pallas_call(
+        functools.partial(scale_kernel, plan, m, places),
+        out_shape=array(2 * places[0][2] * rows, width, dtype=F32),
+        in_specs=specs,
+        out_specs=HBM,
+        scratch_shapes=[pltpu.VMEM((count, rows, width), F32), pltpu.SemaphoreType.DMA((count,))],
+        input_output_aliases={} if whole is None else {1: 0},
+        compiler_params=pltpu.CompilerParams(vmem_limit_bytes=12 * 2**20),
+        cost_estimate=pl.CostEstimate(flops=0, bytes_accessed=1 << 20, transcendentals=0),
+    )(*args)
+
+
+def relay_kernel(plan, own, ahead, out):
+    wide = own.shape[1]
+    width = wide - plan.heads * HD
+    out[:, :width] = add(own[:, :width], ahead[:, :width])
+    out[:, width:wide] = own[:, width:]
+    out[:, wide:] = ahead[:, width:]
 
 
 def combine_kernel(plan, place, *refs):
-    n, hcols = plan.n, plan.heads * HD
+    hcols = plan.heads * HD
     received, (node_grad, attended) = refs[:-2], refs[-2:]
     width = node_grad.shape[1]
-    pieces = [x[:, width : width + hcols] for x in received[:n]]
-    terms = [x[:, :width] for x in received[:n]]
-    total = terms[0].astype(F32)
-    for term in terms[1:]:
-        total = total + term.astype(F32)
+    total = received[0][:, :width].astype(F32)
+    for x in received[1:]:
+        total = total + x[:, :width].astype(F32)
     node_grad[...] = total.astype(BF16)
-    for k, piece in enumerate(pieces):
-        start = (place[0] ^ k) * hcols
-        if hcols % 128 == 0:
-            attended[:, pl.ds(pl.multiple_of(start, hcols), hcols)] = piece
-        else:
-            attended[k, :, :] = piece
+    slot = 0
+    for x in received:
+        for at in range(width, x.shape[1], hcols):
+            if hcols % 128 == 0:
+                start = pl.multiple_of((place[0] ^ slot) * hcols, hcols)
+                attended[:, pl.ds(start, hcols)] = x[:, at : at + hcols]
+            else:
+                attended[slot, :, :] = x[:, at : at + hcols]
+            slot += 1
 
 
 def size(x):
@@ -281,19 +313,11 @@
     return (a.astype(F32) + b.astype(F32)).astype(BF16)
 
 
-def exchange_slots(plan, sends, n):
-    return [sends[0]] + [swap(sends[k], "seq", k) for k in range(1, n)]
-
-
-def gather_slots(x, z, n):
+def gather_slots(x, n):
     if n != 4:
         return [x] + [swap(x, "seq", k) for k in range(1, n)]
-    far = swap(x, "seq", 2)
-    near = swap(x, "seq", 1)
-    ends = lax.ppermute(far, "seq", [(2, 3), (1, 0)])
-    middle = lax.ppermute(after(x, far), "seq", [(1, 2), (2, 1)])
-    inner = (z == 1) | (z == 2)
-    return [x, near, far, jnp.where(inner, middle, ends)]
+    far, near = swap(x, "seq", 2), swap(x, "seq", 1)
+    return [x, near, far, swap(far, "seq", 1)]
 
 
 def local(node_feats, qkv_weight, block_pairs, grad_out):
@@ -305,7 +329,7 @@
     nodes, heads = plan.nodes, plan.heads
     core = c % 2
 
-    xs = gather_slots(feats, z, n)
+    xs = gather_slots(feats, n)
     hcols = heads * HD
 
     def for_slot(k):
@@ -396,7 +420,14 @@
         [core.reshape(1), qkv_weight, sums, *grad_t],
         scalar=True,
     )
-    received = exchange_slots(plan, sends, n)
+    if n == 4:
+        ahead = swap(sends[3], "seq", 1)
+        (pair,) = call(
+            relay_kernel, plan, [array(rows, width + 2 * hcols)], [], 0, [sends[2], ahead]
+        )
+        received = [sends[0], swap(after(sends[1], ahead), "seq", 1), swap(pair, "seq", 2)]
+    else:
+        received = [sends[0]] + [swap(sends[k], "seq", k) for k in range(1, n)]
 
     bits = []
     while 2 << len(bits) < m:
@@ -412,15 +443,14 @@
             gots = [across(part, stage) for part in parts]
             parts = [add(part, got) for part, got in zip(parts, gots)]
         gots = [swap(part, "clus", 1) for part in parts]
-        (result,) = call(
-            lambda *a: scale_kernel(a[0], m, *a[1:]),
-            plan,
-            [array(plan.columns, width, dtype=F32)],
-            [],
-            0,
-            [core.reshape(1), *parts, *gots],
-            scalar=True,
-        )
+        count, result = len(parts), None
+        for i, (part, got) in enumerate(zip(parts, gots)):
+            if i + 1 < count:
+                places = [(True, i, count), (False, i, count)]
+                result = scaled(plan, m, core, [part, got], places, result)
+            else:
+                result = scaled(plan, m, core, [part], [(True, i, count)], result)
+                result = scaled(plan, m, core, [got], [(False, i, count)], result)
         return result
 
     gots = [across(part, 0) for part in parts]

time: 75.7 us -> 67.9 us (0.90)
  the two profiles are of different devices: /device:TPU:14 before, /device:TPU:0 now
where the time goes in v5:
time: 67.9 us; the launch traced here: 67.6 us
  waiting for transfers between devices  27.2 us (40%)
  starting transfers between devices  18.1 us (27%)
  Pallas kernels  14.7 us (22%)
  local copies, waits for them, and re-layouts  4.5 us (7%)
  other arithmetic  1.53 us (2%)
  between operations  1.44 us (2%)
    ppermute x12, waiting for transfers between devices, swap(): return lax.ppermute(x, axis, [(i, i ^ bits) for i in range(size)])  17.6 us
    ppermute x12, starting transfers between devices, swap(): return lax.ppermute(x, axis, [(i, i ^ bits) for i in range(size)])  13.9 us
    pallas_call x8, Pallas kernels, call(): pl.pallas_call(functools.partial(kernel, plan), out_shape=out_shape, in_s...  11.6 us
    ppermute x4, waiting for transfers between devices, across(): return lax.ppermute(x, 'clus', pairs)  9.55 us
    ppermute x4, starting transfers between devices, across(): return lax.ppermute(x, 'clus', pairs)  4.25 us
    pallas_call x3, Pallas kernels, scaled(): pl.pallas_call(functools.partial(scale_kernel, plan, m, places), out_shap...  3.1 us
    unnamed x8, local copies, waits for them, and re-layouts  2.37 us
    dynamic_slice x1, local copies, waits for them, and re-layouts, for_slot(): return lax.dynamic_slice_in_dim(grad_out[0], (z ^ k) * hcols, hcols, 1)  1.6 us
  transfers between devices with their start and end apart: 16, of which 6 were waited for; matrix products, arithmetic and copies ran while one was open for 5% of the time, Pallas kernels for 18%

profile of v5, /device:TPU:0, one launch (start us, length us, event | category | flops | bytes accessed | tf_op | source)
XLA Modules:
  0.0 67.6 jit_solution(4639785189107365210)
XLA Ops:
  0.6 3.1 %collective-permute-start.4 = (bf16[128,1024]{1,0:T(8,128)(2,1)}, bf16[128,1024]{1,0:T(8,128)(2,1)S(1)}, u32[]{:S(2)}, u32[]{:S(2)}) collective-permute-start(bf16[128,1024]{1,0:T(8,128)(2,1)} %bitcast.24), channel_id=1, source_target_pairs={{0,8},{8,0},{16,24},{24,16},{1,9},{9,1},{17,25},{25,17},{2,10},{10... | collective-permute-start | bytes 786440 | tf_op jit(solution)/shard_map/ppermute | solution.py:305
  3.7 2.6 %collective-permute-start.5 = (bf16[128,1024]{1,0:T(8,128)(2,1)}, bf16[128,1024]{1,0:T(8,128)(2,1)}, u32[]{:S(2)}, u32[]{:S(2)}) collective-permute-start(bf16[128,1024]{1,0:T(8,128)(2,1)} %bitcast.25), channel_id=1, source_target_pairs={{0,16},{8,24},{16,0},{24,8},{1,17},{9,25},{17,1},{25,9},{2,18},{10... | collective-permute-start | bytes 786440 | tf_op jit(solution)/shard_map/ppermute | solution.py:305
  6.3 0.7 %broadcast_xor_fusion = s32[8,2]{0,1:T(2,128)S(1)} fusion(s32[]{:T(128)} %axis_index.23, s32[1,8,2]{1,2,0:T(2,128)} %param.8), kind=kLoop, calls=%fused_computation.23 | loop fusion | flops 16 | bytes 132 | tf_op jit(solution)/shard_map/xor | solution.py:354
  7.0 0.1 broadcast_compare_fusion
  7.1 0.1 and_reduce_fusion
  7.2 1.6 %dynamic-slice_bitcast_fusion = (bf16[128,256]{1,0:T(8,128)(2,1)S(1)}, bf16[128,256]{1,0:T(8,128)(2,1)}, bf16[128,256]{1,0:T(8,128)(2,1)S(1)}, bf16[128,256]{1,0:T(8,128)(2,1)S(1)}) fusion(bf16[1,128,1024]{2,1,0:T(8,128)(2,1)} %param.9, s32[]{:T(128)S(6)} %select_n.72, s32[]{:T(128)S(6)} %select_n.70, s32[]{:T(128)S(6)} %select_n.69, s32[]{:T(128)S(6)} %select_n.71), kind=kLoop, calls=%fused_computation.5 | loop fusion | bytes 524304 | tf_op jit(solution)/shard_map/dynamic_slice | solution.py:336
  8.8 0.1 compare_convert_fusion.refs_5_
  8.9 9.4 %collective-permute-done.5.refs_2_ = bf16[128,1024]{1,0:T(8,128)(2,1)} collective-permute-done((bf16[128,1024]{1,0:T(8,128)(2,1)}, bf16[128,1024]{1,0:T(8,128)(2,1)}, u32[]{:S(2)}, u32[]{:S(2)}) %collective-permute-start.5) | collective-permute-done | bytes 262176 | tf_op jit(solution)/shard_map/ppermute | solution.py:305
  18.4 0.4 collective-permute-start.6
  18.8 0.0 collective-permute-done.4.refs_1_
  18.8 0.0 copy-start
  18.8 1.4 %copy-done = bf16[768,1024]{1,0:T(8,128)(2,1)S(1)} copy-done((bf16[768,1024]{1,0:T(8,128)(2,1)S(1)}, bf16[768,1024]{1,0:T(8,128)(2,1)}, u32[]{:S(2)}) %copy-start) | copy-done | bytes 1572888
  20.2 0.0 copy-start.2
  20.2 0.9 %copy-done.2 = bf16[1,128,1024]{2,1,0:T(8,128)(2,1)S(1)} copy-done((bf16[1,128,1024]{2,1,0:T(8,128)(2,1)S(1)}, bf16[1,128,1024]{2,1,0:T(8,128)(2,1)}, u32[]{:S(2)}) %copy-start.2) | copy-done | bytes 262168
  21.2 0.0 copy-start.1
  21.2 1.9 %shard_map.67 = (bf16[384,1024]{1,0:T(8,128)(2,1)S(1)}, bf16[384,768]{1,0:T(8,128)(2,1)S(1)}) custom-call(bf16[128,1024]{1,0:T(8,128)(2,1)S(1)} %bitcast.26, bf16[128,1024]{1,0:T(8,128)(2,1)S(1)} %collective-permute-done.4.refs_1_, bf16[128,1024]{1,0:T(8,128)(2,1)} %collective-permute-done.5.refs_2_, bf16[768,1024]{1,0:T(8,128)(2,1)S(1)} %copy-done), custom_call_target="tpu_custom_call" | custom-call | flops 603979776 | bytes 4194304 | tf_op jit(solution)/shard_map/pallas_call | solution.py:288
  23.1 1.7 %collective-permute-start.7 = (bf16[128,256]{1,0:T(8,128)(2,1)}, bf16[128,256]{1,0:T(8,128)(2,1)S(1)}, u32[]{:S(2)}, u32[]{:S(2)}) collective-permute-start(bf16[128,256]{1,0:T(8,128)(2,1)} %get-tuple-element.50), channel_id=1, source_target_pairs={{0,8},{8,0},{16,24},{24,16},{1,9},{9,1},{17,25},{25,17},{2,10},{10... | collective-permute-start | bytes 196616 | tf_op jit(solution)/shard_map/ppermute | solution.py:305
  24.7 1.1 %collective-permute-start.8 = (bf16[128,256]{1,0:T(8,128)(2,1)S(1)}, bf16[128,256]{1,0:T(8,128)(2,1)S(1)}, u32[]{:S(2)}, u32[]{:S(2)}) collective-permute-start(bf16[128,256]{1,0:T(8,128)(2,1)S(1)} %get-tuple-element.51), channel_id=1, source_target_pairs={{0,16},{8,24},{16,0},{24,8},{1,17},{9,25},{17,1},{25,9},{2,18},{10... | collective-permute-start | bytes 196616 | tf_op jit(solution)/shard_map/ppermute | solution.py:305
  25.9 1.7 %collective-permute-start.9 = (bf16[128,256]{1,0:T(8,128)(2,1)S(1)}, bf16[128,256]{1,0:T(8,128)(2,1)S(1)}, u32[]{:S(2)}, u32[]{:S(2)}) collective-permute-start(bf16[128,256]{1,0:T(8,128)(2,1)S(1)} %get-tuple-element.52), channel_id=1, source_target_pairs={{0,24},{8,16},{16,8},{24,0},{1,25},{9,17},{17,9},{25,1},{2,26},{10... | collective-permute-start | bytes 196616 | tf_op jit(solution)/shard_map/ppermute | solution.py:305
  27.5 0.0 collective-permute-done.6.refs_2_
  27.6 0.0 copy-done.1
  27.6 4.0 %shard_map.68 = (bf16[4,512,512]{2,1,0:T(8,128)(2,1)S(1)}, f32[512,256]{1,0:T(8,128)S(1)}, bf16[512,1024]{1,0:T(8,128)(2,1)S(1)}, bf16[512,768]{1,0:T(8,128)(2,1)S(1)}) custom-call(bf16[384,768]{1,0:T(8,128)(2,1)S(1)} %get-tuple-element.45.refs_0_, bf16[384,1024]{1,0:T(8,128)(2,1)S(1)} %get-tuple-element.46.refs_1_, ...), custom_call_target="tpu_custom_call" | custom-call | flops 268435456 | bytes 4194304 | tf_op jit(solution)/shard_map/pallas_call | solution.py:288
  31.5 0.0 collective-permute-done.7.a_3_
  31.5 0.0 collective-permute-done.8.a_4_
  31.6 0.5 collective-permute-done.9.a_5_
  32.0 1.7 %shard_map.70 = (bf16[384,512]{1,0:T(8,128)(2,1)S(1)}, bf16[384,1024]{1,0:T(8,128)(2,1)S(1)}) custom-call(s32[1]{0:T(128)} %bitcast.12.a_0_, bf16[512,768]{1,0:T(8,128)(2,1)S(1)} %get-tuple-element.48.a_1_, bf16[128,256]{1,0:T(8,128)(2,1)S(1)} %get-tuple-element.49.a_2_, bf16[128,256]{1,0:T(8,128)(2,1)S(1)} %collective-permute-done.7.a_3_, ...), custom_call_target="tpu_custom_call" | custom-call | flops 671088640 | bytes 4194304 | tf_op jit(solution)/shard_map/pallas_call | solution.py:288
  33.7 0.1 collective-permute-start.13
  33.8 1.2 %shard_map.69.refs_3_.grad_ref = bf16[384,512]{1,0:T(8,128)(2,1)S(1)} custom-call(s32[1]{0:T(128)} %bitcast.2.a_0_.refs_0_, bf16[512,768]{1,0:T(8,128)(2,1)S(1)} %get-tuple-element.48.a_1_, bf16[128,256]{1,0:T(8,128)(2,1)S(1)} %get-tuple-element.49.a_2_, bf16[128,256]{1,0:T(8,128)(2,1)S(1)} %collective-permute-done.7.a_3_, ...), custom_call_target="tpu_custom_call" | custom-call | flops 268435456 | bytes 4194304 | tf_op jit(solution)/shard_map/pallas_call | solution.py:288
  35.0 0.0 copy-start.3
  35.1 1.3 %shard_map.71 = (bf16[128,1280]{1,0:T(8,128)(2,1)S(1)}, bf16[128,1280]{1,0:T(8,128)(2,1)S(1)}, bf16[128,1280]{1,0:T(8,128)(2,1)S(1)}, bf16[128,1280]{1,0:T(8,128)(2,1)S(1)}) custom-call(s32[1]{0:T(128)} %bitcast.2.a_0_.refs_0_, bf16[768,1024]{1,0:T(8,128)(2,1)S(1)} %copy-done.1, f32[512,256]{1,0:T(8,128)S(1)} %get-tuple-element.47.a_7_.refs_2_, ...), custom_call_target="tpu_custom_call" | custom-call | flops 805306368 | bytes 4194304 | tf_op jit(solution)/shard_map/pallas_call | solution.py:288
  36.4 0.8 %collective-permute-start.10 = (bf16[128,1280]{1,0:T(8,128)(2,1)S(1)}, bf16[128,1280]{1,0:T(8,128)(2,1)S(1)}, u32[]{:S(2)}, u32[]{:S(2)}) collective-permute-start(bf16[128,1280]{1,0:T(8,128)(2,1)S(1)} %get-tuple-element.58), channel_id=1, source_target_pairs={{0,8},{8,0},{16,24},{24,16},{1,9},{9,1},{17,25},{25,17},{2,10},{10... | collective-permute-start | bytes 983048 | tf_op jit(solution)/shard_map/ppermute | solution.py:305
  37.2 0.0 collective-permute-done.13.got_ref
  37.2 0.6 shard_map.73
  37.8 1.6 %collective-permute-start.14 = (bf16[192,1024]{1,0:T(8,128)(2,1)S(1)}, bf16[192,1024]{1,0:T(8,128)(2,1)S(1)}, u32[]{:S(2)}, u32[]{:S(2)}) collective-permute-start(bf16[192,1024]{1,0:T(8,128)(2,1)S(1)} %get-tuple-element.62), channel_id=1, source_target_pairs={{0,2},{1,5},{2,0},{3,7},{4,6},{5,1},{6,4},{7,3},{8,10},{9,13},{10,... | collective-permute-start | bytes 1179656 | tf_op jit(solution)/shard_map/ppermute | solution.py:438
  39.3 0.5 collective-permute-start.15
  39.9 6.7 %collective-permute-done.10.ahead = bf16[128,1280]{1,0:T(8,128)(2,1)S(1)} collective-permute-done((bf16[128,1280]{1,0:T(8,128)(2,1)S(1)}, bf16[128,1280]{1,0:T(8,128)(2,1)S(1)}, u32[]{:S(2)}, u32[]{:S(2)}) %collective-permute-start.10) | collective-permute-done | bytes 327712 | tf_op jit(solution)/shard_map/ppermute | solution.py:305
  46.5 0.1 shard_map.72
  46.6 1.4 %collective-permute-start.12 = (bf16[128,1536]{1,0:T(8,128)(2,1)S(1)}, bf16[128,1536]{1,0:T(8,128)(2,1)S(1)}, u32[]{:S(2)}, u32[]{:S(2)}) collective-permute-start(bf16[128,1536]{1,0:T(8,128)(2,1)S(1)} %shard_map.72), channel_id=1, source_target_pairs={{0,16},{8,24},{16,0},{24,8},{1,17},{9,25},{17,1},{25,9},{2,18},{10... | collective-permute-start | bytes 1179656 | tf_op jit(solution)/shard_map/ppermute | solution.py:305
  48.0 1.0 %collective-permute-start.11 = (bf16[128,1280]{1,0:T(8,128)(2,1)S(1)}, bf16[128,1280]{1,0:T(8,128)(2,1)S(1)}, u32[]{:S(2)}, u32[]{:S(2)}) collective-permute-start(bf16[128,1280]{1,0:T(8,128)(2,1)S(1)} %get-tuple-element.59), channel_id=1, source_target_pairs={{0,8},{8,0},{16,24},{24,16},{1,9},{9,1},{17,25},{25,17},{2,10},{10... | collective-permute-start | bytes 983048 | tf_op jit(solution)/shard_map/ppermute | solution.py:305
  48.9 0.0 copy-done.3
  48.9 0.5 slice.14
  50.1 0.0 collective-permute-done.14
  50.1 0.0 collective-permute-done.15
  50.1 15.6 %conditional.1 = (f32[768,1024]{1,0:T(8,128)}) conditional(s32[]{:T(128)} %bitcast.13, () %tuple.19, (s32[]{:T(128)}, bf16[192,1024]{1,0:T(8,128)(2,1)S(1)}, bf16[192,1024]{1,0:T(8,128)(2,1)S(1)}, bf16[192,1024]{1,0:T(8,128)(2,1)S(1)}, bf16[192,1024]{1,0:T(8,128)(2,1)S(1)}) %tuple.20), branch_computations={%region_1.2_spmd, %region_2.3_spmd} | conditional | flops 3145728 | bytes 14155944 | solution.py:457
  50.1 0.1 add_convert_fusion.3
  50.3 1.6 %collective-permute-start = (bf16[192,1024]{1,0:T(8,128)(2,1)S(1)}, bf16[192,1024]{1,0:T(8,128)(2,1)S(1)}, u32[]{:S(2)}, u32[]{:S(2)}) collective-permute-start(bf16[192,1024]{1,0:T(8,128)(2,1)S(1)} %add_convert_fusion.3), channel_id=1, source_target_pairs={{0,4},{1,3},{2,6},{3,1},{4,0},{5,7},{6,2},{7,5},{8,12},{9,11},{10,... | collective-permute-start | bytes 1179656 | tf_op jit(solution)/shard_map/cond/branch_1_fun/ppermute | solution.py:438
  51.8 0.1 add_convert_fusion.1
  52.0 0.6 collective-permute-start.2
  52.6 5.5 %collective-permute-done = bf16[192,1024]{1,0:T(8,128)(2,1)S(1)} collective-permute-done((bf16[192,1024]{1,0:T(8,128)(2,1)S(1)}, bf16[192,1024]{1,0:T(8,128)(2,1)S(1)}, u32[]{:S(2)}, u32[]{:S(2)}) %collective-permute-start) | collective-permute-done | bytes 393248 | tf_op jit(solution)/shard_map/cond/branch_1_fun/ppermute | solution.py:438
  58.1 0.1 add_convert_fusion.2.refs_0_
  58.2 0.1 collective-permute-start.1
  58.3 4.0 %collective-permute-done.2 = bf16[192,1024]{1,0:T(8,128)(2,1)S(1)} collective-permute-done((bf16[192,1024]{1,0:T(8,128)(2,1)S(1)}, bf16[192,1024]{1,0:T(8,128)(2,1)S(1)}, u32[]{:S(2)}, u32[]{:S(2)}) %collective-permute-start.2) | collective-permute-done | bytes 393248 | tf_op jit(solution)/shard_map/cond/branch_1_fun/ppermute | solution.py:438
  62.3 0.1 add_convert_fusion.refs_1_
  62.5 0.1 collective-permute-start.3
  62.5 0.0 collective-permute-done.1.refs_1_
  62.6 1.2 %branch_1_fun.3.refs_0_ = f32[768,1024]{1,0:T(8,128)} custom-call(s32[1]{0:T(128)} %bitcast.which, bf16[192,1024]{1,0:T(8,128)(2,1)S(1)} %add_convert_fusion.2.refs_0_, bf16[192,1024]{1,0:T(8,128)(2,1)S(1)} %collective-permute-done.1.refs_1_), custom_call_target="tpu_custom_call" | custom-call | bytes 1048576 | tf_op jit(solution)/shard_map/cond/branch_1_fun/pallas_call | solution.py:242
  63.8 0.9 %branch_1_fun.4.refs_0_ = f32[768,1024]{1,0:T(8,128)} custom-call(s32[1]{0:T(128)} %bitcast.which, f32[768,1024]{1,0:T(8,128)} %branch_1_fun.3.refs_0_, bf16[192,1024]{1,0:T(8,128)(2,1)S(1)} %add_convert_fusion.refs_1_), custom_call_target="tpu_custom_call", output_to_operand_aliasing={{}: (1, {})} | custom-call | bytes 1048576 | tf_op jit(solution)/shard_map/cond/branch_1_fun/pallas_call | solution.py:242
  64.7 0.0 collective-permute-done.3.refs_1_
  64.7 0.9 %branch_1_fun.5 = f32[768,1024]{1,0:T(8,128)} custom-call(s32[1]{0:T(128)} %bitcast.which, f32[768,1024]{1,0:T(8,128)} %branch_1_fun.4.refs_0_, bf16[192,1024]{1,0:T(8,128)(2,1)S(1)} %collective-permute-done.3.refs_1_), custom_call_target="tpu_custom_call", output_to_operand_aliasing={{}: (1, {})} | custom-call | bytes 1048576 | tf_op jit(solution)/shard_map/cond/branch_1_fun/pallas_call | solution.py:242
  65.7 0.0 collective-permute-done.11.refs_1_
  65.7 1.0 %collective-permute-done.12.refs_2_ = bf16[128,1536]{1,0:T(8,128)(2,1)S(1)} collective-permute-done((bf16[128,1536]{1,0:T(8,128)(2,1)S(1)}, bf16[128,1536]{1,0:T(8,128)(2,1)S(1)}, u32[]{:S(2)}, u32[]{:S(2)}) %collective-permute-start.12) | collective-permute-done | bytes 393248 | tf_op jit(solution)/shard_map/ppermute | solution.py:305
  66.7 0.8 %shard_map.74 = (bf16[128,1024]{1,0:T(8,128)(2,1)}, bf16[128,1024]{1,0:T(8,128)(2,1)}) custom-call(s32[1]{0:T(128)} %bitcast.1.place, bf16[128,1280]{1,0:T(8,128)(2,1)S(1)} %get-tuple-element.64.refs_0_, bf16[128,1280]{1,0:T(8,128)(2,1)S(1)} %collective-permute-done.11.refs_1_, bf16[128,1536]{1,0:T(8,128)(2,1)S(1)} %collective-permute-done.12.refs_2_), custom_call_target="tpu_custom_call" | custom-call | bytes 4194304 | tf_op jit(solution)/shard_map/pallas_call | solution.py:288
  (7 shorter events, 0.1 us)
Async XLA Ops:
  0.6 18.2 %collective-permute-start.4 = (bf16[128,1024]{1,0:T(8,128)(2,1)}, bf16[128,1024]{1,0:T(8,128)(2,1)S(1)}, u32[]{:S(2)}, u32[]{:S(2)}) collective-permute-start(bf16[128,1024]{1,0:T(8,128)(2,1)} %bitcast.24), channel_id=1, source_target_pairs={{0,8},{8,0},{16,24},{24,16},{1,9},{9,1},{17,25},{25,17},{2,10},{10... | collective-permute-start | bytes 786440 | tf_op jit(solution)/shard_map/ppermute | solution.py:305
  3.7 14.7 %collective-permute-start.5 = (bf16[128,1024]{1,0:T(8,128)(2,1)}, bf16[128,1024]{1,0:T(8,128)(2,1)}, u32[]{:S(2)}, u32[]{:S(2)}) collective-permute-start(bf16[128,1024]{1,0:T(8,128)(2,1)} %bitcast.25), channel_id=1, source_target_pairs={{0,16},{8,24},{16,0},{24,8},{1,17},{9,25},{17,1},{25,9},{2,18},{10... | collective-permute-start | bytes 786440 | tf_op jit(solution)/shard_map/ppermute | solution.py:305
  18.4 9.1 %collective-permute-start.6 = (bf16[128,1024]{1,0:T(8,128)(2,1)}, bf16[128,1024]{1,0:T(8,128)(2,1)}, u32[]{:S(2)}, u32[]{:S(2)}) collective-permute-start(bf16[128,1024]{1,0:T(8,128)(2,1)} %collective-permute-done.5.refs_2_), channel_id=1, source_target_pairs={{0,8},{8,0},{16,24},{24,16},{1,9},{9,1},{17,25},{25,17},{2,10},{10... | collective-permute-start | bytes 786440 | tf_op jit(solution)/shard_map/ppermute | solution.py:305
  18.8 1.4 %copy-start = (bf16[768,1024]{1,0:T(8,128)(2,1)S(1)}, bf16[768,1024]{1,0:T(8,128)(2,1)}, u32[]{:S(2)}) copy-start(bf16[768,1024]{1,0:T(8,128)(2,1)} %refs_1_.1) | copy-start | bytes 4718596
  20.2 0.9 %copy-start.2 = (bf16[1,128,1024]{2,1,0:T(8,128)(2,1)S(1)}, bf16[1,128,1024]{2,1,0:T(8,128)(2,1)}, u32[]{:S(2)}) copy-start(bf16[1,128,1024]{2,1,0:T(8,128)(2,1)} %param.6) | copy-start | bytes 786436
  21.2 6.4 %copy-start.1 = (bf16[768,1024]{1,0:T(8,128)(2,1)S(1)}, bf16[768,1024]{1,0:T(8,128)(2,1)}, u32[]{:S(2)}) copy-start(bf16[768,1024]{1,0:T(8,128)(2,1)} %refs_1_.1) | copy-start | bytes 4718596
  23.1 8.5 %collective-permute-start.7 = (bf16[128,256]{1,0:T(8,128)(2,1)}, bf16[128,256]{1,0:T(8,128)(2,1)S(1)}, u32[]{:S(2)}, u32[]{:S(2)}) collective-permute-start(bf16[128,256]{1,0:T(8,128)(2,1)} %get-tuple-element.50), channel_id=1, source_target_pairs={{0,8},{8,0},{16,24},{24,16},{1,9},{9,1},{17,25},{25,17},{2,10},{10... | collective-permute-start | bytes 196616 | tf_op jit(solution)/shard_map/ppermute | solution.py:305
  24.7 6.8 %collective-permute-start.8 = (bf16[128,256]{1,0:T(8,128)(2,1)S(1)}, bf16[128,256]{1,0:T(8,128)(2,1)S(1)}, u32[]{:S(2)}, u32[]{:S(2)}) collective-permute-start(bf16[128,256]{1,0:T(8,128)(2,1)S(1)} %get-tuple-element.51), channel_id=1, source_target_pairs={{0,16},{8,24},{16,0},{24,8},{1,17},{9,25},{17,1},{25,9},{2,18},{10... | collective-permute-start | bytes 196616 | tf_op jit(solution)/shard_map/ppermute | solution.py:305
  25.9 6.2 %collective-permute-start.9 = (bf16[128,256]{1,0:T(8,128)(2,1)S(1)}, bf16[128,256]{1,0:T(8,128)(2,1)S(1)}, u32[]{:S(2)}, u32[]{:S(2)}) collective-permute-start(bf16[128,256]{1,0:T(8,128)(2,1)S(1)} %get-tuple-element.52), channel_id=1, source_target_pairs={{0,24},{8,16},{16,8},{24,0},{1,25},{9,17},{17,9},{25,1},{2,26},{10... | collective-permute-start | bytes 196616 | tf_op jit(solution)/shard_map/ppermute | solution.py:305
  33.7 3.4 %collective-permute-start.13 = (bf16[384,1024]{1,0:T(8,128)(2,1)S(1)}, bf16[384,1024]{1,0:T(8,128)(2,1)S(1)}, u32[]{:S(2)}, u32[]{:S(2)}) collective-permute-start(bf16[384,1024]{1,0:T(8,128)(2,1)S(1)} %get-tuple-element.61), channel_id=1, source_target_pairs={{0,1},{1,0},{2,3},{3,2},{4,5},{5,4},{6,7},{7,6},{8,9},{9,8},{10,11... | collective-permute-start | bytes 2359304 | tf_op jit(solution)/shard_map/ppermute | solution.py:305
  35.0 13.9 %copy-start.3 = (s32[1,8,2]{1,2,0:T(2,128)S(1)}, s32[1,8,2]{1,2,0:T(2,128)}, u32[]{:S(2)}) copy-start(s32[1,8,2]{1,2,0:T(2,128)} %param.8) | copy-start | bytes 196
  36.4 10.2 %collective-permute-start.10 = (bf16[128,1280]{1,0:T(8,128)(2,1)S(1)}, bf16[128,1280]{1,0:T(8,128)(2,1)S(1)}, u32[]{:S(2)}, u32[]{:S(2)}) collective-permute-start(bf16[128,1280]{1,0:T(8,128)(2,1)S(1)} %get-tuple-element.58), channel_id=1, source_target_pairs={{0,8},{8,0},{16,24},{24,16},{1,9},{9,1},{17,25},{25,17},{2,10},{10... | collective-permute-start | bytes 983048 | tf_op jit(solution)/shard_map/ppermute | solution.py:305
  37.8 12.3 %collective-permute-start.14 = (bf16[192,1024]{1,0:T(8,128)(2,1)S(1)}, bf16[192,1024]{1,0:T(8,128)(2,1)S(1)}, u32[]{:S(2)}, u32[]{:S(2)}) collective-permute-start(bf16[192,1024]{1,0:T(8,128)(2,1)S(1)} %get-tuple-element.62), channel_id=1, source_target_pairs={{0,2},{1,5},{2,0},{3,7},{4,6},{5,1},{6,4},{7,3},{8,10},{9,13},{10,... | collective-permute-start | bytes 1179656 | tf_op jit(solution)/shard_map/ppermute | solution.py:438
  39.3 10.8 %collective-permute-start.15 = (bf16[192,1024]{1,0:T(8,128)(2,1)S(1)}, bf16[192,1024]{1,0:T(8,128)(2,1)S(1)}, u32[]{:S(2)}, u32[]{:S(2)}) collective-permute-start(bf16[192,1024]{1,0:T(8,128)(2,1)S(1)} %get-tuple-element.63), channel_id=1, source_target_pairs={{0,2},{1,5},{2,0},{3,7},{4,6},{5,1},{6,4},{7,3},{8,10},{9,13},{10,... | collective-permute-start | bytes 1179656 | tf_op jit(solution)/shard_map/ppermute | solution.py:438
  46.6 20.1 %collective-permute-start.12 = (bf16[128,1536]{1,0:T(8,128)(2,1)S(1)}, bf16[128,1536]{1,0:T(8,128)(2,1)S(1)}, u32[]{:S(2)}, u32[]{:S(2)}) collective-permute-start(bf16[128,1536]{1,0:T(8,128)(2,1)S(1)} %shard_map.72), channel_id=1, source_target_pairs={{0,16},{8,24},{16,0},{24,8},{1,17},{9,25},{17,1},{25,9},{2,18},{10... | collective-permute-start | bytes 1179656 | tf_op jit(solution)/shard_map/ppermute | solution.py:305
  48.0 17.7 %collective-permute-start.11 = (bf16[128,1280]{1,0:T(8,128)(2,1)S(1)}, bf16[128,1280]{1,0:T(8,128)(2,1)S(1)}, u32[]{:S(2)}, u32[]{:S(2)}) collective-permute-start(bf16[128,1280]{1,0:T(8,128)(2,1)S(1)} %get-tuple-element.59), channel_id=1, source_target_pairs={{0,8},{8,0},{16,24},{24,16},{1,9},{9,1},{17,25},{25,17},{2,10},{10... | collective-permute-start | bytes 983048 | tf_op jit(solution)/shard_map/ppermute | solution.py:305
  50.3 7.8 %collective-permute-start = (bf16[192,1024]{1,0:T(8,128)(2,1)S(1)}, bf16[192,1024]{1,0:T(8,128)(2,1)S(1)}, u32[]{:S(2)}, u32[]{:S(2)}) collective-permute-start(bf16[192,1024]{1,0:T(8,128)(2,1)S(1)} %add_convert_fusion.3), channel_id=1, source_target_pairs={{0,4},{1,3},{2,6},{3,1},{4,0},{5,7},{6,2},{7,5},{8,12},{9,11},{10,... | collective-permute-start | bytes 1179656 | tf_op jit(solution)/shard_map/cond/branch_1_fun/ppermute | solution.py:438
  52.0 10.3 %collective-permute-start.2 = (bf16[192,1024]{1,0:T(8,128)(2,1)S(1)}, bf16[192,1024]{1,0:T(8,128)(2,1)S(1)}, u32[]{:S(2)}, u32[]{:S(2)}) collective-permute-start(bf16[192,1024]{1,0:T(8,128)(2,1)S(1)} %add_convert_fusion.1), channel_id=1, source_target_pairs={{0,4},{1,3},{2,6},{3,1},{4,0},{5,7},{6,2},{7,5},{8,12},{9,11},{10,... | collective-permute-start | bytes 1179656 | tf_op jit(solution)/shard_map/cond/branch_1_fun/ppermute | solution.py:438
  58.2 4.3 %collective-permute-start.1 = (bf16[192,1024]{1,0:T(8,128)(2,1)S(1)}, bf16[192,1024]{1,0:T(8,128)(2,1)S(1)}, u32[]{:S(2)}, u32[]{:S(2)}) collective-permute-start(bf16[192,1024]{1,0:T(8,128)(2,1)S(1)} %add_convert_fusion.2.refs_0_), channel_id=1, source_target_pairs={{0,1},{1,0},{2,3},{3,2},{4,5},{5,4},{6,7},{7,6},{8,9},{9,8},{10,11... | collective-permute-start | bytes 1179656 | tf_op jit(solution)/shard_map/cond/branch_1_fun/ppermute | solution.py:305
  62.5 2.3 %collective-permute-start.3 = (bf16[192,1024]{1,0:T(8,128)(2,1)S(1)}, bf16[192,1024]{1,0:T(8,128)(2,1)S(1)}, u32[]{:S(2)}, u32[]{:S(2)}) collective-permute-start(bf16[192,1024]{1,0:T(8,128)(2,1)S(1)} %add_convert_fusion.refs_1_), channel_id=1, source_target_pairs={{0,1},{1,0},{2,3},{3,2},{4,5},{5,4},{6,7},{7,6},{8,9},{9,8},{10,11... | collective-permute-start | bytes 1179656 | tf_op jit(solution)/shard_map/cond/branch_1_fun/ppermute | solution.py:305

commit v6 on v5

--- a/solution.py
+++ b/solution.py
@@ -51,11 +51,20 @@
     return lax.broadcasted_iota(jnp.int32, shape, 1) % (2 * HD) < HD
 
 
+def first_kernel(plan, x, weight, weight_out, qkv, mark, sem):
+    copy = pltpu.make_async_copy(weight, weight_out, sem)
+    copy.start()
+    copy.wait()
+    qkv[...] = mm(x[...], weight_out[...], NT).astype(BF16)
+    mark[...] = qkv[: mark.shape[0], : mark.shape[1]]
+
+
 def project_kernel(plan, *refs):
-    feats, (weight, full_ref, qkv_ref) = refs[: plan.n - 1], refs[plan.n - 1 :]
-    for s, x in enumerate(feats):
-        full_ref[s * plan.rows : (s + 1) * plan.rows, :] = x[...]
-    qkv_ref[...] = mm(full_ref[...], weight[...], NT).astype(BF16)
+    own, feats, (weight, qkv) = refs[0], refs[1:-2], refs[-2:]
+    qkv[: plan.rows, :] = own[...]
+    for s, x in enumerate(feats, 1):
+        here = slice(s * plan.rows, (s + 1) * plan.rows)
+        qkv[here, :] = mm(x[...], weight[...], NT).astype(BF16)
 
 
 def load_tile(plan, qkv, group, t, q_s, k_s, v_s):
@@ -110,14 +119,15 @@
 
 def forward_kernel(plan, *refs):
     n, rows = plan.n, plan.rows
-    known, known_x, last, weight, key_bias, row_hot = refs[:6]
-    low_ref, sum_ref, full_ref, qkv = refs[6:10]
-    q_s, k_s, v_s, ka_s = refs[10:]
+    known, feats, (weight, key_bias, row_hot) = refs[0], refs[1 : 1 + n], refs[1 + n : 4 + n]
+    low_ref, sum_ref, full_ref, qkv = refs[4 + n : 8 + n]
+    pieces = refs[8 + n : -4]
+    q_s, k_s, v_s, ka_s = refs[-4:]
+    for s, x in enumerate(feats):
+        full_ref[s * rows : (s + 1) * rows, :] = x[...]
     earlier = (n - 1) * rows
-    full_ref[:earlier, :] = known_x[...]
-    full_ref[earlier:, :] = last[...]
     qkv[:earlier, :] = known[...]
-    qkv[earlier:, :] = mm(last[...], weight[...], NT).astype(BF16)
+    qkv[earlier:, :] = mm(feats[-1][...], weight[...], NT).astype(BF16)
     for group in range(plan.groups):
         for t in range(plan.tiles):
             load_tile(plan, qkv, group, t, q_s, k_s, v_s)
@@ -136,6 +146,12 @@
                     sum_ref[here, lanes] = merge(plan, h, mm(low, v_s[...]), sum_ref[here, lanes])
 
                 chunks(plan, one_chunk)
+    for out in pieces:
+        hcols = sum_ref.shape[1]
+        for i in range(2):
+            here = slice((2 + i) * rows, (3 + i) * rows)
+            out[:, i * hcols : (i + 1) * hcols] = sum_ref[here, :].astype(BF16)
+
 
 def backward_kernel(plan, with_weight, *refs):
     n, rows, tile = plan.n, plan.rows, plan.tile
@@ -199,12 +215,12 @@
     wgrad_ref[...] = mm(grad_ref[...], full_ref[...]).astype(BF16)
 
 
-def term_kernel(plan, *refs):
+def term_kernel(plan, slots, *refs):
     which, weight, sum_ref = refs[:3]
     grads = refs[3 : 3 + plan.groups]
     sends = refs[3 + plan.groups :]
     width = weight.shape[1]
-    for s in reversed(range(plan.n)):
+    for s, out in zip(slots, sends):
         here = slice(s * plan.rows, (s + 1) * plan.rows)
         total = None
         for i, grad in enumerate(grads):
@@ -215,8 +231,9 @@
                 here_w = slice(None)
             part = mm(grad[:, here], weight[here_w, :], TN)
             total = part if total is None else total + part
-        sends[s][:, :width] = total.astype(BF16)
-        sends[s][:, width:] = sum_ref[here, :].astype(BF16)
+        out[:, :width] = total.astype(BF16)
+        if out.shape[1] > width:
+            out[:, width:] = sum_ref[here, :].astype(BF16)
 
 
 def scale_kernel(plan, m, places, which, *refs):
@@ -251,44 +268,48 @@
     )(*args)
 
 
-def relay_kernel(plan, own, ahead, out):
-    wide = own.shape[1]
-    width = wide - plan.heads * HD
-    out[:, :width] = add(own[:, :width], ahead[:, :width])
-    out[:, width:wide] = own[:, width:]
-    out[:, wide:] = ahead[:, width:]
-
-
-def combine_kernel(plan, place, *refs):
+def add_kernel(plan, one, other, out):
+    out[...] = add(one[...], other[...])
+
+
+def beside_kernel(plan, one, other, out):
+    wide = one.shape[1]
+    out[:, :wide] = one[...]
+    out[:, wide:] = other[:, other.shape[1] // 2 :]
+
+
+def combine_kernel(plan, pieces, place, *refs):
     hcols = plan.heads * HD
     received, (node_grad, attended) = refs[:-2], refs[-2:]
     width = node_grad.shape[1]
     total = received[0][:, :width].astype(F32)
     for x in received[1:]:
-        total = total + x[:, :width].astype(F32)
+        if x.shape[1] >= width:
+            total = total + x[:, :width].astype(F32)
     node_grad[...] = total.astype(BF16)
-    slot = 0
-    for x in received:
-        for at in range(width, x.shape[1], hcols):
-            if hcols % 128 == 0:
-                start = pl.multiple_of((place[0] ^ slot) * hcols, hcols)
-                attended[:, pl.ds(start, hcols)] = x[:, at : at + hcols]
-            else:
-                attended[slot, :, :] = x[:, at : at + hcols]
-            slot += 1
+    for slot, (i, at) in enumerate(pieces):
+        piece = received[i][:, at : at + hcols]
+        if hcols % 128 == 0:
+            start = pl.multiple_of((place[0] ^ slot) * hcols, hcols)
+            attended[:, pl.ds(start, hcols)] = piece
+        else:
+            attended[slot, :, :] = piece
 
 
 def size(x):
     return math.prod(x.shape) * jnp.dtype(x.dtype).itemsize
 
 
-def call(kernel, plan, out_shape, scratch, flops, args, scalar=False):
-    held = sum(map(size, out_shape)) + sum(map(size, scratch)) + sum(map(size, args))
+def call(kernel, plan, out_shape, scratch, flops, args, scalar=False, far=()):
+    arrays = [x for x in scratch if hasattr(x, "dtype") and len(x.shape) > 0]
+    held = sum(map(size, out_shape)) + sum(map(size, arrays)) + sum(map(size, args))
     held += 32 * plan.chunk * plan.nodes + 24 * plan.nodes * 2 * HD + 8 * 2**20
     return pl.pallas_call(
         functools.partial(kernel, plan),
         out_shape=out_shape,
-        in_specs=[SMEM if scalar and i == 0 else VMEM for i in range(len(args))],
+        in_specs=[
+            SMEM if scalar and i == 0 else HBM if i in far else VMEM for i in range(len(args))
+        ],
         out_specs=[VMEM] * len(out_shape),
         scratch_shapes=scratch,
         compiler_params=pltpu.CompilerParams(vmem_limit_bytes=min(held, 60 * 2**20)),
@@ -311,13 +332,6 @@
 
 def add(a, b):
     return (a.astype(F32) + b.astype(F32)).astype(BF16)
-
-
-def gather_slots(x, n):
-    if n != 4:
-        return [x] + [swap(x, "seq", k) for k in range(1, n)]
-    far, near = swap(x, "seq", 2), swap(x, "seq", 1)
-    return [x, near, far, swap(far, "seq", 1)]
 
 
 def local(node_feats, qkv_weight, block_pairs, grad_out):
@@ -329,28 +343,42 @@
     nodes, heads = plan.nodes, plan.heads
     core = c % 2
 
-    xs = gather_slots(feats, n)
     hcols = heads * HD
 
     def for_slot(k):
         return lax.dynamic_slice_in_dim(grad_out[0], (z ^ k) * hcols, hcols, 1)
 
+    qkv_weight, own, mark = call(
+        first_kernel,
+        plan,
+        [array(plan.columns, width), array(rows, plan.columns), array(16, 128)],
+        [pltpu.SemaphoreType.DMA(())],
+        2 * rows * plan.columns * width,
+        [feats, qkv_weight],
+        far=(1,),
+    )
+    if n == 4:
+        far, near = swap(feats, "seq", 2), swap(feats, "seq", 1)
+        xs = [feats, near, far, swap(after(far, mark), "seq", 1)]
+    else:
+        xs = [feats] + [swap(feats, "seq", k) for k in range(1, n)]
     earlier = nodes - rows
-    known_x, known = call(
+    (known,) = call(
         project_kernel,
         plan,
-        [array(earlier, width), array(earlier, plan.columns)],
+        [array(earlier, plan.columns)],
         [],
         2 * earlier * plan.columns * width,
-        [*xs[:-1], qkv_weight],
-    )
-
-    own, *sent = after([for_slot(k) for k in range(n)], known)
-    grads = [own] + [swap(sent[k - 1], "seq", k) for k in range(1, n)]
+        [own, *xs[1:-1], qkv_weight],
+    )
+
+    listed = block_pairs[0]
+    always, known = lax.optimization_barrier((listed[0, 0] >= 0, known))
+    mine, *sent = after([for_slot(k) for k in range(n)], known)
+    grads = [mine] + [swap(sent[k - 1], "seq", k) for k in range(1, n)]
 
     per_dev = rows // BLOCK
     blocks = nodes // BLOCK
-    listed = block_pairs[0]
     place = ((listed // per_dev) ^ z) * per_dev + listed % per_dev
     ids = jnp.arange(blocks, dtype=jnp.int32)
     row_ids = jnp.arange(2 * HD, dtype=jnp.int32) % HD
@@ -364,13 +392,14 @@
     def tiles(count):
         return [pltpu.VMEM((nodes, plan.tile), BF16)] * count
 
-    low, sums, full, qkv = call(
+    low, sums, full, qkv, *beyond = call(
         forward_kernel,
         plan,
-        [array(heads, nodes, nodes), array(nodes, hcols, dtype=F32), array(nodes, width), array(nodes, plan.columns)],
+        [array(heads, nodes, nodes), array(nodes, hcols, dtype=F32), array(nodes, width), array(nodes, plan.columns)]
+        + [array(rows, 2 * hcols)] * (n == 4),
         tiles(3) + [pltpu.VMEM((nodes, 2 * HD), BF16)],
         4 * nodes * nodes * HD * heads,
-        [known, known_x, xs[-1], qkv_weight, key_bias, row_hot],
+        [known, *xs, qkv_weight, key_bias, row_hot],
     )
     scratch = tiles(4) + [pltpu.VMEM((nodes, nodes), BF16), pltpu.VMEM((nodes, plan.tile), F32)]
     flops = 8 * nodes * nodes * HD * plan.gheads
@@ -411,23 +440,37 @@
         keep = lax.dynamic_slice_in_dim(wgrad, core * half, half, 0)
         send = lax.dynamic_slice_in_dim(wgrad, (1 - core) * half, half, 0)
         parts = [add(keep, swap(send, "clus", 1))]
-    sends = call(
-        term_kernel,
-        plan,
-        [array(rows, width + hcols)] * n,
-        [],
-        count * plan.groups,
-        [core.reshape(1), qkv_weight, sums, *grad_t],
-        scalar=True,
-    )
+    def terms(slots, wide, *done):
+        return call(
+            lambda *a: term_kernel(a[0], slots, *a[1:]),
+            plan,
+            [array(rows, width + hcols * extra) for extra in wide],
+            [],
+            count * plan.groups * len(slots) // n,
+            [core.reshape(1), qkv_weight, after(sums, *done), *grad_t],
+            scalar=True,
+        )
+
     if n == 4:
-        ahead = swap(sends[3], "seq", 1)
-        (pair,) = call(
-            relay_kernel, plan, [array(rows, width + 2 * hcols)], [], 0, [sends[2], ahead]
+        (ahead,) = terms([3], [0])
+        ahead = swap(ahead, "seq", 1)
+        own_term, near, far_term = terms([0, 1, 2], [1, 1, 0], parts)
+        across_z = swap(after(beyond[0], parts), "seq", 2)
+        (pair,) = call(add_kernel, plan, [array(rows, width)], [], 0, [far_term, ahead])
+        (near,) = call(
+            beside_kernel,
+            plan,
+            [array(rows, width + 2 * hcols)],
+            [],
+            0,
+            [near, across_z],
         )
-        received = [sends[0], swap(after(sends[1], ahead), "seq", 1), swap(pair, "seq", 2)]
+        received = [own_term, swap(near, "seq", 1), swap(pair, "seq", 2), across_z]
+        places = [(0, width), (1, width), (3, 0), (1, width + hcols)]
     else:
+        sends = terms(range(n), [1] * n)
         received = [sends[0]] + [swap(sends[k], "seq", k) for k in range(1, n)]
+        places = [(k, width) for k in range(n)]
 
     bits = []
     while 2 << len(bits) < m:
@@ -455,7 +498,7 @@
 
     gots = [across(part, 0) for part in parts]
     weight_grad = lax.cond(
-        listed[0, 0] >= 0,
+        always,
         finish,
         lambda parts, gots: jnp.zeros((plan.columns, width), F32),
         parts,
@@ -465,7 +508,7 @@
     received = after(received, weight_grad)
     aligned = hcols % 128 == 0
     node_grad, attended = call(
-        combine_kernel,
+        lambda *a: combine_kernel(a[0], places, *a[1:]),
         plan,
         [array(rows, width), array(rows, n * hcols) if aligned else array(n, rows, hcols)],
         [],

time: 67.9 us -> 65.6 us (0.966)
  waiting for transfers between devices: 27.2 us -> 20.3 us
  starting transfers between devices: 18.1 us -> 21.1 us
  other arithmetic: 1.53 us -> 2.53 us
    ppermute x12 -> x13, waiting for transfers between devices: 17.6 us -> 11.2 us  [swap(): return lax.ppermute(x, axis, [(i, i ^ bits) for i in range(size)])]
    ppermute x12 -> x13, starting transfers between devices: 13.9 us -> 16.9 us  [swap(): return lax.ppermute(x, axis, [(i, i ^ bits) for i in range(size)])]
    convert_element_type x4, other arithmetic: 0.52 us -> 1.52 us  [add(): return (a.astype(F32) + b.astype(F32)).astype(BF16)]
    slice x1, local copies, waits for them, and re-layouts: 0.51 us -> 1.19 us  [local(): always, known = lax.optimization_barrier((listed[0, 0] >= 0, known))]
    pallas_call x8 -> x11, Pallas kernels: 11.6 us -> 12.2 us  [call(): pl.pallas_call(functools.partial(kernel, plan), out_shape=out_shape, in_s...]
    unnamed x8 -> x6, local copies, waits for them, and re-layouts: 2.37 us -> 2.36 us
  transfers between devices with their start and end apart: 16 -> 17, of which waited for: 6 -> 6; matrix products, arithmetic and copies ran while one was open for 5% -> 7% of each run, Pallas kernels for 18% -> 20%
where the time goes in v6:
time: 65.6 us; the launch traced here: 65.3 us
  starting transfers between devices  21.1 us (32%)
  waiting for transfers between devices  20.3 us (31%)
  Pallas kernels  15.3 us (23%)
  local copies, waits for them, and re-layouts  4.55 us (7%)
  other arithmetic  2.53 us (4%)
  between operations  1.47 us (2%)
    ppermute x13, starting transfers between devices, swap(): return lax.ppermute(x, axis, [(i, i ^ bits) for i in range(size)])  16.9 us
    pallas_call x11, Pallas kernels, call(): pl.pallas_call(functools.partial(kernel, plan), out_shape=out_shape, in_s...  12.2 us
    ppermute x13, waiting for transfers between devices, swap(): return lax.ppermute(x, axis, [(i, i ^ bits) for i in range(size)])  11.2 us
    ppermute x4, waiting for transfers between devices, across(): return lax.ppermute(x, 'clus', pairs)  9.04 us
    ppermute x4, starting transfers between devices, across(): return lax.ppermute(x, 'clus', pairs)  4.18 us
    pallas_call x3, Pallas kernels, scaled(): pl.pallas_call(functools.partial(scale_kernel, plan, m, places), out_shap...  3.1 us
    unnamed x6, local copies, waits for them, and re-layouts  2.36 us
    convert_element_type x4, other arithmetic, add(): return (a.astype(F32) + b.astype(F32)).astype(BF16)  1.52 us
  transfers between devices with their start and end apart: 17, of which 6 were waited for; matrix products, arithmetic and copies ran while one was open for 7% of the time, Pallas kernels for 20%

profile of v6, /device:TPU:0, one launch (start us, length us, event | category | flops | bytes accessed | tf_op | source)
XLA Modules:
  0.0 65.3 jit_solution(14323970535357830230)
XLA Ops:
  0.6 0.0 copy-start.2
  0.6 3.1 %collective-permute-start.4 = (bf16[128,1024]{1,0:T(8,128)(2,1)}, bf16[128,1024]{1,0:T(8,128)(2,1)S(1)}, u32[]{:S(2)}, u32[]{:S(2)}) collective-permute-start(bf16[128,1024]{1,0:T(8,128)(2,1)} %bitcast.23), channel_id=1, source_target_pairs={{0,8},{8,0},{16,24},{24,16},{1,9},{9,1},{17,25},{25,17},{2,10},{10... | collective-permute-start | bytes 786440 | tf_op jit(solution)/shard_map/ppermute | solution.py:326
  3.7 2.6 %collective-permute-start.5 = (bf16[128,1024]{1,0:T(8,128)(2,1)}, bf16[128,1024]{1,0:T(8,128)(2,1)S(1)}, u32[]{:S(2)}, u32[]{:S(2)}) collective-permute-start(bf16[128,1024]{1,0:T(8,128)(2,1)} %bitcast.24), channel_id=1, source_target_pairs={{0,16},{8,24},{16,0},{24,8},{1,17},{9,25},{17,1},{25,9},{2,18},{10... | collective-permute-start | bytes 786440 | tf_op jit(solution)/shard_map/ppermute | solution.py:326
  6.3 0.7 %broadcast_xor_fusion = s32[8,2]{0,1:T(2,128)S(1)} fusion(s32[]{:T(128)} %axis_index.23, s32[1,8,2]{1,2,0:T(2,128)} %param.8), kind=kLoop, calls=%fused_computation.23 | loop fusion | flops 16 | bytes 132 | tf_op jit(solution)/shard_map/xor | solution.py:382
  7.0 0.1 broadcast_compare_fusion
  7.1 0.1 and_reduce_fusion
  7.2 1.0 %dynamic-slice_bitcast_fusion = (bf16[128,256]{1,0:T(8,128)(2,1)S(1)}, bf16[128,256]{1,0:T(8,128)(2,1)S(1)}, bf16[128,256]{1,0:T(8,128)(2,1)S(1)}, bf16[128,256]{1,0:T(8,128)(2,1)S(1)}) fusion(bf16[1,128,1024]{2,1,0:T(8,128)(2,1)} %param.9, s32[]{:T(128)S(6)} %select_n.72, s32[]{:T(128)S(6)} %select_n.70, s32[]{:T(128)S(6)} %select_n.69, s32[]{:T(128)S(6)} %select_n.71), kind=kLoop, calls=%fused_computation.5 | loop fusion | bytes 524304 | tf_op jit(solution)/shard_map/dynamic_slice | solution.py:349
  8.2 1.2 %slice.11 = s32[1,1]{0,1:T(1,128)} slice(s32[8,2]{0,1:T(2,128)} %bitcast.28), slice={[0:1], [0:1]} | slice | bytes 8 | tf_op jit(solution)/shard_map/slice | solution.py:376
  10.0 0.0 copy-start
  10.0 1.4 %copy-done = bf16[768,1024]{1,0:T(8,128)(2,1)S(1)} copy-done((bf16[768,1024]{1,0:T(8,128)(2,1)S(1)}, bf16[768,1024]{1,0:T(8,128)(2,1)}, u32[]{:S(2)}) %copy-start) | copy-done | bytes 1572888
  11.4 0.0 copy-start.1
  11.4 0.9 %copy-done.1 = bf16[1,128,1024]{2,1,0:T(8,128)(2,1)S(1)} copy-done((bf16[1,128,1024]{2,1,0:T(8,128)(2,1)S(1)}, bf16[1,128,1024]{2,1,0:T(8,128)(2,1)}, u32[]{:S(2)}) %copy-start.1) | copy-done | bytes 262168
  12.4 1.2 %shard_map.67 = (bf16[768,1024]{1,0:T(8,128)(2,1)S(1)}, bf16[128,768]{1,0:T(8,128)(2,1)S(1)}, bf16[16,128]{1,0:T(8,128)(2,1)}) custom-call(bf16[128,1024]{1,0:T(8,128)(2,1)S(1)} %bitcast.25, bf16[768,1024]{1,0:T(8,128)(2,1)S(1)} %copy-done), custom_call_target="tpu_custom_call" | custom-call | flops 201326592 | bytes 4194304 | tf_op jit(solution)/shard_map/pallas_call | solution.py:307
  13.6 0.1 compare_convert_fusion.refs_7_
  13.7 4.6 %collective-permute-done.5.refs_2_.refs_3_ = bf16[128,1024]{1,0:T(8,128)(2,1)S(1)} collective-permute-done((bf16[128,1024]{1,0:T(8,128)(2,1)}, bf16[128,1024]{1,0:T(8,128)(2,1)S(1)}, u32[]{:S(2)}, u32[]{:S(2)}) %collective-permute-start.5) | collective-permute-done | bytes 262176 | tf_op jit(solution)/shard_map/ppermute | solution.py:326
  18.3 0.4 collective-permute-start.6
  18.7 0.0 collective-permute-done.4.refs_1_.refs_2_
  18.7 1.1 %shard_map.68.refs_0_ = bf16[384,768]{1,0:T(8,128)(2,1)S(1)} custom-call(bf16[128,768]{1,0:T(8,128)(2,1)S(1)} %get-tuple-element.50.refs_0_, bf16[128,1024]{1,0:T(8,128)(2,1)S(1)} %collective-permute-done.4.refs_1_.refs_2_, bf16[128,1024]{1,0:T(8,128)(2,1)S(1)} %collective-permute-done.5.refs_2_.refs_3_, ...), custom_call_target="tpu_custom_call" | custom-call | flops 603979776 | bytes 4194304 | tf_op jit(solution)/shard_map/pallas_call | solution.py:307
  19.9 1.7 %collective-permute-start.7 = (bf16[128,256]{1,0:T(8,128)(2,1)S(1)}, bf16[128,256]{1,0:T(8,128)(2,1)S(1)}, u32[]{:S(2)}, u32[]{:S(2)}) collective-permute-start(bf16[128,256]{1,0:T(8,128)(2,1)S(1)} %get-tuple-element.55), channel_id=1, source_target_pairs={{0,8},{8,0},{16,24},{24,16},{1,9},{9,1},{17,25},{25,17},{2,10},{10... | collective-permute-start | bytes 196616 | tf_op jit(solution)/shard_map/ppermute | solution.py:326
  21.5 1.2 %collective-permute-start.8 = (bf16[128,256]{1,0:T(8,128)(2,1)S(1)}, bf16[128,256]{1,0:T(8,128)(2,1)S(1)}, u32[]{:S(2)}, u32[]{:S(2)}) collective-permute-start(bf16[128,256]{1,0:T(8,128)(2,1)S(1)} %get-tuple-element.56), channel_id=1, source_target_pairs={{0,16},{8,24},{16,0},{24,8},{1,17},{9,25},{17,1},{25,9},{2,18},{10... | collective-permute-start | bytes 196616 | tf_op jit(solution)/shard_map/ppermute | solution.py:326
  22.7 1.6 %collective-permute-start.9 = (bf16[128,256]{1,0:T(8,128)(2,1)S(1)}, bf16[128,256]{1,0:T(8,128)(2,1)S(1)}, u32[]{:S(2)}, u32[]{:S(2)}) collective-permute-start(bf16[128,256]{1,0:T(8,128)(2,1)S(1)} %get-tuple-element.57), channel_id=1, source_target_pairs={{0,24},{8,16},{16,8},{24,0},{1,25},{9,17},{17,9},{25,1},{2,26},{10... | collective-permute-start | bytes 196616 | tf_op jit(solution)/shard_map/ppermute | solution.py:326
  24.3 1.7 %collective-permute-done.6.refs_4_ = bf16[128,1024]{1,0:T(8,128)(2,1)} collective-permute-done((bf16[128,1024]{1,0:T(8,128)(2,1)S(1)}, bf16[128,1024]{1,0:T(8,128)(2,1)}, u32[]{:S(2)}, u32[]{:S(2)}) %collective-permute-start.6) | collective-permute-done | bytes 262176 | tf_op jit(solution)/shard_map/ppermute | solution.py:326
  26.1 0.0 copy-done.2
  26.1 4.0 %shard_map.69 = (bf16[4,512,512]{2,1,0:T(8,128)(2,1)S(1)}, f32[512,256]{1,0:T(8,128)S(1)}, bf16[512,1024]{1,0:T(8,128)(2,1)S(1)}, bf16[512,768]{1,0:T(8,128)(2,1)S(1)}, bf16[128,512]{1,0:T(8,128)(2,1)S(1)}) custom-call(bf16[384,768]{1,0:T(8,128)(2,1)S(1)} %shard_map.68.refs_0_, bf16[128,1024]{1,0:T(8,128)(2,1)S(1)} %bitcast.26, ...), custom_call_target="tpu_custom_call" | custom-call | flops 268435456 | bytes 4194304 | tf_op jit(solution)/shard_map/pallas_call | solution.py:307
  30.0 0.0 collective-permute-done.7.a_3_
  30.0 0.0 collective-permute-done.8.a_4_
  30.1 0.0 collective-permute-done.9.a_5_
  30.1 1.7 %shard_map.71 = (bf16[384,512]{1,0:T(8,128)(2,1)S(1)}, bf16[384,1024]{1,0:T(8,128)(2,1)S(1)}) custom-call(s32[1]{0:T(128)} %bitcast.13.a_0_, bf16[512,768]{1,0:T(8,128)(2,1)S(1)} %get-tuple-element.53.a_1_, bf16[128,256]{1,0:T(8,128)(2,1)S(1)} %get-tuple-element.54.a_2_, bf16[128,256]{1,0:T(8,128)(2,1)S(1)} %collective-permute-done.7.a_3_, ...), custom_call_target="tpu_custom_call" | custom-call | flops 671088640 | bytes 4194304 | tf_op jit(solution)/shard_map/pallas_call | solution.py:307
  31.8 0.1 collective-permute-start.10
  31.8 1.2 %shard_map.70.grad_ref.a_3_ = bf16[384,512]{1,0:T(8,128)(2,1)S(1)} custom-call(s32[1]{0:T(128)} %bitcast.2.a_0_, bf16[512,768]{1,0:T(8,128)(2,1)S(1)} %get-tuple-element.53.a_1_, bf16[128,256]{1,0:T(8,128)(2,1)S(1)} %get-tuple-element.54.a_2_, bf16[128,256]{1,0:T(8,128)(2,1)S(1)} %collective-permute-done.7.a_3_, ...), custom_call_target="tpu_custom_call" | custom-call | flops 268435456 | bytes 4194304 | tf_op jit(solution)/shard_map/pallas_call | solution.py:307
  33.1 0.5 shard_map.75
  33.6 2.1 %collective-permute-start.13 = (bf16[128,1024]{1,0:T(8,128)(2,1)S(1)}, bf16[128,1024]{1,0:T(8,128)(2,1)S(1)}, u32[]{:S(2)}, u32[]{:S(2)}) collective-permute-start(bf16[128,1024]{1,0:T(8,128)(2,1)S(1)} %shard_map.75), channel_id=1, source_target_pairs={{0,8},{8,0},{16,24},{24,16},{1,9},{9,1},{17,25},{25,17},{2,10},{10... | collective-permute-start | bytes 786440 | tf_op jit(solution)/shard_map/ppermute | solution.py:326
  35.6 0.0 collective-permute-done.10.got_ref
  35.6 0.6 shard_map.72
  36.2 0.5 collective-permute-start.11
  36.7 1.5 %collective-permute-start.15 = (bf16[192,1024]{1,0:T(8,128)(2,1)S(1)}, bf16[192,1024]{1,0:T(8,128)(2,1)S(1)}, u32[]{:S(2)}, u32[]{:S(2)}) collective-permute-start(bf16[192,1024]{1,0:T(8,128)(2,1)S(1)} %get-tuple-element.61), channel_id=1, source_target_pairs={{0,2},{1,5},{2,0},{3,7},{4,6},{5,1},{6,4},{7,3},{8,10},{9,13},{10,... | collective-permute-start | bytes 1179656 | tf_op jit(solution)/shard_map/ppermute | solution.py:481
  38.2 0.5 collective-permute-start.16
  38.8 1.0 %shard_map.73 = (bf16[128,1280]{1,0:T(8,128)(2,1)S(1)}, bf16[128,1280]{1,0:T(8,128)(2,1)S(1)}, bf16[128,1024]{1,0:T(8,128)(2,1)S(1)}) custom-call(s32[1]{0:T(128)} %bitcast.2.a_0_, bf16[768,1024]{1,0:T(8,128)(2,1)S(1)} %get-tuple-element.49.refs_3_.refs_5_.a_1_, f32[512,256]{1,0:T(8,128)S(1)} %get-tuple-element.63.a_7_.a_2_, ...), custom_call_target="tpu_custom_call" | custom-call | flops 603979776 | bytes 4194304 | tf_op jit(solution)/shard_map/pallas_call | solution.py:307
  39.8 4.9 %collective-permute-done.11.other.a_4_ = bf16[128,512]{1,0:T(8,128)(2,1)S(1)} collective-permute-done((bf16[128,512]{1,0:T(8,128)(2,1)S(1)}, bf16[128,512]{1,0:T(8,128)(2,1)S(1)}, u32[]{:S(2)}, u32[]{:S(2)}) %collective-permute-start.11) | collective-permute-done | bytes 131104 | tf_op jit(solution)/shard_map/ppermute | solution.py:326
  44.7 2.4 %collective-permute-start.12 = (bf16[128,1536]{1,0:T(8,128)(2,1)S(1)}, bf16[128,1536]{1,0:T(8,128)(2,1)S(1)}, u32[]{:S(2)}, u32[]{:S(2)}) collective-permute-start(bf16[128,1536]{1,0:T(8,128)(2,1)S(1)} %shard_map.74), channel_id=1, source_target_pairs={{0,8},{8,0},{16,24},{24,16},{1,9},{9,1},{17,25},{25,17},{2,10},{10... | collective-permute-start | bytes 1179656 | tf_op jit(solution)/shard_map/ppermute | solution.py:326
  47.1 0.0 collective-permute-done.13.other
  47.1 0.1 shard_map.76
  47.2 1.1 %collective-permute-start.14 = (bf16[128,1024]{1,0:T(8,128)(2,1)S(1)}, bf16[128,1024]{1,0:T(8,128)(2,1)S(1)}, u32[]{:S(2)}, u32[]{:S(2)}) collective-permute-start(bf16[128,1024]{1,0:T(8,128)(2,1)S(1)} %shard_map.76), channel_id=1, source_target_pairs={{0,16},{8,24},{16,0},{24,8},{1,17},{9,25},{17,1},{25,9},{2,18},{10... | collective-permute-start | bytes 786440 | tf_op jit(solution)/shard_map/ppermute | solution.py:326
  48.3 0.0 collective-permute-done.15
  48.3 0.5 collective-permute-done.16
  48.8 15.5 %conditional.1 = (f32[768,1024]{1,0:T(8,128)}) conditional(s32[]{:T(128)} %convert_element_type.47, () %tuple.24, (s32[]{:T(128)}, bf16[192,1024]{1,0:T(8,128)(2,1)S(1)}, bf16[192,1024]{1,0:T(8,128)(2,1)S(1)}, bf16[192,1024]{1,0:T(8,128)(2,1)S(1)}, bf16[192,1024]{1,0:T(8,128)(2,1)}) %tuple.25), branch_computations={%region_1.2_spmd, %region_2.3_spmd} | conditional | flops 3145728 | bytes 14155944 | solution.py:500
  48.8 0.1 add_convert_fusion.3
  49.0 1.6 %collective-permute-start = (bf16[192,1024]{1,0:T(8,128)(2,1)S(1)}, bf16[192,1024]{1,0:T(8,128)(2,1)S(1)}, u32[]{:S(2)}, u32[]{:S(2)}) collective-permute-start(bf16[192,1024]{1,0:T(8,128)(2,1)S(1)} %add_convert_fusion.3), channel_id=1, source_target_pairs={{0,4},{1,3},{2,6},{3,1},{4,0},{5,7},{6,2},{7,5},{8,12},{9,11},{10,... | collective-permute-start | bytes 1179656 | tf_op jit(solution)/shard_map/cond/branch_1_fun/ppermute | solution.py:481
  50.5 1.1 %add_convert_fusion.1 = bf16[192,1024]{1,0:T(8,128)(2,1)S(1)} fusion(bf16[192,1024]{1,0:T(8,128)(2,1)} %get-tuple-element.17, bf16[192,1024]{1,0:T(8,128)(2,1)S(1)} %get-tuple-element.16), kind=kLoop, calls=%fused_computation.1 | loop fusion | flops 786432 | bytes 1179648 | tf_op jit(solution)/shard_map/cond/branch_1_fun/convert_element_type | solution.py:334
  51.7 0.6 collective-permute-start.2
  52.3 4.5 %collective-permute-done = bf16[192,1024]{1,0:T(8,128)(2,1)S(1)} collective-permute-done((bf16[192,1024]{1,0:T(8,128)(2,1)S(1)}, bf16[192,1024]{1,0:T(8,128)(2,1)S(1)}, u32[]{:S(2)}, u32[]{:S(2)}) %collective-permute-start) | collective-permute-done | bytes 393248 | tf_op jit(solution)/shard_map/cond/branch_1_fun/ppermute | solution.py:481
  56.8 0.1 add_convert_fusion.2.refs_0_
  56.9 0.1 collective-permute-start.1
  57.0 4.0 %collective-permute-done.2 = bf16[192,1024]{1,0:T(8,128)(2,1)S(1)} collective-permute-done((bf16[192,1024]{1,0:T(8,128)(2,1)S(1)}, bf16[192,1024]{1,0:T(8,128)(2,1)S(1)}, u32[]{:S(2)}, u32[]{:S(2)}) %collective-permute-start.2) | collective-permute-done | bytes 393248 | tf_op jit(solution)/shard_map/cond/branch_1_fun/ppermute | solution.py:481
  61.0 0.1 add_convert_fusion.refs_1_
  61.2 0.1 collective-permute-start.3
  61.2 0.0 collective-permute-done.1.refs_1_
  61.2 1.2 %branch_1_fun.3.refs_0_ = f32[768,1024]{1,0:T(8,128)} custom-call(s32[1]{0:T(128)} %bitcast.which, bf16[192,1024]{1,0:T(8,128)(2,1)S(1)} %add_convert_fusion.2.refs_0_, bf16[192,1024]{1,0:T(8,128)(2,1)S(1)} %collective-permute-done.1.refs_1_), custom_call_target="tpu_custom_call" | custom-call | bytes 1048576 | tf_op jit(solution)/shard_map/cond/branch_1_fun/pallas_call | solution.py:259
  62.5 0.9 %branch_1_fun.4.refs_0_ = f32[768,1024]{1,0:T(8,128)} custom-call(s32[1]{0:T(128)} %bitcast.which, f32[768,1024]{1,0:T(8,128)} %branch_1_fun.3.refs_0_, bf16[192,1024]{1,0:T(8,128)(2,1)S(1)} %add_convert_fusion.refs_1_), custom_call_target="tpu_custom_call", output_to_operand_aliasing={{}: (1, {})} | custom-call | bytes 1048576 | tf_op jit(solution)/shard_map/cond/branch_1_fun/pallas_call | solution.py:259
  63.4 0.0 collective-permute-done.3.refs_1_
  63.4 0.9 %branch_1_fun.5 = f32[768,1024]{1,0:T(8,128)} custom-call(s32[1]{0:T(128)} %bitcast.which, f32[768,1024]{1,0:T(8,128)} %branch_1_fun.4.refs_0_, bf16[192,1024]{1,0:T(8,128)(2,1)S(1)} %collective-permute-done.3.refs_1_), custom_call_target="tpu_custom_call", output_to_operand_aliasing={{}: (1, {})} | custom-call | bytes 1048576 | tf_op jit(solution)/shard_map/cond/branch_1_fun/pallas_call | solution.py:259
  64.4 0.0 collective-permute-done.14.a_3_
  64.4 0.0 collective-permute-done.12.a_2_
  64.4 0.9 %shard_map.77 = (bf16[128,1024]{1,0:T(8,128)(2,1)}, bf16[128,1024]{1,0:T(8,128)(2,1)}) custom-call(s32[1]{0:T(128)} %bitcast.1.a_0_, bf16[128,1280]{1,0:T(8,128)(2,1)S(1)} %get-tuple-element.71.a_1_, bf16[128,1536]{1,0:T(8,128)(2,1)S(1)} %collective-permute-done.12.a_2_, bf16[128,1024]{1,0:T(8,128)(2,1)S(1)} %collective-permute-done.14.a_3_, ...), custom_call_target="tpu_custom_call" | custom-call | bytes 4194304 | tf_op jit(solution)/shard_map/pallas_call | solution.py:307
  (8 shorter events, 0.1 us)
Async XLA Ops:
  0.6 25.4 %copy-start.2 = (bf16[1,128,1024]{2,1,0:T(8,128)(2,1)S(1)}, bf16[1,128,1024]{2,1,0:T(8,128)(2,1)}, u32[]{:S(2)}) copy-start(bf16[1,128,1024]{2,1,0:T(8,128)(2,1)} %param.6) | copy-start | bytes 786436
  0.6 18.1 %collective-permute-start.4 = (bf16[128,1024]{1,0:T(8,128)(2,1)}, bf16[128,1024]{1,0:T(8,128)(2,1)S(1)}, u32[]{:S(2)}, u32[]{:S(2)}) collective-permute-start(bf16[128,1024]{1,0:T(8,128)(2,1)} %bitcast.23), channel_id=1, source_target_pairs={{0,8},{8,0},{16,24},{24,16},{1,9},{9,1},{17,25},{25,17},{2,10},{10... | collective-permute-start | bytes 786440 | tf_op jit(solution)/shard_map/ppermute | solution.py:326
  3.7 14.6 %collective-permute-start.5 = (bf16[128,1024]{1,0:T(8,128)(2,1)}, bf16[128,1024]{1,0:T(8,128)(2,1)S(1)}, u32[]{:S(2)}, u32[]{:S(2)}) collective-permute-start(bf16[128,1024]{1,0:T(8,128)(2,1)} %bitcast.24), channel_id=1, source_target_pairs={{0,16},{8,24},{16,0},{24,8},{1,17},{9,25},{17,1},{25,9},{2,18},{10... | collective-permute-start | bytes 786440 | tf_op jit(solution)/shard_map/ppermute | solution.py:326
  10.0 1.4 %copy-start = (bf16[768,1024]{1,0:T(8,128)(2,1)S(1)}, bf16[768,1024]{1,0:T(8,128)(2,1)}, u32[]{:S(2)}) copy-start(bf16[768,1024]{1,0:T(8,128)(2,1)} %weight.1) | copy-start | bytes 4718596
  11.4 0.9 %copy-start.1 = (bf16[1,128,1024]{2,1,0:T(8,128)(2,1)S(1)}, bf16[1,128,1024]{2,1,0:T(8,128)(2,1)}, u32[]{:S(2)}) copy-start(bf16[1,128,1024]{2,1,0:T(8,128)(2,1)} %param.6) | copy-start | bytes 786436
  18.3 7.7 %collective-permute-start.6 = (bf16[128,1024]{1,0:T(8,128)(2,1)S(1)}, bf16[128,1024]{1,0:T(8,128)(2,1)}, u32[]{:S(2)}, u32[]{:S(2)}) collective-permute-start(bf16[128,1024]{1,0:T(8,128)(2,1)S(1)} %collective-permute-done.5.refs_2_.refs_3_), channel_id=1, source_target_pairs={{0,8},{8,0},{16,24},{24,16},{1,9},{9,1},{17,25},{25,17},{2,10},{10... | collective-permute-start | bytes 786440 | tf_op jit(solution)/shard_map/ppermute | solution.py:326
  19.9 10.2 %collective-permute-start.7 = (bf16[128,256]{1,0:T(8,128)(2,1)S(1)}, bf16[128,256]{1,0:T(8,128)(2,1)S(1)}, u32[]{:S(2)}, u32[]{:S(2)}) collective-permute-start(bf16[128,256]{1,0:T(8,128)(2,1)S(1)} %get-tuple-element.55), channel_id=1, source_target_pairs={{0,8},{8,0},{16,24},{24,16},{1,9},{9,1},{17,25},{25,17},{2,10},{10... | collective-permute-start | bytes 196616 | tf_op jit(solution)/shard_map/ppermute | solution.py:326
  21.5 8.5 %collective-permute-start.8 = (bf16[128,256]{1,0:T(8,128)(2,1)S(1)}, bf16[128,256]{1,0:T(8,128)(2,1)S(1)}, u32[]{:S(2)}, u32[]{:S(2)}) collective-permute-start(bf16[128,256]{1,0:T(8,128)(2,1)S(1)} %get-tuple-element.56), channel_id=1, source_target_pairs={{0,16},{8,24},{16,0},{24,8},{1,17},{9,25},{17,1},{25,9},{2,18},{10... | collective-permute-start | bytes 196616 | tf_op jit(solution)/shard_map/ppermute | solution.py:326
  22.7 7.3 %collective-permute-start.9 = (bf16[128,256]{1,0:T(8,128)(2,1)S(1)}, bf16[128,256]{1,0:T(8,128)(2,1)S(1)}, u32[]{:S(2)}, u32[]{:S(2)}) collective-permute-start(bf16[128,256]{1,0:T(8,128)(2,1)S(1)} %get-tuple-element.57), channel_id=1, source_target_pairs={{0,24},{8,16},{16,8},{24,0},{1,25},{9,17},{17,9},{25,1},{2,26},{10... | collective-permute-start | bytes 196616 | tf_op jit(solution)/shard_map/ppermute | solution.py:326
  31.8 3.9 %collective-permute-start.10 = (bf16[384,1024]{1,0:T(8,128)(2,1)S(1)}, bf16[384,1024]{1,0:T(8,128)(2,1)S(1)}, u32[]{:S(2)}, u32[]{:S(2)}) collective-permute-start(bf16[384,1024]{1,0:T(8,128)(2,1)S(1)} %get-tuple-element.60), channel_id=1, source_target_pairs={{0,1},{1,0},{2,3},{3,2},{4,5},{5,4},{6,7},{7,6},{8,9},{9,8},{10,11... | collective-permute-start | bytes 2359304 | tf_op jit(solution)/shard_map/ppermute | solution.py:326
  33.6 13.6 %collective-permute-start.13 = (bf16[128,1024]{1,0:T(8,128)(2,1)S(1)}, bf16[128,1024]{1,0:T(8,128)(2,1)S(1)}, u32[]{:S(2)}, u32[]{:S(2)}) collective-permute-start(bf16[128,1024]{1,0:T(8,128)(2,1)S(1)} %shard_map.75), channel_id=1, source_target_pairs={{0,8},{8,0},{16,24},{24,16},{1,9},{9,1},{17,25},{25,17},{2,10},{10... | collective-permute-start | bytes 786440 | tf_op jit(solution)/shard_map/ppermute | solution.py:326
  36.2 8.5 %collective-permute-start.11 = (bf16[128,512]{1,0:T(8,128)(2,1)S(1)}, bf16[128,512]{1,0:T(8,128)(2,1)S(1)}, u32[]{:S(2)}, u32[]{:S(2)}) collective-permute-start(bf16[128,512]{1,0:T(8,128)(2,1)S(1)} %get-tuple-element.68), channel_id=1, source_target_pairs={{0,16},{8,24},{16,0},{24,8},{1,17},{9,25},{17,1},{25,9},{2,18},{10... | collective-permute-start | bytes 393224 | tf_op jit(solution)/shard_map/ppermute | solution.py:326
  36.7 11.6 %collective-permute-start.15 = (bf16[192,1024]{1,0:T(8,128)(2,1)S(1)}, bf16[192,1024]{1,0:T(8,128)(2,1)S(1)}, u32[]{:S(2)}, u32[]{:S(2)}) collective-permute-start(bf16[192,1024]{1,0:T(8,128)(2,1)S(1)} %get-tuple-element.61), channel_id=1, source_target_pairs={{0,2},{1,5},{2,0},{3,7},{4,6},{5,1},{6,4},{7,3},{8,10},{9,13},{10,... | collective-permute-start | bytes 1179656 | tf_op jit(solution)/shard_map/ppermute | solution.py:481
  38.2 10.6 %collective-permute-start.16 = (bf16[192,1024]{1,0:T(8,128)(2,1)S(1)}, bf16[192,1024]{1,0:T(8,128)(2,1)}, u32[]{:S(2)}, u32[]{:S(2)}) collective-permute-start(bf16[192,1024]{1,0:T(8,128)(2,1)S(1)} %get-tuple-element.62), channel_id=1, source_target_pairs={{0,2},{1,5},{2,0},{3,7},{4,6},{5,1},{6,4},{7,3},{8,10},{9,13},{10,... | collective-permute-start | bytes 1179656 | tf_op jit(solution)/shard_map/ppermute | solution.py:481
  44.7 19.7 %collective-permute-start.12 = (bf16[128,1536]{1,0:T(8,128)(2,1)S(1)}, bf16[128,1536]{1,0:T(8,128)(2,1)S(1)}, u32[]{:S(2)}, u32[]{:S(2)}) collective-permute-start(bf16[128,1536]{1,0:T(8,128)(2,1)S(1)} %shard_map.74), channel_id=1, source_target_pairs={{0,8},{8,0},{16,24},{24,16},{1,9},{9,1},{17,25},{25,17},{2,10},{10... | collective-permute-start | bytes 1179656 | tf_op jit(solution)/shard_map/ppermute | solution.py:326
  47.2 17.2 %collective-permute-start.14 = (bf16[128,1024]{1,0:T(8,128)(2,1)S(1)}, bf16[128,1024]{1,0:T(8,128)(2,1)S(1)}, u32[]{:S(2)}, u32[]{:S(2)}) collective-permute-start(bf16[128,1024]{1,0:T(8,128)(2,1)S(1)} %shard_map.76), channel_id=1, source_target_pairs={{0,16},{8,24},{16,0},{24,8},{1,17},{9,25},{17,1},{25,9},{2,18},{10... | collective-permute-start | bytes 786440 | tf_op jit(solution)/shard_map/ppermute | solution.py:326
  49.0 7.8 %collective-permute-start = (bf16[192,1024]{1,0:T(8,128)(2,1)S(1)}, bf16[192,1024]{1,0:T(8,128)(2,1)S(1)}, u32[]{:S(2)}, u32[]{:S(2)}) collective-permute-start(bf16[192,1024]{1,0:T(8,128)(2,1)S(1)} %add_convert_fusion.3), channel_id=1, source_target_pairs={{0,4},{1,3},{2,6},{3,1},{4,0},{5,7},{6,2},{7,5},{8,12},{9,11},{10,... | collective-permute-start | bytes 1179656 | tf_op jit(solution)/shard_map/cond/branch_1_fun/ppermute | solution.py:481
  51.7 9.3 %collective-permute-start.2 = (bf16[192,1024]{1,0:T(8,128)(2,1)S(1)}, bf16[192,1024]{1,0:T(8,128)(2,1)S(1)}, u32[]{:S(2)}, u32[]{:S(2)}) collective-permute-start(bf16[192,1024]{1,0:T(8,128)(2,1)S(1)} %add_convert_fusion.1), channel_id=1, source_target_pairs={{0,4},{1,3},{2,6},{3,1},{4,0},{5,7},{6,2},{7,5},{8,12},{9,11},{10,... | collective-permute-start | bytes 1179656 | tf_op jit(solution)/shard_map/cond/branch_1_fun/ppermute | solution.py:481
  56.9 4.3 %collective-permute-start.1 = (bf16[192,1024]{1,0:T(8,128)(2,1)S(1)}, bf16[192,1024]{1,0:T(8,128)(2,1)S(1)}, u32[]{:S(2)}, u32[]{:S(2)}) collective-permute-start(bf16[192,1024]{1,0:T(8,128)(2,1)S(1)} %add_convert_fusion.2.refs_0_), channel_id=1, source_target_pairs={{0,1},{1,0},{2,3},{3,2},{4,5},{5,4},{6,7},{7,6},{8,9},{9,8},{10,11... | collective-permute-start | bytes 1179656 | tf_op jit(solution)/shard_map/cond/branch_1_fun/ppermute | solution.py:326
  61.2 2.3 %collective-permute-start.3 = (bf16[192,1024]{1,0:T(8,128)(2,1)S(1)}, bf16[192,1024]{1,0:T(8,128)(2,1)S(1)}, u32[]{:S(2)}, u32[]{:S(2)}) collective-permute-start(bf16[192,1024]{1,0:T(8,128)(2,1)S(1)} %add_convert_fusion.refs_1_), channel_id=1, source_target_pairs={{0,1},{1,0},{2,3},{3,2},{4,5},{5,4},{6,7},{7,6},{8,9},{9,8},{10,11... | collective-permute-start | bytes 1179656 | tf_op jit(solution)/shard_map/cond/branch_1_fun/ppermute | solution.py:326

commit v7 on v6

--- a/solution.py
+++ b/solution.py
@@ -60,7 +60,7 @@
 
 
 def project_kernel(plan, *refs):
-    own, feats, (weight, qkv) = refs[0], refs[1:-2], refs[-2:]
+    own, feats, (weight, qkv) = refs[0], refs[-3:0:-1], refs[-2:]
     qkv[: plan.rows, :] = own[...]
     for s, x in enumerate(feats, 1):
         here = slice(s * plan.rows, (s + 1) * plan.rows)
@@ -369,7 +369,7 @@
         [array(earlier, plan.columns)],
         [],
         2 * earlier * plan.columns * width,
-        [own, *xs[1:-1], qkv_weight],
+        [own, *xs[-2:0:-1], qkv_weight],
     )
 
     listed = block_pairs[0]
@@ -486,14 +486,12 @@
             gots = [across(part, stage) for part in parts]
             parts = [add(part, got) for part, got in zip(parts, gots)]
         gots = [swap(part, "clus", 1) for part in parts]
-        count, result = len(parts), None
+        held, places = [], []
         for i, (part, got) in enumerate(zip(parts, gots)):
-            if i + 1 < count:
-                places = [(True, i, count), (False, i, count)]
-                result = scaled(plan, m, core, [part, got], places, result)
-            else:
-                result = scaled(plan, m, core, [part], [(True, i, count)], result)
-                result = scaled(plan, m, core, [got], [(False, i, count)], result)
+            held += [part, got]
+            places += [(True, i, len(parts)), (False, i, len(parts))]
+        result = scaled(plan, m, core, held[:-1], places[:-1])
+        result = scaled(plan, m, core, held[-1:], places[-1:], result)
         return result
 
     gots = [across(part, 0) for part in parts]

time: 65.6 us -> 65.1 us (level)
  Pallas kernels: 15.3 us -> 14.6 us
    pallas_call x3 -> x2, Pallas kernels: 3.1 us -> 2.42 us  [scaled(): pl.pallas_call(functools.partial(scale_kernel, plan, m, places), out_shap...]
  transfers between devices with their start and end apart: 17 -> 17, of which waited for: 6 -> 7; matrix products, arithmetic and copies ran while one was open for 7% -> 7% of each run, Pallas kernels for 20% -> 19%
where the time goes in v7:
time: 65.1 us; the launch traced here: 64.8 us
  starting transfers between devices  21.1 us (32%)
  waiting for transfers between devices  20.5 us (31%)
  Pallas kernels  14.6 us (22%)
  local copies, waits for them, and re-layouts  4.54 us (7%)
  other arithmetic  2.53 us (4%)
  between operations  1.47 us (2%)
    ppermute x13, starting transfers between devices, swap(): return lax.ppermute(x, axis, [(i, i ^ bits) for i in range(size)])  16.9 us
    pallas_call x11, Pallas kernels, call(): pl.pallas_call(functools.partial(kernel, plan), out_shape=out_shape, in_s...  12.2 us
    ppermute x13, waiting for transfers between devices, swap(): return lax.ppermute(x, axis, [(i, i ^ bits) for i in range(size)])  11.4 us
    ppermute x4, waiting for transfers between devices, across(): return lax.ppermute(x, 'clus', pairs)  9.04 us
    ppermute x4, starting transfers between devices, across(): return lax.ppermute(x, 'clus', pairs)  4.18 us
    pallas_call x2, Pallas kernels, scaled(): pl.pallas_call(functools.partial(scale_kernel, plan, m, places), out_shap...  2.42 us
    unnamed x6, local copies, waits for them, and re-layouts  2.36 us
    convert_element_type x4, other arithmetic, add(): return (a.astype(F32) + b.astype(F32)).astype(BF16)  1.52 us
  transfers between devices with their start and end apart: 17, of which 7 were waited for; matrix products, arithmetic and copies ran while one was open for 7% of the time, Pallas kernels for 19%

profile of v7, /device:TPU:0, one launch (start us, length us, event | category | flops | bytes accessed | tf_op | source)
XLA Modules:
  0.0 64.8 jit_solution(13817012819472403121)
XLA Ops:
  0.6 0.0 copy-start.2
  0.6 3.1 %collective-permute-start.5 = (bf16[128,1024]{1,0:T(8,128)(2,1)}, bf16[128,1024]{1,0:T(8,128)(2,1)S(1)}, u32[]{:S(2)}, u32[]{:S(2)}) collective-permute-start(bf16[128,1024]{1,0:T(8,128)(2,1)} %bitcast.23), channel_id=1, source_target_pairs={{0,8},{8,0},{16,24},{24,16},{1,9},{9,1},{17,25},{25,17},{2,10},{10... | collective-permute-start | bytes 786440 | tf_op jit(solution)/shard_map/ppermute | solution.py:326
  3.7 2.6 %collective-permute-start.4 = (bf16[128,1024]{1,0:T(8,128)(2,1)}, bf16[128,1024]{1,0:T(8,128)(2,1)S(1)}, u32[]{:S(2)}, u32[]{:S(2)}) collective-permute-start(bf16[128,1024]{1,0:T(8,128)(2,1)} %bitcast.24), channel_id=1, source_target_pairs={{0,16},{8,24},{16,0},{24,8},{1,17},{9,25},{17,1},{25,9},{2,18},{10... | collective-permute-start | bytes 786440 | tf_op jit(solution)/shard_map/ppermute | solution.py:326
  6.3 0.7 %broadcast_xor_fusion = s32[8,2]{0,1:T(2,128)S(1)} fusion(s32[]{:T(128)} %axis_index.23, s32[1,8,2]{1,2,0:T(2,128)} %param.8), kind=kLoop, calls=%fused_computation.23 | loop fusion | flops 16 | bytes 132 | tf_op jit(solution)/shard_map/xor | solution.py:382
  7.0 0.1 broadcast_compare_fusion
  7.1 0.1 and_reduce_fusion
  7.2 1.0 %dynamic-slice_bitcast_fusion = (bf16[128,256]{1,0:T(8,128)(2,1)S(1)}, bf16[128,256]{1,0:T(8,128)(2,1)S(1)}, bf16[128,256]{1,0:T(8,128)(2,1)S(1)}, bf16[128,256]{1,0:T(8,128)(2,1)S(1)}) fusion(bf16[1,128,1024]{2,1,0:T(8,128)(2,1)} %param.9, s32[]{:T(128)S(6)} %select_n.72, s32[]{:T(128)S(6)} %select_n.70, s32[]{:T(128)S(6)} %select_n.69, s32[]{:T(128)S(6)} %select_n.71), kind=kLoop, calls=%fused_computation.5 | loop fusion | bytes 524304 | tf_op jit(solution)/shard_map/dynamic_slice | solution.py:349
  8.2 1.2 %slice.11 = s32[1,1]{0,1:T(1,128)} slice(s32[8,2]{0,1:T(2,128)} %bitcast.28), slice={[0:1], [0:1]} | slice | bytes 8 | tf_op jit(solution)/shard_map/slice | solution.py:376
  10.0 0.0 copy-start
  10.0 1.4 %copy-done = bf16[768,1024]{1,0:T(8,128)(2,1)S(1)} copy-done((bf16[768,1024]{1,0:T(8,128)(2,1)S(1)}, bf16[768,1024]{1,0:T(8,128)(2,1)}, u32[]{:S(2)}) %copy-start) | copy-done | bytes 1572888
  11.4 0.0 copy-start.1
  11.4 0.9 %copy-done.1 = bf16[1,128,1024]{2,1,0:T(8,128)(2,1)S(1)} copy-done((bf16[1,128,1024]{2,1,0:T(8,128)(2,1)S(1)}, bf16[1,128,1024]{2,1,0:T(8,128)(2,1)}, u32[]{:S(2)}) %copy-start.1) | copy-done | bytes 262168
  12.4 1.2 %shard_map.67 = (bf16[768,1024]{1,0:T(8,128)(2,1)S(1)}, bf16[128,768]{1,0:T(8,128)(2,1)S(1)}, bf16[16,128]{1,0:T(8,128)(2,1)}) custom-call(bf16[128,1024]{1,0:T(8,128)(2,1)S(1)} %bitcast.25, bf16[768,1024]{1,0:T(8,128)(2,1)S(1)} %copy-done), custom_call_target="tpu_custom_call" | custom-call | flops 201326592 | bytes 4194304 | tf_op jit(solution)/shard_map/pallas_call | solution.py:307
  13.6 0.1 compare_convert_fusion.refs_7_
  13.7 4.6 %collective-permute-done.4.refs_1_.refs_3_ = bf16[128,1024]{1,0:T(8,128)(2,1)S(1)} collective-permute-done((bf16[128,1024]{1,0:T(8,128)(2,1)}, bf16[128,1024]{1,0:T(8,128)(2,1)S(1)}, u32[]{:S(2)}, u32[]{:S(2)}) %collective-permute-start.4) | collective-permute-done | bytes 262176 | tf_op jit(solution)/shard_map/ppermute | solution.py:326
  18.3 0.4 collective-permute-start.6
  18.7 0.0 collective-permute-done.5.refs_2_
  18.7 1.1 %shard_map.68.refs_0_ = bf16[384,768]{1,0:T(8,128)(2,1)S(1)} custom-call(bf16[128,768]{1,0:T(8,128)(2,1)S(1)} %get-tuple-element.50.refs_0_, bf16[128,1024]{1,0:T(8,128)(2,1)S(1)} %collective-permute-done.4.refs_1_.refs_3_, bf16[128,1024]{1,0:T(8,128)(2,1)S(1)} %collective-permute-done.5.refs_2_, bf16[768,1024]{1,0:T(8,128)(2,1)S(1)} %get-tuple-element.49.refs_3_.refs_5_.a_1_), custom_call_target="tpu_custom_call" | custom-call | flops 603979776 | bytes 4194304 | tf_op jit(solution)/shard_map/pallas_call | solution.py:307
  19.9 1.7 %collective-permute-start.7 = (bf16[128,256]{1,0:T(8,128)(2,1)S(1)}, bf16[128,256]{1,0:T(8,128)(2,1)S(1)}, u32[]{:S(2)}, u32[]{:S(2)}) collective-permute-start(bf16[128,256]{1,0:T(8,128)(2,1)S(1)} %get-tuple-element.55), channel_id=1, source_target_pairs={{0,8},{8,0},{16,24},{24,16},{1,9},{9,1},{17,25},{25,17},{2,10},{10... | collective-permute-start | bytes 196616 | tf_op jit(solution)/shard_map/ppermute | solution.py:326
  21.5 1.2 %collective-permute-start.8 = (bf16[128,256]{1,0:T(8,128)(2,1)S(1)}, bf16[128,256]{1,0:T(8,128)(2,1)S(1)}, u32[]{:S(2)}, u32[]{:S(2)}) collective-permute-start(bf16[128,256]{1,0:T(8,128)(2,1)S(1)} %get-tuple-element.56), channel_id=1, source_target_pairs={{0,16},{8,24},{16,0},{24,8},{1,17},{9,25},{17,1},{25,9},{2,18},{10... | collective-permute-start | bytes 196616 | tf_op jit(solution)/shard_map/ppermute | solution.py:326
  22.7 1.6 %collective-permute-start.9 = (bf16[128,256]{1,0:T(8,128)(2,1)S(1)}, bf16[128,256]{1,0:T(8,128)(2,1)S(1)}, u32[]{:S(2)}, u32[]{:S(2)}) collective-permute-start(bf16[128,256]{1,0:T(8,128)(2,1)S(1)} %get-tuple-element.57), channel_id=1, source_target_pairs={{0,24},{8,16},{16,8},{24,0},{1,25},{9,17},{17,9},{25,1},{2,26},{10... | collective-permute-start | bytes 196616 | tf_op jit(solution)/shard_map/ppermute | solution.py:326
  24.3 1.7 %collective-permute-done.6.refs_4_ = bf16[128,1024]{1,0:T(8,128)(2,1)} collective-permute-done((bf16[128,1024]{1,0:T(8,128)(2,1)S(1)}, bf16[128,1024]{1,0:T(8,128)(2,1)}, u32[]{:S(2)}, u32[]{:S(2)}) %collective-permute-start.6) | collective-permute-done | bytes 262176 | tf_op jit(solution)/shard_map/ppermute | solution.py:326
  26.1 0.0 copy-done.2
  26.1 4.0 %shard_map.69 = (bf16[4,512,512]{2,1,0:T(8,128)(2,1)S(1)}, f32[512,256]{1,0:T(8,128)S(1)}, bf16[512,1024]{1,0:T(8,128)(2,1)S(1)}, bf16[512,768]{1,0:T(8,128)(2,1)S(1)}, bf16[128,512]{1,0:T(8,128)(2,1)S(1)}) custom-call(bf16[384,768]{1,0:T(8,128)(2,1)S(1)} %shard_map.68.refs_0_, bf16[128,1024]{1,0:T(8,128)(2,1)S(1)} %bitcast.26, ...), custom_call_target="tpu_custom_call" | custom-call | flops 268435456 | bytes 4194304 | tf_op jit(solution)/shard_map/pallas_call | solution.py:307
  30.0 0.0 collective-permute-done.7.a_3_
  30.0 0.0 collective-permute-done.8.a_4_
  30.1 0.0 collective-permute-done.9.a_5_
  30.1 1.7 %shard_map.71 = (bf16[384,512]{1,0:T(8,128)(2,1)S(1)}, bf16[384,1024]{1,0:T(8,128)(2,1)S(1)}) custom-call(s32[1]{0:T(128)} %bitcast.13.a_0_, bf16[512,768]{1,0:T(8,128)(2,1)S(1)} %get-tuple-element.53.a_1_, bf16[128,256]{1,0:T(8,128)(2,1)S(1)} %get-tuple-element.54.a_2_, bf16[128,256]{1,0:T(8,128)(2,1)S(1)} %collective-permute-done.7.a_3_, ...), custom_call_target="tpu_custom_call" | custom-call | flops 671088640 | bytes 4194304 | tf_op jit(solution)/shard_map/pallas_call | solution.py:307
  31.8 0.1 collective-permute-start.10
  31.8 1.2 %shard_map.70.grad_ref.a_3_ = bf16[384,512]{1,0:T(8,128)(2,1)S(1)} custom-call(s32[1]{0:T(128)} %bitcast.2.a_0_, bf16[512,768]{1,0:T(8,128)(2,1)S(1)} %get-tuple-element.53.a_1_, bf16[128,256]{1,0:T(8,128)(2,1)S(1)} %get-tuple-element.54.a_2_, bf16[128,256]{1,0:T(8,128)(2,1)S(1)} %collective-permute-done.7.a_3_, ...), custom_call_target="tpu_custom_call" | custom-call | flops 268435456 | bytes 4194304 | tf_op jit(solution)/shard_map/pallas_call | solution.py:307
  33.1 0.5 shard_map.75
  33.6 2.1 %collective-permute-start.13 = (bf16[128,1024]{1,0:T(8,128)(2,1)S(1)}, bf16[128,1024]{1,0:T(8,128)(2,1)S(1)}, u32[]{:S(2)}, u32[]{:S(2)}) collective-permute-start(bf16[128,1024]{1,0:T(8,128)(2,1)S(1)} %shard_map.75), channel_id=1, source_target_pairs={{0,8},{8,0},{16,24},{24,16},{1,9},{9,1},{17,25},{25,17},{2,10},{10... | collective-permute-start | bytes 786440 | tf_op jit(solution)/shard_map/ppermute | solution.py:326
  35.6 0.0 collective-permute-done.10.got_ref
  35.6 0.6 shard_map.72
  36.2 0.5 collective-permute-start.11
  36.7 1.5 %collective-permute-start.15 = (bf16[192,1024]{1,0:T(8,128)(2,1)S(1)}, bf16[192,1024]{1,0:T(8,128)(2,1)S(1)}, u32[]{:S(2)}, u32[]{:S(2)}) collective-permute-start(bf16[192,1024]{1,0:T(8,128)(2,1)S(1)} %get-tuple-element.61), channel_id=1, source_target_pairs={{0,2},{1,5},{2,0},{3,7},{4,6},{5,1},{6,4},{7,3},{8,10},{9,13},{10,... | collective-permute-start | bytes 1179656 | tf_op jit(solution)/shard_map/ppermute | solution.py:481
  38.2 0.5 collective-permute-start.16
  38.8 1.0 %shard_map.73 = (bf16[128,1280]{1,0:T(8,128)(2,1)S(1)}, bf16[128,1280]{1,0:T(8,128)(2,1)S(1)}, bf16[128,1024]{1,0:T(8,128)(2,1)S(1)}) custom-call(s32[1]{0:T(128)} %bitcast.2.a_0_, bf16[768,1024]{1,0:T(8,128)(2,1)S(1)} %get-tuple-element.49.refs_3_.refs_5_.a_1_, f32[512,256]{1,0:T(8,128)S(1)} %get-tuple-element.63.a_7_.a_2_, ...), custom_call_target="tpu_custom_call" | custom-call | flops 603979776 | bytes 4194304 | tf_op jit(solution)/shard_map/pallas_call | solution.py:307
  39.8 4.9 %collective-permute-done.11.other.a_4_ = bf16[128,512]{1,0:T(8,128)(2,1)S(1)} collective-permute-done((bf16[128,512]{1,0:T(8,128)(2,1)S(1)}, bf16[128,512]{1,0:T(8,128)(2,1)S(1)}, u32[]{:S(2)}, u32[]{:S(2)}) %collective-permute-start.11) | collective-permute-done | bytes 131104 | tf_op jit(solution)/shard_map/ppermute | solution.py:326
  44.7 2.4 %collective-permute-start.12 = (bf16[128,1536]{1,0:T(8,128)(2,1)S(1)}, bf16[128,1536]{1,0:T(8,128)(2,1)S(1)}, u32[]{:S(2)}, u32[]{:S(2)}) collective-permute-start(bf16[128,1536]{1,0:T(8,128)(2,1)S(1)} %shard_map.74), channel_id=1, source_target_pairs={{0,8},{8,0},{16,24},{24,16},{1,9},{9,1},{17,25},{25,17},{2,10},{10... | collective-permute-start | bytes 1179656 | tf_op jit(solution)/shard_map/ppermute | solution.py:326
  47.1 0.0 collective-permute-done.13.other
  47.1 0.1 shard_map.76
  47.2 1.1 %collective-permute-start.14 = (bf16[128,1024]{1,0:T(8,128)(2,1)S(1)}, bf16[128,1024]{1,0:T(8,128)(2,1)S(1)}, u32[]{:S(2)}, u32[]{:S(2)}) collective-permute-start(bf16[128,1024]{1,0:T(8,128)(2,1)S(1)} %shard_map.76), channel_id=1, source_target_pairs={{0,16},{8,24},{16,0},{24,8},{1,17},{9,25},{17,1},{25,9},{2,18},{10... | collective-permute-start | bytes 786440 | tf_op jit(solution)/shard_map/ppermute | solution.py:326
  48.3 0.0 collective-permute-done.15
  48.3 0.5 collective-permute-done.16
  48.8 15.1 %conditional.1 = (f32[768,1024]{1,0:T(8,128)}) conditional(s32[]{:T(128)} %convert_element_type.47, () %tuple.24, (s32[]{:T(128)}, bf16[192,1024]{1,0:T(8,128)(2,1)S(1)}, bf16[192,1024]{1,0:T(8,128)(2,1)S(1)}, bf16[192,1024]{1,0:T(8,128)(2,1)S(1)}, bf16[192,1024]{1,0:T(8,128)(2,1)}) %tuple.25), branch_computations={%region_1.2_spmd, %region_2.3_spmd} | conditional | flops 3145728 | bytes 13107368 | solution.py:498
  48.8 0.1 add_convert_fusion.3
  49.0 1.6 %collective-permute-start = (bf16[192,1024]{1,0:T(8,128)(2,1)S(1)}, bf16[192,1024]{1,0:T(8,128)(2,1)S(1)}, u32[]{:S(2)}, u32[]{:S(2)}) collective-permute-start(bf16[192,1024]{1,0:T(8,128)(2,1)S(1)} %add_convert_fusion.3), channel_id=1, source_target_pairs={{0,4},{1,3},{2,6},{3,1},{4,0},{5,7},{6,2},{7,5},{8,12},{9,11},{10,... | collective-permute-start | bytes 1179656 | tf_op jit(solution)/shard_map/cond/branch_1_fun/ppermute | solution.py:481
  50.6 1.1 %add_convert_fusion.1 = bf16[192,1024]{1,0:T(8,128)(2,1)S(1)} fusion(bf16[192,1024]{1,0:T(8,128)(2,1)} %get-tuple-element.17, bf16[192,1024]{1,0:T(8,128)(2,1)S(1)} %get-tuple-element.16), kind=kLoop, calls=%fused_computation.1 | loop fusion | flops 786432 | bytes 1179648 | tf_op jit(solution)/shard_map/cond/branch_1_fun/convert_element_type | solution.py:334
  51.7 0.6 collective-permute-start.2
  52.3 4.5 %collective-permute-done = bf16[192,1024]{1,0:T(8,128)(2,1)S(1)} collective-permute-done((bf16[192,1024]{1,0:T(8,128)(2,1)S(1)}, bf16[192,1024]{1,0:T(8,128)(2,1)S(1)}, u32[]{:S(2)}, u32[]{:S(2)}) %collective-permute-start) | collective-permute-done | bytes 393248 | tf_op jit(solution)/shard_map/cond/branch_1_fun/ppermute | solution.py:481
  56.8 0.1 add_convert_fusion.2.refs_0_
  56.9 0.1 collective-permute-start.1
  57.0 4.0 %collective-permute-done.2 = bf16[192,1024]{1,0:T(8,128)(2,1)S(1)} collective-permute-done((bf16[192,1024]{1,0:T(8,128)(2,1)S(1)}, bf16[192,1024]{1,0:T(8,128)(2,1)S(1)}, u32[]{:S(2)}, u32[]{:S(2)}) %collective-permute-start.2) | collective-permute-done | bytes 393248 | tf_op jit(solution)/shard_map/cond/branch_1_fun/ppermute | solution.py:481
  61.0 0.1 add_convert_fusion.refs_2_
  61.2 0.1 collective-permute-start.3
  61.2 0.0 collective-permute-done.1.refs_1_
  61.3 1.5 %branch_1_fun.2.refs_0_ = f32[768,1024]{1,0:T(8,128)} custom-call(s32[1]{0:T(128)} %bitcast.which, bf16[192,1024]{1,0:T(8,128)(2,1)S(1)} %add_convert_fusion.2.refs_0_, bf16[192,1024]{1,0:T(8,128)(2,1)S(1)} %collective-permute-done.1.refs_1_, bf16[192,1024]{1,0:T(8,128)(2,1)S(1)} %add_convert_fusion.refs_2_), custom_call_target="tpu_custom_call" | custom-call | bytes 1048576 | tf_op jit(solution)/shard_map/cond/branch_1_fun/pallas_call | solution.py:259
  62.7 0.2 collective-permute-done.3.refs_1_
  63.0 0.9 %branch_1_fun.3 = f32[768,1024]{1,0:T(8,128)} custom-call(s32[1]{0:T(128)} %bitcast.which, f32[768,1024]{1,0:T(8,128)} %branch_1_fun.2.refs_0_, bf16[192,1024]{1,0:T(8,128)(2,1)S(1)} %collective-permute-done.3.refs_1_), custom_call_target="tpu_custom_call", output_to_operand_aliasing={{}: (1, {})} | custom-call | bytes 1048576 | tf_op jit(solution)/shard_map/cond/branch_1_fun/pallas_call | solution.py:259
  63.9 0.0 collective-permute-done.14.a_3_
  63.9 0.0 collective-permute-done.12.a_2_
  63.9 0.9 %shard_map.77 = (bf16[128,1024]{1,0:T(8,128)(2,1)}, bf16[128,1024]{1,0:T(8,128)(2,1)}) custom-call(s32[1]{0:T(128)} %bitcast.1.a_0_, bf16[128,1280]{1,0:T(8,128)(2,1)S(1)} %get-tuple-element.71.a_1_, bf16[128,1536]{1,0:T(8,128)(2,1)S(1)} %collective-permute-done.12.a_2_, bf16[128,1024]{1,0:T(8,128)(2,1)S(1)} %collective-permute-done.14.a_3_, ...), custom_call_target="tpu_custom_call" | custom-call | bytes 4194304 | tf_op jit(solution)/shard_map/pallas_call | solution.py:307
  (8 shorter events, 0.1 us)
Async XLA Ops:
  0.6 25.4 %copy-start.2 = (bf16[1,128,1024]{2,1,0:T(8,128)(2,1)S(1)}, bf16[1,128,1024]{2,1,0:T(8,128)(2,1)}, u32[]{:S(2)}) copy-start(bf16[1,128,1024]{2,1,0:T(8,128)(2,1)} %param.6) | copy-start | bytes 786436
  0.6 18.1 %collective-permute-start.5 = (bf16[128,1024]{1,0:T(8,128)(2,1)}, bf16[128,1024]{1,0:T(8,128)(2,1)S(1)}, u32[]{:S(2)}, u32[]{:S(2)}) collective-permute-start(bf16[128,1024]{1,0:T(8,128)(2,1)} %bitcast.23), channel_id=1, source_target_pairs={{0,8},{8,0},{16,24},{24,16},{1,9},{9,1},{17,25},{25,17},{2,10},{10... | collective-permute-start | bytes 786440 | tf_op jit(solution)/shard_map/ppermute | solution.py:326
  3.7 14.6 %collective-permute-start.4 = (bf16[128,1024]{1,0:T(8,128)(2,1)}, bf16[128,1024]{1,0:T(8,128)(2,1)S(1)}, u32[]{:S(2)}, u32[]{:S(2)}) collective-permute-start(bf16[128,1024]{1,0:T(8,128)(2,1)} %bitcast.24), channel_id=1, source_target_pairs={{0,16},{8,24},{16,0},{24,8},{1,17},{9,25},{17,1},{25,9},{2,18},{10... | collective-permute-start | bytes 786440 | tf_op jit(solution)/shard_map/ppermute | solution.py:326
  10.0 1.4 %copy-start = (bf16[768,1024]{1,0:T(8,128)(2,1)S(1)}, bf16[768,1024]{1,0:T(8,128)(2,1)}, u32[]{:S(2)}) copy-start(bf16[768,1024]{1,0:T(8,128)(2,1)} %weight.1) | copy-start | bytes 4718596
  11.4 0.9 %copy-start.1 = (bf16[1,128,1024]{2,1,0:T(8,128)(2,1)S(1)}, bf16[1,128,1024]{2,1,0:T(8,128)(2,1)}, u32[]{:S(2)}) copy-start(bf16[1,128,1024]{2,1,0:T(8,128)(2,1)} %param.6) | copy-start | bytes 786436
  18.3 7.7 %collective-permute-start.6 = (bf16[128,1024]{1,0:T(8,128)(2,1)S(1)}, bf16[128,1024]{1,0:T(8,128)(2,1)}, u32[]{:S(2)}, u32[]{:S(2)}) collective-permute-start(bf16[128,1024]{1,0:T(8,128)(2,1)S(1)} %collective-permute-done.4.refs_1_.refs_3_), channel_id=1, source_target_pairs={{0,8},{8,0},{16,24},{24,16},{1,9},{9,1},{17,25},{25,17},{2,10},{10... | collective-permute-start | bytes 786440 | tf_op jit(solution)/shard_map/ppermute | solution.py:326
  19.9 10.2 %collective-permute-start.7 = (bf16[128,256]{1,0:T(8,128)(2,1)S(1)}, bf16[128,256]{1,0:T(8,128)(2,1)S(1)}, u32[]{:S(2)}, u32[]{:S(2)}) collective-permute-start(bf16[128,256]{1,0:T(8,128)(2,1)S(1)} %get-tuple-element.55), channel_id=1, source_target_pairs={{0,8},{8,0},{16,24},{24,16},{1,9},{9,1},{17,25},{25,17},{2,10},{10... | collective-permute-start | bytes 196616 | tf_op jit(solution)/shard_map/ppermute | solution.py:326
  21.5 8.5 %collective-permute-start.8 = (bf16[128,256]{1,0:T(8,128)(2,1)S(1)}, bf16[128,256]{1,0:T(8,128)(2,1)S(1)}, u32[]{:S(2)}, u32[]{:S(2)}) collective-permute-start(bf16[128,256]{1,0:T(8,128)(2,1)S(1)} %get-tuple-element.56), channel_id=1, source_target_pairs={{0,16},{8,24},{16,0},{24,8},{1,17},{9,25},{17,1},{25,9},{2,18},{10... | collective-permute-start | bytes 196616 | tf_op jit(solution)/shard_map/ppermute | solution.py:326
  22.7 7.3 %collective-permute-start.9 = (bf16[128,256]{1,0:T(8,128)(2,1)S(1)}, bf16[128,256]{1,0:T(8,128)(2,1)S(1)}, u32[]{:S(2)}, u32[]{:S(2)}) collective-permute-start(bf16[128,256]{1,0:T(8,128)(2,1)S(1)} %get-tuple-element.57), channel_id=1, source_target_pairs={{0,24},{8,16},{16,8},{24,0},{1,25},{9,17},{17,9},{25,1},{2,26},{10... | collective-permute-start | bytes 196616 | tf_op jit(solution)/shard_map/ppermute | solution.py:326
  31.8 3.9 %collective-permute-start.10 = (bf16[384,1024]{1,0:T(8,128)(2,1)S(1)}, bf16[384,1024]{1,0:T(8,128)(2,1)S(1)}, u32[]{:S(2)}, u32[]{:S(2)}) collective-permute-start(bf16[384,1024]{1,0:T(8,128)(2,1)S(1)} %get-tuple-element.60), channel_id=1, source_target_pairs={{0,1},{1,0},{2,3},{3,2},{4,5},{5,4},{6,7},{7,6},{8,9},{9,8},{10,11... | collective-permute-start | bytes 2359304 | tf_op jit(solution)/shard_map/ppermute | solution.py:326
  33.6 13.6 %collective-permute-start.13 = (bf16[128,1024]{1,0:T(8,128)(2,1)S(1)}, bf16[128,1024]{1,0:T(8,128)(2,1)S(1)}, u32[]{:S(2)}, u32[]{:S(2)}) collective-permute-start(bf16[128,1024]{1,0:T(8,128)(2,1)S(1)} %shard_map.75), channel_id=1, source_target_pairs={{0,8},{8,0},{16,24},{24,16},{1,9},{9,1},{17,25},{25,17},{2,10},{10... | collective-permute-start | bytes 786440 | tf_op jit(solution)/shard_map/ppermute | solution.py:326
  36.2 8.5 %collective-permute-start.11 = (bf16[128,512]{1,0:T(8,128)(2,1)S(1)}, bf16[128,512]{1,0:T(8,128)(2,1)S(1)}, u32[]{:S(2)}, u32[]{:S(2)}) collective-permute-start(bf16[128,512]{1,0:T(8,128)(2,1)S(1)} %get-tuple-element.68), channel_id=1, source_target_pairs={{0,16},{8,24},{16,0},{24,8},{1,17},{9,25},{17,1},{25,9},{2,18},{10... | collective-permute-start | bytes 393224 | tf_op jit(solution)/shard_map/ppermute | solution.py:326
  36.7 11.6 %collective-permute-start.15 = (bf16[192,1024]{1,0:T(8,128)(2,1)S(1)}, bf16[192,1024]{1,0:T(8,128)(2,1)S(1)}, u32[]{:S(2)}, u32[]{:S(2)}) collective-permute-start(bf16[192,1024]{1,0:T(8,128)(2,1)S(1)} %get-tuple-element.61), channel_id=1, source_target_pairs={{0,2},{1,5},{2,0},{3,7},{4,6},{5,1},{6,4},{7,3},{8,10},{9,13},{10,... | collective-permute-start | bytes 1179656 | tf_op jit(solution)/shard_map/ppermute | solution.py:481
  38.2 10.6 %collective-permute-start.16 = (bf16[192,1024]{1,0:T(8,128)(2,1)S(1)}, bf16[192,1024]{1,0:T(8,128)(2,1)}, u32[]{:S(2)}, u32[]{:S(2)}) collective-permute-start(bf16[192,1024]{1,0:T(8,128)(2,1)S(1)} %get-tuple-element.62), channel_id=1, source_target_pairs={{0,2},{1,5},{2,0},{3,7},{4,6},{5,1},{6,4},{7,3},{8,10},{9,13},{10,... | collective-permute-start | bytes 1179656 | tf_op jit(solution)/shard_map/ppermute | solution.py:481
  44.7 19.2 %collective-permute-start.12 = (bf16[128,1536]{1,0:T(8,128)(2,1)S(1)}, bf16[128,1536]{1,0:T(8,128)(2,1)S(1)}, u32[]{:S(2)}, u32[]{:S(2)}) collective-permute-start(bf16[128,1536]{1,0:T(8,128)(2,1)S(1)} %shard_map.74), channel_id=1, source_target_pairs={{0,8},{8,0},{16,24},{24,16},{1,9},{9,1},{17,25},{25,17},{2,10},{10... | collective-permute-start | bytes 1179656 | tf_op jit(solution)/shard_map/ppermute | solution.py:326
  47.2 16.7 %collective-permute-start.14 = (bf16[128,1024]{1,0:T(8,128)(2,1)S(1)}, bf16[128,1024]{1,0:T(8,128)(2,1)S(1)}, u32[]{:S(2)}, u32[]{:S(2)}) collective-permute-start(bf16[128,1024]{1,0:T(8,128)(2,1)S(1)} %shard_map.76), channel_id=1, source_target_pairs={{0,16},{8,24},{16,0},{24,8},{1,17},{9,25},{17,1},{25,9},{2,18},{10... | collective-permute-start | bytes 786440 | tf_op jit(solution)/shard_map/ppermute | solution.py:326
  49.0 7.8 %collective-permute-start = (bf16[192,1024]{1,0:T(8,128)(2,1)S(1)}, bf16[192,1024]{1,0:T(8,128)(2,1)S(1)}, u32[]{:S(2)}, u32[]{:S(2)}) collective-permute-start(bf16[192,1024]{1,0:T(8,128)(2,1)S(1)} %add_convert_fusion.3), channel_id=1, source_target_pairs={{0,4},{1,3},{2,6},{3,1},{4,0},{5,7},{6,2},{7,5},{8,12},{9,11},{10,... | collective-permute-start | bytes 1179656 | tf_op jit(solution)/shard_map/cond/branch_1_fun/ppermute | solution.py:481
  51.7 9.3 %collective-permute-start.2 = (bf16[192,1024]{1,0:T(8,128)(2,1)S(1)}, bf16[192,1024]{1,0:T(8,128)(2,1)S(1)}, u32[]{:S(2)}, u32[]{:S(2)}) collective-permute-start(bf16[192,1024]{1,0:T(8,128)(2,1)S(1)} %add_convert_fusion.1), channel_id=1, source_target_pairs={{0,4},{1,3},{2,6},{3,1},{4,0},{5,7},{6,2},{7,5},{8,12},{9,11},{10,... | collective-permute-start | bytes 1179656 | tf_op jit(solution)/shard_map/cond/branch_1_fun/ppermute | solution.py:481
  56.9 4.3 %collective-permute-start.1 = (bf16[192,1024]{1,0:T(8,128)(2,1)S(1)}, bf16[192,1024]{1,0:T(8,128)(2,1)S(1)}, u32[]{:S(2)}, u32[]{:S(2)}) collective-permute-start(bf16[192,1024]{1,0:T(8,128)(2,1)S(1)} %add_convert_fusion.2.refs_0_), channel_id=1, source_target_pairs={{0,1},{1,0},{2,3},{3,2},{4,5},{5,4},{6,7},{7,6},{8,9},{9,8},{10,11... | collective-permute-start | bytes 1179656 | tf_op jit(solution)/shard_map/cond/branch_1_fun/ppermute | solution.py:326
  61.2 1.8 %collective-permute-start.3 = (bf16[192,1024]{1,0:T(8,128)(2,1)S(1)}, bf16[192,1024]{1,0:T(8,128)(2,1)S(1)}, u32[]{:S(2)}, u32[]{:S(2)}) collective-permute-start(bf16[192,1024]{1,0:T(8,128)(2,1)S(1)} %add_convert_fusion.refs_2_), channel_id=1, source_target_pairs={{0,1},{1,0},{2,3},{3,2},{4,5},{5,4},{6,7},{7,6},{8,9},{9,8},{10,11... | collective-permute-start | bytes 1179656 | tf_op jit(solution)/shard_map/cond/branch_1_fun/ppermute | solution.py:326

commit v8 on v7

--- a/solution.py
+++ b/solution.py
@@ -121,7 +121,6 @@
     n, rows = plan.n, plan.rows
     known, feats, (weight, key_bias, row_hot) = refs[0], refs[1 : 1 + n], refs[1 + n : 4 + n]
     low_ref, sum_ref, full_ref, qkv = refs[4 + n : 8 + n]
-    pieces = refs[8 + n : -4]
     q_s, k_s, v_s, ka_s = refs[-4:]
     for s, x in enumerate(feats):
         full_ref[s * rows : (s + 1) * rows, :] = x[...]
@@ -146,11 +145,6 @@
                     sum_ref[here, lanes] = merge(plan, h, mm(low, v_s[...]), sum_ref[here, lanes])
 
                 chunks(plan, one_chunk)
-    for out in pieces:
-        hcols = sum_ref.shape[1]
-        for i in range(2):
-            here = slice((2 + i) * rows, (3 + i) * rows)
-            out[:, i * hcols : (i + 1) * hcols] = sum_ref[here, :].astype(BF16)
 
 
 def backward_kernel(plan, with_weight, *refs):
@@ -268,14 +262,12 @@
     )(*args)
 
 
-def add_kernel(plan, one, other, out):
-    out[...] = add(one[...], other[...])
-
-
-def beside_kernel(plan, one, other, out):
-    wide = one.shape[1]
-    out[:, :wide] = one[...]
-    out[:, wide:] = other[:, other.shape[1] // 2 :]
+def relay_kernel(plan, own, ahead, out):
+    wide = own.shape[1]
+    width = wide - plan.heads * HD
+    out[:, :width] = add(own[:, :width], ahead[:, :width])
+    out[:, width:wide] = own[:, width:]
+    out[:, wide:] = ahead[:, width:]
 
 
 def combine_kernel(plan, pieces, place, *refs):
@@ -359,7 +351,7 @@
     )
     if n == 4:
         far, near = swap(feats, "seq", 2), swap(feats, "seq", 1)
-        xs = [feats, near, far, swap(after(far, mark), "seq", 1)]
+        xs = [feats, near, far, jnp.where(z < n, swap(after(far, mark), "seq", 1), near)]
     else:
         xs = [feats] + [swap(feats, "seq", k) for k in range(1, n)]
     earlier = nodes - rows
@@ -392,11 +384,10 @@
     def tiles(count):
         return [pltpu.VMEM((nodes, plan.tile), BF16)] * count
 
-    low, sums, full, qkv, *beyond = call(
+    low, sums, full, qkv = call(
         forward_kernel,
         plan,
-        [array(heads, nodes, nodes), array(nodes, hcols, dtype=F32), array(nodes, width), array(nodes, plan.columns)]
-        + [array(rows, 2 * hcols)] * (n == 4),
+        [array(heads, nodes, nodes), array(nodes, hcols, dtype=F32), array(nodes, width), array(nodes, plan.columns)],
         tiles(3) + [pltpu.VMEM((nodes, 2 * HD), BF16)],
         4 * nodes * nodes * HD * heads,
         [known, *xs, qkv_weight, key_bias, row_hot],
@@ -452,21 +443,14 @@
         )
 
     if n == 4:
-        (ahead,) = terms([3], [0])
+        (ahead,) = terms([3], [1])
         ahead = swap(ahead, "seq", 1)
-        own_term, near, far_term = terms([0, 1, 2], [1, 1, 0], parts)
-        across_z = swap(after(beyond[0], parts), "seq", 2)
-        (pair,) = call(add_kernel, plan, [array(rows, width)], [], 0, [far_term, ahead])
-        (near,) = call(
-            beside_kernel,
-            plan,
-            [array(rows, width + 2 * hcols)],
-            [],
-            0,
-            [near, across_z],
+        own_term, near, far_term = terms([0, 1, 2], [1, 1, 1], parts)
+        (pair,) = call(
+            relay_kernel, plan, [array(rows, width + 2 * hcols)], [], 0, [far_term, ahead]
         )
-        received = [own_term, swap(near, "seq", 1), swap(pair, "seq", 2), across_z]
-        places = [(0, width), (1, width), (3, 0), (1, width + hcols)]
+        received = [own_term, swap(after(near, ahead), "seq", 1), swap(pair, "seq", 2)]
+        places = [(0, width), (1, width), (2, width), (2, width + hcols)]
     else:
         sends = terms(range(n), [1] * n)
         received = [sends[0]] + [swap(sends[k], "seq", k) for k in range(1, n)]

time: 65.1 us -> 64.4 us (0.989)
  waiting for transfers between devices: 20.5 us -> 23.1 us
  starting transfers between devices: 21.1 us -> 19.7 us
  other arithmetic: 2.53 us -> 1.57 us
  Pallas kernels: 14.6 us -> 13.7 us
    ppermute x4, waiting for transfers between devices: 9.04 us -> 10.5 us  [across(): return lax.ppermute(x, 'clus', pairs)]
    ppermute x13 -> x12, starting transfers between devices: 16.9 us -> 15.5 us  [swap(): return lax.ppermute(x, axis, [(i, i ^ bits) for i in range(size)])]
    ppermute x13 -> x12, waiting for transfers between devices: 11.4 us -> 12.6 us  [swap(): return lax.ppermute(x, axis, [(i, i ^ bits) for i in range(size)])]
    convert_element_type x4, other arithmetic: 1.52 us -> 0.53 us  [add(): return (a.astype(F32) + b.astype(F32)).astype(BF16)]
    pallas_call x11 -> x10, Pallas kernels: 12.2 us -> 11.2 us  [call(): pl.pallas_call(functools.partial(kernel, plan), out_shape=out_shape, in_s...]
  transfers between devices with their start and end apart: 17 -> 16, of which waited for: 7 -> 9; matrix products, arithmetic and copies ran while one was open for 7% -> 6% of each run, Pallas kernels for 19% -> 17%
where the time goes in v8:
time: 64.4 us; the launch traced here: 64.2 us
  waiting for transfers between devices  23.1 us (36%)
  starting transfers between devices  19.7 us (31%)
  Pallas kernels  13.7 us (21%)
  local copies, waits for them, and re-layouts  4.54 us (7%)
  other arithmetic  1.57 us (2%)
  between operations  1.47 us (2%)
    ppermute x12, starting transfers between devices, swap(): return lax.ppermute(x, axis, [(i, i ^ bits) for i in range(size)])  15.5 us
    ppermute x12, waiting for transfers between devices, swap(): return lax.ppermute(x, axis, [(i, i ^ bits) for i in range(size)])  12.6 us
    pallas_call x10, Pallas kernels, call(): pl.pallas_call(functools.partial(kernel, plan), out_shape=out_shape, in_s...  11.2 us
    ppermute x4, waiting for transfers between devices, across(): return lax.ppermute(x, 'clus', pairs)  10.5 us
    ppermute x4, starting transfers between devices, across(): return lax.ppermute(x, 'clus', pairs)  4.25 us
    pallas_call x2, Pallas kernels, scaled(): pl.pallas_call(functools.partial(scale_kernel, plan, m, places), out_shap...  2.42 us
    unnamed x6, local copies, waits for them, and re-layouts  2.36 us
  transfers between devices with their start and end apart: 16, of which 9 were waited for; matrix products, arithmetic and copies ran while one was open for 6% of the time, Pallas kernels for 17%

profile of v8, /device:TPU:0, one launch (start us, length us, event | category | flops | bytes accessed | tf_op | source)
XLA Modules:
  0.0 64.2 jit_solution(16717929734530544341)
XLA Ops:
  0.6 3.1 %collective-permute-start.5 = (bf16[128,1024]{1,0:T(8,128)(2,1)}, bf16[128,1024]{1,0:T(8,128)(2,1)S(1)}, u32[]{:S(2)}, u32[]{:S(2)}) collective-permute-start(bf16[128,1024]{1,0:T(8,128)(2,1)} %bitcast.23), channel_id=1, source_target_pairs={{0,8},{8,0},{16,24},{24,16},{1,9},{9,1},{17,25},{25,17},{2,10},{10... | collective-permute-start | bytes 786440 | tf_op jit(solution)/shard_map/ppermute | solution.py:318
  3.7 2.6 %collective-permute-start.4 = (bf16[128,1024]{1,0:T(8,128)(2,1)}, bf16[128,1024]{1,0:T(8,128)(2,1)S(1)}, u32[]{:S(2)}, u32[]{:S(2)}) collective-permute-start(bf16[128,1024]{1,0:T(8,128)(2,1)} %bitcast.24), channel_id=1, source_target_pairs={{0,16},{8,24},{16,0},{24,8},{1,17},{9,25},{17,1},{25,9},{2,18},{10... | collective-permute-start | bytes 786440 | tf_op jit(solution)/shard_map/ppermute | solution.py:318
  6.3 0.7 %broadcast_xor_fusion = s32[8,2]{0,1:T(2,128)S(1)} fusion(s32[]{:T(128)} %axis_index.23, s32[1,8,2]{1,2,0:T(2,128)} %param.8), kind=kLoop, calls=%fused_computation.24 | loop fusion | flops 16 | bytes 132 | tf_op jit(solution)/shard_map/xor | solution.py:374
  7.0 0.1 broadcast_compare_fusion
  7.1 0.1 compare_convert_fusion.refs_7_
  7.2 0.0 copy-start.2
  7.2 0.1 and_reduce_fusion
  7.3 1.0 %dynamic-slice_bitcast_fusion = (bf16[128,256]{1,0:T(8,128)(2,1)S(1)}, bf16[128,256]{1,0:T(8,128)(2,1)S(1)}, bf16[128,256]{1,0:T(8,128)(2,1)S(1)}, bf16[128,256]{1,0:T(8,128)(2,1)S(1)}) fusion(bf16[1,128,1024]{2,1,0:T(8,128)(2,1)} %param.9, s32[]{:T(128)S(6)} %select_n.82, s32[]{:T(128)S(6)} %select_n.80, s32[]{:T(128)S(6)} %select_n.79, s32[]{:T(128)S(6)} %select_n.81), kind=kLoop, calls=%fused_computation.6 | loop fusion | bytes 524304 | tf_op jit(solution)/shard_map/dynamic_slice | solution.py:341
  8.3 1.2 %slice.11 = s32[1,1]{0,1:T(1,128)} slice(s32[8,2]{0,1:T(2,128)} %bitcast.28), slice={[0:1], [0:1]} | slice | bytes 8 | tf_op jit(solution)/shard_map/slice | solution.py:368
  10.2 0.0 copy-start
  10.2 1.4 %copy-done = bf16[768,1024]{1,0:T(8,128)(2,1)S(1)} copy-done((bf16[768,1024]{1,0:T(8,128)(2,1)S(1)}, bf16[768,1024]{1,0:T(8,128)(2,1)}, u32[]{:S(2)}) %copy-start) | copy-done | bytes 1572888
  11.6 0.0 copy-start.1
  11.6 0.9 %copy-done.1 = bf16[1,128,1024]{2,1,0:T(8,128)(2,1)S(1)} copy-done((bf16[1,128,1024]{2,1,0:T(8,128)(2,1)S(1)}, bf16[1,128,1024]{2,1,0:T(8,128)(2,1)}, u32[]{:S(2)}) %copy-start.1) | copy-done | bytes 262168
  12.5 1.2 %shard_map.67 = (bf16[768,1024]{1,0:T(8,128)(2,1)S(1)}, bf16[128,768]{1,0:T(8,128)(2,1)S(1)}, bf16[16,128]{1,0:T(8,128)(2,1)}) custom-call(bf16[128,1024]{1,0:T(8,128)(2,1)S(1)} %bitcast.25, bf16[768,1024]{1,0:T(8,128)(2,1)S(1)} %copy-done), custom_call_target="tpu_custom_call" | custom-call | flops 201326592 | bytes 4194304 | tf_op jit(solution)/shard_map/pallas_call | solution.py:299
  13.7 4.6 %collective-permute-done.4.refs_1_.refs_3_ = bf16[128,1024]{1,0:T(8,128)(2,1)S(1)} collective-permute-done((bf16[128,1024]{1,0:T(8,128)(2,1)}, bf16[128,1024]{1,0:T(8,128)(2,1)S(1)}, u32[]{:S(2)}, u32[]{:S(2)}) %collective-permute-start.4) | collective-permute-done | bytes 262176 | tf_op jit(solution)/shard_map/ppermute | solution.py:318
  18.3 0.4 collective-permute-start.6
  18.7 0.0 collective-permute-done.5.refs_2_
  18.7 1.2 %shard_map.68.refs_0_ = bf16[384,768]{1,0:T(8,128)(2,1)S(1)} custom-call(bf16[128,768]{1,0:T(8,128)(2,1)S(1)} %get-tuple-element.48.refs_0_, bf16[128,1024]{1,0:T(8,128)(2,1)S(1)} %collective-permute-done.4.refs_1_.refs_3_, bf16[128,1024]{1,0:T(8,128)(2,1)S(1)} %collective-permute-done.5.refs_2_, bf16[768,1024]{1,0:T(8,128)(2,1)S(1)} %get-tuple-element.47.refs_3_.refs_5_.a_1_), custom_call_target="tpu_custom_call" | custom-call | flops 603979776 | bytes 4194304 | tf_op jit(solution)/shard_map/pallas_call | solution.py:299
  19.9 1.7 %collective-permute-start.7 = (bf16[128,256]{1,0:T(8,128)(2,1)S(1)}, bf16[128,256]{1,0:T(8,128)(2,1)S(1)}, u32[]{:S(2)}, u32[]{:S(2)}) collective-permute-start(bf16[128,256]{1,0:T(8,128)(2,1)S(1)} %get-tuple-element.53), channel_id=1, source_target_pairs={{0,8},{8,0},{16,24},{24,16},{1,9},{9,1},{17,25},{25,17},{2,10},{10... | collective-permute-start | bytes 196616 | tf_op jit(solution)/shard_map/ppermute | solution.py:318
  21.5 1.2 %collective-permute-start.8 = (bf16[128,256]{1,0:T(8,128)(2,1)S(1)}, bf16[128,256]{1,0:T(8,128)(2,1)S(1)}, u32[]{:S(2)}, u32[]{:S(2)}) collective-permute-start(bf16[128,256]{1,0:T(8,128)(2,1)S(1)} %get-tuple-element.54), channel_id=1, source_target_pairs={{0,16},{8,24},{16,0},{24,8},{1,17},{9,25},{17,1},{25,9},{2,18},{10... | collective-permute-start | bytes 196616 | tf_op jit(solution)/shard_map/ppermute | solution.py:318
  22.7 1.6 %collective-permute-start.9 = (bf16[128,256]{1,0:T(8,128)(2,1)S(1)}, bf16[128,256]{1,0:T(8,128)(2,1)S(1)}, u32[]{:S(2)}, u32[]{:S(2)}) collective-permute-start(bf16[128,256]{1,0:T(8,128)(2,1)S(1)} %get-tuple-element.55), channel_id=1, source_target_pairs={{0,24},{8,16},{16,8},{24,0},{1,25},{9,17},{17,9},{25,1},{2,26},{10... | collective-permute-start | bytes 196616 | tf_op jit(solution)/shard_map/ppermute | solution.py:318
  24.3 1.6 %collective-permute-done.6 = bf16[128,1024]{1,0:T(8,128)(2,1)S(1)} collective-permute-done((bf16[128,1024]{1,0:T(8,128)(2,1)S(1)}, bf16[128,1024]{1,0:T(8,128)(2,1)S(1)}, u32[]{:S(2)}, u32[]{:S(2)}) %collective-permute-start.6) | collective-permute-done | bytes 262176 | tf_op jit(solution)/shard_map/ppermute | solution.py:318
  26.0 0.0 copy-done.2
  26.0 3.0 %shard_map.69 = (bf16[4,512,512]{2,1,0:T(8,128)(2,1)S(1)}, f32[512,256]{1,0:T(8,128)S(1)}, bf16[512,1024]{1,0:T(8,128)(2,1)S(1)}, bf16[512,768]{1,0:T(8,128)(2,1)S(1)}) custom-call(bf16[384,768]{1,0:T(8,128)(2,1)S(1)} %shard_map.68.refs_0_, bf16[128,1024]{1,0:T(8,128)(2,1)S(1)} %bitcast.26, bf16[128,1024]{1,0:T(8,128)(2,1)S(1)} %collective-permute-done.5.refs_2_, ...), custom_call_target="tpu_custom_call" | custom-call | flops 268435456 | bytes 4194304 | tf_op jit(solution)/shard_map/pallas_call | solution.py:299
  29.0 0.0 collective-permute-done.7.a_3_
  29.0 0.0 collective-permute-done.8.a_4_
  29.0 0.5 collective-permute-done.9.a_5_
  29.5 1.7 %shard_map.71 = (bf16[384,512]{1,0:T(8,128)(2,1)S(1)}, bf16[384,1024]{1,0:T(8,128)(2,1)S(1)}) custom-call(s32[1]{0:T(128)} %bitcast.13.a_0_, bf16[512,768]{1,0:T(8,128)(2,1)S(1)} %get-tuple-element.51.a_1_, bf16[128,256]{1,0:T(8,128)(2,1)S(1)} %get-tuple-element.52.a_2_, bf16[128,256]{1,0:T(8,128)(2,1)S(1)} %collective-permute-done.7.a_3_, ...), custom_call_target="tpu_custom_call" | custom-call | flops 671088640 | bytes 4194304 | tf_op jit(solution)/shard_map/pallas_call | solution.py:299
  31.2 0.1 collective-permute-start.10
  31.2 1.2 %shard_map.70.grad_ref.a_3_ = bf16[384,512]{1,0:T(8,128)(2,1)S(1)} custom-call(s32[1]{0:T(128)} %bitcast.2.a_0_, bf16[512,768]{1,0:T(8,128)(2,1)S(1)} %get-tuple-element.51.a_1_, bf16[128,256]{1,0:T(8,128)(2,1)S(1)} %get-tuple-element.52.a_2_, bf16[128,256]{1,0:T(8,128)(2,1)S(1)} %collective-permute-done.7.a_3_, ...), custom_call_target="tpu_custom_call" | custom-call | flops 268435456 | bytes 4194304 | tf_op jit(solution)/shard_map/pallas_call | solution.py:299
  32.5 0.5 shard_map.74
  32.9 1.6 %collective-permute-start.11 = (bf16[128,1280]{1,0:T(8,128)(2,1)S(1)}, bf16[128,1280]{1,0:T(8,128)(2,1)S(1)}, u32[]{:S(2)}, u32[]{:S(2)}) collective-permute-start(bf16[128,1280]{1,0:T(8,128)(2,1)S(1)} %shard_map.74), channel_id=1, source_target_pairs={{0,8},{8,0},{16,24},{24,16},{1,9},{9,1},{17,25},{25,17},{2,10},{10... | collective-permute-start | bytes 983048 | tf_op jit(solution)/shard_map/ppermute | solution.py:318
  34.6 0.0 collective-permute-done.10.got_ref
  34.6 0.6 shard_map.72
  35.2 1.6 %collective-permute-start.14 = (bf16[192,1024]{1,0:T(8,128)(2,1)S(1)}, bf16[192,1024]{1,0:T(8,128)(2,1)S(1)}, u32[]{:S(2)}, u32[]{:S(2)}) collective-permute-start(bf16[192,1024]{1,0:T(8,128)(2,1)S(1)} %get-tuple-element.59), channel_id=1, source_target_pairs={{0,2},{1,5},{2,0},{3,7},{4,6},{5,1},{6,4},{7,3},{8,10},{9,13},{10,... | collective-permute-start | bytes 1179656 | tf_op jit(solution)/shard_map/ppermute | solution.py:465
  36.8 0.5 collective-permute-start.15
  37.3 1.0 %shard_map.73 = (bf16[128,1280]{1,0:T(8,128)(2,1)S(1)}, bf16[128,1280]{1,0:T(8,128)(2,1)S(1)}, bf16[128,1280]{1,0:T(8,128)(2,1)S(1)}) custom-call(s32[1]{0:T(128)} %bitcast.2.a_0_, bf16[768,1024]{1,0:T(8,128)(2,1)S(1)} %get-tuple-element.47.refs_3_.refs_5_.a_1_, f32[512,256]{1,0:T(8,128)S(1)} %get-tuple-element.61.a_7_.a_2_, ...), custom_call_target="tpu_custom_call" | custom-call | flops 603979776 | bytes 4194304 | tf_op jit(solution)/shard_map/pallas_call | solution.py:299
  38.3 4.8 %collective-permute-done.11.ahead = bf16[128,1280]{1,0:T(8,128)(2,1)S(1)} collective-permute-done((bf16[128,1280]{1,0:T(8,128)(2,1)S(1)}, bf16[128,1280]{1,0:T(8,128)(2,1)S(1)}, u32[]{:S(2)}, u32[]{:S(2)}) %collective-permute-start.11) | collective-permute-done | bytes 327712 | tf_op jit(solution)/shard_map/ppermute | solution.py:318
  43.1 0.1 shard_map.75
  43.2 1.7 %collective-permute-start.13 = (bf16[128,1536]{1,0:T(8,128)(2,1)S(1)}, bf16[128,1536]{1,0:T(8,128)(2,1)S(1)}, u32[]{:S(2)}, u32[]{:S(2)}) collective-permute-start(bf16[128,1536]{1,0:T(8,128)(2,1)S(1)} %shard_map.75), channel_id=1, source_target_pairs={{0,16},{8,24},{16,0},{24,8},{1,17},{9,25},{17,1},{25,9},{2,18},{10... | collective-permute-start | bytes 1179656 | tf_op jit(solution)/shard_map/ppermute | solution.py:318
  44.9 1.4 %collective-permute-start.12 = (bf16[128,1280]{1,0:T(8,128)(2,1)S(1)}, bf16[128,1280]{1,0:T(8,128)(2,1)S(1)}, u32[]{:S(2)}, u32[]{:S(2)}) collective-permute-start(bf16[128,1280]{1,0:T(8,128)(2,1)S(1)} %get-tuple-element.65), channel_id=1, source_target_pairs={{0,8},{8,0},{16,24},{24,16},{1,9},{9,1},{17,25},{25,17},{2,10},{10... | collective-permute-start | bytes 983048 | tf_op jit(solution)/shard_map/ppermute | solution.py:318
  46.3 0.0 collective-permute-done.14
  46.3 1.0 %collective-permute-done.15 = bf16[192,1024]{1,0:T(8,128)(2,1)S(1)} collective-permute-done((bf16[192,1024]{1,0:T(8,128)(2,1)S(1)}, bf16[192,1024]{1,0:T(8,128)(2,1)S(1)}, u32[]{:S(2)}, u32[]{:S(2)}) %collective-permute-start.15) | collective-permute-done | bytes 393248 | tf_op jit(solution)/shard_map/ppermute | solution.py:465
  47.3 15.1 %conditional.1 = (f32[768,1024]{1,0:T(8,128)}) conditional(s32[]{:T(128)} %convert_element_type.47, () %tuple.24, (s32[]{:T(128)}, bf16[192,1024]{1,0:T(8,128)(2,1)S(1)}, bf16[192,1024]{1,0:T(8,128)(2,1)S(1)}, bf16[192,1024]{1,0:T(8,128)(2,1)S(1)}, bf16[192,1024]{1,0:T(8,128)(2,1)S(1)}) %tuple.25), branch_computations={%region_1.2_spmd, %region_2.3_spmd} | conditional | flops 3145728 | bytes 13107368 | solution.py:482
  47.3 0.1 add_convert_fusion.3
  47.4 1.6 %collective-permute-start = (bf16[192,1024]{1,0:T(8,128)(2,1)S(1)}, bf16[192,1024]{1,0:T(8,128)(2,1)S(1)}, u32[]{:S(2)}, u32[]{:S(2)}) collective-permute-start(bf16[192,1024]{1,0:T(8,128)(2,1)S(1)} %add_convert_fusion.3), channel_id=1, source_target_pairs={{0,4},{1,3},{2,6},{3,1},{4,0},{5,7},{6,2},{7,5},{8,12},{9,11},{10,... | collective-permute-start | bytes 1179656 | tf_op jit(solution)/shard_map/cond/branch_1_fun/ppermute | solution.py:465
  49.0 0.1 add_convert_fusion.1
  49.1 0.6 collective-permute-start.2
  49.7 5.5 %collective-permute-done = bf16[192,1024]{1,0:T(8,128)(2,1)S(1)} collective-permute-done((bf16[192,1024]{1,0:T(8,128)(2,1)S(1)}, bf16[192,1024]{1,0:T(8,128)(2,1)S(1)}, u32[]{:S(2)}, u32[]{:S(2)}) %collective-permute-start) | collective-permute-done | bytes 393248 | tf_op jit(solution)/shard_map/cond/branch_1_fun/ppermute | solution.py:465
  55.2 0.1 add_convert_fusion.2.refs_0_
  55.4 0.1 collective-permute-start.1
  55.5 4.0 %collective-permute-done.2 = bf16[192,1024]{1,0:T(8,128)(2,1)S(1)} collective-permute-done((bf16[192,1024]{1,0:T(8,128)(2,1)S(1)}, bf16[192,1024]{1,0:T(8,128)(2,1)S(1)}, u32[]{:S(2)}, u32[]{:S(2)}) %collective-permute-start.2) | collective-permute-done | bytes 393248 | tf_op jit(solution)/shard_map/cond/branch_1_fun/ppermute | solution.py:465
  59.5 0.1 add_convert_fusion.refs_2_
  59.6 0.1 collective-permute-start.3
  59.7 0.0 collective-permute-done.1.refs_1_
  59.7 1.5 %branch_1_fun.2.refs_0_ = f32[768,1024]{1,0:T(8,128)} custom-call(s32[1]{0:T(128)} %bitcast.which, bf16[192,1024]{1,0:T(8,128)(2,1)S(1)} %add_convert_fusion.2.refs_0_, bf16[192,1024]{1,0:T(8,128)(2,1)S(1)} %collective-permute-done.1.refs_1_, bf16[192,1024]{1,0:T(8,128)(2,1)S(1)} %add_convert_fusion.refs_2_), custom_call_target="tpu_custom_call" | custom-call | bytes 1048576 | tf_op jit(solution)/shard_map/cond/branch_1_fun/pallas_call | solution.py:253
  61.2 0.2 collective-permute-done.3.refs_1_
  61.4 0.9 %branch_1_fun.3 = f32[768,1024]{1,0:T(8,128)} custom-call(s32[1]{0:T(128)} %bitcast.which, f32[768,1024]{1,0:T(8,128)} %branch_1_fun.2.refs_0_, bf16[192,1024]{1,0:T(8,128)(2,1)S(1)} %collective-permute-done.3.refs_1_), custom_call_target="tpu_custom_call", output_to_operand_aliasing={{}: (1, {})} | custom-call | bytes 1048576 | tf_op jit(solution)/shard_map/cond/branch_1_fun/pallas_call | solution.py:253
  62.3 0.0 collective-permute-done.12.a_2_
  62.3 1.0 %collective-permute-done.13.a_3_ = bf16[128,1536]{1,0:T(8,128)(2,1)S(1)} collective-permute-done((bf16[128,1536]{1,0:T(8,128)(2,1)S(1)}, bf16[128,1536]{1,0:T(8,128)(2,1)S(1)}, u32[]{:S(2)}, u32[]{:S(2)}) %collective-permute-start.13) | collective-permute-done | bytes 393248 | tf_op jit(solution)/shard_map/ppermute | solution.py:318
  63.3 0.8 %shard_map.76 = (bf16[128,1024]{1,0:T(8,128)(2,1)}, bf16[128,1024]{1,0:T(8,128)(2,1)}) custom-call(s32[1]{0:T(128)} %bitcast.1.a_0_, bf16[128,1280]{1,0:T(8,128)(2,1)S(1)} %get-tuple-element.68.a_1_, bf16[128,1280]{1,0:T(8,128)(2,1)S(1)} %collective-permute-done.12.a_2_, bf16[128,1536]{1,0:T(8,128)(2,1)S(1)} %collective-permute-done.13.a_3_), custom_call_target="tpu_custom_call" | custom-call | bytes 4194304 | tf_op jit(solution)/shard_map/pallas_call | solution.py:299
  (8 shorter events, 0.1 us)
Async XLA Ops:
  0.6 18.1 %collective-permute-start.5 = (bf16[128,1024]{1,0:T(8,128)(2,1)}, bf16[128,1024]{1,0:T(8,128)(2,1)S(1)}, u32[]{:S(2)}, u32[]{:S(2)}) collective-permute-start(bf16[128,1024]{1,0:T(8,128)(2,1)} %bitcast.23), channel_id=1, source_target_pairs={{0,8},{8,0},{16,24},{24,16},{1,9},{9,1},{17,25},{25,17},{2,10},{10... | collective-permute-start | bytes 786440 | tf_op jit(solution)/shard_map/ppermute | solution.py:318
  3.7 14.6 %collective-permute-start.4 = (bf16[128,1024]{1,0:T(8,128)(2,1)}, bf16[128,1024]{1,0:T(8,128)(2,1)S(1)}, u32[]{:S(2)}, u32[]{:S(2)}) collective-permute-start(bf16[128,1024]{1,0:T(8,128)(2,1)} %bitcast.24), channel_id=1, source_target_pairs={{0,16},{8,24},{16,0},{24,8},{1,17},{9,25},{17,1},{25,9},{2,18},{10... | collective-permute-start | bytes 786440 | tf_op jit(solution)/shard_map/ppermute | solution.py:318
  7.2 18.8 %copy-start.2 = (bf16[1,128,1024]{2,1,0:T(8,128)(2,1)S(1)}, bf16[1,128,1024]{2,1,0:T(8,128)(2,1)}, u32[]{:S(2)}) copy-start(bf16[1,128,1024]{2,1,0:T(8,128)(2,1)} %param.6) | copy-start | bytes 786436
  10.2 1.4 %copy-start = (bf16[768,1024]{1,0:T(8,128)(2,1)S(1)}, bf16[768,1024]{1,0:T(8,128)(2,1)}, u32[]{:S(2)}) copy-start(bf16[768,1024]{1,0:T(8,128)(2,1)} %weight.1) | copy-start | bytes 4718596
  11.6 0.9 %copy-start.1 = (bf16[1,128,1024]{2,1,0:T(8,128)(2,1)S(1)}, bf16[1,128,1024]{2,1,0:T(8,128)(2,1)}, u32[]{:S(2)}) copy-start(bf16[1,128,1024]{2,1,0:T(8,128)(2,1)} %param.6) | copy-start | bytes 786436
  18.3 7.6 %collective-permute-start.6 = (bf16[128,1024]{1,0:T(8,128)(2,1)S(1)}, bf16[128,1024]{1,0:T(8,128)(2,1)S(1)}, u32[]{:S(2)}, u32[]{:S(2)}) collective-permute-start(bf16[128,1024]{1,0:T(8,128)(2,1)S(1)} %collective-permute-done.4.refs_1_.refs_3_), channel_id=1, source_target_pairs={{0,8},{8,0},{16,24},{24,16},{1,9},{9,1},{17,25},{25,17},{2,10},{10... | collective-permute-start | bytes 786440 | tf_op jit(solution)/shard_map/ppermute | solution.py:318
  19.9 9.1 %collective-permute-start.7 = (bf16[128,256]{1,0:T(8,128)(2,1)S(1)}, bf16[128,256]{1,0:T(8,128)(2,1)S(1)}, u32[]{:S(2)}, u32[]{:S(2)}) collective-permute-start(bf16[128,256]{1,0:T(8,128)(2,1)S(1)} %get-tuple-element.53), channel_id=1, source_target_pairs={{0,8},{8,0},{16,24},{24,16},{1,9},{9,1},{17,25},{25,17},{2,10},{10... | collective-permute-start | bytes 196616 | tf_op jit(solution)/shard_map/ppermute | solution.py:318
  21.5 7.5 %collective-permute-start.8 = (bf16[128,256]{1,0:T(8,128)(2,1)S(1)}, bf16[128,256]{1,0:T(8,128)(2,1)S(1)}, u32[]{:S(2)}, u32[]{:S(2)}) collective-permute-start(bf16[128,256]{1,0:T(8,128)(2,1)S(1)} %get-tuple-element.54), channel_id=1, source_target_pairs={{0,16},{8,24},{16,0},{24,8},{1,17},{9,25},{17,1},{25,9},{2,18},{10... | collective-permute-start | bytes 196616 | tf_op jit(solution)/shard_map/ppermute | solution.py:318
  22.7 6.8 %collective-permute-start.9 = (bf16[128,256]{1,0:T(8,128)(2,1)S(1)}, bf16[128,256]{1,0:T(8,128)(2,1)S(1)}, u32[]{:S(2)}, u32[]{:S(2)}) collective-permute-start(bf16[128,256]{1,0:T(8,128)(2,1)S(1)} %get-tuple-element.55), channel_id=1, source_target_pairs={{0,24},{8,16},{16,8},{24,0},{1,25},{9,17},{17,9},{25,1},{2,26},{10... | collective-permute-start | bytes 196616 | tf_op jit(solution)/shard_map/ppermute | solution.py:318
  31.2 3.4 %collective-permute-start.10 = (bf16[384,1024]{1,0:T(8,128)(2,1)S(1)}, bf16[384,1024]{1,0:T(8,128)(2,1)S(1)}, u32[]{:S(2)}, u32[]{:S(2)}) collective-permute-start(bf16[384,1024]{1,0:T(8,128)(2,1)S(1)} %get-tuple-element.58), channel_id=1, source_target_pairs={{0,1},{1,0},{2,3},{3,2},{4,5},{5,4},{6,7},{7,6},{8,9},{9,8},{10,11... | collective-permute-start | bytes 2359304 | tf_op jit(solution)/shard_map/ppermute | solution.py:318
  32.9 10.2 %collective-permute-start.11 = (bf16[128,1280]{1,0:T(8,128)(2,1)S(1)}, bf16[128,1280]{1,0:T(8,128)(2,1)S(1)}, u32[]{:S(2)}, u32[]{:S(2)}) collective-permute-start(bf16[128,1280]{1,0:T(8,128)(2,1)S(1)} %shard_map.74), channel_id=1, source_target_pairs={{0,8},{8,0},{16,24},{24,16},{1,9},{9,1},{17,25},{25,17},{2,10},{10... | collective-permute-start | bytes 983048 | tf_op jit(solution)/shard_map/ppermute | solution.py:318
  35.2 11.1 %collective-permute-start.14 = (bf16[192,1024]{1,0:T(8,128)(2,1)S(1)}, bf16[192,1024]{1,0:T(8,128)(2,1)S(1)}, u32[]{:S(2)}, u32[]{:S(2)}) collective-permute-start(bf16[192,1024]{1,0:T(8,128)(2,1)S(1)} %get-tuple-element.59), channel_id=1, source_target_pairs={{0,2},{1,5},{2,0},{3,7},{4,6},{5,1},{6,4},{7,3},{8,10},{9,13},{10,... | collective-permute-start | bytes 1179656 | tf_op jit(solution)/shard_map/ppermute | solution.py:465
  36.8 10.5 %collective-permute-start.15 = (bf16[192,1024]{1,0:T(8,128)(2,1)S(1)}, bf16[192,1024]{1,0:T(8,128)(2,1)S(1)}, u32[]{:S(2)}, u32[]{:S(2)}) collective-permute-start(bf16[192,1024]{1,0:T(8,128)(2,1)S(1)} %get-tuple-element.60), channel_id=1, source_target_pairs={{0,2},{1,5},{2,0},{3,7},{4,6},{5,1},{6,4},{7,3},{8,10},{9,13},{10,... | collective-permute-start | bytes 1179656 | tf_op jit(solution)/shard_map/ppermute | solution.py:465
  43.2 20.1 %collective-permute-start.13 = (bf16[128,1536]{1,0:T(8,128)(2,1)S(1)}, bf16[128,1536]{1,0:T(8,128)(2,1)S(1)}, u32[]{:S(2)}, u32[]{:S(2)}) collective-permute-start(bf16[128,1536]{1,0:T(8,128)(2,1)S(1)} %shard_map.75), channel_id=1, source_target_pairs={{0,16},{8,24},{16,0},{24,8},{1,17},{9,25},{17,1},{25,9},{2,18},{10... | collective-permute-start | bytes 1179656 | tf_op jit(solution)/shard_map/ppermute | solution.py:318
  44.9 17.5 %collective-permute-start.12 = (bf16[128,1280]{1,0:T(8,128)(2,1)S(1)}, bf16[128,1280]{1,0:T(8,128)(2,1)S(1)}, u32[]{:S(2)}, u32[]{:S(2)}) collective-permute-start(bf16[128,1280]{1,0:T(8,128)(2,1)S(1)} %get-tuple-element.65), channel_id=1, source_target_pairs={{0,8},{8,0},{16,24},{24,16},{1,9},{9,1},{17,25},{25,17},{2,10},{10... | collective-permute-start | bytes 983048 | tf_op jit(solution)/shard_map/ppermute | solution.py:318
  47.4 7.8 %collective-permute-start = (bf16[192,1024]{1,0:T(8,128)(2,1)S(1)}, bf16[192,1024]{1,0:T(8,128)(2,1)S(1)}, u32[]{:S(2)}, u32[]{:S(2)}) collective-permute-start(bf16[192,1024]{1,0:T(8,128)(2,1)S(1)} %add_convert_fusion.3), channel_id=1, source_target_pairs={{0,4},{1,3},{2,6},{3,1},{4,0},{5,7},{6,2},{7,5},{8,12},{9,11},{10,... | collective-permute-start | bytes 1179656 | tf_op jit(solution)/shard_map/cond/branch_1_fun/ppermute | solution.py:465
  49.1 10.3 %collective-permute-start.2 = (bf16[192,1024]{1,0:T(8,128)(2,1)S(1)}, bf16[192,1024]{1,0:T(8,128)(2,1)S(1)}, u32[]{:S(2)}, u32[]{:S(2)}) collective-permute-start(bf16[192,1024]{1,0:T(8,128)(2,1)S(1)} %add_convert_fusion.1), channel_id=1, source_target_pairs={{0,4},{1,3},{2,6},{3,1},{4,0},{5,7},{6,2},{7,5},{8,12},{9,11},{10,... | collective-permute-start | bytes 1179656 | tf_op jit(solution)/shard_map/cond/branch_1_fun/ppermute | solution.py:465
  55.4 4.3 %collective-permute-start.1 = (bf16[192,1024]{1,0:T(8,128)(2,1)S(1)}, bf16[192,1024]{1,0:T(8,128)(2,1)S(1)}, u32[]{:S(2)}, u32[]{:S(2)}) collective-permute-start(bf16[192,1024]{1,0:T(8,128)(2,1)S(1)} %add_convert_fusion.2.refs_0_), channel_id=1, source_target_pairs={{0,1},{1,0},{2,3},{3,2},{4,5},{5,4},{6,7},{7,6},{8,9},{9,8},{10,11... | collective-permute-start | bytes 1179656 | tf_op jit(solution)/shard_map/cond/branch_1_fun/ppermute | solution.py:318
  59.6 1.8 %collective-permute-start.3 = (bf16[192,1024]{1,0:T(8,128)(2,1)S(1)}, bf16[192,1024]{1,0:T(8,128)(2,1)S(1)}, u32[]{:S(2)}, u32[]{:S(2)}) collective-permute-start(bf16[192,1024]{1,0:T(8,128)(2,1)S(1)} %add_convert_fusion.refs_2_), channel_id=1, source_target_pairs={{0,1},{1,0},{2,3},{3,2},{4,5},{5,4},{6,7},{7,6},{8,9},{9,8},{10,11... | collective-permute-start | bytes 1179656 | tf_op jit(solution)/shard_map/cond/branch_1_fun/ppermute | solution.py:318

commit v9 on v8

--- a/solution.py
+++ b/solution.py
@@ -120,8 +120,8 @@
 def forward_kernel(plan, *refs):
     n, rows = plan.n, plan.rows
     known, feats, (weight, key_bias, row_hot) = refs[0], refs[1 : 1 + n], refs[1 + n : 4 + n]
-    low_ref, sum_ref, full_ref, qkv = refs[4 + n : 8 + n]
-    q_s, k_s, v_s, ka_s = refs[-4:]
+    low_ref, sum_ref, full_ref, tiles_ref = refs[4 + n : 8 + n]
+    qkv, ka_s = refs[8 + n :]
     for s, x in enumerate(feats):
         full_ref[s * rows : (s + 1) * rows, :] = x[...]
     earlier = (n - 1) * rows
@@ -129,6 +129,8 @@
     qkv[earlier:, :] = mm(feats[-1][...], weight[...], NT).astype(BF16)
     for group in range(plan.groups):
         for t in range(plan.tiles):
+            tile = group * plan.tiles + t
+            q_s, k_s, v_s = (tiles_ref.at[3 * tile + i] for i in range(3))
             load_tile(plan, qkv, group, t, q_s, k_s, v_s)
             lanes = slice(plan.feature(group, t), plan.feature(group, t) + plan.tile)
             for h in range(plan.per_tile):
@@ -150,7 +152,7 @@
 def backward_kernel(plan, with_weight, *refs):
     n, rows, tile = plan.n, plan.rows, plan.tile
     group = refs[0][0] if plan.groups > 1 else 0
-    qkv, grads = refs[1], refs[2 : 2 + n]
+    tiles_ref, grads = refs[1], refs[2 : 2 + n]
     low_ref, sum_ref = refs[2 + n : 4 + n]
     at = 4 + n
     if with_weight:
@@ -161,13 +163,14 @@
     if with_weight:
         wgrad_ref = refs[at]
         at += 1
-    q_s, k_s, v_s, g_s, ds_s, dq_s = refs[at:]
+    k_s, g_s, ds_s, dq_s = refs[at:]
     for t in range(plan.tiles):
-        load_tile(plan, qkv, group, t, q_s, k_s, v_s)
+        index = 3 * (group * plan.tiles + t)
+        q_s, v_s = tiles_ref.at[index], tiles_ref.at[index + 2]
         feature = plan.feature(group, t)
         for s in range(n):
             g_s[s * rows : (s + 1) * rows, :] = grads[s][:, pl.ds(feature, tile)]
-        k_s[...] = (k_s[...].astype(F32) * HD ** -0.5).astype(BF16)
+        k_s[...] = (tiles_ref[index + 1].astype(F32) * HD ** -0.5).astype(BF16)
         q_t = q_s[...].T
         g_t = g_s[...].T
         for h in range(plan.per_tile):
@@ -384,17 +387,18 @@
     def tiles(count):
         return [pltpu.VMEM((nodes, plan.tile), BF16)] * count
 
-    low, sums, full, qkv = call(
+    low, sums, full, projected = call(
         forward_kernel,
         plan,
-        [array(heads, nodes, nodes), array(nodes, hcols, dtype=F32), array(nodes, width), array(nodes, plan.columns)],
-        tiles(3) + [pltpu.VMEM((nodes, 2 * HD), BF16)],
+        [array(heads, nodes, nodes), array(nodes, hcols, dtype=F32), array(nodes, width)]
+        + [array(3 * heads // plan.per_tile, nodes, plan.tile)],
+        [pltpu.VMEM((nodes, plan.columns), BF16), pltpu.VMEM((nodes, 2 * HD), BF16)],
         4 * nodes * nodes * HD * heads,
         [known, *xs, qkv_weight, key_bias, row_hot],
     )
-    scratch = tiles(4) + [pltpu.VMEM((nodes, nodes), BF16), pltpu.VMEM((nodes, plan.tile), F32)]
+    scratch = tiles(2) + [pltpu.VMEM((nodes, nodes), BF16), pltpu.VMEM((nodes, plan.tile), F32)]
     flops = 8 * nodes * nodes * HD * plan.gheads
-    common = [qkv, *grads, low, sums]
+    common = [projected, *grads, low, sums]
     grad_t = []
     if plan.groups > 1:
         grad_other, wgrad_other = call(
@@ -414,7 +418,7 @@
         [array(plan.gcols, nodes)],
         scratch,
         flops,
-        [core.reshape(1), qkv, *grads, low, sums],
+        [core.reshape(1), projected, *grads, low, sums],
         scalar=True,
     )
     grad_t = [grad_own, *grad_t]

time: 64.4 us -> 64.3 us (level)
  no operation moved by 1% of the time
where the time goes in v9:
time: 64.3 us; the launch traced here: 64 us
  waiting for transfers between devices  23.1 us (36%)
  starting transfers between devices  19.8 us (31%)
  Pallas kernels  13.5 us (21%)
  local copies, waits for them, and re-layouts  4.54 us (7%)
  other arithmetic  1.57 us (2%)
  between operations  1.47 us (2%)
    ppermute x12, starting transfers between devices, swap(): return lax.ppermute(x, axis, [(i, i ^ bits) for i in range(size)])  15.5 us
    ppermute x12, waiting for transfers between devices, swap(): return lax.ppermute(x, axis, [(i, i ^ bits) for i in range(size)])  12.6 us
    pallas_call x10, Pallas kernels, call(): pl.pallas_call(functools.partial(kernel, plan), out_shape=out_shape, in_s...  11.1 us
    ppermute x4, waiting for transfers between devices, across(): return lax.ppermute(x, 'clus', pairs)  10.5 us
    ppermute x4, starting transfers between devices, across(): return lax.ppermute(x, 'clus', pairs)  4.25 us
    pallas_call x2, Pallas kernels, scaled(): pl.pallas_call(functools.partial(scale_kernel, plan, m, places), out_shap...  2.42 us
    unnamed x6, local copies, waits for them, and re-layouts  2.36 us
  transfers between devices with their start and end apart: 16, of which 9 were waited for; matrix products, arithmetic and copies ran while one was open for 6% of the time, Pallas kernels for 17%

profile of v9, /device:TPU:0, one launch (start us, length us, event | category | flops | bytes accessed | tf_op | source)
XLA Modules:
  0.0 64.0 jit_solution(1055077925990112907)
XLA Ops:
  0.6 3.1 %collective-permute-start.5 = (bf16[128,1024]{1,0:T(8,128)(2,1)}, bf16[128,1024]{1,0:T(8,128)(2,1)S(1)}, u32[]{:S(2)}, u32[]{:S(2)}) collective-permute-start(bf16[128,1024]{1,0:T(8,128)(2,1)} %bitcast.23), channel_id=1, source_target_pairs={{0,8},{8,0},{16,24},{24,16},{1,9},{9,1},{17,25},{25,17},{2,10},{10... | collective-permute-start | bytes 786440 | tf_op jit(solution)/shard_map/ppermute | solution.py:321
  3.7 2.6 %collective-permute-start.4 = (bf16[128,1024]{1,0:T(8,128)(2,1)}, bf16[128,1024]{1,0:T(8,128)(2,1)S(1)}, u32[]{:S(2)}, u32[]{:S(2)}) collective-permute-start(bf16[128,1024]{1,0:T(8,128)(2,1)} %bitcast.24), channel_id=1, source_target_pairs={{0,16},{8,24},{16,0},{24,8},{1,17},{9,25},{17,1},{25,9},{2,18},{10... | collective-permute-start | bytes 786440 | tf_op jit(solution)/shard_map/ppermute | solution.py:321
  6.3 0.7 %broadcast_xor_fusion = s32[8,2]{0,1:T(2,128)S(1)} fusion(s32[]{:T(128)} %axis_index.23, s32[1,8,2]{1,2,0:T(2,128)} %param.8), kind=kLoop, calls=%fused_computation.24 | loop fusion | flops 16 | bytes 132 | tf_op jit(solution)/shard_map/xor | solution.py:377
  7.0 0.1 broadcast_compare_fusion
  7.1 0.1 compare_convert_fusion.refs_7_
  7.2 0.0 copy-start.2
  7.2 0.1 and_reduce_fusion
  7.3 1.0 %dynamic-slice_bitcast_fusion = (bf16[128,256]{1,0:T(8,128)(2,1)S(1)}, bf16[128,256]{1,0:T(8,128)(2,1)S(1)}, bf16[128,256]{1,0:T(8,128)(2,1)S(1)}, bf16[128,256]{1,0:T(8,128)(2,1)S(1)}) fusion(bf16[1,128,1024]{2,1,0:T(8,128)(2,1)} %param.9, s32[]{:T(128)S(6)} %select_n.82, s32[]{:T(128)S(6)} %select_n.80, s32[]{:T(128)S(6)} %select_n.79, s32[]{:T(128)S(6)} %select_n.81), kind=kLoop, calls=%fused_computation.6 | loop fusion | bytes 524304 | tf_op jit(solution)/shard_map/dynamic_slice | solution.py:344
  8.3 1.2 %slice.11 = s32[1,1]{0,1:T(1,128)} slice(s32[8,2]{0,1:T(2,128)} %bitcast.28), slice={[0:1], [0:1]} | slice | bytes 8 | tf_op jit(solution)/shard_map/slice | solution.py:371
  10.2 0.0 copy-start
  10.2 1.4 %copy-done = bf16[768,1024]{1,0:T(8,128)(2,1)S(1)} copy-done((bf16[768,1024]{1,0:T(8,128)(2,1)S(1)}, bf16[768,1024]{1,0:T(8,128)(2,1)}, u32[]{:S(2)}) %copy-start) | copy-done | bytes 1572888
  11.6 0.0 copy-start.1
  11.6 0.9 %copy-done.1 = bf16[1,128,1024]{2,1,0:T(8,128)(2,1)S(1)} copy-done((bf16[1,128,1024]{2,1,0:T(8,128)(2,1)S(1)}, bf16[1,128,1024]{2,1,0:T(8,128)(2,1)}, u32[]{:S(2)}) %copy-start.1) | copy-done | bytes 262168
  12.5 1.2 %shard_map.67 = (bf16[768,1024]{1,0:T(8,128)(2,1)S(1)}, bf16[128,768]{1,0:T(8,128)(2,1)S(1)}, bf16[16,128]{1,0:T(8,128)(2,1)}) custom-call(bf16[128,1024]{1,0:T(8,128)(2,1)S(1)} %bitcast.25, bf16[768,1024]{1,0:T(8,128)(2,1)S(1)} %copy-done), custom_call_target="tpu_custom_call" | custom-call | flops 201326592 | bytes 4194304 | tf_op jit(solution)/shard_map/pallas_call | solution.py:302
  13.7 4.6 %collective-permute-done.4.refs_1_.refs_3_ = bf16[128,1024]{1,0:T(8,128)(2,1)S(1)} collective-permute-done((bf16[128,1024]{1,0:T(8,128)(2,1)}, bf16[128,1024]{1,0:T(8,128)(2,1)S(1)}, u32[]{:S(2)}, u32[]{:S(2)}) %collective-permute-start.4) | collective-permute-done | bytes 262176 | tf_op jit(solution)/shard_map/ppermute | solution.py:321
  18.3 0.4 collective-permute-start.6
  18.7 0.0 collective-permute-done.5.refs_2_
  18.7 1.2 %shard_map.68.refs_0_ = bf16[384,768]{1,0:T(8,128)(2,1)S(1)} custom-call(bf16[128,768]{1,0:T(8,128)(2,1)S(1)} %get-tuple-element.48.refs_0_, bf16[128,1024]{1,0:T(8,128)(2,1)S(1)} %collective-permute-done.4.refs_1_.refs_3_, bf16[128,1024]{1,0:T(8,128)(2,1)S(1)} %collective-permute-done.5.refs_2_, bf16[768,1024]{1,0:T(8,128)(2,1)S(1)} %get-tuple-element.47.refs_3_.refs_5_.a_1_), custom_call_target="tpu_custom_call" | custom-call | flops 603979776 | bytes 4194304 | tf_op jit(solution)/shard_map/pallas_call | solution.py:302
  19.9 1.7 %collective-permute-start.7 = (bf16[128,256]{1,0:T(8,128)(2,1)S(1)}, bf16[128,256]{1,0:T(8,128)(2,1)S(1)}, u32[]{:S(2)}, u32[]{:S(2)}) collective-permute-start(bf16[128,256]{1,0:T(8,128)(2,1)S(1)} %get-tuple-element.53), channel_id=1, source_target_pairs={{0,8},{8,0},{16,24},{24,16},{1,9},{9,1},{17,25},{25,17},{2,10},{10... | collective-permute-start | bytes 196616 | tf_op jit(solution)/shard_map/ppermute | solution.py:321
  21.5 1.2 %collective-permute-start.8 = (bf16[128,256]{1,0:T(8,128)(2,1)S(1)}, bf16[128,256]{1,0:T(8,128)(2,1)S(1)}, u32[]{:S(2)}, u32[]{:S(2)}) collective-permute-start(bf16[128,256]{1,0:T(8,128)(2,1)S(1)} %get-tuple-element.54), channel_id=1, source_target_pairs={{0,16},{8,24},{16,0},{24,8},{1,17},{9,25},{17,1},{25,9},{2,18},{10... | collective-permute-start | bytes 196616 | tf_op jit(solution)/shard_map/ppermute | solution.py:321
  22.7 1.6 %collective-permute-start.9 = (bf16[128,256]{1,0:T(8,128)(2,1)S(1)}, bf16[128,256]{1,0:T(8,128)(2,1)S(1)}, u32[]{:S(2)}, u32[]{:S(2)}) collective-permute-start(bf16[128,256]{1,0:T(8,128)(2,1)S(1)} %get-tuple-element.55), channel_id=1, source_target_pairs={{0,24},{8,16},{16,8},{24,0},{1,25},{9,17},{17,9},{25,1},{2,26},{10... | collective-permute-start | bytes 196616 | tf_op jit(solution)/shard_map/ppermute | solution.py:321
  24.3 1.6 %collective-permute-done.6 = bf16[128,1024]{1,0:T(8,128)(2,1)S(1)} collective-permute-done((bf16[128,1024]{1,0:T(8,128)(2,1)S(1)}, bf16[128,1024]{1,0:T(8,128)(2,1)S(1)}, u32[]{:S(2)}, u32[]{:S(2)}) %collective-permute-start.6) | collective-permute-done | bytes 262176 | tf_op jit(solution)/shard_map/ppermute | solution.py:321
  26.0 0.0 copy-done.2
  26.0 3.0 %shard_map.69 = (bf16[4,512,512]{2,1,0:T(8,128)(2,1)S(1)}, f32[512,256]{1,0:T(8,128)S(1)}, bf16[512,1024]{1,0:T(8,128)(2,1)S(1)}, bf16[6,512,128]{2,1,0:T(8,128)(2,1)S(1)}) custom-call(bf16[384,768]{1,0:T(8,128)(2,1)S(1)} %shard_map.68.refs_0_, bf16[128,1024]{1,0:T(8,128)(2,1)S(1)} %bitcast.26, bf16[128,1024]{1,0:T(8,128)(2,1)S(1)} %collective-permute-done.5.refs_2_, ...), custom_call_target="tpu_custom_call" | custom-call | flops 268435456 | bytes 4194304 | tf_op jit(solution)/shard_map/pallas_call | solution.py:302
  29.0 0.0 collective-permute-done.7.a_3_
  29.0 0.0 collective-permute-done.8.a_4_
  29.0 0.5 collective-permute-done.9.a_5_
  29.5 1.6 %shard_map.71 = (bf16[384,512]{1,0:T(8,128)(2,1)S(1)}, bf16[384,1024]{1,0:T(8,128)(2,1)S(1)}) custom-call(s32[1]{0:T(128)} %bitcast.13.a_0_, bf16[6,512,128]{2,1,0:T(8,128)(2,1)S(1)} %get-tuple-element.51.a_1_, bf16[128,256]{1,0:T(8,128)(2,1)S(1)} %get-tuple-element.52.a_2_, bf16[128,256]{1,0:T(8,128)(2,1)S(1)} %collective-permute-done.7.a_3_, ...), custom_call_target="tpu_custom_call" | custom-call | flops 671088640 | bytes 4194304 | tf_op jit(solution)/shard_map/pallas_call | solution.py:302
  31.1 0.1 collective-permute-start.10
  31.2 1.2 %shard_map.70.grad_ref.a_3_ = bf16[384,512]{1,0:T(8,128)(2,1)S(1)} custom-call(s32[1]{0:T(128)} %bitcast.2.a_0_, bf16[6,512,128]{2,1,0:T(8,128)(2,1)S(1)} %get-tuple-element.51.a_1_, bf16[128,256]{1,0:T(8,128)(2,1)S(1)} %get-tuple-element.52.a_2_, bf16[128,256]{1,0:T(8,128)(2,1)S(1)} %collective-permute-done.7.a_3_, ...), custom_call_target="tpu_custom_call" | custom-call | flops 268435456 | bytes 4194304 | tf_op jit(solution)/shard_map/pallas_call | solution.py:302
  32.3 0.5 shard_map.74
  32.8 1.6 %collective-permute-start.11 = (bf16[128,1280]{1,0:T(8,128)(2,1)S(1)}, bf16[128,1280]{1,0:T(8,128)(2,1)S(1)}, u32[]{:S(2)}, u32[]{:S(2)}) collective-permute-start(bf16[128,1280]{1,0:T(8,128)(2,1)S(1)} %shard_map.74), channel_id=1, source_target_pairs={{0,8},{8,0},{16,24},{24,16},{1,9},{9,1},{17,25},{25,17},{2,10},{10... | collective-permute-start | bytes 983048 | tf_op jit(solution)/shard_map/ppermute | solution.py:321
  34.5 0.0 collective-permute-done.10.got_ref
  34.5 0.6 shard_map.72
  35.1 1.6 %collective-permute-start.14 = (bf16[192,1024]{1,0:T(8,128)(2,1)S(1)}, bf16[192,1024]{1,0:T(8,128)(2,1)S(1)}, u32[]{:S(2)}, u32[]{:S(2)}) collective-permute-start(bf16[192,1024]{1,0:T(8,128)(2,1)S(1)} %get-tuple-element.59), channel_id=1, source_target_pairs={{0,2},{1,5},{2,0},{3,7},{4,6},{5,1},{6,4},{7,3},{8,10},{9,13},{10,... | collective-permute-start | bytes 1179656 | tf_op jit(solution)/shard_map/ppermute | solution.py:469
  36.6 0.5 collective-permute-start.15
  37.2 1.0 %shard_map.73 = (bf16[128,1280]{1,0:T(8,128)(2,1)S(1)}, bf16[128,1280]{1,0:T(8,128)(2,1)S(1)}, bf16[128,1280]{1,0:T(8,128)(2,1)S(1)}) custom-call(s32[1]{0:T(128)} %bitcast.2.a_0_, bf16[768,1024]{1,0:T(8,128)(2,1)S(1)} %get-tuple-element.47.refs_3_.refs_5_.a_1_, f32[512,256]{1,0:T(8,128)S(1)} %get-tuple-element.61.a_7_.a_2_, ...), custom_call_target="tpu_custom_call" | custom-call | flops 603979776 | bytes 4194304 | tf_op jit(solution)/shard_map/pallas_call | solution.py:302
  38.2 4.8 %collective-permute-done.11.ahead = bf16[128,1280]{1,0:T(8,128)(2,1)S(1)} collective-permute-done((bf16[128,1280]{1,0:T(8,128)(2,1)S(1)}, bf16[128,1280]{1,0:T(8,128)(2,1)S(1)}, u32[]{:S(2)}, u32[]{:S(2)}) %collective-permute-start.11) | collective-permute-done | bytes 327712 | tf_op jit(solution)/shard_map/ppermute | solution.py:321
  43.0 0.1 shard_map.75
  43.1 1.7 %collective-permute-start.13 = (bf16[128,1536]{1,0:T(8,128)(2,1)S(1)}, bf16[128,1536]{1,0:T(8,128)(2,1)S(1)}, u32[]{:S(2)}, u32[]{:S(2)}) collective-permute-start(bf16[128,1536]{1,0:T(8,128)(2,1)S(1)} %shard_map.75), channel_id=1, source_target_pairs={{0,16},{8,24},{16,0},{24,8},{1,17},{9,25},{17,1},{25,9},{2,18},{10... | collective-permute-start | bytes 1179656 | tf_op jit(solution)/shard_map/ppermute | solution.py:321
  44.7 1.4 %collective-permute-start.12 = (bf16[128,1280]{1,0:T(8,128)(2,1)S(1)}, bf16[128,1280]{1,0:T(8,128)(2,1)S(1)}, u32[]{:S(2)}, u32[]{:S(2)}) collective-permute-start(bf16[128,1280]{1,0:T(8,128)(2,1)S(1)} %get-tuple-element.65), channel_id=1, source_target_pairs={{0,8},{8,0},{16,24},{24,16},{1,9},{9,1},{17,25},{25,17},{2,10},{10... | collective-permute-start | bytes 983048 | tf_op jit(solution)/shard_map/ppermute | solution.py:321
  46.2 0.0 collective-permute-done.14
  46.2 0.9 %collective-permute-done.15 = bf16[192,1024]{1,0:T(8,128)(2,1)S(1)} collective-permute-done((bf16[192,1024]{1,0:T(8,128)(2,1)S(1)}, bf16[192,1024]{1,0:T(8,128)(2,1)S(1)}, u32[]{:S(2)}, u32[]{:S(2)}) %collective-permute-start.15) | collective-permute-done | bytes 393248 | tf_op jit(solution)/shard_map/ppermute | solution.py:469
  47.1 15.1 %conditional.1 = (f32[768,1024]{1,0:T(8,128)}) conditional(s32[]{:T(128)} %convert_element_type.47, () %tuple.24, (s32[]{:T(128)}, bf16[192,1024]{1,0:T(8,128)(2,1)S(1)}, bf16[192,1024]{1,0:T(8,128)(2,1)S(1)}, bf16[192,1024]{1,0:T(8,128)(2,1)S(1)}, bf16[192,1024]{1,0:T(8,128)(2,1)S(1)}) %tuple.25), branch_computations={%region_1.2_spmd, %region_2.3_spmd} | conditional | flops 3145728 | bytes 13107368 | solution.py:486
  47.1 0.1 add_convert_fusion.3
  47.3 1.6 %collective-permute-start = (bf16[192,1024]{1,0:T(8,128)(2,1)S(1)}, bf16[192,1024]{1,0:T(8,128)(2,1)S(1)}, u32[]{:S(2)}, u32[]{:S(2)}) collective-permute-start(bf16[192,1024]{1,0:T(8,128)(2,1)S(1)} %add_convert_fusion.3), channel_id=1, source_target_pairs={{0,4},{1,3},{2,6},{3,1},{4,0},{5,7},{6,2},{7,5},{8,12},{9,11},{10,... | collective-permute-start | bytes 1179656 | tf_op jit(solution)/shard_map/cond/branch_1_fun/ppermute | solution.py:469
  48.9 0.1 add_convert_fusion.1
  49.0 0.6 collective-permute-start.2
  49.6 5.5 %collective-permute-done = bf16[192,1024]{1,0:T(8,128)(2,1)S(1)} collective-permute-done((bf16[192,1024]{1,0:T(8,128)(2,1)S(1)}, bf16[192,1024]{1,0:T(8,128)(2,1)S(1)}, u32[]{:S(2)}, u32[]{:S(2)}) %collective-permute-start) | collective-permute-done | bytes 393248 | tf_op jit(solution)/shard_map/cond/branch_1_fun/ppermute | solution.py:469
  55.1 0.1 add_convert_fusion.2.refs_0_
  55.3 0.1 collective-permute-start.1
  55.3 4.0 %collective-permute-done.2 = bf16[192,1024]{1,0:T(8,128)(2,1)S(1)} collective-permute-done((bf16[192,1024]{1,0:T(8,128)(2,1)S(1)}, bf16[192,1024]{1,0:T(8,128)(2,1)S(1)}, u32[]{:S(2)}, u32[]{:S(2)}) %collective-permute-start.2) | collective-permute-done | bytes 393248 | tf_op jit(solution)/shard_map/cond/branch_1_fun/ppermute | solution.py:469
  59.3 0.1 add_convert_fusion.refs_2_
  59.5 0.1 collective-permute-start.3
  59.5 0.0 collective-permute-done.1.refs_1_
  59.6 1.5 %branch_1_fun.2.refs_0_ = f32[768,1024]{1,0:T(8,128)} custom-call(s32[1]{0:T(128)} %bitcast.which, bf16[192,1024]{1,0:T(8,128)(2,1)S(1)} %add_convert_fusion.2.refs_0_, bf16[192,1024]{1,0:T(8,128)(2,1)S(1)} %collective-permute-done.1.refs_1_, bf16[192,1024]{1,0:T(8,128)(2,1)S(1)} %add_convert_fusion.refs_2_), custom_call_target="tpu_custom_call" | custom-call | bytes 1048576 | tf_op jit(solution)/shard_map/cond/branch_1_fun/pallas_call | solution.py:256
  61.0 0.2 collective-permute-done.3.refs_1_
  61.3 0.9 %branch_1_fun.3 = f32[768,1024]{1,0:T(8,128)} custom-call(s32[1]{0:T(128)} %bitcast.which, f32[768,1024]{1,0:T(8,128)} %branch_1_fun.2.refs_0_, bf16[192,1024]{1,0:T(8,128)(2,1)S(1)} %collective-permute-done.3.refs_1_), custom_call_target="tpu_custom_call", output_to_operand_aliasing={{}: (1, {})} | custom-call | bytes 1048576 | tf_op jit(solution)/shard_map/cond/branch_1_fun/pallas_call | solution.py:256
  62.2 0.0 collective-permute-done.12.a_2_
  62.2 1.0 %collective-permute-done.13.a_3_ = bf16[128,1536]{1,0:T(8,128)(2,1)S(1)} collective-permute-done((bf16[128,1536]{1,0:T(8,128)(2,1)S(1)}, bf16[128,1536]{1,0:T(8,128)(2,1)S(1)}, u32[]{:S(2)}, u32[]{:S(2)}) %collective-permute-start.13) | collective-permute-done | bytes 393248 | tf_op jit(solution)/shard_map/ppermute | solution.py:321
  63.2 0.8 %shard_map.76 = (bf16[128,1024]{1,0:T(8,128)(2,1)}, bf16[128,1024]{1,0:T(8,128)(2,1)}) custom-call(s32[1]{0:T(128)} %bitcast.1.a_0_, bf16[128,1280]{1,0:T(8,128)(2,1)S(1)} %get-tuple-element.68.a_1_, bf16[128,1280]{1,0:T(8,128)(2,1)S(1)} %collective-permute-done.12.a_2_, bf16[128,1536]{1,0:T(8,128)(2,1)S(1)} %collective-permute-done.13.a_3_), custom_call_target="tpu_custom_call" | custom-call | bytes 4194304 | tf_op jit(solution)/shard_map/pallas_call | solution.py:302
  (8 shorter events, 0.1 us)
Async XLA Ops:
  0.6 18.1 %collective-permute-start.5 = (bf16[128,1024]{1,0:T(8,128)(2,1)}, bf16[128,1024]{1,0:T(8,128)(2,1)S(1)}, u32[]{:S(2)}, u32[]{:S(2)}) collective-permute-start(bf16[128,1024]{1,0:T(8,128)(2,1)} %bitcast.23), channel_id=1, source_target_pairs={{0,8},{8,0},{16,24},{24,16},{1,9},{9,1},{17,25},{25,17},{2,10},{10... | collective-permute-start | bytes 786440 | tf_op jit(solution)/shard_map/ppermute | solution.py:321
  3.7 14.6 %collective-permute-start.4 = (bf16[128,1024]{1,0:T(8,128)(2,1)}, bf16[128,1024]{1,0:T(8,128)(2,1)S(1)}, u32[]{:S(2)}, u32[]{:S(2)}) collective-permute-start(bf16[128,1024]{1,0:T(8,128)(2,1)} %bitcast.24), channel_id=1, source_target_pairs={{0,16},{8,24},{16,0},{24,8},{1,17},{9,25},{17,1},{25,9},{2,18},{10... | collective-permute-start | bytes 786440 | tf_op jit(solution)/shard_map/ppermute | solution.py:321
  7.2 18.8 %copy-start.2 = (bf16[1,128,1024]{2,1,0:T(8,128)(2,1)S(1)}, bf16[1,128,1024]{2,1,0:T(8,128)(2,1)}, u32[]{:S(2)}) copy-start(bf16[1,128,1024]{2,1,0:T(8,128)(2,1)} %param.6) | copy-start | bytes 786436
  10.2 1.4 %copy-start = (bf16[768,1024]{1,0:T(8,128)(2,1)S(1)}, bf16[768,1024]{1,0:T(8,128)(2,1)}, u32[]{:S(2)}) copy-start(bf16[768,1024]{1,0:T(8,128)(2,1)} %weight.1) | copy-start | bytes 4718596
  11.6 0.9 %copy-start.1 = (bf16[1,128,1024]{2,1,0:T(8,128)(2,1)S(1)}, bf16[1,128,1024]{2,1,0:T(8,128)(2,1)}, u32[]{:S(2)}) copy-start(bf16[1,128,1024]{2,1,0:T(8,128)(2,1)} %param.6) | copy-start | bytes 786436
  18.3 7.6 %collective-permute-start.6 = (bf16[128,1024]{1,0:T(8,128)(2,1)S(1)}, bf16[128,1024]{1,0:T(8,128)(2,1)S(1)}, u32[]{:S(2)}, u32[]{:S(2)}) collective-permute-start(bf16[128,1024]{1,0:T(8,128)(2,1)S(1)} %collective-permute-done.4.refs_1_.refs_3_), channel_id=1, source_target_pairs={{0,8},{8,0},{16,24},{24,16},{1,9},{9,1},{17,25},{25,17},{2,10},{10... | collective-permute-start | bytes 786440 | tf_op jit(solution)/shard_map/ppermute | solution.py:321
  19.9 9.1 %collective-permute-start.7 = (bf16[128,256]{1,0:T(8,128)(2,1)S(1)}, bf16[128,256]{1,0:T(8,128)(2,1)S(1)}, u32[]{:S(2)}, u32[]{:S(2)}) collective-permute-start(bf16[128,256]{1,0:T(8,128)(2,1)S(1)} %get-tuple-element.53), channel_id=1, source_target_pairs={{0,8},{8,0},{16,24},{24,16},{1,9},{9,1},{17,25},{25,17},{2,10},{10... | collective-permute-start | bytes 196616 | tf_op jit(solution)/shard_map/ppermute | solution.py:321
  21.5 7.5 %collective-permute-start.8 = (bf16[128,256]{1,0:T(8,128)(2,1)S(1)}, bf16[128,256]{1,0:T(8,128)(2,1)S(1)}, u32[]{:S(2)}, u32[]{:S(2)}) collective-permute-start(bf16[128,256]{1,0:T(8,128)(2,1)S(1)} %get-tuple-element.54), channel_id=1, source_target_pairs={{0,16},{8,24},{16,0},{24,8},{1,17},{9,25},{17,1},{25,9},{2,18},{10... | collective-permute-start | bytes 196616 | tf_op jit(solution)/shard_map/ppermute | solution.py:321
  22.7 6.8 %collective-permute-start.9 = (bf16[128,256]{1,0:T(8,128)(2,1)S(1)}, bf16[128,256]{1,0:T(8,128)(2,1)S(1)}, u32[]{:S(2)}, u32[]{:S(2)}) collective-permute-start(bf16[128,256]{1,0:T(8,128)(2,1)S(1)} %get-tuple-element.55), channel_id=1, source_target_pairs={{0,24},{8,16},{16,8},{24,0},{1,25},{9,17},{17,9},{25,1},{2,26},{10... | collective-permute-start | bytes 196616 | tf_op jit(solution)/shard_map/ppermute | solution.py:321
  31.1 3.4 %collective-permute-start.10 = (bf16[384,1024]{1,0:T(8,128)(2,1)S(1)}, bf16[384,1024]{1,0:T(8,128)(2,1)S(1)}, u32[]{:S(2)}, u32[]{:S(2)}) collective-permute-start(bf16[384,1024]{1,0:T(8,128)(2,1)S(1)} %get-tuple-element.58), channel_id=1, source_target_pairs={{0,1},{1,0},{2,3},{3,2},{4,5},{5,4},{6,7},{7,6},{8,9},{9,8},{10,11... | collective-permute-start | bytes 2359304 | tf_op jit(solution)/shard_map/ppermute | solution.py:321
  32.8 10.2 %collective-permute-start.11 = (bf16[128,1280]{1,0:T(8,128)(2,1)S(1)}, bf16[128,1280]{1,0:T(8,128)(2,1)S(1)}, u32[]{:S(2)}, u32[]{:S(2)}) collective-permute-start(bf16[128,1280]{1,0:T(8,128)(2,1)S(1)} %shard_map.74), channel_id=1, source_target_pairs={{0,8},{8,0},{16,24},{24,16},{1,9},{9,1},{17,25},{25,17},{2,10},{10... | collective-permute-start | bytes 983048 | tf_op jit(solution)/shard_map/ppermute | solution.py:321
  35.1 11.1 %collective-permute-start.14 = (bf16[192,1024]{1,0:T(8,128)(2,1)S(1)}, bf16[192,1024]{1,0:T(8,128)(2,1)S(1)}, u32[]{:S(2)}, u32[]{:S(2)}) collective-permute-start(bf16[192,1024]{1,0:T(8,128)(2,1)S(1)} %get-tuple-element.59), channel_id=1, source_target_pairs={{0,2},{1,5},{2,0},{3,7},{4,6},{5,1},{6,4},{7,3},{8,10},{9,13},{10,... | collective-permute-start | bytes 1179656 | tf_op jit(solution)/shard_map/ppermute | solution.py:469
  36.6 10.5 %collective-permute-start.15 = (bf16[192,1024]{1,0:T(8,128)(2,1)S(1)}, bf16[192,1024]{1,0:T(8,128)(2,1)S(1)}, u32[]{:S(2)}, u32[]{:S(2)}) collective-permute-start(bf16[192,1024]{1,0:T(8,128)(2,1)S(1)} %get-tuple-element.60), channel_id=1, source_target_pairs={{0,2},{1,5},{2,0},{3,7},{4,6},{5,1},{6,4},{7,3},{8,10},{9,13},{10,... | collective-permute-start | bytes 1179656 | tf_op jit(solution)/shard_map/ppermute | solution.py:469
  43.1 20.1 %collective-permute-start.13 = (bf16[128,1536]{1,0:T(8,128)(2,1)S(1)}, bf16[128,1536]{1,0:T(8,128)(2,1)S(1)}, u32[]{:S(2)}, u32[]{:S(2)}) collective-permute-start(bf16[128,1536]{1,0:T(8,128)(2,1)S(1)} %shard_map.75), channel_id=1, source_target_pairs={{0,16},{8,24},{16,0},{24,8},{1,17},{9,25},{17,1},{25,9},{2,18},{10... | collective-permute-start | bytes 1179656 | tf_op jit(solution)/shard_map/ppermute | solution.py:321
  44.7 17.5 %collective-permute-start.12 = (bf16[128,1280]{1,0:T(8,128)(2,1)S(1)}, bf16[128,1280]{1,0:T(8,128)(2,1)S(1)}, u32[]{:S(2)}, u32[]{:S(2)}) collective-permute-start(bf16[128,1280]{1,0:T(8,128)(2,1)S(1)} %get-tuple-element.65), channel_id=1, source_target_pairs={{0,8},{8,0},{16,24},{24,16},{1,9},{9,1},{17,25},{25,17},{2,10},{10... | collective-permute-start | bytes 983048 | tf_op jit(solution)/shard_map/ppermute | solution.py:321
  47.3 7.8 %collective-permute-start = (bf16[192,1024]{1,0:T(8,128)(2,1)S(1)}, bf16[192,1024]{1,0:T(8,128)(2,1)S(1)}, u32[]{:S(2)}, u32[]{:S(2)}) collective-permute-start(bf16[192,1024]{1,0:T(8,128)(2,1)S(1)} %add_convert_fusion.3), channel_id=1, source_target_pairs={{0,4},{1,3},{2,6},{3,1},{4,0},{5,7},{6,2},{7,5},{8,12},{9,11},{10,... | collective-permute-start | bytes 1179656 | tf_op jit(solution)/shard_map/cond/branch_1_fun/ppermute | solution.py:469
  49.0 10.3 %collective-permute-start.2 = (bf16[192,1024]{1,0:T(8,128)(2,1)S(1)}, bf16[192,1024]{1,0:T(8,128)(2,1)S(1)}, u32[]{:S(2)}, u32[]{:S(2)}) collective-permute-start(bf16[192,1024]{1,0:T(8,128)(2,1)S(1)} %add_convert_fusion.1), channel_id=1, source_target_pairs={{0,4},{1,3},{2,6},{3,1},{4,0},{5,7},{6,2},{7,5},{8,12},{9,11},{10,... | collective-permute-start | bytes 1179656 | tf_op jit(solution)/shard_map/cond/branch_1_fun/ppermute | solution.py:469
  55.3 4.3 %collective-permute-start.1 = (bf16[192,1024]{1,0:T(8,128)(2,1)S(1)}, bf16[192,1024]{1,0:T(8,128)(2,1)S(1)}, u32[]{:S(2)}, u32[]{:S(2)}) collective-permute-start(bf16[192,1024]{1,0:T(8,128)(2,1)S(1)} %add_convert_fusion.2.refs_0_), channel_id=1, source_target_pairs={{0,1},{1,0},{2,3},{3,2},{4,5},{5,4},{6,7},{7,6},{8,9},{9,8},{10,11... | collective-permute-start | bytes 1179656 | tf_op jit(solution)/shard_map/cond/branch_1_fun/ppermute | solution.py:321
  59.5 1.8 %collective-permute-start.3 = (bf16[192,1024]{1,0:T(8,128)(2,1)S(1)}, bf16[192,1024]{1,0:T(8,128)(2,1)S(1)}, u32[]{:S(2)}, u32[]{:S(2)}) collective-permute-start(bf16[192,1024]{1,0:T(8,128)(2,1)S(1)} %add_convert_fusion.refs_2_), channel_id=1, source_target_pairs={{0,1},{1,0},{2,3},{3,2},{4,5},{5,4},{6,7},{7,6},{8,9},{9,8},{10,11... | collective-permute-start | bytes 1179656 | tf_op jit(solution)/shard_map/cond/branch_1_fun/ppermute | solution.py:321
